TPU v7x, 32 devices: a whole 2x2x4 slice. The times are simulated.
32 devices in a mesh: lon: 8 (over y, x, core), lat: 4 (over z).
Axes of the slice: x: 2, y: 2, z: 4, core: 2. Of those that a mesh axis runs over, the one named last changes fastest.
Arguments:
- field: bfloat16 [16, 8192, 128], P('lat', 'lon'), may hold values from -6 to 6
- conv_weight: bfloat16 [2, 3, 3, 3, 128, 128], replicated, may hold values from -0.1875 to 0.1875
- conv_bias: float32 [2, 3, 128], replicated, may hold values from -3 to 3
- spec_real: bfloat16 [2, 128, 128, 128], P(None, 'lon'), may hold values from -1.5 to 1.5
- spec_imag: bfloat16 [2, 128, 128, 128], P(None, 'lon'), may hold values from -1.5 to 1.5
Outputs:
- result: bfloat16 [16, 8192, 128], P('lat', 'lon')
All inputs are finite; a program needn't handle non-finite values.
Results may differ from a plain program's by a relative error of at most 0.0045.
Values may be sent and summed in bfloat16 or wider, within the bound.
No kernel may reach another device: no remote copies, remote signals or barrier semaphores. Data moves between devices by JAX's collectives and lax.ppermute only.
A program may use at most 64 MiB of HBM per device.

v0:
```python
import math

import jax
import jax.numpy as jnp
import ml_dtypes
import numpy as np
from jax import lax
from jax.experimental import pallas as pl
from jax.experimental.pallas import tpu as pltpu
from jax.sharding import PartitionSpec as P

BLOCKS = 2
CONVS = 3
PAD = 16
BF = jnp.bfloat16
F32 = jnp.float32
VMEM = pl.BlockSpec(memory_space=pltpu.VMEM)
PARAMS = pltpu.CompilerParams(vmem_limit_bytes=56 << 20)


def tile_of(width):
    best = 16
    for size in range(16, 400, 16):
        if width % size == 0:
            best = size
    return best


def build_weights(kernels, packed, layer):
    c = kernels.shape[-1]
    zero = jnp.zeros((c, c), BF)
    for tap in range(3):
        w0, w1, w2 = (kernels[layer, a, tap] for a in range(3))
        o = 2 * c * tap
        packed[layer, o : o + c, :c] = w0
        packed[layer, o : o + c, c:] = zero
        packed[layer, o + c : o + 2 * c, :c] = w1
        packed[layer, o + c : o + 2 * c, c:] = w0
        o = 6 * c + 2 * c * tap
        packed[layer, o : o + c, :c] = w2
        packed[layer, o : o + c, c:] = w1
        packed[layer, o + c : o + 2 * c, :c] = zero
        packed[layer, o + c : o + 2 * c, c:] = w2


def put_row(wide, pair, half, parts):
    c = wide.shape[2] // 6
    lanes = slice(2 * c + half * c, 2 * c + (half + 1) * c)
    for start, value in parts:
        wide[pair, start : start + value.shape[0], lanes] = value


def spread(wide, pair, line, tile):
    c2 = wide.shape[2] // 3
    for start in range(0, wide.shape[1], tile):
        wide[pair, start : start + tile, :c2] = line[pl.ds(start + 7, tile)].astype(BF)
        wide[pair, start : start + tile, 2 * c2 :] = line[pl.ds(start + 9, tile)].astype(BF)


def clear_line(line):
    line[0:8] = jnp.zeros((8, line.shape[1]), F32)
    end = line.shape[0]
    line[end - 8 : end] = jnp.zeros((8, line.shape[1]), F32)


def conv_stack(first, second, line, packed, bias, edge, rows, emit):
    width = first.shape[1]
    c2 = first.shape[2] // 3
    tile = tile_of(width)
    top, bottom = edge[0:1], edge[1:2]
    one = jnp.ones_like(top)
    buffers = (first, second)
    for layer in range(CONVS):
        src, dst = buffers[layer % 2], buffers[(layer + 1) % 2]
        pairs = rows // 2 + 2 - layer
        both = jnp.concatenate([bias[layer : layer + 1]] * 2, axis=1)
        masks = {}
        if layer == 0:
            masks = {0: (top, top), pairs - 1: (bottom, bottom)}
        elif layer == 1:
            masks = {0: (top, one), pairs - 1: (one, bottom)}
        for pair in range(pairs):
            for start in range(0, width, tile):
                cells = slice(start, start + tile)
                left = jnp.concatenate([src[pair, cells], src[pair + 1, cells]], axis=1)
                y = jnp.dot(left, packed[layer], preferred_element_type=F32) + both
                y = 0.5 * y
                y = y * (1.0 + jnp.tanh(y))
                if pair in masks:
                    y = y * jnp.concatenate(masks[pair], axis=1)
                if layer == CONVS - 1:
                    emit(pair, start, y.astype(BF))
                else:
                    dst[pair, cells, c2 : 2 * c2] = y.astype(BF)
                    line[start + 8 : start + 8 + tile] = y
            if layer < CONVS - 1:
                spread(dst, pair, line, tile)


def transform(forward, held, pair, part):
    cells = forward.shape[1]
    c2 = held.shape[2]
    both = jnp.dot(forward[...], held[pair, PAD : PAD + cells], preferred_element_type=F32)
    modes2 = both.shape[0] // 2
    part[:, pair * c2 : (pair + 1) * c2] = (both[:modes2] + both[modes2:]).astype(BF)


def row_parts(row, rows, own, up, down, own_edge, up_edge, down_edge):
    if row < 0:
        body, edge, at = up, up_edge, row + 3
    elif row < rows:
        body, edge, at = own, own_edge, row
    else:
        body, edge, at = down, down_edge, row - rows
    cells = body.shape[1]
    return [(0, edge[at, :PAD]), (PAD, body[at]), (PAD + cells, edge[at, PAD:])]


def first_kernel(
    own, up, down, own_edge, up_edge, down_edge, kernels, bias, edge, forward,
    part, hidden, to_up, to_down, first, second, line, packed, held,
):
    rows, cells, c = own.shape
    width = cells + 2 * PAD
    tile = tile_of(width)
    for layer in range(CONVS):
        build_weights(kernels, packed, layer)
    clear_line(line)
    for pair in range(rows // 2 + 3):
        for half in range(2):
            parts = row_parts(
                2 * pair - 3 + half, rows, own, up, down, own_edge, up_edge, down_edge
            )
            put_row(first, pair, half, parts)
        line[8 : 8 + width] = first[pair, :, 2 * c : 4 * c].astype(F32)
        spread(first, pair, line, tile)

    def emit(pair, start, y):
        span = slice(start, start + tile)
        held[pair, span] = y
        for half in range(2):
            row = 2 * pair + half
            value = y[:, half * c : (half + 1) * c]
            hidden[row, span] = value
            if row < 3:
                to_down[row, span] = value
            if row >= rows - 3:
                to_up[row - (rows - 3), span] = value

    conv_stack(first, second, line, packed, bias, edge, rows, emit)
    for pair in range(rows // 2):
        transform(forward, held, pair, part)


def mix_kernel(gathered, turn, real, imag, *rest):
    outs, (spread_in, spread_out) = rest[:-2], rest[-2:]
    modes, c = real.shape[0], real.shape[1]
    summed = jnp.dot(turn[...], gathered[...], preferred_element_type=F32)
    summed = summed[: 2 * modes] + summed[2 * modes :]
    rows = summed.shape[1] // c
    for half in range(2):
        for row in range(rows):
            spread_in[pl.ds(half * rows + row, modes, stride=2 * rows), :] = summed[
                half * modes : (half + 1) * modes, row * c : (row + 1) * c
            ]
    sign = jnp.where(lax.broadcasted_iota(jnp.int32, (2 * rows, c), 0) < rows, -1.0, 1.0)
    for k in range(modes):
        wide = spread_in[2 * rows * k : 2 * rows * (k + 1)]
        high = wide.astype(BF)
        low = (wide - high.astype(F32)).astype(BF)
        both = jnp.concatenate([high, low], axis=0)
        weight = jnp.concatenate([real[k], imag[k]], axis=1)
        out = jnp.dot(both, weight, preferred_element_type=F32)
        out = out[: 2 * rows] + out[2 * rows :]
        turned = pltpu.roll(out[:, c:], rows, 0)
        spread_out[2 * rows * k : 2 * rows * (k + 1)] = out[:, :c] + sign * turned
    for half in range(2):
        for row in range(rows):
            value = spread_out[pl.ds(half * rows + row, modes, stride=2 * rows), :].astype(BF)
            span = slice(half * modes, (half + 1) * modes)
            outs[0][span, row * c : (row + 1) * c] = value
            if len(outs) > 1:
                if row < 3:
                    outs[2][span, row * c : (row + 1) * c] = value
                if row >= rows - 3:
                    at = row - (rows - 3)
                    outs[1][span, at * c : (at + 1) * c] = value


def middle_kernel(
    own, up, down, own_edge, up_edge, down_edge, hidden, from_up, from_down, mixed, inverse,
    kernels, bias, edge, forward, part, state, hidden_out,
    first, second, line, packed, held,
):
    rows, cells, c = own.shape
    width = cells + 2 * PAD
    tile = tile_of(width)
    for layer in range(CONVS):
        build_weights(kernels, packed, layer)
    clear_line(line)
    top, bottom = edge[0:1], edge[1:2]
    one = jnp.ones_like(top)

    def keep(row):
        return top if row < 0 else (one if row < rows else bottom)

    for pair in range(rows // 2 + 3):
        names = [2 * pair - 3, 2 * pair - 2]
        for half, row in enumerate(names):
            parts = row_parts(row, rows, own, up, down, own_edge, up_edge, down_edge)
            put_row(first, pair, half, parts)
        mask = jnp.concatenate([keep(row) for row in names], axis=1)
        for start in range(0, width, tile):
            span = slice(start, start + tile)
            old = first[pair, span, 2 * c : 4 * c].astype(F32)
            pieces = []
            for row in names:
                if row < 0:
                    pieces.append(from_up[row + 3, span])
                elif row < rows:
                    pieces.append(hidden[row, span])
                else:
                    pieces.append(from_down[row - rows, span])
            conv = jnp.concatenate(pieces, axis=1).astype(F32)
            wave = jnp.dot(
                inverse[span],
                mixed[:, 2 * c * pair : 2 * c * (pair + 1)],
                preferred_element_type=F32,
            )
            new = jnp.tanh(old + conv + wave)
            if min(names) < 0 or max(names) >= rows:
                new = new * mask
            first[pair, span, 2 * c : 4 * c] = new.astype(BF)
            line[start + 8 : start + 8 + tile] = new
        spread(first, pair, line, tile)
        for half, row in enumerate(names):
            if 0 <= row < rows:
                lanes = slice((2 + half) * c, (3 + half) * c)
                state[row] = first[pair, PAD : PAD + cells, lanes]

    def emit(pair, start, y):
        span = slice(start, start + tile)
        held[pair, span] = y
        for half in range(2):
            hidden_out[2 * pair + half, span] = y[:, half * c : (half + 1) * c]

    conv_stack(first, second, line, packed, bias, edge, rows, emit)
    for pair in range(rows // 2):
        transform(forward, held, pair, part)


def last_kernel(state, hidden, mixed, inverse, result):
    rows, cells, c = state.shape
    for pair in range(rows // 2):
        wave = jnp.dot(
            inverse[PAD : PAD + cells],
            mixed[:, 2 * c * pair : 2 * c * (pair + 1)],
            preferred_element_type=F32,
        )
        for half in range(2):
            row = 2 * pair + half
            total = state[row].astype(F32) + hidden[row, PAD : PAD + cells].astype(F32)
            total = total + wave[:, half * c : (half + 1) * c]
            result[row] = jnp.tanh(total).astype(BF)


def forward_table(cells, lon_total, modes, lon_size):
    waves = np.arange(modes)
    theta = (2 * np.pi / lon_total) * (np.outer(waves, np.arange(cells)) % lon_total)
    full = np.stack([np.cos(theta), -np.sin(theta)], 0)
    full = full.reshape(2, lon_size, modes // lon_size, cells).transpose(1, 0, 2, 3)
    full = full.reshape(2 * modes, cells).astype(np.float32)
    high = full.astype(ml_dtypes.bfloat16)
    low = (full - high.astype(np.float32)).astype(ml_dtypes.bfloat16)
    return np.concatenate([high, low], 0)


def turn_table(me, lon_size, local, scale):
    waves = me * local + jnp.arange(local, dtype=jnp.int32)
    source = jnp.arange(lon_size, dtype=jnp.int32)
    phase = (source[None, :] * waves[:, None] % lon_size).astype(F32)
    phase = phase * (2.0 * math.pi / lon_size)
    cos, sin = scale * jnp.cos(phase), scale * jnp.sin(phase)
    eye = jnp.eye(local, dtype=F32)
    cos, sin = cos[:, :, None] * eye[:, None, :], sin[:, :, None] * eye[:, None, :]
    real = jnp.stack([cos, sin], axis=2)
    imag = jnp.stack([-sin, cos], axis=2)
    full = jnp.concatenate([real, imag], axis=0).reshape(2 * local, lon_size * 2 * local)
    high = full.astype(BF)
    low = (full - high.astype(F32)).astype(BF)
    return jnp.concatenate([high, low], axis=0)


def inverse_table(first_cell, width, lon_total, modes, lon_size):
    column = jnp.arange(2 * modes, dtype=jnp.int32)
    local = modes // lon_size
    waves = column // (2 * local) * local + column % local
    imaginary = column // local % 2 == 1
    cells = first_cell + jnp.arange(width, dtype=jnp.int32)
    cells = (cells + lon_total) % lon_total
    product = cells[:, None] * waves[None, :] % lon_total
    theta = product.astype(F32) * (2.0 * math.pi / lon_total)
    weight = jnp.where(waves == 0, 1.0, 2.0).astype(F32)[None, :]
    return (jnp.where(imaginary[None, :], -jnp.sin(theta), jnp.cos(theta)) * weight).astype(BF)


def lat_moves(above, below):
    size = lax.axis_size("lat")
    up = [(i, i + 1) for i in range(size - 1)]
    down = [(i + 1, i) for i in range(size - 1)]
    return lax.ppermute(above, "lat", up), lax.ppermute(below, "lat", down)


def shape(*dims):
    return jax.ShapeDtypeStruct(dims, BF)


def conv_scratch(rows, width, c):
    return [
        pltpu.VMEM((rows // 2 + 3, width, 6 * c), BF),
        pltpu.VMEM((rows // 2 + 2, width, 6 * c), BF),
        pltpu.VMEM((width + 16, 2 * c), F32),
        pltpu.VMEM((CONVS, 12 * c, 2 * c), BF),
        pltpu.VMEM((rows // 2, width, 2 * c), BF),
    ]


def call(kernel, args, outs, scratch):
    return pl.pallas_call(
        kernel,
        out_shape=outs,
        in_specs=[VMEM] * len(args),
        out_specs=[VMEM] * len(outs),
        scratch_shapes=scratch,
        compiler_params=PARAMS,
    )(*args)


def per_device(field, conv_weight, conv_bias, spec_real, spec_imag):
    rows, cells, c = field.shape
    width = cells + 2 * PAD
    lon_size, lat_size = lax.axis_size("lon"), lax.axis_size("lat")
    lon_me, lat_me = lax.axis_index("lon"), lax.axis_index("lat")
    lon_total = cells * lon_size
    local = spec_real.shape[1]
    modes = local * lon_size

    up, down = lat_moves(field[rows - 3 :], field[:3])
    right = [(i, (i + 1) % lon_size) for i in range(lon_size)]
    left = [(j, i) for i, j in right]
    from_left = lax.ppermute(field[:, cells - PAD :], "lon", right)
    from_right = lax.ppermute(field[:, :PAD], "lon", left)
    own_edge = jnp.concatenate([from_left, from_right], axis=1)
    up_edge, down_edge = lat_moves(own_edge[rows - 3 :], own_edge[:3])

    forward = jnp.asarray(forward_table(cells, lon_total, modes, lon_size))
    turn = turn_table(lon_me, lon_size, local, 1.0 / lon_total)
    inverse = inverse_table(lon_me * cells - PAD, width, lon_total, modes, lon_size)
    flags = jnp.stack([lat_me > 0, lat_me < lat_size - 1]).astype(F32)
    edge = jnp.broadcast_to(flags[:, None], (2, c))

    pieces = (field, up, down, own_edge, up_edge, down_edge)
    part, hidden, to_up, to_down = call(
        first_kernel,
        pieces + (conv_weight[0], conv_bias[0], edge, forward),
        [
            shape(2 * modes, rows * c),
            shape(rows, width, c),
            shape(3, width, c),
            shape(3, width, c),
        ],
        conv_scratch(rows, width, c),
    )
    from_up, from_down = lat_moves(to_up, to_down)

    def mix(part, block, halo):
        chunks = part.reshape(lon_size, 2 * local, rows * c)
        chunks = lax.all_to_all(chunks, "lon", 0, 0)
        outs = [shape(2 * local, rows * c)]
        if halo:
            outs += [shape(2 * local, 3 * c)] * 2
        line = pltpu.VMEM((2 * rows * local, c), F32)
        got = call(
            mix_kernel,
            (chunks.reshape(2 * modes, rows * c), turn, spec_real[block], spec_imag[block]),
            outs,
            [line, line],
        )
        mixed = got[0]
        if halo:
            above, below = lat_moves(got[1], got[2])
            mixed = jnp.concatenate([above, mixed, below], axis=1)
        return lax.all_gather(mixed, "lon", axis=0, tiled=True)

    mixed = mix(part, 0, True)
    part, state, hidden = call(
        middle_kernel,
        pieces
        + (hidden, from_up, from_down, mixed, inverse)
        + (conv_weight[1], conv_bias[1], edge, forward),
        [shape(2 * modes, rows * c), shape(rows, cells, c), shape(rows, width, c)],
        conv_scratch(rows, width, c),
    )
    mixed = mix(part, 1, False)
    (result,) = call(last_kernel, (state, hidden, mixed, inverse), [shape(rows, cells, c)], [])
    return result


def solution(mesh):
    return jax.shard_map(
        per_device,
        mesh=mesh,
        in_specs=(
            P("lat", "lon", None),
            P(),
            P(),
            P(None, "lon", None, None),
            P(None, "lon", None, None),
        ),
        out_specs=P("lat", "lon", None),
        check_vma=False,
    )
```

profile of v0, /device:TPU:0, one launch (start us, length us, event | category | flops | bytes accessed | tf_op | source)
XLA Modules:
  0.0 133.2 jit_solution(2251847984782561685)
XLA Ops:
  0.0 1.3 %fusion.19 = (bf16[4,16,128]{2,1,0:T(8,128)(2,1)S(1)}, bf16[4,16,128]{2,1,0:T(8,128)(2,1)}) fusion(bf16[4,1024,128]{2,1,0:T(8,128)(2,1)} %own.3), kind=kLoop, calls=%fused_computation.64 | loop fusion | bytes 65536 | tf_op jit(solution)/shard_map/slice | solution.py:352
  1.3 3.3 %collective-permute-start.3 = (bf16[4,16,128]{2,1,0:T(8,128)(2,1)S(1)}, bf16[4,16,128]{2,1,0:T(8,128)(2,1)S(1)}, u32[]{:S(2)}, u32[]{:S(2)}) collective-permute-start(bf16[4,16,128]{2,1,0:T(8,128)(2,1)S(1)} %get-tuple-element.33), channel_id=1, source_target_pairs={{4,0},{8,4},{12,8},{16,12},{20,16},{24,20},{28,24},{0,28},{5,1},{9... | collective-permute-start | bytes 49160 | tf_op jit(solution)/shard_map/ppermute | solution.py:352
  4.7 0.0 collective-permute-start.2
  4.7 2.7 %fusion.20 = (bf16[3,1024,128]{2,1,0:T(8,128)(2,1)}, bf16[3,1024,128]{2,1,0:T(8,128)(2,1)}) fusion(bf16[4,1024,128]{2,1,0:T(8,128)(2,1)} %own.3), kind=kLoop, calls=%fused_computation.65 | loop fusion | bytes 3145728 | tf_op jit(solution)/shard_map/slice | solution.py:348
  7.4 1.3 collective-permute-start.1
  8.7 4.6 %collective-permute-start = (bf16[3,1024,128]{2,1,0:T(8,128)(2,1)}, bf16[3,1024,128]{2,1,0:T(8,128)(2,1)S(1)}, u32[]{:S(2)}, u32[]{:S(2)}) collective-permute-start(bf16[3,1024,128]{2,1,0:T(8,128)(2,1)} %get-tuple-element.36), channel_id=1, source_target_pairs={{0,1},{1,2},{2,3},{4,5},{5,6},{6,7},{8,9},{9,10},{10,11},{12,13},{... | collective-permute-start | bytes 2359304 | tf_op jit(solution)/shard_map/ppermute | solution.py:311
  13.3 0.6 fusion.14
  13.9 0.6 fusion.22
  14.5 0.6 add_select_fusion.1
  15.1 0.1 sine_multiply_fusion
  15.2 0.1 maximum_maximum_fusion
  15.3 0.1 copy.10
  15.4 1.3 slice_bitcast_fusion
  16.7 0.6 pad_maximum_fusion.1.turn
  17.3 0.0 collective-permute-done.2
  17.4 0.0 collective-permute-done.3
  17.4 1.3 collective-permute-start.5
  18.7 4.5 %collective-permute-start.4 = (bf16[3,32,128]{2,1,0:T(8,128)(2,1)S(1)}, bf16[3,32,128]{2,1,0:T(8,128)(2,1)S(1)}, u32[]{:S(2)}, u32[]{:S(2)}) collective-permute-start(bf16[3,32,128]{2,1,0:T(8,128)(2,1)S(1)} %get-tuple-element.38), channel_id=1, source_target_pairs={{0,1},{1,2},{2,3},{4,5},{5,6},{6,7},{8,9},{9,10},{10,11},{12,13},{... | collective-permute-start | bytes 73736 | tf_op jit(solution)/shard_map/ppermute | solution.py:311
  23.3 0.1 add_convert_fusion
  23.4 0.5 copy.18
  23.9 5.3 %collective-permute-done.5.down_edge = bf16[3,32,128]{2,1,0:T(8,128)(2,1)S(1)} collective-permute-done((bf16[3,32,128]{2,1,0:T(8,128)(2,1)S(1)}, bf16[3,32,128]{2,1,0:T(8,128)(2,1)S(1)}, u32[]{:S(2)}, u32[]{:S(2)}) %collective-permute-start.5) | collective-permute-done | bytes 24608 | tf_op jit(solution)/shard_map/ppermute | solution.py:311
  29.2 1.2 collective-permute-done.4.up_edge
  30.4 0.0 collective-permute-done.1.down
  30.4 0.7 broadcast_in_dim.15.edge
  31.1 0.2 copy-done
  31.3 0.3 copy-done.1
  31.6 13.3 %shard_map.64 = (bf16[256,512]{1,0:T(8,128)(2,1)}, bf16[4,1056,128]{2,1,0:T(8,128)(2,1)}, bf16[3,1056,128]{2,1,0:T(8,128)(2,1)}, bf16[3,1056,128]{2,1,0:T(8,128)(2,1)}) custom-call(bf16[4,1024,128]{2,1,0:T(8,128)(2,1)} %own.3, bf16[3,1024,128]{2,1,0:T(8,128)(2,1)} %copy-done.1, bf16[3,1024,128]{2,1,0:T(8,128)(2,1)} %copy-done, ...), custom_call_target="tpu_custom_call" | custom-call | tf_op jit(solution)/shard_map/pallas_call | solution.py:329
  44.9 3.6 %all-to-all-start = ((bf16[8,32,512]{2,1,0:T(8,128)(2,1)}), bf16[8,32,512]{2,1,0:T(8,128)(2,1)S(1)}, u32[]{:S(2)}, u32[]{:S(2)}) async-start(bf16[8,32,512]{2,1,0:T(8,128)(2,1)} %bitcast.28), calls=%async_computation | async-start | bytes 524288 | tf_op jit(solution)/shard_map/all_to_all | solution.py:378
  48.5 2.6 %slice_bitcast_fusion.2 = (bf16[16,128,128]{2,1,0:T(8,128)(2,1)}, bf16[16,128,128]{2,1,0:T(8,128)(2,1)}, bf16[16,128,128]{2,1,0:T(8,128)(2,1)}, bf16[16,128,128]{2,1,0:T(8,128)(2,1)}) fusion(bf16[2,16,128,128]{3,2,1,0:T(8,128)(2,1)S(1)} %copy-done.4, bf16[2,16,128,128]{3,2,1,0:T(8,128)(2,1)} %param.9), kind=kLoop, calls=%fused_computation.11 | loop fusion | bytes 4194304 | tf_op jit(solution)/shard_map/squeeze | solution.py:385
  51.1 4.4 %collective-permute-start.6 = (bf16[3,1056,128]{2,1,0:T(8,128)(2,1)}, bf16[3,1056,128]{2,1,0:T(8,128)(2,1)S(1)}, u32[]{:S(2)}, u32[]{:S(2)}) collective-permute-start(bf16[3,1056,128]{2,1,0:T(8,128)(2,1)} %get-tuple-element.16), channel_id=1, source_target_pairs={{0,1},{1,2},{2,3},{4,5},{5,6},{6,7},{8,9},{9,10},{10,11},{12,13},{... | collective-permute-start | bytes 2433032 | tf_op jit(solution)/shard_map/ppermute | solution.py:311
  55.5 1.3 collective-permute-start.7
  56.8 0.7 copy-done.3
  57.5 2.4 %shard_map.65 = (bf16[32,512]{1,0:T(8,128)(2,1)}, bf16[32,384]{1,0:T(8,128)(2,1)}, bf16[32,384]{1,0:T(8,128)(2,1)}) custom-call(bf16[256,512]{1,0:T(8,128)(2,1)} %bitcast.25, bf16[64,256]{1,0:T(8,128)(2,1)} %pad_maximum_fusion.1.turn, bf16[16,128,128]{2,1,0:T(8,128)(2,1)} %get-tuple-element.46.real, bf16[16,128,128]{2,1,0:T(8,128)(2,1)} %get-tuple-element.30.imag), custom_call_target="tpu_custom_call" | custom-call | tf_op jit(solution)/shard_map/pallas_call | solution.py:329
  59.9 4.5 %collective-permute-start.8 = (bf16[32,384]{1,0:T(8,128)(2,1)}, bf16[32,384]{1,0:T(8,128)(2,1)S(1)}, u32[]{:S(2)}, u32[]{:S(2)}) collective-permute-start(bf16[32,384]{1,0:T(8,128)(2,1)} %get-tuple-element.19), channel_id=1, source_target_pairs={{0,1},{1,2},{2,3},{4,5},{5,6},{6,7},{8,9},{9,10},{10,11},{12,13},{... | collective-permute-start | bytes 73736 | tf_op jit(solution)/shard_map/ppermute | solution.py:311
  64.5 1.3 collective-permute-start.9
  65.8 5.7 %multiply_convert_fusion.inverse = bf16[1056,256]{1,0:T(8,128)(2,1)} fusion(f32[256]{0:T(256)S(1)} %compare_select_fusion.2, s32[256]{0:T(256)S(1)} %copy-done.14, s32[1056]{0:T(1024)S(1)} %copy-done.10, pred[256]{0:T(512)(128)(4,1)S(1)} %fusion.18), kind=kLoop, calls=%fused_computation.8 | loop fusion | flops 4866048 | bytes 547200 | tf_op jit(solution)/shard_map/convert_element_type | solution.py:304
  71.4 0.6 copy.17
  72.0 2.0 %collective-permute-done.8 = bf16[32,384]{1,0:T(8,128)(2,1)S(1)} collective-permute-done((bf16[32,384]{1,0:T(8,128)(2,1)}, bf16[32,384]{1,0:T(8,128)(2,1)S(1)}, u32[]{:S(2)}, u32[]{:S(2)}) %collective-permute-start.8) | collective-permute-done | bytes 24608 | tf_op jit(solution)/shard_map/ppermute | solution.py:311
  74.1 4.2 %collective-permute-done.9 = bf16[32,384]{1,0:T(8,128)(2,1)S(1)} collective-permute-done((bf16[32,384]{1,0:T(8,128)(2,1)}, bf16[32,384]{1,0:T(8,128)(2,1)S(1)}, u32[]{:S(2)}, u32[]{:S(2)}) %collective-permute-start.9) | collective-permute-done | bytes 24608 | tf_op jit(solution)/shard_map/ppermute | solution.py:311
  78.2 0.8 pad_maximum_fusion
  79.0 11.5 %all_gather.6.mixed = bf16[256,1280]{1,0:T(8,128)(2,1)} all-gather(bf16[32,1280]{1,0:T(8,128)(2,1)S(1)} %pad_maximum_fusion), channel_id=1, replica_groups=mesh['lon'=8,'lat'=4] {'lon'}, dimensions={0}, use_global_device_ids=true | all-gather | bytes 737280 | tf_op jit(solution)/shard_map/all_gather | solution.py:393
  90.5 0.9 copy-done.5
  91.4 0.3 copy-done.6
  91.7 14.9 %shard_map.66 = (bf16[256,512]{1,0:T(8,128)(2,1)}, bf16[4,1024,128]{2,1,0:T(8,128)(2,1)}, bf16[4,1056,128]{2,1,0:T(8,128)(2,1)}) custom-call(bf16[4,1024,128]{2,1,0:T(8,128)(2,1)} %own.3, bf16[3,1024,128]{2,1,0:T(8,128)(2,1)} %copy-done.1, bf16[3,1024,128]{2,1,0:T(8,128)(2,1)} %copy-done, bf16[4,32,128]{2,1,0:T(8,128)(2,1)} %copy-done.7, ...), custom_call_target="tpu_custom_call" | custom-call | tf_op jit(solution)/shard_map/pallas_call | solution.py:329
  106.5 11.0 %all_to_all.10 = bf16[8,32,512]{2,1,0:T(8,128)(2,1)} all-to-all(bf16[8,32,512]{2,1,0:T(8,128)(2,1)} %bitcast.29), channel_id=1, replica_groups=mesh['lon'=8,'lat'=4] {'lon'}, dimensions={0} | all-to-all | bytes 524288 | tf_op jit(solution)/shard_map/all_to_all | solution.py:378
  117.5 2.3 %shard_map.67 = bf16[32,512]{1,0:T(8,128)(2,1)} custom-call(bf16[256,512]{1,0:T(8,128)(2,1)} %bitcast.26, bf16[64,256]{1,0:T(8,128)(2,1)} %pad_maximum_fusion.1.turn, bf16[16,128,128]{2,1,0:T(8,128)(2,1)} %get-tuple-element.47.real, bf16[16,128,128]{2,1,0:T(8,128)(2,1)} %get-tuple-element.29.imag), custom_call_target="tpu_custom_call" | custom-call | tf_op jit(solution)/shard_map/pallas_call | solution.py:329
  119.9 10.1 %all_gather.7.mixed = bf16[256,512]{1,0:T(8,128)(2,1)} all-gather(bf16[32,512]{1,0:T(8,128)(2,1)} %shard_map.67), channel_id=1, replica_groups=mesh['lon'=8,'lat'=4] {'lon'}, dimensions={0}, use_global_device_ids=true | all-gather | bytes 294912 | tf_op jit(solution)/shard_map/all_gather | solution.py:393
  130.0 3.2 %shard_map.68 = bf16[4,1024,128]{2,1,0:T(8,128)(2,1)} custom-call(bf16[4,1024,128]{2,1,0:T(8,128)(2,1)} %get-tuple-element.22.state, bf16[4,1056,128]{2,1,0:T(8,128)(2,1)} %get-tuple-element.23.hidden, bf16[256,512]{1,0:T(8,128)(2,1)} %all_gather.7.mixed, bf16[1056,256]{1,0:T(8,128)(2,1)} %multiply_convert_fusion.inverse), custom_call_target="tpu_custom_call" | custom-call | tf_op jit(solution)/shard_map/pallas_call | solution.py:329
  (38 shorter events, 0.1 us)
Async XLA Ops:
  1.3 16.0 %collective-permute-start.3 = (bf16[4,16,128]{2,1,0:T(8,128)(2,1)S(1)}, bf16[4,16,128]{2,1,0:T(8,128)(2,1)S(1)}, u32[]{:S(2)}, u32[]{:S(2)}) collective-permute-start(bf16[4,16,128]{2,1,0:T(8,128)(2,1)S(1)} %get-tuple-element.33), channel_id=1, source_target_pairs={{4,0},{8,4},{12,8},{16,12},{20,16},{24,20},{28,24},{0,28},{5,1},{9... | collective-permute-start | bytes 49160 | tf_op jit(solution)/shard_map/ppermute | solution.py:352
  4.7 9.3 %copy-start.13 = (f32[2,3,128]{2,0,1:T(2,128)S(1)}, f32[2,3,128]{2,0,1:T(2,128)}, u32[]{:S(2)}) copy-start(f32[2,3,128]{2,0,1:T(2,128)} %param.8) | copy-start | bytes 9220
  4.7 12.7 %collective-permute-start.2 = (bf16[4,16,128]{2,1,0:T(8,128)(2,1)}, bf16[4,16,128]{2,1,0:T(8,128)(2,1)S(1)}, u32[]{:S(2)}, u32[]{:S(2)}) collective-permute-start(bf16[4,16,128]{2,1,0:T(8,128)(2,1)} %get-tuple-element.34), channel_id=1, source_target_pairs={{0,4},{4,8},{8,12},{12,16},{16,20},{20,24},{24,28},{28,0},{1,5},{5... | collective-permute-start | bytes 49160 | tf_op jit(solution)/shard_map/ppermute | solution.py:351
  4.7 10.7 %copy-start.2 = (bf16[2,3,3,3,128,128]{5,4,3,2,1,0:T(8,128)(2,1)S(1)}, bf16[2,3,3,3,128,128]{5,4,3,2,1,0:T(8,128)(2,1)}, u32[]{:S(2)}) copy-start(bf16[2,3,3,3,128,128]{5,4,3,2,1,0:T(8,128)(2,1)} %param.7) | copy-start | bytes 5308420
  7.4 23.0 %collective-permute-start.1 = (bf16[3,1024,128]{2,1,0:T(8,128)(2,1)}, bf16[3,1024,128]{2,1,0:T(8,128)(2,1)S(1)}, u32[]{:S(2)}, u32[]{:S(2)}) collective-permute-start(bf16[3,1024,128]{2,1,0:T(8,128)(2,1)} %get-tuple-element.35), channel_id=1, source_target_pairs={{1,0},{2,1},{3,2},{5,4},{6,5},{7,6},{9,8},{10,9},{11,10},{13,12},{... | collective-permute-start | bytes 2359304 | tf_op jit(solution)/shard_map/ppermute | solution.py:311
  8.7 21.7 %collective-permute-start = (bf16[3,1024,128]{2,1,0:T(8,128)(2,1)}, bf16[3,1024,128]{2,1,0:T(8,128)(2,1)S(1)}, u32[]{:S(2)}, u32[]{:S(2)}) collective-permute-start(bf16[3,1024,128]{2,1,0:T(8,128)(2,1)} %get-tuple-element.36), channel_id=1, source_target_pairs={{0,1},{1,2},{2,3},{4,5},{5,6},{6,7},{8,9},{9,10},{10,11},{12,13},{... | collective-permute-start | bytes 2359304 | tf_op jit(solution)/shard_map/ppermute | solution.py:311
  15.4 8.0 %copy-start.12 = (f32[1,3,128]{2,0,1:T(1,128)S(1)}, f32[1,3,128]{2,0,1:T(1,128)}, u32[]{:S(2)}) copy-start(f32[1,3,128]{2,0,1:T(1,128)} %get-tuple-element.43) | copy-start | bytes 4612
  17.4 13.7 %copy-start.7 = (bf16[4,32,128]{2,1,0:T(8,128)(2,1)}, bf16[4,32,128]{2,1,0:T(8,128)(2,1)S(1)}, u32[]{:S(2)}) copy-start(bf16[4,32,128]{2,1,0:T(8,128)(2,1)S(1)} %constant_dynamic-update-slice_fusion.own_edge) | copy-start | bytes 98308
  17.4 11.8 %collective-permute-start.5 = (bf16[3,32,128]{2,1,0:T(8,128)(2,1)S(1)}, bf16[3,32,128]{2,1,0:T(8,128)(2,1)S(1)}, u32[]{:S(2)}, u32[]{:S(2)}) collective-permute-start(bf16[3,32,128]{2,1,0:T(8,128)(2,1)S(1)} %get-tuple-element.37), channel_id=1, source_target_pairs={{1,0},{2,1},{3,2},{5,4},{6,5},{7,6},{9,8},{10,9},{11,10},{13,12},{... | collective-permute-start | bytes 73736 | tf_op jit(solution)/shard_map/ppermute | solution.py:311
  18.7 11.7 %collective-permute-start.4 = (bf16[3,32,128]{2,1,0:T(8,128)(2,1)S(1)}, bf16[3,32,128]{2,1,0:T(8,128)(2,1)S(1)}, u32[]{:S(2)}, u32[]{:S(2)}) collective-permute-start(bf16[3,32,128]{2,1,0:T(8,128)(2,1)S(1)} %get-tuple-element.38), channel_id=1, source_target_pairs={{0,1},{1,2},{2,3},{4,5},{5,6},{6,7},{8,9},{9,10},{10,11},{12,13},{... | collective-permute-start | bytes 73736 | tf_op jit(solution)/shard_map/ppermute | solution.py:311
  29.2 1.9 %copy-start.8 = (bf16[3,32,128]{2,1,0:T(8,128)(2,1)}, bf16[3,32,128]{2,1,0:T(8,128)(2,1)S(1)}, u32[]{:S(2)}) copy-start(bf16[3,32,128]{2,1,0:T(8,128)(2,1)S(1)} %collective-permute-done.5.down_edge) | copy-start | bytes 73732
  30.4 0.7 copy-start.9
  30.4 0.9 copy-start
  30.4 1.2 copy-start.1
  31.6 16.9 %copy-start.4 = (bf16[2,16,128,128]{3,2,1,0:T(8,128)(2,1)S(1)}, bf16[2,16,128,128]{3,2,1,0:T(8,128)(2,1)}, u32[]{:S(2)}) copy-start(bf16[2,16,128,128]{3,2,1,0:T(8,128)(2,1)} %param.10) | copy-start | bytes 3145732
  44.9 12.0 %all-to-all-start = ((bf16[8,32,512]{2,1,0:T(8,128)(2,1)}), bf16[8,32,512]{2,1,0:T(8,128)(2,1)S(1)}, u32[]{:S(2)}, u32[]{:S(2)}) async-start(bf16[8,32,512]{2,1,0:T(8,128)(2,1)} %bitcast.28), calls=%async_computation | async-start | bytes 524288 | tf_op jit(solution)/shard_map/all_to_all | solution.py:378
  51.1 14.6 %copy-start.10 = (s32[1056]{0:T(1024)S(1)}, s32[1056]{0:T(1024)}, u32[]{:S(2)}) copy-start(s32[1056]{0:T(1024)} %add_select_fusion.1) | copy-start | bytes 12676
  51.1 14.7 %copy-start.14 = (s32[256]{0:T(256)S(1)}, s32[256]{0:T(256)}, u32[]{:S(2)}) copy-start(s32[256]{0:T(256)} %fusion.14) | copy-start | bytes 3076
  51.1 39.4 %collective-permute-start.6 = (bf16[3,1056,128]{2,1,0:T(8,128)(2,1)}, bf16[3,1056,128]{2,1,0:T(8,128)(2,1)S(1)}, u32[]{:S(2)}, u32[]{:S(2)}) collective-permute-start(bf16[3,1056,128]{2,1,0:T(8,128)(2,1)} %get-tuple-element.16), channel_id=1, source_target_pairs={{0,1},{1,2},{2,3},{4,5},{5,6},{6,7},{8,9},{9,10},{10,11},{12,13},{... | collective-permute-start | bytes 2433032 | tf_op jit(solution)/shard_map/ppermute | solution.py:311
  55.5 35.0 %collective-permute-start.7 = (bf16[3,1056,128]{2,1,0:T(8,128)(2,1)}, bf16[3,1056,128]{2,1,0:T(8,128)(2,1)S(1)}, u32[]{:S(2)}, u32[]{:S(2)}) collective-permute-start(bf16[3,1056,128]{2,1,0:T(8,128)(2,1)} %get-tuple-element.17), channel_id=1, source_target_pairs={{1,0},{2,1},{3,2},{5,4},{6,5},{7,6},{9,8},{10,9},{11,10},{13,12},{... | collective-permute-start | bytes 2433032 | tf_op jit(solution)/shard_map/ppermute | solution.py:311
  56.8 0.7 copy-start.3
  57.5 13.9 %copy-start.11 = (f32[1,3,128]{2,0,1:T(1,128)S(1)}, f32[1,3,128]{2,0,1:T(1,128)}, u32[]{:S(2)}) copy-start(f32[1,3,128]{2,0,1:T(1,128)} %get-tuple-element.42) | copy-start | bytes 4612
  59.9 14.1 %collective-permute-start.8 = (bf16[32,384]{1,0:T(8,128)(2,1)}, bf16[32,384]{1,0:T(8,128)(2,1)S(1)}, u32[]{:S(2)}, u32[]{:S(2)}) collective-permute-start(bf16[32,384]{1,0:T(8,128)(2,1)} %get-tuple-element.19), channel_id=1, source_target_pairs={{0,1},{1,2},{2,3},{4,5},{5,6},{6,7},{8,9},{9,10},{10,11},{12,13},{... | collective-permute-start | bytes 73736 | tf_op jit(solution)/shard_map/ppermute | solution.py:311
  64.5 13.8 %collective-permute-start.9 = (bf16[32,384]{1,0:T(8,128)(2,1)}, bf16[32,384]{1,0:T(8,128)(2,1)S(1)}, u32[]{:S(2)}, u32[]{:S(2)}) collective-permute-start(bf16[32,384]{1,0:T(8,128)(2,1)} %get-tuple-element.21), channel_id=1, source_target_pairs={{1,0},{2,1},{3,2},{5,4},{6,5},{7,6},{9,8},{10,9},{11,10},{13,12},{... | collective-permute-start | bytes 73736 | tf_op jit(solution)/shard_map/ppermute | solution.py:311
  90.5 0.9 copy-start.5
  90.5 1.2 copy-start.6
where the time goes:
time: 134 us; the launch traced here: 133 us
  Pallas kernels  36.1 us (27%)
  blocking collectives  32.6 us (24%)
  starting transfers between devices  30.2 us (23%)
  local copies, waits for them, and re-layouts  12.9 us (10%)
  waiting for transfers between devices  12.7 us (9%)
  other arithmetic  8.52 us (6%)
    pallas_call x5, Pallas kernels, call(): pl.pallas_call(kernel, out_shape=outs, in_specs=[VMEM] * len(args), out_s...  36.1 us
    ppermute x8, starting transfers between devices, lat_moves(): return (lax.ppermute(above, 'lat', up), lax.ppermute(below, 'lat', down))  23.2 us
    all_gather x2, blocking collectives, mix(): return lax.all_gather(mixed, 'lon', axis=0, tiled=True)  21.6 us
    ppermute x8, waiting for transfers between devices, lat_moves(): return (lax.ppermute(above, 'lat', up), lax.ppermute(below, 'lat', down))  12.7 us
    all_to_all x1, blocking collectives, mix(): chunks = lax.all_to_all(chunks, 'lon', 0, 0)  11 us
    convert_element_type x1, other arithmetic, inverse_table(): (jnp.where(imaginary[None, :], -jnp.sin(theta), jnp.cos(theta)) * weight)...  5.66 us
    all_to_all x1, starting transfers between devices, mix(): chunks = lax.all_to_all(chunks, 'lon', 0, 0)  3.6 us
    unnamed x33, local copies, waits for them, and re-layouts  3.49 us
  transfers between devices with their start and end apart: 11, of which 4 were waited for; matrix products, arithmetic and copies ran while one was open for 13% of the time, Pallas kernels for 2%

commit v1 on v0

v1 whole, which is shorter than its diff:
```python
import math

import jax
import jax.numpy as jnp
import ml_dtypes
import numpy as np
from jax import lax
from jax.experimental import pallas as pl
from jax.experimental.pallas import tpu as pltpu
from jax.sharding import PartitionSpec as P

BLOCKS = 2
CONVS = 3
PAD = 16
RUNS = 16
HALO = 3
WINOGRAD = True
BF = jnp.bfloat16
F32 = jnp.float32
VMEM = pl.BlockSpec(memory_space=pltpu.VMEM)
SMEM = pl.BlockSpec(memory_space=pltpu.SMEM)
PARAMS = pltpu.CompilerParams(vmem_limit_bytes=56 << 20)


def tile_of(tiles):
    return max(n for n in range(1, 12) if tiles % n == 0) * RUNS


def pack_row(line, wide, row):
    c = line.shape[1]
    run = line.shape[0] // RUNS
    for cell in range(run):
        lanes = slice(cell % 2 * c, (cell % 2 + 1) * c)
        at = RUNS * (cell // 2 + 1)
        wide[row, at : at + RUNS, lanes] = line[pl.ds(cell, RUNS, stride=run), :].astype(BF)


def close_row(wide, row):
    c = wide.shape[2] // 2
    end = wide.shape[1] - RUNS
    before = wide[row, end - RUNS : end, c:].astype(F32)
    wide[row, 0:RUNS, c:] = pltpu.roll(before, 1, 0).astype(BF)
    after = wide[row, RUNS : 2 * RUNS, :c].astype(F32)
    wide[row, end : end + RUNS, :c] = pltpu.roll(after, RUNS - 1, 0).astype(BF)


def build_weights(kernels, block, packed, layer):
    c = kernels.shape[-1]
    zero = jnp.zeros((c, c), BF)
    for tap in range(3):
        g0, g1, g2 = (kernels[block, layer, a, tap].astype(F32) for a in range(3))
        if WINOGRAD:
            outer = g0 + g2
            parts = (0.5 * g0, 0.25 * (outer + g1), 0.25 * (outer - g1), 0.5 * g2)
        else:
            parts = (0.5 * g0, 0.5 * g1, 0.5 * g2)
        for i, part in enumerate(parts):
            value = part.astype(BF)
            for cell in range(2):
                source = cell + tap - 1
                at = {0: 0, 1: c, 2: 2 * c, -1: 3 * c}[source]
                packed[layer, i, at : at + c, cell * c : (cell + 1) * c] = value
    for i in range(packed.shape[1]):
        packed[layer, i, 2 * c : 3 * c, :c] = zero
        packed[layer, i, 3 * c :, c:] = zero


def window(wide, row, start, size):
    c = wide.shape[2] // 2
    here = wide[row, start + RUNS : start + RUNS + size]
    after = wide[row, start + 2 * RUNS : start + 2 * RUNS + size, :c]
    before = wide[row, start : start + size, c:]
    return jnp.concatenate([here, after, before], axis=1)


def dot(a, b):
    return jnp.dot(a, b, preferred_element_type=F32)


def silu_of_half(half):
    return half + half * jnp.tanh(half)


def conv_pair(src, row, start, size, packed, layer):
    d = [window(src, row + i, start, size) for i in range(4)]
    if WINOGRAD:
        inputs = (d[0] - d[2], d[1] + d[2], d[2] - d[1], d[1] - d[3])
        m = [dot(x, packed[layer, i]) for i, x in enumerate(inputs)]
        return (m[1] + m[2]) + m[0], m[1] - m[2] - m[3]
    w = jnp.concatenate([packed[layer, i] for i in range(3)], axis=0)
    return tuple(dot(jnp.concatenate(d[i : i + 3], axis=1), w) for i in range(2))


def conv_stack(first, second, packed, bias, edge, rows, emit):
    width = first.shape[1] - 2 * RUNS
    tile = tile_of(width // RUNS)
    buffers = (first, second)
    for layer in range(CONVS):
        src, dst = buffers[layer % 2], buffers[(layer + 1) % 2]
        outs = rows + 2 * (CONVS - 1 - layer)
        halo = CONVS - 1 - layer
        both = 0.5 * jnp.concatenate([bias[layer : layer + 1]] * 2, axis=1)
        for pair in range(0, outs, 2):
            for start in range(0, width, tile):
                sums = conv_pair(src, pair, start, tile, packed, layer)
                for i, total in enumerate(sums):
                    row = pair + i - halo
                    y = silu_of_half(total + both)
                    if row < 0:
                        y = y * edge[0]
                    elif row >= rows:
                        y = y * edge[1]
                    if layer == CONVS - 1:
                        emit(row, start, y.astype(BF))
                    else:
                        dst[pair + i, start + RUNS : start + RUNS + tile] = y.astype(BF)
            if layer < CONVS - 1:
                for i in range(2):
                    close_row(dst, pair + i)


def transform(forward, leak, bias, held, part):
    rows, c = held.shape[0], held.shape[2] // 2
    half = 0.5 * bias[CONVS - 1 : CONVS]
    level = silu_of_half(half)
    for row in range(0, rows, 2):
        cells = [
            jnp.concatenate([held[row + i, :, e * c : (e + 1) * c] for i in range(2)], axis=1)
            for e in range(2)
        ]
        both = dot(forward[...], jnp.concatenate(cells, axis=0))
        modes2 = both.shape[0] // 2
        total = both[:modes2] + both[modes2:]
        total = total - leak[...] * jnp.concatenate([level, level], axis=1)
        part[:, row * c : (row + 2) * c] = total.astype(BF)


def first_kernel(
    own, up, down, own_edge, up_edge, down_edge, kernels, bias, edge, forward, leak,
    part, hidden, to_up, to_down, packed_field,
    first, second, line, packed, held,
):
    rows, cells, c = own.shape
    for layer in range(CONVS):
        build_weights(kernels, 0, packed, layer)
    for at in range(rows + 2 * HALO):
        row = at - HALO
        if row < 0:
            body, ends, source = up, up_edge, row + HALO
        elif row < rows:
            body, ends, source = own, own_edge, row
        else:
            body, ends, source = down, down_edge, row - rows
        line[at % 2, 0:PAD] = ends[source, :PAD].astype(F32)
        line[at % 2, PAD : PAD + cells] = body[source].astype(F32)
        line[at % 2, PAD + cells :] = ends[source, PAD:].astype(F32)
        pack_row(line.at[at % 2], first, at)
        close_row(first, at)
        packed_field[at] = first[at, RUNS : first.shape[1] - RUNS]

    def emit(row, start, y):
        span = slice(start, start + y.shape[0])
        held[row, span] = y
        hidden[row, span] = y
        if row < HALO:
            to_down[row, span] = y
        if row >= rows - HALO:
            to_up[row - (rows - HALO), span] = y

    conv_stack(first, second, packed, bias, edge, rows, emit)
    transform(forward, leak, bias, held, part)


def mix_kernel(gathered, turn, real, imag, bias, owner, *rest):
    outs, (spread_in, spread_out) = rest[:-2], rest[-2:]
    modes, c = real.shape[1], real.shape[2]
    summed = jnp.dot(turn[...], gathered[...], preferred_element_type=F32)
    summed = summed[: 2 * modes] + summed[2 * modes :]
    rows = summed.shape[1] // c
    level = owner[0] * silu_of_half(0.5 * bias[CONVS - 1 : CONVS])
    for half in range(2):
        for row in range(rows):
            spread_in[pl.ds(half * rows + row, modes, stride=2 * rows), :] = summed[
                half * modes : (half + 1) * modes, row * c : (row + 1) * c
            ]
    spread_in[0:rows] = spread_in[0:rows] + level
    sign = jnp.where(lax.broadcasted_iota(jnp.int32, (2 * rows, c), 0) < rows, -1.0, 1.0)
    for k in range(modes):
        wide = spread_in[2 * rows * k : 2 * rows * (k + 1)]
        high = wide.astype(BF)
        low = (wide - high.astype(F32)).astype(BF)
        both = jnp.concatenate([high, low], axis=0)
        weight = jnp.concatenate([real[0, k], imag[0, k]], axis=1)
        out = jnp.dot(both, weight, preferred_element_type=F32)
        out = out[: 2 * rows] + out[2 * rows :]
        turned = pltpu.roll(out[:, c:], rows, 0)
        spread_out[2 * rows * k : 2 * rows * (k + 1)] = out[:, :c] + sign * turned
    for half in range(2):
        for row in range(rows):
            value = spread_out[pl.ds(half * rows + row, modes, stride=2 * rows), :].astype(BF)
            span = slice(half * modes, (half + 1) * modes)
            outs[0][span, row * c : (row + 1) * c] = value
            if len(outs) > 1:
                if row < HALO:
                    outs[2][span, row * c : (row + 1) * c] = value
                if row >= rows - HALO:
                    at = row - (rows - HALO)
                    outs[1][span, at * c : (at + 1) * c] = value


def middle_kernel(
    packed_field, hidden, from_up, from_down, mixed, inverse,
    kernels, bias, edge, forward, leak,
    part, state, hidden_out,
    first, second, packed, held,
):
    rows, width, c = hidden.shape[0], hidden.shape[1], hidden.shape[2] // 2
    tile = tile_of(width // RUNS)
    for layer in range(CONVS):
        build_weights(kernels, 1, packed, layer)
    for at in range(0, rows + 2 * HALO, 2):
        lanes = slice(at * c, (at + 2) * c)
        for start in range(0, width, tile):
            span = slice(start, start + tile)
            waves = [dot(inverse[e, span], mixed[:, lanes]) for e in range(2)]
            for i in range(2):
                row = at + i - HALO
                if row < 0:
                    conv = from_up[row + HALO, span]
                elif row < rows:
                    conv = hidden[row, span]
                else:
                    conv = from_down[row - rows, span]
                wave = jnp.concatenate([w[:, i * c : (i + 1) * c] for w in waves], axis=1)
                new = packed_field[at + i, span].astype(F32) + conv.astype(F32) + wave
                new = jnp.tanh(new)
                if row < 0:
                    new = new * edge[0]
                elif row >= rows:
                    new = new * edge[1]
                new = new.astype(BF)
                first[at + i, start + RUNS : start + RUNS + tile] = new
                if 0 <= row < rows:
                    state[row, span] = new
        for i in range(2):
            close_row(first, at + i)

    def emit(row, start, y):
        span = slice(start, start + y.shape[0])
        held[row, span] = y
        hidden_out[row, span] = y

    conv_stack(first, second, packed, bias, edge, rows, emit)
    transform(forward, leak, bias, held, part)


def last_kernel(state, hidden, mixed, inverse, result, line):
    rows, width, c = state.shape[0], state.shape[1], state.shape[2] // 2
    cells = result.shape[1]
    run = 2 * width // RUNS
    for pair in range(0, rows, 2):
        waves = [dot(inverse[e], mixed[:, pair * c : (pair + 2) * c]) for e in range(2)]
        for i in range(2):
            row = pair + i
            for e in range(2):
                lanes = slice(e * c, (e + 1) * c)
                total = state[row, :, lanes].astype(F32) + hidden[row, :, lanes].astype(F32)
                total = jnp.tanh(total + waves[e][:, i * c : (i + 1) * c])
                for u in range(width // RUNS):
                    value = total[u * RUNS : (u + 1) * RUNS]
                    line[i, pl.ds(2 * u + e, RUNS, stride=run), :] = value
            result[row] = line[i, PAD : PAD + cells].astype(BF)


def cell_order(width):
    run = width // RUNS
    cell = np.arange(width // 2) // RUNS * 2 + np.arange(width // 2) % RUNS * run
    return np.stack([cell, cell + 1])


def forward_table(cells, lon_total, modes, lon_size):
    order = cell_order(cells + 2 * PAD).reshape(-1) - PAD
    inside = (order >= 0) & (order < cells)
    waves = np.arange(modes)
    theta = (2 * np.pi / lon_total) * (np.outer(waves, order) % lon_total)
    full = np.stack([np.cos(theta), -np.sin(theta)], 0) * inside
    full = full.reshape(2, lon_size, modes // lon_size, -1).transpose(1, 0, 2, 3)
    full = full.reshape(2 * modes, -1).astype(np.float32)
    leak = full.astype(np.float64).sum(1, keepdims=True).astype(np.float32)
    high = full.astype(ml_dtypes.bfloat16)
    low = (full - high.astype(np.float32)).astype(ml_dtypes.bfloat16)
    return np.concatenate([high, low], 0), leak


def turn_table(me, lon_size, local, scale):
    waves = me * local + jnp.arange(local, dtype=jnp.int32)
    source = jnp.arange(lon_size, dtype=jnp.int32)
    phase = (source[None, :] * waves[:, None] % lon_size).astype(F32)
    phase = phase * (2.0 * math.pi / lon_size)
    cos, sin = scale * jnp.cos(phase), scale * jnp.sin(phase)
    eye = jnp.eye(local, dtype=F32)
    cos, sin = cos[:, :, None] * eye[:, None, :], sin[:, :, None] * eye[:, None, :]
    real = jnp.stack([cos, sin], axis=2)
    imag = jnp.stack([-sin, cos], axis=2)
    full = jnp.concatenate([real, imag], axis=0).reshape(2 * local, lon_size * 2 * local)
    high = full.astype(BF)
    low = (full - high.astype(F32)).astype(BF)
    return jnp.concatenate([high, low], axis=0)


def inverse_table(first_cell, width, lon_total, modes, lon_size):
    column = np.arange(2 * modes)
    local = modes // lon_size
    waves = column // (2 * local) * local + column % local
    imaginary = column // local % 2 == 1
    cells = first_cell + lon_total + jnp.asarray(cell_order(width), jnp.int32)
    product = cells[:, :, None] % lon_total * waves.astype(np.int32) % lon_total
    theta = product.astype(F32) * (2.0 * math.pi / lon_total)
    weight = np.where(waves == 0, 1.0, 2.0).astype(np.float32)
    return (jnp.where(imaginary, -jnp.sin(theta), jnp.cos(theta)) * weight).astype(BF)


def lat_moves(above, below):
    size = lax.axis_size("lat")
    up = [(i, i + 1) for i in range(size - 1)]
    down = [(i + 1, i) for i in range(size - 1)]
    return lax.ppermute(above, "lat", up), lax.ppermute(below, "lat", down)


def shape(*dims):
    return jax.ShapeDtypeStruct(dims, BF)


def conv_scratch(rows, width, c):
    return [
        pltpu.VMEM((rows + 2 * HALO, width // 2 + 2 * RUNS, 2 * c), BF),
        pltpu.VMEM((rows + 2 * HALO - 2, width // 2 + 2 * RUNS, 2 * c), BF),
        pltpu.VMEM((CONVS, 4 if WINOGRAD else 3, 4 * c, 2 * c), BF),
        pltpu.VMEM((rows, width // 2, 2 * c), BF),
    ]


def call(kernel, args, outs, scratch, in_specs=None, grid=()):
    return pl.pallas_call(
        kernel,
        grid=grid,
        out_shape=outs,
        in_specs=in_specs or [VMEM] * len(args),
        out_specs=[VMEM] * len(outs),
        scratch_shapes=scratch,
        compiler_params=PARAMS,
    )(*args)


def per_device(field, conv_weight, conv_bias, spec_real, spec_imag):
    rows, cells, c = field.shape
    width = cells + 2 * PAD
    half = width // 2
    lon_size, lat_size = lax.axis_size("lon"), lax.axis_size("lat")
    lon_me, lat_me = lax.axis_index("lon"), lax.axis_index("lat")
    lon_total = cells * lon_size
    local = spec_real.shape[1]
    modes = local * lon_size

    above, below = field[rows - HALO :], field[:HALO]
    up, down = lat_moves(above, below)
    above, below, last, leading = lax.optimization_barrier(
        (above, below, field[:, cells - PAD :], field[:, :PAD])
    )
    right = [(i, (i + 1) % lon_size) for i in range(lon_size)]
    left = [(j, i) for i, j in right]
    from_left = lax.ppermute(last, "lon", right)
    from_right = lax.ppermute(leading, "lon", left)
    own_edge = jnp.concatenate([from_left, from_right], axis=1)
    up_edge, down_edge = lat_moves(own_edge[rows - HALO :], own_edge[:HALO])

    forward, leak = forward_table(cells, lon_total, modes, lon_size)
    forward, leak = jnp.asarray(forward), jnp.asarray(leak)
    turn = turn_table(lon_me, lon_size, local, 1.0 / lon_total)
    inverse = inverse_table(lon_me * cells - PAD, width, lon_total, modes, lon_size)
    edge = jnp.stack([lat_me > 0, lat_me < lat_size - 1]).astype(F32)
    owner = (lon_me == 0).astype(F32).reshape(1)
    up, turn, inverse, edge, owner = lax.optimization_barrier((up, turn, inverse, edge, owner))

    part, hidden, to_up, to_down, packed_field = call(
        first_kernel,
        (field, up, down, own_edge, up_edge, down_edge)
        + (conv_weight, conv_bias[0], edge, forward, leak),
        [
            shape(2 * modes, rows * c),
            shape(rows, half, 2 * c),
            shape(HALO, half, 2 * c),
            shape(HALO, half, 2 * c),
            shape(rows + 2 * HALO, half, 2 * c),
        ],
        (lambda s: s[:2] + [pltpu.VMEM((2, width, c), F32)] + s[2:])(conv_scratch(rows, width, c)),
        in_specs=[VMEM] * 8 + [SMEM] + [VMEM] * 2,
    )
    from_up, from_down = lat_moves(to_up, to_down)

    def mix(part, block, halo):
        chunks = part.reshape(lon_size, 2 * local, rows * c)
        chunks = lax.all_to_all(chunks, "lon", 0, 0)
        widths = [rows * c] + ([HALO * c] * 2 if halo else [])
        line = pltpu.VMEM((2 * rows * local, c), F32)
        weights = pl.BlockSpec((1, local, c, c), lambda i: (block, 0, 0, 0))
        got = call(
            mix_kernel,
            (chunks.reshape(2 * modes, rows * c), turn, spec_real, spec_imag)
            + (conv_bias[block], owner),
            [shape(2 * local, n) for n in widths],
            [line, line],
            in_specs=[VMEM, VMEM, weights, weights, VMEM, SMEM],
            grid=(1,),
        )
        mixed = got[0]
        if halo:
            above, below = lat_moves(got[1], got[2])
            mixed = jnp.concatenate([above, mixed, below], axis=1)
        return lax.all_gather(mixed, "lon", axis=0, tiled=True)

    mixed = mix(part, 0, True)
    part, state, hidden = call(
        middle_kernel,
        (packed_field, hidden, from_up, from_down, mixed, inverse)
        + (conv_weight, conv_bias[1], edge, forward, leak),
        [shape(2 * modes, rows * c), shape(rows, half, 2 * c), shape(rows, half, 2 * c)],
        conv_scratch(rows, width, c),
        in_specs=[VMEM] * 8 + [SMEM] + [VMEM] * 2,
    )
    mixed = mix(part, 1, False)
    (result,) = call(
        last_kernel,
        (state, hidden, mixed, inverse),
        [shape(rows, cells, c)],
        [pltpu.VMEM((2, width, c), F32)],
    )
    return result


def solution(mesh):
    return jax.shard_map(
        per_device,
        mesh=mesh,
        in_specs=(
            P("lat", "lon", None),
            P(),
            P(),
            P(None, "lon", None, None),
            P(None, "lon", None, None),
        ),
        out_specs=P("lat", "lon", None),
        check_vma=False,
    )
```

time: 134 us -> 122 us (0.910)
  blocking collectives: 32.6 us -> 42.4 us
  waiting for transfers between devices: 12.7 us -> 4.29 us
  local copies, waits for them, and re-layouts: 12.9 us -> 5.66 us
  starting transfers between devices: 30.2 us -> 26.8 us
  Pallas kernels: 36.1 us -> 33.9 us
    all_to_all x1 -> x2, blocking collectives: 11 us -> 21.9 us  [mix(): chunks = lax.all_to_all(chunks, 'lon', 0, 0)]
    ppermute x8, waiting for transfers between devices: 12.7 us -> 4.28 us  [lat_moves(): return (lax.ppermute(above, 'lat', up), lax.ppermute(below, 'lat', down))]
    squeeze x2 -> x0, local copies, waits for them, and re-layouts: 3.96 us -> none  [the longest x1 2.64 us: mix(): spec_imag[block]]
    all_to_all x1 -> x0, starting transfers between devices: 3.6 us -> none  [mix(): chunks = lax.all_to_all(chunks, 'lon', 0, 0)]
    pallas_call x5, Pallas kernels: 36.1 us -> 33.9 us  [call(): pl.pallas_call(kernel, grid=grid, out_shape=outs, in_specs=in_specs or [V...]
    slice x3, local copies, waits for them, and re-layouts: 4.09 us -> 2.28 us  [the longest x1 1.53 us: per_device(): above, below = (field[rows - HALO:], field[:HALO])]
    unnamed x33 -> x27, local copies, waits for them, and re-layouts: 3.49 us -> 3.31 us
  transfers between devices with their start and end apart: 11 -> 10, of which waited for: 4 -> 2; matrix products, arithmetic and copies ran while one was open for 13% -> 8% of each run, Pallas kernels for 2% -> 2%
where the time goes in v1:
time: 122 us; the launch traced here: 121 us
  blocking collectives  42.4 us (35%)
  Pallas kernels  33.9 us (28%)
  starting transfers between devices  26.8 us (22%)
  other arithmetic  7.88 us (6%)
  local copies, waits for them, and re-layouts  5.66 us (5%)
  waiting for transfers between devices  4.29 us (4%)
    pallas_call x5, Pallas kernels, call(): pl.pallas_call(kernel, grid=grid, out_shape=outs, in_specs=in_specs or [V...  33.9 us
    ppermute x8, starting transfers between devices, lat_moves(): return (lax.ppermute(above, 'lat', up), lax.ppermute(below, 'lat', down))  24.1 us
    all_to_all x2, blocking collectives, mix(): chunks = lax.all_to_all(chunks, 'lon', 0, 0)  21.9 us
    all_gather x2, blocking collectives, mix(): return lax.all_gather(mixed, 'lon', axis=0, tiled=True)  20.5 us
    convert_element_type x1, other arithmetic, inverse_table(): (jnp.where(imaginary, -jnp.sin(theta), jnp.cos(theta)) * weight).astype(BF)  5.65 us
    ppermute x8, waiting for transfers between devices, lat_moves(): return (lax.ppermute(above, 'lat', up), lax.ppermute(below, 'lat', down))  4.28 us
    unnamed x27, local copies, waits for them, and re-layouts  3.31 us
    ppermute x1, starting transfers between devices, per_device(): from_right = lax.ppermute(leading, 'lon', left)  2.64 us
  transfers between devices with their start and end apart: 10, of which 2 were waited for; matrix products, arithmetic and copies ran while one was open for 8% of the time, Pallas kernels for 2%

profile of v1, /device:TPU:0, one launch (start us, length us, event | category | flops | bytes accessed | tf_op | source)
XLA Modules:
  0.0 121.1 jit_solution(1012136445537600961)
XLA Ops:
  0.0 1.5 %fusion.13 = (bf16[3,1024,128]{2,1,0:T(8,128)(2,1)S(1)}, bf16[3,1024,128]{2,1,0:T(8,128)(2,1)S(1)}) fusion(bf16[4,1024,128]{2,1,0:T(8,128)(2,1)} %own.1), kind=kLoop, calls=%fused_computation.41 | loop fusion | bytes 3145728 | tf_op jit(solution)/shard_map/slice | solution.py:365
  1.5 0.0 copy-start.8
  1.6 1.3 %collective-permute-start.1 = (bf16[3,1024,128]{2,1,0:T(8,128)(2,1)S(1)}, bf16[3,1024,128]{2,1,0:T(8,128)(2,1)S(1)}, u32[]{:S(2)}, u32[]{:S(2)}) collective-permute-start(bf16[3,1024,128]{2,1,0:T(8,128)(2,1)S(1)} %get-tuple-element.45), channel_id=1, source_target_pairs={{1,0},{2,1},{3,2},{5,4},{6,5},{7,6},{9,8},{10,9},{11,10},{13,12},{... | collective-permute-start | bytes 2359304 | tf_op jit(solution)/shard_map/ppermute | solution.py:327
  2.9 5.6 %collective-permute-start = (bf16[3,1024,128]{2,1,0:T(8,128)(2,1)S(1)}, bf16[3,1024,128]{2,1,0:T(8,128)(2,1)S(1)}, u32[]{:S(2)}, u32[]{:S(2)}) collective-permute-start(bf16[3,1024,128]{2,1,0:T(8,128)(2,1)S(1)} %get-tuple-element.46), channel_id=1, source_target_pairs={{0,1},{1,2},{2,3},{4,5},{5,6},{6,7},{8,9},{9,10},{10,11},{12,13},{... | collective-permute-start | bytes 2359304 | tf_op jit(solution)/shard_map/ppermute | solution.py:327
  8.5 0.7 fusion.12
  9.2 0.0 collective-permute-start.2
  9.2 2.6 %collective-permute-start.3 = (bf16[4,16,128]{2,1,0:T(8,128)(2,1)S(1)}, bf16[4,16,128]{2,1,0:T(8,128)(2,1)S(1)}, u32[]{:S(2)}, u32[]{:S(2)}) collective-permute-start(bf16[4,16,128]{2,1,0:T(8,128)(2,1)S(1)} %get-tuple-element.25), channel_id=1, source_target_pairs={{4,0},{8,4},{12,8},{16,12},{20,16},{24,20},{28,24},{0,28},{5,1},{9... | collective-permute-start | bytes 49160 | tf_op jit(solution)/shard_map/ppermute | solution.py:373
  11.9 0.1 sine_multiply_fusion
  11.9 0.1 maximum_maximum_fusion
  12.1 0.1 copy.14
  12.1 0.0 copy-done.7
  12.2 0.0 copy-done.9
  12.2 5.6 %multiply_convert_fusion.inverse = bf16[2,528,256]{2,1,0:T(8,128)(2,1)} fusion(f32[256]{0:T(256)S(1)} %copy-done.9, s32[256]{0:T(256)S(1)} %copy-done.10, s32[2,528]{1,0:T(2,128)S(1)} %and_select_fusion, pred[256]{0:T(512)(128)(4,1)S(1)} %copy-done.11), kind=kLoop, calls=%fused_computation.8 | loop fusion | flops 4866048 | bytes 547200 | tf_op jit(solution)/shard_map/convert_element_type | solution.py:320
  17.9 0.6 pad_maximum_fusion.1.turn
  18.5 0.0 collective-permute-done.2
  18.5 0.0 collective-permute-done.3
  18.5 1.3 %collective-permute-start.5 = (bf16[3,32,128]{2,1,0:T(8,128)(2,1)S(1)}, bf16[3,32,128]{2,1,0:T(8,128)(2,1)S(1)}, u32[]{:S(2)}, u32[]{:S(2)}) collective-permute-start(bf16[3,32,128]{2,1,0:T(8,128)(2,1)S(1)} %get-tuple-element.47), channel_id=1, source_target_pairs={{1,0},{2,1},{3,2},{5,4},{6,5},{7,6},{9,8},{10,9},{11,10},{13,12},{... | collective-permute-start | bytes 73736 | tf_op jit(solution)/shard_map/ppermute | solution.py:327
  19.8 4.5 %collective-permute-start.4 = (bf16[3,32,128]{2,1,0:T(8,128)(2,1)S(1)}, bf16[3,32,128]{2,1,0:T(8,128)(2,1)S(1)}, u32[]{:S(2)}, u32[]{:S(2)}) collective-permute-start(bf16[3,32,128]{2,1,0:T(8,128)(2,1)S(1)} %get-tuple-element.48), channel_id=1, source_target_pairs={{0,1},{1,2},{2,3},{4,5},{5,6},{6,7},{8,9},{9,10},{10,11},{12,13},{... | collective-permute-start | bytes 73736 | tf_op jit(solution)/shard_map/ppermute | solution.py:327
  24.4 0.7 add_convert_fusion.edge
  25.0 0.6 copy.23
  25.6 0.0 collective-permute-done.up
  25.6 0.0 collective-permute-done.5.down_edge
  25.6 0.2 collective-permute-done.4.up_edge
  25.9 0.0 collective-permute-done.1.down
  25.9 0.6 copy-done.3
  26.5 0.0 copy-done.6
  26.5 0.3 copy-done.2
  26.8 12.8 %shard_map.109 = (bf16[256,512]{1,0:T(8,128)(2,1)}, bf16[4,528,256]{2,1,0:T(8,128)(2,1)}, bf16[3,528,256]{2,1,0:T(8,128)(2,1)}, bf16[3,528,256]{2,1,0:T(8,128)(2,1)}, bf16[10,528,256]{2,1,0:T(8,128)(2,1)}) custom-call(bf16[4,1024,128]{2,1,0:T(8,128)(2,1)} %own.1, bf16[3,1024,128]{2,1,0:T(8,128)(2,1)} %copy-done.3, bf16[3,1024,128]{2,1,0:T(8,128)(2,1)} %copy-done.2, ...), custom_call_target="tpu_custom_call" | custom-call | tf_op jit(solution)/shard_map/pallas_call | solution.py:344
  39.6 4.3 %collective-permute-start.6 = (bf16[3,528,256]{2,1,0:T(8,128)(2,1)}, bf16[3,528,256]{2,1,0:T(8,128)(2,1)S(1)}, u32[]{:S(2)}, u32[]{:S(2)}) collective-permute-start(bf16[3,528,256]{2,1,0:T(8,128)(2,1)} %get-tuple-element.29), channel_id=1, source_target_pairs={{0,1},{1,2},{2,3},{4,5},{5,6},{6,7},{8,9},{9,10},{10,11},{12,13},{... | collective-permute-start | bytes 2433032 | tf_op jit(solution)/shard_map/ppermute | solution.py:327
  43.9 1.3 %collective-permute-start.7 = (bf16[3,528,256]{2,1,0:T(8,128)(2,1)}, bf16[3,528,256]{2,1,0:T(8,128)(2,1)S(1)}, u32[]{:S(2)}, u32[]{:S(2)}) collective-permute-start(bf16[3,528,256]{2,1,0:T(8,128)(2,1)} %get-tuple-element.30), channel_id=1, source_target_pairs={{1,0},{2,1},{3,2},{5,4},{6,5},{7,6},{9,8},{10,9},{11,10},{13,12},{... | collective-permute-start | bytes 2433032 | tf_op jit(solution)/shard_map/ppermute | solution.py:327
  45.2 11.0 %all_to_all.10 = bf16[8,32,512]{2,1,0:T(8,128)(2,1)} all-to-all(bf16[8,32,512]{2,1,0:T(8,128)(2,1)} %bitcast.17), channel_id=1, replica_groups=mesh['lon'=8,'lat'=4] {'lon'}, dimensions={0} | all-to-all | bytes 524288 | tf_op jit(solution)/shard_map/all_to_all | solution.py:403
  56.2 2.4 %shard_map.110 = (bf16[32,512]{1,0:T(8,128)(2,1)}, bf16[32,384]{1,0:T(8,128)(2,1)}, bf16[32,384]{1,0:T(8,128)(2,1)}) custom-call(bf16[256,512]{1,0:T(8,128)(2,1)} %bitcast.14, bf16[64,256]{1,0:T(8,128)(2,1)} %pad_maximum_fusion.1.turn, bf16[2,16,128,128]{3,2,1,0:T(8,128)(2,1)} %real.3, bf16[2,16,128,128]{3,2,1,0:T(8,128)(2,1)} %imag.3, f32[3,128]{1,0:T(4,128)} %bitcast.20, ...), custom_call_target="tpu_custom_call" | custom-call | tf_op jit(solution)/shard_map/pallas_call | solution.py:344
  58.6 4.5 %collective-permute-start.8 = (bf16[32,384]{1,0:T(8,128)(2,1)}, bf16[32,384]{1,0:T(8,128)(2,1)S(1)}, u32[]{:S(2)}, u32[]{:S(2)}) collective-permute-start(bf16[32,384]{1,0:T(8,128)(2,1)} %get-tuple-element.34), channel_id=1, source_target_pairs={{0,1},{1,2},{2,3},{4,5},{5,6},{6,7},{8,9},{9,10},{10,11},{12,13},{... | collective-permute-start | bytes 73736 | tf_op jit(solution)/shard_map/ppermute | solution.py:327
  63.1 1.3 %collective-permute-start.9 = (bf16[32,384]{1,0:T(8,128)(2,1)}, bf16[32,384]{1,0:T(8,128)(2,1)S(1)}, u32[]{:S(2)}, u32[]{:S(2)}) collective-permute-start(bf16[32,384]{1,0:T(8,128)(2,1)} %get-tuple-element.36), channel_id=1, source_target_pairs={{1,0},{2,1},{3,2},{5,4},{6,5},{7,6},{9,8},{10,9},{11,10},{13,12},{... | collective-permute-start | bytes 73736 | tf_op jit(solution)/shard_map/ppermute | solution.py:327
  64.4 0.6 copy.22
  65.0 0.0 collective-permute-done.8
  65.0 4.0 %collective-permute-done.9 = bf16[32,384]{1,0:T(8,128)(2,1)S(1)} collective-permute-done((bf16[32,384]{1,0:T(8,128)(2,1)}, bf16[32,384]{1,0:T(8,128)(2,1)S(1)}, u32[]{:S(2)}, u32[]{:S(2)}) %collective-permute-start.9) | collective-permute-done | bytes 24608 | tf_op jit(solution)/shard_map/ppermute | solution.py:327
  69.0 0.8 pad_maximum_fusion
  69.8 10.4 %all_gather.6.mixed = bf16[256,1280]{1,0:T(8,128)(2,1)} all-gather(bf16[32,1280]{1,0:T(8,128)(2,1)S(1)} %pad_maximum_fusion), channel_id=1, replica_groups=mesh['lon'=8,'lat'=4] {'lon'}, dimensions={0}, use_global_device_ids=true | all-gather | bytes 737280 | tf_op jit(solution)/shard_map/all_gather | solution.py:420
  80.2 0.0 collective-permute-done.6.from_up
  80.2 0.0 collective-permute-done.7.from_down
  80.2 0.9 copy-done
  81.1 0.3 copy-done.1
  81.4 13.0 %shard_map.111 = (bf16[256,512]{1,0:T(8,128)(2,1)}, bf16[4,528,256]{2,1,0:T(8,128)(2,1)}, bf16[4,528,256]{2,1,0:T(8,128)(2,1)}) custom-call(bf16[10,528,256]{2,1,0:T(8,128)(2,1)} %get-tuple-element.27.packed_field, bf16[4,528,256]{2,1,0:T(8,128)(2,1)} %get-tuple-element.28.hidden, bf16[3,528,256]{2,1,0:T(8,128)(2,1)} %copy-done, ...), custom_call_target="tpu_custom_call" | custom-call | tf_op jit(solution)/shard_map/pallas_call | solution.py:344
  94.3 11.0 %all_to_all.11 = bf16[8,32,512]{2,1,0:T(8,128)(2,1)} all-to-all(bf16[8,32,512]{2,1,0:T(8,128)(2,1)} %bitcast.18), channel_id=1, replica_groups=mesh['lon'=8,'lat'=4] {'lon'}, dimensions={0} | all-to-all | bytes 524288 | tf_op jit(solution)/shard_map/all_to_all | solution.py:403
  105.3 2.3 %shard_map.112 = bf16[32,512]{1,0:T(8,128)(2,1)} custom-call(bf16[256,512]{1,0:T(8,128)(2,1)} %bitcast.15, bf16[64,256]{1,0:T(8,128)(2,1)} %pad_maximum_fusion.1.turn, bf16[2,16,128,128]{3,2,1,0:T(8,128)(2,1)} %real.3, bf16[2,16,128,128]{3,2,1,0:T(8,128)(2,1)} %imag.3, f32[3,128]{1,0:T(4,128)} %bitcast.22, f32[1]{0:T(128)} %bitcast.3.owner), custom_call_target="tpu_custom_call" | custom-call | tf_op jit(solution)/shard_map/pallas_call | solution.py:344
  107.7 10.1 %all_gather.7.mixed = bf16[256,512]{1,0:T(8,128)(2,1)} all-gather(bf16[32,512]{1,0:T(8,128)(2,1)} %shard_map.112), channel_id=1, replica_groups=mesh['lon'=8,'lat'=4] {'lon'}, dimensions={0}, use_global_device_ids=true | all-gather | bytes 294912 | tf_op jit(solution)/shard_map/all_gather | solution.py:420
  117.8 3.4 %shard_map.113 = bf16[4,1024,128]{2,1,0:T(8,128)(2,1)} custom-call(bf16[4,528,256]{2,1,0:T(8,128)(2,1)} %get-tuple-element.38.state, bf16[4,528,256]{2,1,0:T(8,128)(2,1)} %get-tuple-element.39.hidden, bf16[256,512]{1,0:T(8,128)(2,1)} %all_gather.7.mixed, bf16[2,528,256]{2,1,0:T(8,128)(2,1)} %multiply_convert_fusion.inverse), custom_call_target="tpu_custom_call" | custom-call | tf_op jit(solution)/shard_map/pallas_call | solution.py:344
  (25 shorter events, 0.1 us)
Async XLA Ops:
  0.0 12.1 %copy-start.7 = (s32[2,528]{1,0:T(2,128)S(1)}, s32[2,528]{1,0:T(2,128)}, u32[]{:S(2)}) copy-start(s32[2,528]{1,0:T(2,128)} %constant.76.clone) | copy-start | bytes 12676
  0.0 12.2 %copy-start.9 = (f32[256]{0:T(256)S(1)}, f32[256]{0:T(256)}, u32[]{:S(2)}) copy-start(f32[256]{0:T(256)} %constant.79.clone) | copy-start | bytes 3076
  0.0 12.2 %copy-start.10 = (s32[256]{0:T(256)S(1)}, s32[256]{0:T(256)}, u32[]{:S(2)}) copy-start(s32[256]{0:T(256)} %constant.77.clone) | copy-start | bytes 3076
  0.0 12.2 %copy-start.11 = (pred[256]{0:T(512)(128)(4,1)S(1)}, pred[256]{0:T(512)(128)(4,1)}, u32[]{:S(2)}) copy-start(pred[256]{0:T(512)(128)(4,1)} %constant.78.clone) | copy-start | bytes 772
  1.5 16.3 %copy-start.8 = (f32[2,3,128]{2,0,1:T(2,128)S(1)}, f32[2,3,128]{2,0,1:T(2,128)}, u32[]{:S(2)}) copy-start(f32[2,3,128]{2,0,1:T(2,128)} %param.13) | copy-start | bytes 9220
  1.6 24.3 %collective-permute-start.1 = (bf16[3,1024,128]{2,1,0:T(8,128)(2,1)S(1)}, bf16[3,1024,128]{2,1,0:T(8,128)(2,1)S(1)}, u32[]{:S(2)}, u32[]{:S(2)}) collective-permute-start(bf16[3,1024,128]{2,1,0:T(8,128)(2,1)S(1)} %get-tuple-element.45), channel_id=1, source_target_pairs={{1,0},{2,1},{3,2},{5,4},{6,5},{7,6},{9,8},{10,9},{11,10},{13,12},{... | collective-permute-start | bytes 2359304 | tf_op jit(solution)/shard_map/ppermute | solution.py:327
  2.9 22.8 %collective-permute-start = (bf16[3,1024,128]{2,1,0:T(8,128)(2,1)S(1)}, bf16[3,1024,128]{2,1,0:T(8,128)(2,1)S(1)}, u32[]{:S(2)}, u32[]{:S(2)}) collective-permute-start(bf16[3,1024,128]{2,1,0:T(8,128)(2,1)S(1)} %get-tuple-element.46), channel_id=1, source_target_pairs={{0,1},{1,2},{2,3},{4,5},{5,6},{6,7},{8,9},{9,10},{10,11},{12,13},{... | collective-permute-start | bytes 2359304 | tf_op jit(solution)/shard_map/ppermute | solution.py:327
  9.2 9.3 %collective-permute-start.2 = (bf16[4,16,128]{2,1,0:T(8,128)(2,1)S(1)}, bf16[4,16,128]{2,1,0:T(8,128)(2,1)S(1)}, u32[]{:S(2)}, u32[]{:S(2)}) collective-permute-start(bf16[4,16,128]{2,1,0:T(8,128)(2,1)S(1)} %get-tuple-element.24), channel_id=1, source_target_pairs={{0,4},{4,8},{8,12},{12,16},{16,20},{20,24},{24,28},{28,0},{1,5},{5... | collective-permute-start | bytes 49160 | tf_op jit(solution)/shard_map/ppermute | solution.py:372
  9.2 9.3 %collective-permute-start.3 = (bf16[4,16,128]{2,1,0:T(8,128)(2,1)S(1)}, bf16[4,16,128]{2,1,0:T(8,128)(2,1)S(1)}, u32[]{:S(2)}, u32[]{:S(2)}) collective-permute-start(bf16[4,16,128]{2,1,0:T(8,128)(2,1)S(1)} %get-tuple-element.25), channel_id=1, source_target_pairs={{4,0},{8,4},{12,8},{16,12},{20,16},{24,20},{28,24},{0,28},{5,1},{9... | collective-permute-start | bytes 49160 | tf_op jit(solution)/shard_map/ppermute | solution.py:373
  18.5 7.4 %copy-start.4 = (bf16[4,32,128]{2,1,0:T(8,128)(2,1)}, bf16[4,32,128]{2,1,0:T(8,128)(2,1)S(1)}, u32[]{:S(2)}) copy-start(bf16[4,32,128]{2,1,0:T(8,128)(2,1)S(1)} %constant_dynamic-update-slice_fusion.own_edge) | copy-start | bytes 98308
  18.5 7.1 %collective-permute-start.5 = (bf16[3,32,128]{2,1,0:T(8,128)(2,1)S(1)}, bf16[3,32,128]{2,1,0:T(8,128)(2,1)S(1)}, u32[]{:S(2)}, u32[]{:S(2)}) collective-permute-start(bf16[3,32,128]{2,1,0:T(8,128)(2,1)S(1)} %get-tuple-element.47), channel_id=1, source_target_pairs={{1,0},{2,1},{3,2},{5,4},{6,5},{7,6},{9,8},{10,9},{11,10},{13,12},{... | collective-permute-start | bytes 73736 | tf_op jit(solution)/shard_map/ppermute | solution.py:327
  19.8 6.1 %collective-permute-start.4 = (bf16[3,32,128]{2,1,0:T(8,128)(2,1)S(1)}, bf16[3,32,128]{2,1,0:T(8,128)(2,1)S(1)}, u32[]{:S(2)}, u32[]{:S(2)}) collective-permute-start(bf16[3,32,128]{2,1,0:T(8,128)(2,1)S(1)} %get-tuple-element.48), channel_id=1, source_target_pairs={{0,1},{1,2},{2,3},{4,5},{5,6},{6,7},{8,9},{9,10},{10,11},{12,13},{... | collective-permute-start | bytes 73736 | tf_op jit(solution)/shard_map/ppermute | solution.py:327
  25.6 0.9 copy-start.3
  25.6 0.9 copy-start.5
  25.9 0.7 copy-start.6
  25.9 0.9 copy-start.2
  39.6 40.5 %collective-permute-start.6 = (bf16[3,528,256]{2,1,0:T(8,128)(2,1)}, bf16[3,528,256]{2,1,0:T(8,128)(2,1)S(1)}, u32[]{:S(2)}, u32[]{:S(2)}) collective-permute-start(bf16[3,528,256]{2,1,0:T(8,128)(2,1)} %get-tuple-element.29), channel_id=1, source_target_pairs={{0,1},{1,2},{2,3},{4,5},{5,6},{6,7},{8,9},{9,10},{10,11},{12,13},{... | collective-permute-start | bytes 2433032 | tf_op jit(solution)/shard_map/ppermute | solution.py:327
  43.9 36.3 %collective-permute-start.7 = (bf16[3,528,256]{2,1,0:T(8,128)(2,1)}, bf16[3,528,256]{2,1,0:T(8,128)(2,1)S(1)}, u32[]{:S(2)}, u32[]{:S(2)}) collective-permute-start(bf16[3,528,256]{2,1,0:T(8,128)(2,1)} %get-tuple-element.30), channel_id=1, source_target_pairs={{1,0},{2,1},{3,2},{5,4},{6,5},{7,6},{9,8},{10,9},{11,10},{13,12},{... | collective-permute-start | bytes 2433032 | tf_op jit(solution)/shard_map/ppermute | solution.py:327
  58.6 6.4 %collective-permute-start.8 = (bf16[32,384]{1,0:T(8,128)(2,1)}, bf16[32,384]{1,0:T(8,128)(2,1)S(1)}, u32[]{:S(2)}, u32[]{:S(2)}) collective-permute-start(bf16[32,384]{1,0:T(8,128)(2,1)} %get-tuple-element.34), channel_id=1, source_target_pairs={{0,1},{1,2},{2,3},{4,5},{5,6},{6,7},{8,9},{9,10},{10,11},{12,13},{... | collective-permute-start | bytes 73736 | tf_op jit(solution)/shard_map/ppermute | solution.py:327
  63.1 5.9 %collective-permute-start.9 = (bf16[32,384]{1,0:T(8,128)(2,1)}, bf16[32,384]{1,0:T(8,128)(2,1)S(1)}, u32[]{:S(2)}, u32[]{:S(2)}) collective-permute-start(bf16[32,384]{1,0:T(8,128)(2,1)} %get-tuple-element.36), channel_id=1, source_target_pairs={{1,0},{2,1},{3,2},{5,4},{6,5},{7,6},{9,8},{10,9},{11,10},{13,12},{... | collective-permute-start | bytes 73736 | tf_op jit(solution)/shard_map/ppermute | solution.py:327
  80.2 0.9 copy-start
  80.2 1.2 copy-start.1

commit v2 on v1

--- a/solution.py
+++ b/solution.py
@@ -18,8 +18,9 @@
 BF = jnp.bfloat16
 F32 = jnp.float32
 VMEM = pl.BlockSpec(memory_space=pltpu.VMEM)
-SMEM = pl.BlockSpec(memory_space=pltpu.SMEM)
-PARAMS = pltpu.CompilerParams(vmem_limit_bytes=56 << 20)
+ANY = pl.BlockSpec(memory_space=pl.ANY)
+HBM = pl.BlockSpec(memory_space=pltpu.HBM)
+PARAMS = pltpu.CompilerParams(vmem_limit_bytes=28 << 20)
 
 
 def tile_of(tiles):
@@ -136,15 +137,27 @@
 
 
 def first_kernel(
-    own, up, down, own_edge, up_edge, down_edge, kernels, bias, edge, forward, leak,
+    own, far_up, far_down, own_edge, up_edge, down_edge, kernels, bias, forward, leak,
     part, hidden, to_up, to_down, packed_field,
-    first, second, line, packed, held,
+    first, second, line, packed, held, up, down, sems,
 ):
     rows, cells, c = own.shape
+    edge = lat_edges()
+    copies = [
+        pltpu.make_async_copy(far_up, up, sems.at[0]),
+        pltpu.make_async_copy(far_down, down, sems.at[1]),
+    ]
+    for copy in copies:
+        copy.start()
     for layer in range(CONVS):
         build_weights(kernels, 0, packed, layer)
-    for at in range(rows + 2 * HALO):
+    order = [*range(HALO, HALO + rows), *range(HALO), *range(rows + HALO, rows + 2 * HALO)]
+    for at in order:
         row = at - HALO
+        if row == -HALO:
+            copies[0].wait()
+        if row == rows:
+            copies[1].wait()
         if row < 0:
             body, ends, source = up, up_edge, row + HALO
         elif row < rows:
@@ -171,13 +184,14 @@
     transform(forward, leak, bias, held, part)
 
 
-def mix_kernel(gathered, turn, real, imag, bias, owner, *rest):
+def mix_kernel(gathered, turn, real, imag, bias, *rest):
+    me = lax.axis_index("lon")
     outs, (spread_in, spread_out) = rest[:-2], rest[-2:]
     modes, c = real.shape[1], real.shape[2]
-    summed = jnp.dot(turn[...], gathered[...], preferred_element_type=F32)
+    summed = jnp.dot(turn[me], gathered[...], preferred_element_type=F32)
     summed = summed[: 2 * modes] + summed[2 * modes :]
     rows = summed.shape[1] // c
-    level = owner[0] * silu_of_half(0.5 * bias[CONVS - 1 : CONVS])
+    level = (me == 0).astype(F32) * silu_of_half(0.5 * bias[CONVS - 1 : CONVS])
     for half in range(2):
         for row in range(rows):
             spread_in[pl.ds(half * rows + row, modes, stride=2 * rows), :] = summed[
@@ -210,10 +224,11 @@
 
 def middle_kernel(
     packed_field, hidden, from_up, from_down, mixed, inverse,
-    kernels, bias, edge, forward, leak,
+    kernels, bias, forward, leak,
     part, state, hidden_out,
     first, second, packed, held,
 ):
+    edge = lat_edges()
     rows, width, c = hidden.shape[0], hidden.shape[1], hidden.shape[2] // 2
     tile = tile_of(width // RUNS)
     for layer in range(CONVS):
@@ -292,32 +307,78 @@
     return np.concatenate([high, low], 0), leak
 
 
-def turn_table(me, lon_size, local, scale):
-    waves = me * local + jnp.arange(local, dtype=jnp.int32)
-    source = jnp.arange(lon_size, dtype=jnp.int32)
-    phase = (source[None, :] * waves[:, None] % lon_size).astype(F32)
-    phase = phase * (2.0 * math.pi / lon_size)
-    cos, sin = scale * jnp.cos(phase), scale * jnp.sin(phase)
-    eye = jnp.eye(local, dtype=F32)
-    cos, sin = cos[:, :, None] * eye[:, None, :], sin[:, :, None] * eye[:, None, :]
-    real = jnp.stack([cos, sin], axis=2)
-    imag = jnp.stack([-sin, cos], axis=2)
-    full = jnp.concatenate([real, imag], axis=0).reshape(2 * local, lon_size * 2 * local)
-    high = full.astype(BF)
-    low = (full - high.astype(F32)).astype(BF)
-    return jnp.concatenate([high, low], axis=0)
-
-
-def inverse_table(first_cell, width, lon_total, modes, lon_size):
+def turn_table(lon_size, local, scale):
+    waves = np.arange(lon_size)[:, None, None] * local + np.arange(local)[:, None]
+    phase = np.arange(lon_size) * waves % lon_size * (2 * np.pi / lon_size)
+    cos, sin = scale * np.cos(phase), scale * np.sin(phase)
+    eye = np.eye(local)
+    cos, sin = (x[:, :, :, None] * eye[:, None, :] for x in (cos, sin))
+    real = np.stack([cos, sin], axis=3)
+    imag = np.stack([-sin, cos], axis=3)
+    full = np.concatenate([real, imag], axis=1)
+    full = full.reshape(lon_size, 2 * local, lon_size * 2 * local).astype(np.float32)
+    high = full.astype(ml_dtypes.bfloat16)
+    low = (full - high.astype(np.float32)).astype(ml_dtypes.bfloat16)
+    return np.concatenate([high, low], axis=1)
+
+
+def inverse_parts(cells, lon_total, modes, lon_size):
     column = np.arange(2 * modes)
     local = modes // lon_size
     waves = column // (2 * local) * local + column % local
     imaginary = column // local % 2 == 1
-    cells = first_cell + lon_total + jnp.asarray(cell_order(width), jnp.int32)
-    product = cells[:, :, None] % lon_total * waves.astype(np.int32) % lon_total
-    theta = product.astype(F32) * (2.0 * math.pi / lon_total)
-    weight = np.where(waves == 0, 1.0, 2.0).astype(np.float32)
-    return (jnp.where(imaginary, -jnp.sin(theta), jnp.cos(theta)) * weight).astype(BF)
+    order = cell_order(cells + 2 * PAD) - PAD
+    theta = (2 * np.pi / lon_total) * (order[:, :, None] * waves % lon_total)
+    weight = np.where(waves == 0, 1.0, 2.0)
+    cos, sin = weight * np.cos(theta), weight * np.sin(theta)
+    by_cos = np.where(imaginary, -sin, cos).astype(np.float32)
+    by_sin = np.where(imaginary, -cos, -sin).astype(np.float32)
+    return waves.astype(np.int32), by_cos, by_sin
+
+
+def phase_table(cells, lon_total, modes, lon_size):
+    waves = inverse_parts(cells, lon_total, modes, lon_size)[0]
+    phase = np.arange(lon_size)[:, None] * waves % lon_size * (2 * np.pi / lon_size)
+    return np.stack([np.cos(phase), np.sin(phase)], 1).astype(np.float32)
+
+
+def slice_kernel(field, above, below, sems):
+    rows = field.shape[0]
+    first = pltpu.make_async_copy(field.at[rows - HALO :], above, sems.at[0])
+    second = pltpu.make_async_copy(field.at[:HALO], below, sems.at[1])
+    first.start()
+    second.start()
+    first.wait()
+    second.wait()
+
+
+def side_kernel(field, after, last, leading, sems):
+    cells = field.shape[1]
+    first = pltpu.make_async_copy(field.at[:, cells - PAD :], last, sems.at[0])
+    second = pltpu.make_async_copy(field.at[:, :PAD], leading, sems.at[1])
+    first.start()
+    second.start()
+    first.wait()
+    second.wait()
+
+
+def edge_kernel(from_left, from_right, by_cos, by_sin, phase, edges, above, below, inverse):
+    rows = from_left.shape[0]
+    for row in range(rows):
+        both = jnp.concatenate([from_left[row], from_right[row]], axis=0)
+        edges[row] = both
+        if row < HALO:
+            below[row] = both
+        if row >= rows - HALO:
+            above[row - (rows - HALO)] = both
+    turn = phase[lax.axis_index("lon")]
+    for e in range(2):
+        inverse[e] = (by_cos[e] * turn[0:1] + by_sin[e] * turn[1:2]).astype(BF)
+
+
+def lat_edges():
+    me, size = lax.axis_index("lat"), lax.axis_size("lat")
+    return [(me > 0).astype(F32), (me < size - 1).astype(F32)]
 
 
 def lat_moves(above, below):
@@ -332,6 +393,11 @@
 
 
 def conv_scratch(rows, width, c):
+    got = middle_scratch(rows, width, c)
+    return got[:2] + [pltpu.VMEM((2, width, c), F32)] + got[2:]
+
+
+def middle_scratch(rows, width, c):
     return [
         pltpu.VMEM((rows + 2 * HALO, width // 2 + 2 * RUNS, 2 * c), BF),
         pltpu.VMEM((rows + 2 * HALO - 2, width // 2 + 2 * RUNS, 2 * c), BF),
@@ -340,52 +406,64 @@
     ]
 
 
-def call(kernel, args, outs, scratch, in_specs=None, grid=()):
+def call(kernel, args, outs, scratch, in_specs=None, out_specs=None, grid=()):
     return pl.pallas_call(
         kernel,
         grid=grid,
         out_shape=outs,
         in_specs=in_specs or [VMEM] * len(args),
-        out_specs=[VMEM] * len(outs),
+        out_specs=out_specs or [VMEM] * len(outs),
         scratch_shapes=scratch,
         compiler_params=PARAMS,
-    )(*args)
+    )(*(jnp.asarray(arg) for arg in args))
 
 
 def per_device(field, conv_weight, conv_bias, spec_real, spec_imag):
     rows, cells, c = field.shape
     width = cells + 2 * PAD
     half = width // 2
-    lon_size, lat_size = lax.axis_size("lon"), lax.axis_size("lat")
-    lon_me, lat_me = lax.axis_index("lon"), lax.axis_index("lat")
+    lon_size = lax.axis_size("lon")
     lon_total = cells * lon_size
     local = spec_real.shape[1]
     modes = local * lon_size
 
-    above, below = field[rows - HALO :], field[:HALO]
+    above, below = call(
+        slice_kernel,
+        (field,),
+        [shape(HALO, cells, c)] * 2,
+        [pltpu.SemaphoreType.DMA((2,))],
+        in_specs=[HBM],
+        out_specs=[ANY] * 2,
+    )
     up, down = lat_moves(above, below)
-    above, below, last, leading = lax.optimization_barrier(
-        (above, below, field[:, cells - PAD :], field[:, :PAD])
+    last, leading = call(
+        side_kernel,
+        (field, above),
+        [shape(rows, PAD, c)] * 2,
+        [pltpu.SemaphoreType.DMA((2,))],
+        in_specs=[HBM, ANY],
+        out_specs=[ANY] * 2,
     )
     right = [(i, (i + 1) % lon_size) for i in range(lon_size)]
     left = [(j, i) for i, j in right]
     from_left = lax.ppermute(last, "lon", right)
     from_right = lax.ppermute(leading, "lon", left)
-    own_edge = jnp.concatenate([from_left, from_right], axis=1)
-    up_edge, down_edge = lat_moves(own_edge[rows - HALO :], own_edge[:HALO])
-
-    forward, leak = forward_table(cells, lon_total, modes, lon_size)
-    forward, leak = jnp.asarray(forward), jnp.asarray(leak)
-    turn = turn_table(lon_me, lon_size, local, 1.0 / lon_total)
-    inverse = inverse_table(lon_me * cells - PAD, width, lon_total, modes, lon_size)
-    edge = jnp.stack([lat_me > 0, lat_me < lat_size - 1]).astype(F32)
-    owner = (lon_me == 0).astype(F32).reshape(1)
-    up, turn, inverse, edge, owner = lax.optimization_barrier((up, turn, inverse, edge, owner))
+    tables = (cells, lon_total, modes, lon_size)
+    _, by_cos, by_sin = inverse_parts(*tables)
+    own_edge, above, below, inverse = call(
+        edge_kernel,
+        (from_left, from_right, by_cos, by_sin, phase_table(*tables)),
+        [shape(rows, 2 * PAD, c)] + [shape(HALO, 2 * PAD, c)] * 2 + [shape(2, half, 2 * modes)],
+        [],
+    )
+    up_edge, down_edge = lat_moves(above, below)
+    forward, leak = forward_table(*tables)
+    turn = turn_table(lon_size, local, 1.0 / lon_total)
 
     part, hidden, to_up, to_down, packed_field = call(
         first_kernel,
         (field, up, down, own_edge, up_edge, down_edge)
-        + (conv_weight, conv_bias[0], edge, forward, leak),
+        + (conv_weight, conv_bias[0], forward, leak),
         [
             shape(2 * modes, rows * c),
             shape(rows, half, 2 * c),
@@ -393,8 +471,10 @@
             shape(HALO, half, 2 * c),
             shape(rows + 2 * HALO, half, 2 * c),
         ],
-        (lambda s: s[:2] + [pltpu.VMEM((2, width, c), F32)] + s[2:])(conv_scratch(rows, width, c)),
-        in_specs=[VMEM] * 8 + [SMEM] + [VMEM] * 2,
+        conv_scratch(rows, width, c)
+        + [pltpu.VMEM((HALO, cells, c), BF)] * 2
+        + [pltpu.SemaphoreType.DMA((2,))],
+        in_specs=[VMEM, ANY, ANY] + [VMEM] * 7,
     )
     from_up, from_down = lat_moves(to_up, to_down)
 
@@ -407,10 +487,10 @@
         got = call(
             mix_kernel,
             (chunks.reshape(2 * modes, rows * c), turn, spec_real, spec_imag)
-            + (conv_bias[block], owner),
+            + (conv_bias[block],),
             [shape(2 * local, n) for n in widths],
             [line, line],
-            in_specs=[VMEM, VMEM, weights, weights, VMEM, SMEM],
+            in_specs=[VMEM, VMEM, weights, weights, VMEM],
             grid=(1,),
         )
         mixed = got[0]
@@ -423,10 +503,9 @@
     part, state, hidden = call(
         middle_kernel,
         (packed_field, hidden, from_up, from_down, mixed, inverse)
-        + (conv_weight, conv_bias[1], edge, forward, leak),
+        + (conv_weight, conv_bias[1], forward, leak),
         [shape(2 * modes, rows * c), shape(rows, half, 2 * c), shape(rows, half, 2 * c)],
-        conv_scratch(rows, width, c),
-        in_specs=[VMEM] * 8 + [SMEM] + [VMEM] * 2,
+        middle_scratch(rows, width, c),
     )
     mixed = mix(part, 1, False)
     (result,) = call(

time: 122 us -> 101 us (0.83)
  Pallas kernels: 33.9 us -> 20.2 us
  waiting for transfers between devices: 4.29 us -> 12.3 us
  other arithmetic: 7.88 us -> 0.01 us
  blocking collectives: 42.4 us -> 37.9 us
  local copies, waits for them, and re-layouts: 5.66 us -> 3.42 us
    pallas_call x5 -> x8, Pallas kernels: 33.9 us -> 20.2 us  [call(): pl.pallas_call(kernel, grid=grid, out_shape=outs, in_specs=in_specs or [V...]
    ppermute x8, waiting for transfers between devices: 4.28 us -> 10.9 us  [lat_moves(): return (lax.ppermute(above, 'lat', up), lax.ppermute(below, 'lat', down))]
    convert_element_type x4 -> x0, other arithmetic: 6.32 us -> none  [the longest x1 5.65 us: inverse_table(): (jnp.where(imaginary, -jnp.sin(theta), jnp.cos(theta)) * weight).astype(BF)]
    all_gather x2, blocking collectives: 20.5 us -> 17.7 us  [mix(): return lax.all_gather(mixed, 'lon', axis=0, tiled=True)]
    slice x3 -> x0, local copies, waits for them, and re-layouts: 2.28 us -> none  [the longest x1 1.53 us: per_device(): above, below = (field[rows - HALO:], field[:HALO])]
    all_to_all x2, blocking collectives: 21.9 us -> 20.1 us  [mix(): chunks = lax.all_to_all(chunks, 'lon', 0, 0)]
    ppermute x1, waiting for transfers between devices: 0.01 us -> 1.41 us  [per_device(): from_left = lax.ppermute(last, 'lon', right)]
    unnamed x27 -> x26, local copies, waits for them, and re-layouts: 3.31 us -> 3.41 us
  transfers between devices with their start and end apart: 10 -> 10, of which waited for: 2 -> 4; matrix products, arithmetic and copies ran while one was open for 8% -> 0% of each run, Pallas kernels for 2% -> 1%
where the time goes in v2:
time: 101 us; the launch traced here: 100 us
  blocking collectives  37.9 us (38%)
  starting transfers between devices  26.4 us (26%)
  Pallas kernels  20.2 us (20%)
  waiting for transfers between devices  12.3 us (12%)
  local copies, waits for them, and re-layouts  3.42 us (3%)
    ppermute x8, starting transfers between devices, lat_moves(): return (lax.ppermute(above, 'lat', up), lax.ppermute(below, 'lat', down))  23.8 us
    pallas_call x8, Pallas kernels, call(): pl.pallas_call(kernel, grid=grid, out_shape=outs, in_specs=in_specs or [V...  20.2 us
    all_to_all x2, blocking collectives, mix(): chunks = lax.all_to_all(chunks, 'lon', 0, 0)  20.1 us
    all_gather x2, blocking collectives, mix(): return lax.all_gather(mixed, 'lon', axis=0, tiled=True)  17.7 us
    ppermute x8, waiting for transfers between devices, lat_moves(): return (lax.ppermute(above, 'lat', up), lax.ppermute(below, 'lat', down))  10.9 us
    unnamed x26, local copies, waits for them, and re-layouts  3.41 us
    ppermute x1, starting transfers between devices, per_device(): from_right = lax.ppermute(leading, 'lon', left)  2.61 us
  transfers between devices with their start and end apart: 10, of which 4 were waited for; matrix products, arithmetic and copies ran while one was open for 0% of the time, Pallas kernels for 1%

profile of v2, /device:TPU:0, one launch (start us, length us, event | category | flops | bytes accessed | tf_op | source)
XLA Modules:
  0.0 100.4 jit_solution(6966508092932147162)
XLA Ops:
  0.0 1.2 %copy-done = bf16[4,1024,128]{2,1,0:T(8,128)(2,1)S(1)} copy-done((bf16[4,1024,128]{2,1,0:T(8,128)(2,1)S(1)}, bf16[4,1024,128]{2,1,0:T(8,128)(2,1)}, u32[]{:S(2)}) %copy-start) | copy-done | bytes 1048600
  1.2 0.1 shard_map.109
  1.4 0.0 copy-start.10
  1.4 1.4 %collective-permute-start.1 = (bf16[3,1024,128]{2,1,0:T(8,128)(2,1)S(1)}, bf16[3,1024,128]{2,1,0:T(8,128)(2,1)S(1)}, u32[]{:S(2)}, u32[]{:S(2)}) collective-permute-start(bf16[3,1024,128]{2,1,0:T(8,128)(2,1)S(1)} %get-tuple-element.25), channel_id=1, source_target_pairs={{1,0},{2,1},{3,2},{5,4},{6,5},{7,6},{9,8},{10,9},{11,10},{13,12},{... | collective-permute-start | bytes 2359304 | tf_op jit(solution)/shard_map/ppermute | solution.py:388
  2.8 5.6 %collective-permute-start = (bf16[3,1024,128]{2,1,0:T(8,128)(2,1)S(1)}, bf16[3,1024,128]{2,1,0:T(8,128)(2,1)S(1)}, u32[]{:S(2)}, u32[]{:S(2)}) collective-permute-start(bf16[3,1024,128]{2,1,0:T(8,128)(2,1)S(1)} %get-tuple-element.24.after), channel_id=1, source_target_pairs={{0,1},{1,2},{2,3},{4,5},{5,6},{6,7},{8,9},{9,10},{10,11},{12,13},{... | collective-permute-start | bytes 2359304 | tf_op jit(solution)/shard_map/ppermute | solution.py:388
  8.4 0.0 copy-start.2
  8.5 0.0 copy-start.11
  8.5 0.1 collective-permute-start.2
  8.6 0.0 copy-start.1
  8.6 0.0 copy-start.3
  8.6 2.6 %collective-permute-start.3 = (bf16[4,16,128]{2,1,0:T(8,128)(2,1)S(1)}, bf16[4,16,128]{2,1,0:T(8,128)(2,1)S(1)}, u32[]{:S(2)}, u32[]{:S(2)}) collective-permute-start(bf16[4,16,128]{2,1,0:T(8,128)(2,1)S(1)} %get-tuple-element.27), channel_id=1, source_target_pairs={{4,0},{8,4},{12,8},{16,12},{20,16},{24,20},{28,24},{0,28},{5,1},{9... | collective-permute-start | bytes 49160 | tf_op jit(solution)/shard_map/ppermute | solution.py:450
  11.2 1.4 %collective-permute-done.2.from_left = bf16[4,16,128]{2,1,0:T(8,128)(2,1)S(1)} collective-permute-done((bf16[4,16,128]{2,1,0:T(8,128)(2,1)S(1)}, bf16[4,16,128]{2,1,0:T(8,128)(2,1)S(1)}, u32[]{:S(2)}, u32[]{:S(2)}) %collective-permute-start.2) | collective-permute-done | bytes 16416 | tf_op jit(solution)/shard_map/ppermute | solution.py:449
  12.6 0.0 collective-permute-done.3.from_right
  12.6 0.0 copy-done.6
  12.6 0.0 copy-done.10
  12.6 1.2 %copy-done.7 = f32[2,528,256]{2,1,0:T(8,128)S(1)} copy-done((f32[2,528,256]{2,1,0:T(8,128)S(1)}, f32[2,528,256]{2,1,0:T(8,128)}, u32[]{:S(2)}) %copy-start.7) | copy-done | bytes 1081368
  13.9 0.1 shard_map.111
  14.0 3.9 %collective-permute-start.4 = (bf16[3,32,128]{2,1,0:T(8,128)(2,1)S(1)}, bf16[3,32,128]{2,1,0:T(8,128)(2,1)S(1)}, u32[]{:S(2)}, u32[]{:S(2)}) collective-permute-start(bf16[3,32,128]{2,1,0:T(8,128)(2,1)S(1)} %get-tuple-element.29), channel_id=1, source_target_pairs={{0,1},{1,2},{2,3},{4,5},{5,6},{6,7},{8,9},{9,10},{10,11},{12,13},{... | collective-permute-start | bytes 73736 | tf_op jit(solution)/shard_map/ppermute | solution.py:388
  17.9 1.3 %collective-permute-start.5 = (bf16[3,32,128]{2,1,0:T(8,128)(2,1)S(1)}, bf16[3,32,128]{2,1,0:T(8,128)(2,1)S(1)}, u32[]{:S(2)}, u32[]{:S(2)}) collective-permute-start(bf16[3,32,128]{2,1,0:T(8,128)(2,1)S(1)} %get-tuple-element.30), channel_id=1, source_target_pairs={{1,0},{2,1},{3,2},{5,4},{6,5},{7,6},{9,8},{10,9},{11,10},{13,12},{... | collective-permute-start | bytes 73736 | tf_op jit(solution)/shard_map/ppermute | solution.py:388
  19.2 0.0 copy-done.11
  19.2 6.4 %collective-permute-done.4.up_edge = bf16[3,32,128]{2,1,0:T(8,128)(2,1)S(1)} collective-permute-done((bf16[3,32,128]{2,1,0:T(8,128)(2,1)S(1)}, bf16[3,32,128]{2,1,0:T(8,128)(2,1)S(1)}, u32[]{:S(2)}, u32[]{:S(2)}) %collective-permute-start.4) | collective-permute-done | bytes 24608 | tf_op jit(solution)/shard_map/ppermute | solution.py:388
  25.7 0.0 collective-permute-done.5.down_edge
  25.7 0.0 collective-permute-done.1.far_down
  25.7 0.0 collective-permute-done.far_up
  25.7 0.0 copy-done.2
  25.7 0.0 copy-done.1
  25.7 0.0 copy-done.3
  25.7 0.0 copy-start.9
  25.7 0.9 copy-done.9
  26.6 8.8 %shard_map.112 = (bf16[256,512]{1,0:T(8,128)(2,1)S(1)}, bf16[4,528,256]{2,1,0:T(8,128)(2,1)S(1)}, bf16[3,528,256]{2,1,0:T(8,128)(2,1)S(1)}, bf16[3,528,256]{2,1,0:T(8,128)(2,1)S(1)}, bf16[10,528,256]{2,1,0:T(8,128)(2,1)S(1)}) custom-call(bf16[4,1024,128]{2,1,0:T(8,128)(2,1)S(1)} %copy-done.1, bf16[3,1024,128]{2,1,0:T(8,128)(2,1)S(1)} %collective-permute-done.far_up, ...), custom_call_target="tpu_custom_call" | custom-call | tf_op jit(solution)/shard_map/pallas_call | solution.py:410
  35.4 4.4 %collective-permute-start.6 = (bf16[3,528,256]{2,1,0:T(8,128)(2,1)S(1)}, bf16[3,528,256]{2,1,0:T(8,128)(2,1)S(1)}, u32[]{:S(2)}, u32[]{:S(2)}) collective-permute-start(bf16[3,528,256]{2,1,0:T(8,128)(2,1)S(1)} %get-tuple-element.33), channel_id=1, source_target_pairs={{0,1},{1,2},{2,3},{4,5},{5,6},{6,7},{8,9},{9,10},{10,11},{12,13},{... | collective-permute-start | bytes 2433032 | tf_op jit(solution)/shard_map/ppermute | solution.py:388
  39.9 1.3 %collective-permute-start.7 = (bf16[3,528,256]{2,1,0:T(8,128)(2,1)S(1)}, bf16[3,528,256]{2,1,0:T(8,128)(2,1)S(1)}, u32[]{:S(2)}, u32[]{:S(2)}) collective-permute-start(bf16[3,528,256]{2,1,0:T(8,128)(2,1)S(1)} %get-tuple-element.34), channel_id=1, source_target_pairs={{1,0},{2,1},{3,2},{5,4},{6,5},{7,6},{9,8},{10,9},{11,10},{13,12},{... | collective-permute-start | bytes 2433032 | tf_op jit(solution)/shard_map/ppermute | solution.py:388
  41.2 10.6 %all_to_all.10 = bf16[8,32,512]{2,1,0:T(8,128)(2,1)S(1)} all-to-all(bf16[8,32,512]{2,1,0:T(8,128)(2,1)S(1)} %bitcast.12), channel_id=1, replica_groups=mesh['lon'=8,'lat'=4] {'lon'}, dimensions={0} | all-to-all | bytes 524288 | tf_op jit(solution)/shard_map/all_to_all | solution.py:483
  51.8 0.0 copy-done.4
  51.8 0.0 copy-done.5
  51.8 0.4 shard_map.113
  52.3 4.5 %collective-permute-start.8 = (bf16[32,384]{1,0:T(8,128)(2,1)S(1)}, bf16[32,384]{1,0:T(8,128)(2,1)S(1)}, u32[]{:S(2)}, u32[]{:S(2)}) collective-permute-start(bf16[32,384]{1,0:T(8,128)(2,1)S(1)} %get-tuple-element.36), channel_id=1, source_target_pairs={{0,1},{1,2},{2,3},{4,5},{5,6},{6,7},{8,9},{9,10},{10,11},{12,13},{... | collective-permute-start | bytes 73736 | tf_op jit(solution)/shard_map/ppermute | solution.py:388
  56.8 1.3 %collective-permute-start.9 = (bf16[32,384]{1,0:T(8,128)(2,1)S(1)}, bf16[32,384]{1,0:T(8,128)(2,1)S(1)}, u32[]{:S(2)}, u32[]{:S(2)}) collective-permute-start(bf16[32,384]{1,0:T(8,128)(2,1)S(1)} %get-tuple-element.38), channel_id=1, source_target_pairs={{1,0},{2,1},{3,2},{5,4},{6,5},{7,6},{9,8},{10,9},{11,10},{13,12},{... | collective-permute-start | bytes 73736 | tf_op jit(solution)/shard_map/ppermute | solution.py:388
  58.1 0.2 collective-permute-done.8
  58.3 4.2 %collective-permute-done.9 = bf16[32,384]{1,0:T(8,128)(2,1)S(1)} collective-permute-done((bf16[32,384]{1,0:T(8,128)(2,1)S(1)}, bf16[32,384]{1,0:T(8,128)(2,1)S(1)}, u32[]{:S(2)}, u32[]{:S(2)}) %collective-permute-start.9) | collective-permute-done | bytes 24608 | tf_op jit(solution)/shard_map/ppermute | solution.py:388
  62.6 9.4 %all_gather.6.mixed = bf16[256,1280]{1,0:T(8,128)(2,1)S(1)} all-gather(bf16[32,1280]{1,0:T(8,128)(2,1)S(1)} %pad_maximum_fusion), channel_id=1, replica_groups=mesh['lon'=8,'lat'=4] {'lon'}, dimensions={0}, use_global_device_ids=true | all-gather | bytes 737280 | tf_op jit(solution)/shard_map/all_gather | solution.py:500
  71.9 0.0 collective-permute-done.6.from_up
  71.9 0.0 collective-permute-done.7.from_down
  71.9 8.6 %shard_map.114 = (bf16[256,512]{1,0:T(8,128)(2,1)S(1)}, bf16[4,528,256]{2,1,0:T(8,128)(2,1)S(1)}, bf16[4,528,256]{2,1,0:T(8,128)(2,1)S(1)}) custom-call(bf16[10,528,256]{2,1,0:T(8,128)(2,1)S(1)} %get-tuple-element.31.packed_field, bf16[4,528,256]{2,1,0:T(8,128)(2,1)S(1)} %get-tuple-element.32.hidden, ...), custom_call_target="tpu_custom_call" | custom-call | tf_op jit(solution)/shard_map/pallas_call | solution.py:410
  80.5 9.5 %all_to_all.11 = bf16[8,32,512]{2,1,0:T(8,128)(2,1)S(1)} all-to-all(bf16[8,32,512]{2,1,0:T(8,128)(2,1)S(1)} %bitcast.13), channel_id=1, replica_groups=mesh['lon'=8,'lat'=4] {'lon'}, dimensions={0} | all-to-all | bytes 524288 | tf_op jit(solution)/shard_map/all_to_all | solution.py:483
  90.0 0.4 shard_map.115
  90.4 8.4 %all_gather.7.mixed = bf16[256,512]{1,0:T(8,128)(2,1)S(1)} all-gather(bf16[32,512]{1,0:T(8,128)(2,1)S(1)} %shard_map.115), channel_id=1, replica_groups=mesh['lon'=8,'lat'=4] {'lon'}, dimensions={0}, use_global_device_ids=true | all-gather | bytes 294912 | tf_op jit(solution)/shard_map/all_gather | solution.py:500
  98.8 1.6 %shard_map.116 = bf16[4,1024,128]{2,1,0:T(8,128)(2,1)} custom-call(bf16[4,528,256]{2,1,0:T(8,128)(2,1)S(1)} %get-tuple-element.40.state, bf16[4,528,256]{2,1,0:T(8,128)(2,1)S(1)} %get-tuple-element.41.hidden, bf16[256,512]{1,0:T(8,128)(2,1)S(1)} %all_gather.7.mixed, bf16[2,528,256]{2,1,0:T(8,128)(2,1)S(1)} %get-tuple-element.39.inverse), custom_call_target="tpu_custom_call" | custom-call | tf_op jit(solution)/shard_map/pallas_call | solution.py:410
  (12 shorter events, 0.1 us)
Async XLA Ops:
  0.0 1.2 %copy-start = (bf16[4,1024,128]{2,1,0:T(8,128)(2,1)S(1)}, bf16[4,1024,128]{2,1,0:T(8,128)(2,1)}, u32[]{:S(2)}) copy-start(bf16[4,1024,128]{2,1,0:T(8,128)(2,1)} %own.1) | copy-start | bytes 3145732
  1.2 11.4 %copy-start.6 = (f32[2,528,256]{2,1,0:T(8,128)S(1)}, f32[2,528,256]{2,1,0:T(8,128)}, u32[]{:S(2)}) copy-start(f32[2,528,256]{2,1,0:T(8,128)} %constant.13.clone.by_sin) | copy-start | bytes 3244036
  1.4 11.3 %copy-start.10 = (f32[8,2,256]{2,1,0:T(2,128)S(1)}, f32[8,2,256]{2,1,0:T(2,128)}, u32[]{:S(2)}) copy-start(f32[8,2,256]{2,1,0:T(2,128)} %constant.14.clone.phase) | copy-start | bytes 49156
  1.4 24.3 %collective-permute-start.1 = (bf16[3,1024,128]{2,1,0:T(8,128)(2,1)S(1)}, bf16[3,1024,128]{2,1,0:T(8,128)(2,1)S(1)}, u32[]{:S(2)}, u32[]{:S(2)}) collective-permute-start(bf16[3,1024,128]{2,1,0:T(8,128)(2,1)S(1)} %get-tuple-element.25), channel_id=1, source_target_pairs={{1,0},{2,1},{3,2},{5,4},{6,5},{7,6},{9,8},{10,9},{11,10},{13,12},{... | collective-permute-start | bytes 2359304 | tf_op jit(solution)/shard_map/ppermute | solution.py:388
  2.8 22.9 %collective-permute-start = (bf16[3,1024,128]{2,1,0:T(8,128)(2,1)S(1)}, bf16[3,1024,128]{2,1,0:T(8,128)(2,1)S(1)}, u32[]{:S(2)}, u32[]{:S(2)}) collective-permute-start(bf16[3,1024,128]{2,1,0:T(8,128)(2,1)S(1)} %get-tuple-element.24.after), channel_id=1, source_target_pairs={{0,1},{1,2},{2,3},{4,5},{5,6},{6,7},{8,9},{9,10},{10,11},{12,13},{... | collective-permute-start | bytes 2359304 | tf_op jit(solution)/shard_map/ppermute | solution.py:388
  8.4 17.3 %copy-start.2 = (bf16[2,3,3,3,128,128]{5,4,3,2,1,0:T(8,128)(2,1)S(1)}, bf16[2,3,3,3,128,128]{5,4,3,2,1,0:T(8,128)(2,1)}, u32[]{:S(2)}) copy-start(bf16[2,3,3,3,128,128]{5,4,3,2,1,0:T(8,128)(2,1)} %kernels.3) | copy-start | bytes 5308420
  8.5 10.7 %copy-start.11 = (f32[2,3,128]{2,0,1:T(2,128)S(1)}, f32[2,3,128]{2,0,1:T(2,128)}, u32[]{:S(2)}) copy-start(f32[2,3,128]{2,0,1:T(2,128)} %param.13) | copy-start | bytes 9220
  8.5 4.1 %collective-permute-start.2 = (bf16[4,16,128]{2,1,0:T(8,128)(2,1)S(1)}, bf16[4,16,128]{2,1,0:T(8,128)(2,1)S(1)}, u32[]{:S(2)}, u32[]{:S(2)}) collective-permute-start(bf16[4,16,128]{2,1,0:T(8,128)(2,1)S(1)} %get-tuple-element.26), channel_id=1, source_target_pairs={{0,4},{4,8},{8,12},{12,16},{16,20},{20,24},{24,28},{28,0},{1,5},{5... | collective-permute-start | bytes 49160 | tf_op jit(solution)/shard_map/ppermute | solution.py:449
  8.6 17.2 %copy-start.1 = (bf16[4,1024,128]{2,1,0:T(8,128)(2,1)S(1)}, bf16[4,1024,128]{2,1,0:T(8,128)(2,1)}, u32[]{:S(2)}) copy-start(bf16[4,1024,128]{2,1,0:T(8,128)(2,1)} %own.1) | copy-start | bytes 3145732
  8.6 17.2 %copy-start.3 = (bf16[512,1056]{1,0:T(8,128)(2,1)S(1)}, bf16[512,1056]{1,0:T(8,128)(2,1)}, u32[]{:S(2)}) copy-start(bf16[512,1056]{1,0:T(8,128)(2,1)} %constant.15.clone.forward) | copy-start | bytes 3244036
  8.6 4.1 %collective-permute-start.3 = (bf16[4,16,128]{2,1,0:T(8,128)(2,1)S(1)}, bf16[4,16,128]{2,1,0:T(8,128)(2,1)S(1)}, u32[]{:S(2)}, u32[]{:S(2)}) collective-permute-start(bf16[4,16,128]{2,1,0:T(8,128)(2,1)S(1)} %get-tuple-element.27), channel_id=1, source_target_pairs={{4,0},{8,4},{12,8},{16,12},{20,16},{24,20},{28,24},{0,28},{5,1},{9... | collective-permute-start | bytes 49160 | tf_op jit(solution)/shard_map/ppermute | solution.py:450
  12.6 1.2 %copy-start.7 = (f32[2,528,256]{2,1,0:T(8,128)S(1)}, f32[2,528,256]{2,1,0:T(8,128)}, u32[]{:S(2)}) copy-start(f32[2,528,256]{2,1,0:T(8,128)} %constant.12.clone.by_cos) | copy-start | bytes 3244036
  14.0 11.7 %collective-permute-start.4 = (bf16[3,32,128]{2,1,0:T(8,128)(2,1)S(1)}, bf16[3,32,128]{2,1,0:T(8,128)(2,1)S(1)}, u32[]{:S(2)}, u32[]{:S(2)}) collective-permute-start(bf16[3,32,128]{2,1,0:T(8,128)(2,1)S(1)} %get-tuple-element.29), channel_id=1, source_target_pairs={{0,1},{1,2},{2,3},{4,5},{5,6},{6,7},{8,9},{9,10},{10,11},{12,13},{... | collective-permute-start | bytes 73736 | tf_op jit(solution)/shard_map/ppermute | solution.py:388
  17.9 7.8 %collective-permute-start.5 = (bf16[3,32,128]{2,1,0:T(8,128)(2,1)S(1)}, bf16[3,32,128]{2,1,0:T(8,128)(2,1)S(1)}, u32[]{:S(2)}, u32[]{:S(2)}) collective-permute-start(bf16[3,32,128]{2,1,0:T(8,128)(2,1)S(1)} %get-tuple-element.30), channel_id=1, source_target_pairs={{1,0},{2,1},{3,2},{5,4},{6,5},{7,6},{9,8},{10,9},{11,10},{13,12},{... | collective-permute-start | bytes 73736 | tf_op jit(solution)/shard_map/ppermute | solution.py:388
  25.7 0.9 copy-start.9
  26.6 25.2 %copy-start.4 = (bf16[2,16,128,128]{3,2,1,0:T(8,128)(2,1)S(1)}, bf16[2,16,128,128]{3,2,1,0:T(8,128)(2,1)}, u32[]{:S(2)}) copy-start(bf16[2,16,128,128]{3,2,1,0:T(8,128)(2,1)} %real.3) | copy-start | bytes 3145732
  26.6 25.2 %copy-start.5 = (bf16[2,16,128,128]{3,2,1,0:T(8,128)(2,1)S(1)}, bf16[2,16,128,128]{3,2,1,0:T(8,128)(2,1)}, u32[]{:S(2)}) copy-start(bf16[2,16,128,128]{3,2,1,0:T(8,128)(2,1)} %imag.3) | copy-start | bytes 3145732
  26.6 25.2 %copy-start.8 = (bf16[8,64,256]{2,1,0:T(8,128)(2,1)S(1)}, bf16[8,64,256]{2,1,0:T(8,128)(2,1)}, u32[]{:S(2)}) copy-start(bf16[8,64,256]{2,1,0:T(8,128)(2,1)} %constant.17.clone.turn) | copy-start | bytes 786436
  35.4 36.5 %collective-permute-start.6 = (bf16[3,528,256]{2,1,0:T(8,128)(2,1)S(1)}, bf16[3,528,256]{2,1,0:T(8,128)(2,1)S(1)}, u32[]{:S(2)}, u32[]{:S(2)}) collective-permute-start(bf16[3,528,256]{2,1,0:T(8,128)(2,1)S(1)} %get-tuple-element.33), channel_id=1, source_target_pairs={{0,1},{1,2},{2,3},{4,5},{5,6},{6,7},{8,9},{9,10},{10,11},{12,13},{... | collective-permute-start | bytes 2433032 | tf_op jit(solution)/shard_map/ppermute | solution.py:388
  39.9 32.0 %collective-permute-start.7 = (bf16[3,528,256]{2,1,0:T(8,128)(2,1)S(1)}, bf16[3,528,256]{2,1,0:T(8,128)(2,1)S(1)}, u32[]{:S(2)}, u32[]{:S(2)}) collective-permute-start(bf16[3,528,256]{2,1,0:T(8,128)(2,1)S(1)} %get-tuple-element.34), channel_id=1, source_target_pairs={{1,0},{2,1},{3,2},{5,4},{6,5},{7,6},{9,8},{10,9},{11,10},{13,12},{... | collective-permute-start | bytes 2433032 | tf_op jit(solution)/shard_map/ppermute | solution.py:388
  52.3 6.1 %collective-permute-start.8 = (bf16[32,384]{1,0:T(8,128)(2,1)S(1)}, bf16[32,384]{1,0:T(8,128)(2,1)S(1)}, u32[]{:S(2)}, u32[]{:S(2)}) collective-permute-start(bf16[32,384]{1,0:T(8,128)(2,1)S(1)} %get-tuple-element.36), channel_id=1, source_target_pairs={{0,1},{1,2},{2,3},{4,5},{5,6},{6,7},{8,9},{9,10},{10,11},{12,13},{... | collective-permute-start | bytes 73736 | tf_op jit(solution)/shard_map/ppermute | solution.py:388
  56.8 5.7 %collective-permute-start.9 = (bf16[32,384]{1,0:T(8,128)(2,1)S(1)}, bf16[32,384]{1,0:T(8,128)(2,1)S(1)}, u32[]{:S(2)}, u32[]{:S(2)}) collective-permute-start(bf16[32,384]{1,0:T(8,128)(2,1)S(1)} %get-tuple-element.38), channel_id=1, source_target_pairs={{1,0},{2,1},{3,2},{5,4},{6,5},{7,6},{9,8},{10,9},{11,10},{13,12},{... | collective-permute-start | bytes 73736 | tf_op jit(solution)/shard_map/ppermute | solution.py:388

commit v3 on v2

v3 whole, which is shorter than its diff:
```python
import math

import jax
import jax.numpy as jnp
import ml_dtypes
import numpy as np
from jax import lax
from jax.experimental import pallas as pl
from jax.experimental.pallas import tpu as pltpu
from jax.sharding import PartitionSpec as P

BLOCKS = 2
CONVS = 3
PAD = 16
RUNS = 16
HALO = 3
WINOGRAD = True
BF = jnp.bfloat16
F32 = jnp.float32
VMEM = pl.BlockSpec(memory_space=pltpu.VMEM)
ANY = pl.BlockSpec(memory_space=pl.ANY)
HBM = pl.BlockSpec(memory_space=pltpu.HBM)
DMA = pltpu.SemaphoreType.DMA
PARAMS = pltpu.CompilerParams(vmem_limit_bytes=28 << 20)


def tile_of(tiles):
    return max(n for n in range(1, 12) if tiles % n == 0) * RUNS


def pack_row(line, wide, row):
    c = line.shape[1]
    run = line.shape[0] // RUNS
    for cell in range(run):
        lanes = slice(cell % 2 * c, (cell % 2 + 1) * c)
        at = RUNS * (cell // 2 + 1)
        wide[row, at : at + RUNS, lanes] = line[pl.ds(cell, RUNS, stride=run), :].astype(BF)


def close_row(wide, row):
    c = wide.shape[2] // 2
    end = wide.shape[1] - RUNS
    before = wide[row, end - RUNS : end, c:].astype(F32)
    wide[row, 0:RUNS, c:] = pltpu.roll(before, 1, 0).astype(BF)
    after = wide[row, RUNS : 2 * RUNS, :c].astype(F32)
    wide[row, end : end + RUNS, :c] = pltpu.roll(after, RUNS - 1, 0).astype(BF)


def build_weights(kernels, block, packed, layer):
    c = kernels.shape[-1]
    zero = jnp.zeros((c, c), BF)
    for tap in range(3):
        g0, g1, g2 = (kernels[block, layer, a, tap].astype(F32) for a in range(3))
        if WINOGRAD:
            outer = g0 + g2
            parts = (0.5 * g0, 0.25 * (outer + g1), 0.25 * (outer - g1), 0.5 * g2)
        else:
            parts = (0.5 * g0, 0.5 * g1, 0.5 * g2)
        for i, part in enumerate(parts):
            value = part.astype(BF)
            for cell in range(2):
                source = cell + tap - 1
                at = {0: 0, 1: c, 2: 2 * c, -1: 3 * c}[source]
                packed[layer, i, at : at + c, cell * c : (cell + 1) * c] = value
    for i in range(packed.shape[1]):
        packed[layer, i, 2 * c : 3 * c, :c] = zero
        packed[layer, i, 3 * c :, c:] = zero


def window(wide, row, start, size):
    c = wide.shape[2] // 2
    here = wide[row, start + RUNS : start + RUNS + size]
    after = wide[row, start + 2 * RUNS : start + 2 * RUNS + size, :c]
    before = wide[row, start : start + size, c:]
    return jnp.concatenate([here, after, before], axis=1)


def dot(a, b):
    return jnp.dot(a, b, preferred_element_type=F32)


def silu_of_half(half):
    return half + half * jnp.tanh(half)


def conv_pair(d, packed, layer):
    if WINOGRAD:
        inputs = (d[0] - d[2], d[1] + d[2], d[2] - d[1], d[1] - d[3])
        m = [dot(x, packed[layer, i]) for i, x in enumerate(inputs)]
        return (m[1] + m[2]) + m[0], m[1] - m[2] - m[3]
    w = jnp.concatenate([packed[layer, i] for i in range(3)], axis=0)
    return tuple(dot(jnp.concatenate(d[i : i + 3], axis=1), w) for i in range(2))


class Rows:
    def __init__(self, *held):
        self.at = {}
        for ref, first in held:
            self.at.update({first + i: (ref, i) for i in range(ref.shape[0])})

    def __getitem__(self, row):
        return self.at[row]


def conv_rows(src, dst, span, layer, packed, bias, edge, rows):
    ref = src[span[0]][0]
    width = ref.shape[1] - 2 * RUNS
    tile = tile_of(width // RUNS)
    both = 0.5 * jnp.concatenate([bias[layer : layer + 1]] * 2, axis=1)
    for pair in range(*span, 2):
        for start in range(0, width, tile):
            sums = conv_pair(
                [window(*src[pair + i - 1], start, tile) for i in range(4)], packed, layer
            )
            for i, total in enumerate(sums):
                row = pair + i
                y = silu_of_half(total + both)
                if row < 0:
                    y = y * edge[0]
                elif row >= rows:
                    y = y * edge[1]
                if callable(dst):
                    dst(row, start, y.astype(BF))
                else:
                    ref, at = dst[row]
                    ref[at, start + RUNS : start + RUNS + tile] = y.astype(BF)
        if not callable(dst):
            for i in range(2):
                close_row(*dst[pair + i])


def transform(forward, leak, bias, held, kept, sent):
    core = lax.rem(lax.axis_index("lon"), 2)
    rows, c = held.shape[0], held.shape[2] // 2
    half = 0.5 * bias[CONVS - 1 : CONVS]
    level = silu_of_half(half)
    for row in range(0, rows, 2):
        cells = [
            jnp.concatenate([held[row + i, :, e * c : (e + 1) * c] for i in range(2)], axis=1)
            for e in range(2)
        ]
        both = dot(forward[core], jnp.concatenate(cells, axis=0))
        modes2 = both.shape[0] // 2
        total = both[:modes2] + both[modes2:]
        total = total - leak[core] * jnp.concatenate([level, level], axis=1)
        lanes = slice(row * c, (row + 2) * c)
        kept[:, lanes] = total[: modes2 // 2]
        sent[:, lanes] = total[modes2 // 2 :]


def pack_cells(body, ends, source, line, wide, at):
    cells = body.shape[1]
    line[0:PAD] = ends[source, :PAD].astype(F32)
    line[PAD : PAD + cells] = body[source].astype(F32)
    line[PAD + cells :] = ends[source, PAD:].astype(F32)
    pack_row(line, wide, at)
    close_row(wide, at)


def lower_part(field, first, second, packed, bias, edge, rows):
    x, y, z = Rows((field, 0)), Rows((first, 2)), Rows((second, 3))
    conv_rows(x, y, (2, rows + 2), 0, packed, bias, edge, rows)
    conv_rows(y, z, (3, rows + 1), 1, packed, bias, edge, rows)


def upper_part(before, field, first, second, more, packed, bias, edge, emit):
    rows = field.shape[0] - HALO
    x = Rows((before, -HALO), (field, 0))
    y = Rows((more[0], -2), (first, 2))
    z = Rows((more[1], -1), (second, 3))
    conv_rows(x, y, (-2, 2), 0, packed, bias, edge, rows)
    conv_rows(y, z, (-1, 3), 1, packed, bias, edge, rows)
    conv_rows(z, emit, (0, rows), 2, packed, bias, edge, rows)


def prepare_kernel(own, own_edge, kernels, field, packed, later, line):
    for layer in range(CONVS):
        build_weights(kernels, 0, packed, layer)
        build_weights(kernels, 1, later, layer)
    for row in range(own.shape[0]):
        pack_cells(own, own_edge, row, line.at[row % 2], field, row)


def first_lower_kernel(down, down_edge, own, packed, bias, after, field, first, second, line):
    rows = own.shape[0]
    field[:rows] = own[...]
    for row in range(HALO):
        pack_cells(down, down_edge, row, line.at[row % 2], field, rows + row)
    lower_part(field, first, second, packed, bias, lat_edges(), rows)


def first_upper_kernel(
    up, up_edge, field, first, second, packed, bias, forward, leak,
    kept, sent, hidden, to_up, to_down, before,
    line, more, most, held,
):
    rows = field.shape[0] - HALO
    for row in range(HALO):
        pack_cells(up, up_edge, row, line.at[row % 2], before, row)

    def emit(row, start, y):
        span = slice(start, start + y.shape[0])
        held[row, span] = y
        hidden[row, span] = y
        if row < HALO:
            to_down[row, span] = y
        if row >= rows - HALO:
            to_up[row - (rows - HALO), span] = y

    upper_part(before, field, first, second, (more, most), packed, bias, lat_edges(), emit)
    transform(forward, leak, bias, held, kept, sent)


def pair_kernel(kept, got, *outs):
    chip = lax.div(lax.axis_index("lon"), 2)
    rows = outs[0].shape[0]
    for step, out in enumerate(outs):
        span = pl.ds(pl.multiple_of((chip ^ step) * rows, rows), rows)
        out[...] = (kept[span, :] + got[span, :]).astype(BF)


def mix_kernel(turn, real, imag, bias, *rest):
    *sums, mixed, spread_in, spread_out = rest
    me = lax.axis_index("lon")
    modes, c = real.shape[1], real.shape[2]
    summed = dot(turn[me], jnp.concatenate([x[...] for x in sums], axis=0))
    summed = summed[: 2 * modes] + summed[2 * modes :]
    rows = summed.shape[1] // c
    level = (me == 0).astype(F32) * silu_of_half(0.5 * bias[CONVS - 1 : CONVS])
    for half in range(2):
        for row in range(rows):
            spread_in[pl.ds(half * rows + row, modes, stride=2 * rows), :] = summed[
                half * modes : (half + 1) * modes, row * c : (row + 1) * c
            ]
    spread_in[0:rows] = spread_in[0:rows] + level
    sign = jnp.where(lax.broadcasted_iota(jnp.int32, (2 * rows, c), 0) < rows, -1.0, 1.0)
    for k in range(modes):
        wide = spread_in[2 * rows * k : 2 * rows * (k + 1)]
        high = wide.astype(BF)
        low = (wide - high.astype(F32)).astype(BF)
        both = jnp.concatenate([high, low], axis=0)
        weight = jnp.concatenate([real[0, k], imag[0, k]], axis=1)
        out = jnp.dot(both, weight, preferred_element_type=F32)
        out = out[: 2 * rows] + out[2 * rows :]
        turned = pltpu.roll(out[:, c:], rows, 0)
        spread_out[2 * rows * k : 2 * rows * (k + 1)] = out[:, :c] + sign * turned
    for half in range(2):
        for row in range(rows):
            value = spread_out[pl.ds(half * rows + row, modes, stride=2 * rows), :].astype(BF)
            span = slice(half * modes, (half + 1) * modes)
            mixed[span, row * c : (row + 1) * c] = value


def halo_kernel(mixed, out):
    lanes = out.shape[1]
    even = lax.rem(lax.axis_index("lon"), 2) == 0

    @pl.when(even)
    def _():
        out[...] = mixed[:, mixed.shape[1] - lanes :]

    @pl.when(jnp.logical_not(even))
    def _():
        out[...] = mixed[:, :lanes]


def pick(mine, other, first):
    even = lax.rem(lax.axis_index("lon"), 2) == 0
    return jnp.where(even == first, mine[...], other[...])


def next_state(old, conv, mixed, inverse, new, at, count, mask):
    c = mixed.shape[1] // conv[0].shape[0]
    width = conv[0].shape[1]
    tile = tile_of(width // RUNS)
    for pair in range(0, count, 2):
        lanes = slice(pair * c, min(pair + 2, count) * c)
        for start in range(0, width, tile):
            span = slice(start, start + tile)
            wide = slice(start + RUNS, start + RUNS + tile)
            waves = [dot(inverse[e, span], mixed[:, lanes]) for e in range(2)]
            for i in range(min(2, count - pair)):
                wave = jnp.concatenate([w[:, i * c : (i + 1) * c] for w in waves], axis=1)
                total = old[0][old[1] + pair + i, wide].astype(F32)
                total = total + conv[0][pair + i, span].astype(F32) + wave
                total = jnp.tanh(total)
                if mask is not None:
                    total = total * mask
                new[at + pair + i, wide] = total.astype(BF)
        for i in range(min(2, count - pair)):
            close_row(new, at + pair + i)


def middle_own_kernel(field, hidden, mixed, inverse, state):
    next_state((field, 0), (hidden,), mixed, inverse, state, 0, hidden.shape[0], None)


def middle_lower_kernel(
    field, from_down, mine, other, own, inverse, packed, bias, state, first, second, mixed_down
):
    rows = own.shape[0]
    edge = lat_edges()
    state[:rows] = own[...]
    mixed_down[...] = pick(mine, other, False)
    next_state((field, rows), (from_down,), mixed_down, inverse, state, rows, HALO, edge[1])
    lower_part(state, first, second, packed, bias, edge, rows)


def middle_upper_kernel(
    before, from_up, mine, other, inverse, state, first, second, packed, bias, forward, leak,
    kept, sent, hidden, above, mixed_up, more, most, held,
):
    edge = lat_edges()
    mixed_up[...] = pick(mine, other, True)
    next_state((before, 0), (from_up,), mixed_up, inverse, above, 0, HALO, edge[0])

    def emit(row, start, y):
        span = slice(start, start + y.shape[0])
        held[row, span] = y
        hidden[row, span] = y

    upper_part(above, state, first, second, (more, most), packed, bias, edge, emit)
    transform(forward, leak, bias, held, kept, sent)


def last_kernel(state, hidden, mixed, inverse, result, line):
    rows, width, c = hidden.shape[0], hidden.shape[1], hidden.shape[2] // 2
    cells = result.shape[1]
    run = 2 * width // RUNS
    for pair in range(0, rows, 2):
        waves = [dot(inverse[e], mixed[:, pair * c : (pair + 2) * c]) for e in range(2)]
        for i in range(2):
            row = pair + i
            for e in range(2):
                lanes = slice(e * c, (e + 1) * c)
                total = state[row, RUNS : RUNS + width, lanes].astype(F32) + hidden[row, :, lanes].astype(F32)
                total = jnp.tanh(total + waves[e][:, i * c : (i + 1) * c])
                for u in range(width // RUNS):
                    value = total[u * RUNS : (u + 1) * RUNS]
                    line[i, pl.ds(2 * u + e, RUNS, stride=run), :] = value
            result[row] = line[i, PAD : PAD + cells].astype(BF)


def cell_order(width):
    run = width // RUNS
    cell = np.arange(width // 2) // RUNS * 2 + np.arange(width // 2) % RUNS * run
    return np.stack([cell, cell + 1])


def forward_table(cells, lon_total, modes, lon_size):
    order = cell_order(cells + 2 * PAD).reshape(-1) - PAD
    inside = (order >= 0) & (order < cells)
    waves = np.arange(modes)
    tables, leaks = [], []
    for core in range(2):
        theta = (2 * np.pi / lon_total) * (np.outer(waves, order + core * cells) % lon_total)
        full = np.stack([np.cos(theta), -np.sin(theta)], 0) * inside
        full = full.reshape(2, lon_size // 2, 2, modes // lon_size, -1)
        full = full.transpose(2, 1, 0, 3, 4)[[core, 1 - core]]
        full = full.reshape(2 * modes, -1).astype(np.float32)
        leaks.append(full.astype(np.float64).sum(1, keepdims=True).astype(np.float32))
        high = full.astype(ml_dtypes.bfloat16)
        low = (full - high.astype(np.float32)).astype(ml_dtypes.bfloat16)
        tables.append(np.concatenate([high, low], 0))
    return np.stack(tables), np.stack(leaks)


def turn_table(lon_size, local, scale):
    chips = lon_size // 2
    me = np.arange(lon_size)[:, None, None]
    waves = me * local + np.arange(local)[:, None]
    source = 2 * ((me // 2) ^ np.arange(chips))
    phase = source * waves % lon_size * (2 * np.pi / lon_size)
    cos, sin = scale * np.cos(phase), scale * np.sin(phase)
    eye = np.eye(local)
    cos, sin = (x[:, :, :, None] * eye[:, None, :] for x in (cos, sin))
    real = np.stack([cos, sin], axis=3)
    imag = np.stack([-sin, cos], axis=3)
    full = np.concatenate([real, imag], axis=1)
    full = full.reshape(lon_size, 2 * local, chips * 2 * local).astype(np.float32)
    high = full.astype(ml_dtypes.bfloat16)
    low = (full - high.astype(np.float32)).astype(ml_dtypes.bfloat16)
    return np.concatenate([high, low], axis=1)


def inverse_parts(cells, lon_total, modes, lon_size):
    column = np.arange(2 * modes)
    local = modes // lon_size
    waves = column // (2 * local) * local + column % local
    imaginary = column // local % 2 == 1
    order = cell_order(cells + 2 * PAD) - PAD
    theta = (2 * np.pi / lon_total) * (order[:, :, None] * waves % lon_total)
    weight = np.where(waves == 0, 1.0, 2.0)
    cos, sin = weight * np.cos(theta), weight * np.sin(theta)
    by_cos = np.where(imaginary, -sin, cos).astype(np.float32)
    by_sin = np.where(imaginary, -cos, -sin).astype(np.float32)
    return waves.astype(np.int32), by_cos, by_sin


def phase_table(cells, lon_total, modes, lon_size):
    waves = inverse_parts(cells, lon_total, modes, lon_size)[0]
    phase = np.arange(lon_size)[:, None] * waves % lon_size * (2 * np.pi / lon_size)
    return np.stack([np.cos(phase), np.sin(phase)], 1).astype(np.float32)


def slice_kernel(field, *rest):
    out, sem = rest[-2:]
    at = 0 if len(rest) == 2 else field.shape[0] - HALO
    copy = pltpu.make_async_copy(field.at[at : at + HALO], out, sem)
    copy.start()
    copy.wait()


def side_kernel(field, after, last, leading, sems):
    cells = field.shape[1]
    first = pltpu.make_async_copy(field.at[:, cells - PAD :], last, sems.at[0])
    second = pltpu.make_async_copy(field.at[:, :PAD], leading, sems.at[1])
    first.start()
    second.start()
    first.wait()
    second.wait()


def edge_kernel(from_left, from_right, edges, below):
    for row in range(from_left.shape[0]):
        both = jnp.concatenate([from_left[row], from_right[row]], axis=0)
        edges[row] = both
        if row < HALO:
            below[row] = both


def copy_kernel(edges, below, above):
    rows = edges.shape[0]
    above[...] = edges[rows - HALO :]


def inverse_kernel(parts, phase, after, inverse):
    turn = phase[lax.axis_index("lon")]
    for e in range(2):
        inverse[e] = (parts[0, e] * turn[0:1] + parts[1, e] * turn[1:2]).astype(BF)


def lat_edges():
    me, size = lax.axis_index("lat"), lax.axis_size("lat")
    return [(me > 0).astype(F32), (me < size - 1).astype(F32)]


def move(array, up):
    size = lax.axis_size("lat")
    pairs = [(i, i + 1) if up else (i + 1, i) for i in range(size - 1)]
    return lax.ppermute(array, "lat", pairs)


def shape(*dims):
    return jax.ShapeDtypeStruct(dims, BF)


def call(kernel, args, outs, scratch, in_specs=None, out_specs=None, grid=()):
    return pl.pallas_call(
        kernel,
        grid=grid,
        out_shape=outs,
        in_specs=in_specs or [VMEM] * len(args),
        out_specs=out_specs or [VMEM] * len(outs),
        scratch_shapes=scratch,
        compiler_params=PARAMS,
    )(*(jnp.asarray(arg) for arg in args))


def per_device(field, conv_weight, conv_bias, spec_real, spec_imag):
    rows, cells, c = field.shape
    width = cells + 2 * PAD
    half = width // 2
    lon_size = lax.axis_size("lon")
    lon_total = cells * lon_size
    local = spec_real.shape[1]
    modes = local * lon_size

    wide = half + 2 * RUNS
    below = call(
        slice_kernel, (field,), [shape(HALO, cells, c)], [DMA], in_specs=[HBM], out_specs=[ANY]
    )[0]
    down = move(below, False)
    above = call(
        slice_kernel,
        (field, below),
        [shape(HALO, cells, c)],
        [DMA],
        in_specs=[HBM, ANY],
        out_specs=[ANY],
    )[0]
    up = move(above, True)
    last, leading = call(
        side_kernel,
        (field, above),
        [shape(rows, PAD, c)] * 2,
        [pltpu.SemaphoreType.DMA((2,))],
        in_specs=[HBM, ANY],
        out_specs=[ANY] * 2,
    )
    right = [(i, (i + 1) % lon_size) for i in range(lon_size)]
    left = [(j, i) for i, j in right]
    from_left = lax.ppermute(last, "lon", right)
    from_right = lax.ppermute(leading, "lon", left)
    own_edge, below = call(
        edge_kernel,
        (from_left, from_right),
        [shape(rows, 2 * PAD, c), shape(HALO, 2 * PAD, c)],
        [],
    )
    down_edge = move(below, False)
    above = call(
        copy_kernel, (own_edge, below), [shape(HALO, 2 * PAD, c)], [], in_specs=[VMEM, ANY]
    )[0]
    up_edge = move(above, True)
    tables = (cells, lon_total, modes, lon_size)
    inverse = call(
        inverse_kernel,
        (np.stack(inverse_parts(*tables)[1:]), phase_table(*tables), above),
        [shape(2, half, 2 * modes)],
        [],
        in_specs=[VMEM, VMEM, ANY],
    )[0]
    forward, leak = forward_table(*tables)
    turn = turn_table(lon_size, local, 1.0 / lon_total)

    line = pltpu.VMEM((2, width, c), F32)
    weights = shape(CONVS, 4 if WINOGRAD else 3, 4 * c, 2 * c)
    lower = [shape(n, wide, 2 * c) for n in (rows + HALO, rows, rows - 2)]
    gathered = pltpu.VMEM((2 * modes, HALO * c), BF)
    upper = [pltpu.VMEM((4, wide, 2 * c), BF)] * 2 + [pltpu.VMEM((rows, half, 2 * c), BF)]
    hidden_shape = shape(rows, half, 2 * c)
    part_shape = [jax.ShapeDtypeStruct((modes, rows * c), F32)] * 2

    own_rows = shape(rows, wide, 2 * c)
    own, packed, later = call(
        prepare_kernel, (field, own_edge, conv_weight), [own_rows, weights, weights], [line]
    )
    low = call(
        first_lower_kernel,
        (down, down_edge, own, packed, conv_bias[0], inverse),
        lower,
        [line],
        in_specs=[VMEM] * 5 + [ANY],
    )
    kept, sent, hidden, to_up, to_down, before = call(
        first_upper_kernel,
        (up, up_edge, *low, packed, conv_bias[0], forward, leak),
        part_shape
        + [hidden_shape]
        + [shape(HALO, half, 2 * c)] * 2
        + [shape(HALO, wide, 2 * c)],
        [line] + upper,
    )
    from_down, from_up = move(to_down, False), move(to_up, True)

    def swap(array, step):
        return lax.ppermute(array, "lon", [(i, i ^ step) for i in range(lon_size)])

    def mix(kept, sent, block):
        chunk = shape(2 * local, rows * c)
        own, *others = call(pair_kernel, (kept, swap(sent, 1)), [chunk] * (lon_size // 2), [])
        sums = [own] + [swap(other, 2 * i + 2) for i, other in enumerate(others)]
        turned = pltpu.VMEM((2 * rows * local, c), F32)
        weights = pl.BlockSpec((1, local, c, c), lambda i: (block, 0, 0, 0))
        (mixed,) = call(
            mix_kernel,
            (turn, spec_real, spec_imag, conv_bias[block], *sums),
            [chunk],
            [turned, turned],
            in_specs=[VMEM, weights, weights] + [VMEM] * (1 + len(sums)),
            grid=(1,),
        )
        return lax.all_gather(mixed, "lon", axis=0, tiled=True)

    mixed = mix(kept, sent, 0)
    halo = call(halo_kernel, (mixed,), [shape(2 * modes, HALO * c)], [])[0]
    lat_size = lax.axis_size("lat")
    ways = []
    for i in range(lon_size):
        for j in range(lat_size - 1):
            here, there = i * lat_size + j, i * lat_size + j + 1
            ways.append((here, there) if i % 2 == 0 else (there, here))
    mine = lax.ppermute(halo, ("lon", "lat"), ways)
    other = swap(mine, 1)
    own = call(middle_own_kernel, (low[0], hidden, mixed, inverse), [own_rows], [])[0]
    state, *low = call(
        middle_lower_kernel,
        (low[0], from_down, mine, other, own, inverse, later, conv_bias[1]),
        lower,
        [gathered],
    )
    kept, sent, hidden = call(
        middle_upper_kernel,
        (before, from_up, mine, other, inverse, state, *low)
        + (later, conv_bias[1], forward, leak),
        part_shape + [hidden_shape],
        [pltpu.VMEM((HALO, wide, 2 * c), BF), gathered] + upper,
    )
    mixed = mix(kept, sent, 1)
    (result,) = call(
        last_kernel, (state, hidden, mixed, inverse), [shape(rows, cells, c)], [line]
    )
    return result


def solution(mesh):
    return jax.shard_map(
        per_device,
        mesh=mesh,
        in_specs=(
            P("lat", "lon", None),
            P(),
            P(),
            P(None, "lon", None, None),
            P(None, "lon", None, None),
        ),
        out_specs=P("lat", "lon", None),
        check_vma=False,
    )
```

time: 101 us -> 94.1 us (0.932)
  blocking collectives: 37.9 us -> 17.6 us
  waiting for transfers between devices: 12.3 us -> 19.2 us
  starting transfers between devices: 26.4 us -> 32.7 us
  Pallas kernels: 20.2 us -> 22.6 us
  local copies, waits for them, and re-layouts: 3.42 us -> 1.29 us
    all_to_all x2 -> x0, blocking collectives: 20.1 us -> none  [mix(): chunks = lax.all_to_all(chunks, 'lon', 0, 0)]
    ppermute x8 -> x16, waiting for transfers between devices: 10.9 us -> 17.7 us  [the longest x9 10.5 us: swap(): return lax.ppermute(array, 'lon', [(i, i ^ step) for i in range(lon_size)])]
    ppermute x8 -> x16, starting transfers between devices: 23.8 us -> 30 us  [the longest x6 18.9 us: move(): return lax.ppermute(array, 'lat', pairs)]
    pallas_call x8 -> x18, Pallas kernels: 20.2 us -> 22.6 us  [call(): pl.pallas_call(kernel, grid=grid, out_shape=outs, in_specs=in_specs or [V...]
    unnamed x26 -> x24, local copies, waits for them, and re-layouts: 3.41 us -> 1.29 us
  transfers between devices with their start and end apart: 10 -> 18, of which waited for: 4 -> 12; matrix products, arithmetic and copies ran while one was open for 0% -> 0% of each run, Pallas kernels for 1% -> 9%
where the time goes in v3:
time: 94.1 us; the launch traced here: 93.8 us
  starting transfers between devices  32.7 us (35%)
  Pallas kernels  22.6 us (24%)
  waiting for transfers between devices  19.2 us (20%)
  blocking collectives  17.6 us (19%)
  local copies, waits for them, and re-layouts  1.29 us (1%)
    pallas_call x18, Pallas kernels, call(): pl.pallas_call(kernel, grid=grid, out_shape=outs, in_specs=in_specs or [V...  22.6 us
    ppermute x6, starting transfers between devices, move(): return lax.ppermute(array, 'lat', pairs)  18.9 us
    all_gather x2, blocking collectives, mix(): return lax.all_gather(mixed, 'lon', axis=0, tiled=True)  17.6 us
    ppermute x9, waiting for transfers between devices, swap(): return lax.ppermute(array, 'lon', [(i, i ^ step) for i in range(lon_size)])  10.5 us
    ppermute x9, starting transfers between devices, swap(): return lax.ppermute(array, 'lon', [(i, i ^ step) for i in range(lon_size)])  7.52 us
    ppermute x6, waiting for transfers between devices, move(): return lax.ppermute(array, 'lat', pairs)  4.26 us
    ppermute x1, starting transfers between devices, per_device(): mine = lax.ppermute(halo, ('lon', 'lat'), ways)  3.64 us
    ppermute x1, waiting for transfers between devices, per_device(): mine = lax.ppermute(halo, ('lon', 'lat'), ways)  2.98 us
  transfers between devices with their start and end apart: 18, of which 12 were waited for; matrix products, arithmetic and copies ran while one was open for 0% of the time, Pallas kernels for 9%

profile of v3, /device:TPU:0, one launch (start us, length us, event | category | flops | bytes accessed | tf_op | source)
XLA Modules:
  0.0 93.8 jit_solution(17450402511834392837)
XLA Ops:
  0.0 1.2 %copy-done = bf16[4,1024,128]{2,1,0:T(8,128)(2,1)S(1)} copy-done((bf16[4,1024,128]{2,1,0:T(8,128)(2,1)S(1)}, bf16[4,1024,128]{2,1,0:T(8,128)(2,1)}, u32[]{:S(2)}) %copy-start) | copy-done | bytes 1048600
  1.2 0.1 shard_map.100.rest_0_
  1.3 1.6 %collective-permute-start = (bf16[3,1024,128]{2,1,0:T(8,128)(2,1)S(1)}, bf16[3,1024,128]{2,1,0:T(8,128)(2,1)S(1)}, u32[]{:S(2)}, u32[]{:S(2)}) collective-permute-start(bf16[3,1024,128]{2,1,0:T(8,128)(2,1)S(1)} %shard_map.100.rest_0_), channel_id=1, source_target_pairs={{1,0},{2,1},{3,2},{5,4},{6,5},{7,6},{9,8},{10,9},{11,10},{13,12},{... | collective-permute-start | bytes 2359304 | tf_op jit(solution)/shard_map/ppermute | solution.py:451
  2.9 0.1 shard_map.101.after
  3.0 5.6 %collective-permute-start.4 = (bf16[3,1024,128]{2,1,0:T(8,128)(2,1)S(1)}, bf16[3,1024,128]{2,1,0:T(8,128)(2,1)S(1)}, u32[]{:S(2)}, u32[]{:S(2)}) collective-permute-start(bf16[3,1024,128]{2,1,0:T(8,128)(2,1)S(1)} %shard_map.101.after), channel_id=1, source_target_pairs={{0,1},{1,2},{2,3},{4,5},{5,6},{6,7},{8,9},{9,10},{10,11},{12,13},{... | collective-permute-start | bytes 2359304 | tf_op jit(solution)/shard_map/ppermute | solution.py:451
  8.6 0.0 copy-start.5
  8.6 0.0 copy-start.9
  8.7 0.1 collective-permute-start.1
  8.7 2.6 %collective-permute-start.2 = (bf16[4,16,128]{2,1,0:T(8,128)(2,1)S(1)}, bf16[4,16,128]{2,1,0:T(8,128)(2,1)S(1)}, u32[]{:S(2)}, u32[]{:S(2)}) collective-permute-start(bf16[4,16,128]{2,1,0:T(8,128)(2,1)S(1)} %get-tuple-element.36), channel_id=1, source_target_pairs={{4,0},{8,4},{12,8},{16,12},{20,16},{24,20},{28,24},{0,28},{5,1},{9... | collective-permute-start | bytes 49160 | tf_op jit(solution)/shard_map/ppermute | solution.py:504
  11.3 1.4 %collective-permute-done.1.from_left = bf16[4,16,128]{2,1,0:T(8,128)(2,1)S(1)} collective-permute-done((bf16[4,16,128]{2,1,0:T(8,128)(2,1)S(1)}, bf16[4,16,128]{2,1,0:T(8,128)(2,1)S(1)}, u32[]{:S(2)}, u32[]{:S(2)}) %collective-permute-start.1) | collective-permute-done | bytes 16416 | tf_op jit(solution)/shard_map/ppermute | solution.py:503
  12.8 0.0 collective-permute-done.2.from_right
  12.8 1.3 %collective-permute-start.3 = (bf16[3,32,128]{2,1,0:T(8,128)(2,1)S(1)}, bf16[3,32,128]{2,1,0:T(8,128)(2,1)S(1)}, u32[]{:S(2)}, u32[]{:S(2)}) collective-permute-start(bf16[3,32,128]{2,1,0:T(8,128)(2,1)S(1)} %get-tuple-element.37.below), channel_id=1, source_target_pairs={{1,0},{2,1},{3,2},{5,4},{6,5},{7,6},{9,8},{10,9},{11,10},{13,12},{... | collective-permute-start | bytes 73736 | tf_op jit(solution)/shard_map/ppermute | solution.py:451
  14.1 4.5 %collective-permute-start.5 = (bf16[3,32,128]{2,1,0:T(8,128)(2,1)S(1)}, bf16[3,32,128]{2,1,0:T(8,128)(2,1)S(1)}, u32[]{:S(2)}, u32[]{:S(2)}) collective-permute-start(bf16[3,32,128]{2,1,0:T(8,128)(2,1)S(1)} %shard_map.105.after), channel_id=1, source_target_pairs={{0,1},{1,2},{2,3},{4,5},{5,6},{6,7},{8,9},{9,10},{10,11},{12,13},{... | collective-permute-start | bytes 73736 | tf_op jit(solution)/shard_map/ppermute | solution.py:451
  18.7 1.5 %shard_map.104 = (bf16[4,560,256]{2,1,0:T(8,128)(2,1)S(1)}, bf16[3,4,512,256]{3,2,1,0:T(8,128)(2,1)S(1)}, bf16[3,4,512,256]{3,2,1,0:T(8,128)(2,1)S(1)}) custom-call(bf16[4,1024,128]{2,1,0:T(8,128)(2,1)S(1)} %copy-done.1, bf16[4,32,128]{2,1,0:T(8,128)(2,1)S(1)} %get-tuple-element.38.own_edge.edges, bf16[2,3,3,3,128,128]{5,4,3,2,1,0:T(8,128)(2,1)S(1)} %copy-done.6), custom_call_target="tpu_custom_call" | custom-call | tf_op jit(solution)/shard_map/pallas_call | solution.py:459
  20.2 0.1 shard_map.106.after.inverse
  20.3 4.2 %collective-permute-done.3.down_edge = bf16[3,32,128]{2,1,0:T(8,128)(2,1)S(1)} collective-permute-done((bf16[3,32,128]{2,1,0:T(8,128)(2,1)S(1)}, bf16[3,32,128]{2,1,0:T(8,128)(2,1)S(1)}, u32[]{:S(2)}, u32[]{:S(2)}) %collective-permute-start.3) | collective-permute-done | bytes 24608 | tf_op jit(solution)/shard_map/ppermute | solution.py:451
  24.6 2.8 %shard_map.107 = (bf16[7,560,256]{2,1,0:T(8,128)(2,1)S(1)}, bf16[4,560,256]{2,1,0:T(8,128)(2,1)S(1)}, bf16[2,560,256]{2,1,0:T(8,128)(2,1)S(1)}) custom-call(bf16[3,1024,128]{2,1,0:T(8,128)(2,1)S(1)} %collective-permute-done.down, bf16[3,32,128]{2,1,0:T(8,128)(2,1)S(1)} %collective-permute-done.3.down_edge, bf16[4,560,256]{2,1,0:T(8,128)(2,1)S(1)} %get-tuple-element.39.own, ...), custom_call_target="tpu_custom_call" | custom-call | tf_op jit(solution)/shard_map/pallas_call | solution.py:459
  27.5 5.8 %shard_map.108 = (f32[128,512]{1,0:T(8,128)S(1)}, f32[128,512]{1,0:T(8,128)S(1)}, bf16[4,528,256]{2,1,0:T(8,128)(2,1)S(1)}, bf16[3,528,256]{2,1,0:T(8,128)(2,1)S...) custom-call(bf16[3,1024,128]{2,1,0:T(8,128)(2,1)S(1)} %collective-permute-done.4.up, ...), custom_call_target="tpu_custom_call" | custom-call | tf_op jit(solution)/shard_map/pallas_call | solution.py:459
  33.3 1.3 %collective-permute-start.6 = (bf16[3,528,256]{2,1,0:T(8,128)(2,1)S(1)}, bf16[3,528,256]{2,1,0:T(8,128)(2,1)S(1)}, u32[]{:S(2)}, u32[]{:S(2)}) collective-permute-start(bf16[3,528,256]{2,1,0:T(8,128)(2,1)S(1)} %get-tuple-element.44), channel_id=1, source_target_pairs={{1,0},{2,1},{3,2},{5,4},{6,5},{7,6},{9,8},{10,9},{11,10},{13,12},{... | collective-permute-start | bytes 2433032 | tf_op jit(solution)/shard_map/ppermute | solution.py:451
  34.6 4.6 %collective-permute-start.13 = (bf16[3,528,256]{2,1,0:T(8,128)(2,1)S(1)}, bf16[3,528,256]{2,1,0:T(8,128)(2,1)S(1)}, u32[]{:S(2)}, u32[]{:S(2)}) collective-permute-start(bf16[3,528,256]{2,1,0:T(8,128)(2,1)S(1)} %get-tuple-element.55), channel_id=1, source_target_pairs={{0,1},{1,2},{2,3},{4,5},{5,6},{6,7},{8,9},{9,10},{10,11},{12,13},{... | collective-permute-start | bytes 2433032 | tf_op jit(solution)/shard_map/ppermute | solution.py:451
  39.2 0.1 collective-permute-start.7
  39.3 1.5 %collective-permute-done.7.got = f32[128,512]{1,0:T(8,128)S(1)} collective-permute-done((f32[128,512]{1,0:T(8,128)S(1)}, f32[128,512]{1,0:T(8,128)S(1)}, u32[]{:S(2)}, u32[]{:S(2)}) %collective-permute-start.7) | collective-permute-done | bytes 262176 | tf_op jit(solution)/shard_map/ppermute | solution.py:558
  40.9 2.7 %collective-permute-start.10 = (bf16[32,512]{1,0:T(8,128)(2,1)S(1)}, bf16[32,512]{1,0:T(8,128)(2,1)S(1)}, u32[]{:S(2)}, u32[]{:S(2)}) collective-permute-start(bf16[32,512]{1,0:T(8,128)(2,1)S(1)} %get-tuple-element.50), channel_id=1, source_target_pairs={{0,24},{4,28},{8,16},{12,20},{16,8},{20,12},{24,0},{28,4},{1,25},{... | collective-permute-start | bytes 98312 | tf_op jit(solution)/shard_map/ppermute | solution.py:558
  43.6 0.5 collective-permute-start.8
  44.1 0.4 collective-permute-start.9
  44.4 1.3 %collective-permute-done.10.rest_3_ = bf16[32,512]{1,0:T(8,128)(2,1)S(1)} collective-permute-done((bf16[32,512]{1,0:T(8,128)(2,1)S(1)}, bf16[32,512]{1,0:T(8,128)(2,1)S(1)}, u32[]{:S(2)}, u32[]{:S(2)}) %collective-permute-start.10) | collective-permute-done | bytes 32800 | tf_op jit(solution)/shard_map/ppermute | solution.py:558
  45.8 1.7 %collective-permute-done.8.rest_1_ = bf16[32,512]{1,0:T(8,128)(2,1)S(1)} collective-permute-done((bf16[32,512]{1,0:T(8,128)(2,1)S(1)}, bf16[32,512]{1,0:T(8,128)(2,1)S(1)}, u32[]{:S(2)}, u32[]{:S(2)}) %collective-permute-start.8) | collective-permute-done | bytes 32800 | tf_op jit(solution)/shard_map/ppermute | solution.py:558
  47.5 0.5 collective-permute-done.9.rest_2_
  48.0 0.4 shard_map.110
  48.4 9.3 %all_gather.6.mixed = bf16[256,512]{1,0:T(8,128)(2,1)S(1)} all-gather(bf16[32,512]{1,0:T(8,128)(2,1)S(1)} %shard_map.110), channel_id=1, replica_groups=mesh['lon'=8,'lat'=4] {'lon'}, dimensions={0}, use_global_device_ids=true | all-gather | bytes 294912 | tf_op jit(solution)/shard_map/all_gather | solution.py:574
  57.8 3.6 %collective-permute-start.11 = (bf16[256,384]{1,0:T(8,128)(2,1)S(1)}, bf16[256,384]{1,0:T(8,128)(2,1)S(1)}, u32[]{:S(2)}, u32[]{:S(2)}) collective-permute-start(bf16[256,384]{1,0:T(8,128)(2,1)S(1)} %shard_map.111), channel_id=1, source_target_pairs={{0,1},{1,2},{2,3},{5,4},{6,5},{7,6},{8,9},{9,10},{10,11},{13,12},{... | collective-permute-start | bytes 589832 | tf_op jit(solution)/shard_map/ppermute | solution.py:584
  61.4 3.0 %collective-permute-done.11.mine = bf16[256,384]{1,0:T(8,128)(2,1)S(1)} collective-permute-done((bf16[256,384]{1,0:T(8,128)(2,1)S(1)}, bf16[256,384]{1,0:T(8,128)(2,1)S(1)}, u32[]{:S(2)}, u32[]{:S(2)}) %collective-permute-start.11) | collective-permute-done | bytes 196640 | tf_op jit(solution)/shard_map/ppermute | solution.py:584
  64.4 0.1 collective-permute-start.12
  64.5 0.6 shard_map.112.own
  65.1 0.7 collective-permute-done.12.other
  65.8 2.9 %shard_map.113 = (bf16[7,560,256]{2,1,0:T(8,128)(2,1)S(1)}, bf16[4,560,256]{2,1,0:T(8,128)(2,1)S(1)}, bf16[2,560,256]{2,1,0:T(8,128)(2,1)S(1)}) custom-call(bf16[7,560,256]{2,1,0:T(8,128)(2,1)S(1)} %get-tuple-element.41.field, bf16[3,528,256]{2,1,0:T(8,128)(2,1)S(1)} %collective-permute-done.6.from_down, bf16[256,384]{1,0:T(8,128)(2,1)S(1)} %collective-permute-done.11.mine, ...), custom_call_target="tpu_custom_call" | custom-call | tf_op jit(solution)/shard_map/pallas_call | solution.py:459
  68.8 6.0 %shard_map.114 = (f32[128,512]{1,0:T(8,128)S(1)}, f32[128,512]{1,0:T(8,128)S(1)}, bf16[4,528,256]{2,1,0:T(8,128)(2,1)S(1)}) custom-call(bf16[3,560,256]{2,1,0:T(8,128)(2,1)S(1)} %get-tuple-element.54.before, bf16[3,528,256]{2,1,0:T(8,128)(2,1)S(1)} %collective-permute-done.13.from_up, bf16[256,384]{1,0:T(8,128)(2,1)S(1)} %collective-permute-done.11.mine, ...), custom_call_target="tpu_custom_call" | custom-call | tf_op jit(solution)/shard_map/pallas_call | solution.py:459
  74.8 0.2 collective-permute-start.14
  75.0 1.4 %collective-permute-done.14.got = f32[128,512]{1,0:T(8,128)S(1)} collective-permute-done((f32[128,512]{1,0:T(8,128)S(1)}, f32[128,512]{1,0:T(8,128)S(1)}, u32[]{:S(2)}, u32[]{:S(2)}) %collective-permute-start.14) | collective-permute-done | bytes 262176 | tf_op jit(solution)/shard_map/ppermute | solution.py:558
  76.4 0.6 collective-permute-start.15
  77.0 1.5 %collective-permute-start.16 = (bf16[32,512]{1,0:T(8,128)(2,1)S(1)}, bf16[32,512]{1,0:T(8,128)(2,1)S(1)}, u32[]{:S(2)}, u32[]{:S(2)}) collective-permute-start(bf16[32,512]{1,0:T(8,128)(2,1)S(1)} %get-tuple-element.63), channel_id=1, source_target_pairs={{0,16},{4,20},{8,24},{12,28},{16,0},{20,4},{24,8},{28,12},{1,17},{... | collective-permute-start | bytes 98312 | tf_op jit(solution)/shard_map/ppermute | solution.py:558
  78.5 1.5 %collective-permute-start.17 = (bf16[32,512]{1,0:T(8,128)(2,1)S(1)}, bf16[32,512]{1,0:T(8,128)(2,1)S(1)}, u32[]{:S(2)}, u32[]{:S(2)}) collective-permute-start(bf16[32,512]{1,0:T(8,128)(2,1)S(1)} %get-tuple-element.64), channel_id=1, source_target_pairs={{0,24},{4,28},{8,16},{12,20},{16,8},{20,12},{24,0},{28,4},{1,25},{... | collective-permute-start | bytes 98312 | tf_op jit(solution)/shard_map/ppermute | solution.py:558
  80.0 0.4 collective-permute-done.15.rest_1_
  80.4 0.5 collective-permute-done.16.rest_2_
  80.9 2.4 %collective-permute-done.17.rest_3_ = bf16[32,512]{1,0:T(8,128)(2,1)S(1)} collective-permute-done((bf16[32,512]{1,0:T(8,128)(2,1)S(1)}, bf16[32,512]{1,0:T(8,128)(2,1)S(1)}, u32[]{:S(2)}, u32[]{:S(2)}) %collective-permute-start.17) | collective-permute-done | bytes 32800 | tf_op jit(solution)/shard_map/ppermute | solution.py:558
  83.3 0.4 shard_map.116
  83.8 8.3 %all_gather.7.mixed = bf16[256,512]{1,0:T(8,128)(2,1)S(1)} all-gather(bf16[32,512]{1,0:T(8,128)(2,1)S(1)} %shard_map.116), channel_id=1, replica_groups=mesh['lon'=8,'lat'=4] {'lon'}, dimensions={0}, use_global_device_ids=true | all-gather | bytes 294912 | tf_op jit(solution)/shard_map/all_gather | solution.py:574
  92.1 1.7 %shard_map.117 = bf16[4,1024,128]{2,1,0:T(8,128)(2,1)} custom-call(bf16[7,560,256]{2,1,0:T(8,128)(2,1)S(1)} %get-tuple-element.53.state, bf16[4,528,256]{2,1,0:T(8,128)(2,1)S(1)} %get-tuple-element.58.hidden, bf16[256,512]{1,0:T(8,128)(2,1)S(1)} %all_gather.7.mixed, bf16[2,528,256]{2,1,0:T(8,128)(2,1)S(1)} %shard_map.106.after.inverse), custom_call_target="tpu_custom_call" | custom-call | tf_op jit(solution)/shard_map/pallas_call | solution.py:459
  (33 shorter events, 0.2 us)
Async XLA Ops:
  0.0 1.2 %copy-start = (bf16[4,1024,128]{2,1,0:T(8,128)(2,1)S(1)}, bf16[4,1024,128]{2,1,0:T(8,128)(2,1)}, u32[]{:S(2)}) copy-start(bf16[4,1024,128]{2,1,0:T(8,128)(2,1)} %own.1) | copy-start | bytes 3145732
  1.3 17.4 %copy-start.10 = (f32[2,3,128]{2,0,1:T(2,128)S(1)}, f32[2,3,128]{2,0,1:T(2,128)}, u32[]{:S(2)}) copy-start(f32[2,3,128]{2,0,1:T(2,128)} %param.12) | copy-start | bytes 9220
  1.3 17.4 %copy-start.1 = (bf16[4,1024,128]{2,1,0:T(8,128)(2,1)S(1)}, bf16[4,1024,128]{2,1,0:T(8,128)(2,1)}, u32[]{:S(2)}) copy-start(bf16[4,1024,128]{2,1,0:T(8,128)(2,1)} %own.1) | copy-start | bytes 3145732
  1.3 17.4 %copy-start.6 = (bf16[2,3,3,3,128,128]{5,4,3,2,1,0:T(8,128)(2,1)S(1)}, bf16[2,3,3,3,128,128]{5,4,3,2,1,0:T(8,128)(2,1)}, u32[]{:S(2)}) copy-start(bf16[2,3,3,3,128,128]{5,4,3,2,1,0:T(8,128)(2,1)} %kernels.1) | copy-start | bytes 5308420
  1.3 23.3 %collective-permute-start = (bf16[3,1024,128]{2,1,0:T(8,128)(2,1)S(1)}, bf16[3,1024,128]{2,1,0:T(8,128)(2,1)S(1)}, u32[]{:S(2)}, u32[]{:S(2)}) collective-permute-start(bf16[3,1024,128]{2,1,0:T(8,128)(2,1)S(1)} %shard_map.100.rest_0_), channel_id=1, source_target_pairs={{1,0},{2,1},{3,2},{5,4},{6,5},{7,6},{9,8},{10,9},{11,10},{13,12},{... | collective-permute-start | bytes 2359304 | tf_op jit(solution)/shard_map/ppermute | solution.py:451
  3.0 24.5 %collective-permute-start.4 = (bf16[3,1024,128]{2,1,0:T(8,128)(2,1)S(1)}, bf16[3,1024,128]{2,1,0:T(8,128)(2,1)S(1)}, u32[]{:S(2)}, u32[]{:S(2)}) collective-permute-start(bf16[3,1024,128]{2,1,0:T(8,128)(2,1)S(1)} %shard_map.101.after), channel_id=1, source_target_pairs={{0,1},{1,2},{2,3},{4,5},{5,6},{6,7},{8,9},{9,10},{10,11},{12,13},{... | collective-permute-start | bytes 2359304 | tf_op jit(solution)/shard_map/ppermute | solution.py:451
  8.6 11.6 %copy-start.5 = (f32[2,2,528,256]{3,2,1,0:T(8,128)S(1)}, f32[2,2,528,256]{3,2,1,0:T(8,128)}, u32[]{:S(2)}) copy-start(f32[2,2,528,256]{3,2,1,0:T(8,128)} %constant.10.clone.parts) | copy-start | bytes 6488068
  8.6 11.6 %copy-start.9 = (f32[8,2,256]{2,1,0:T(2,128)S(1)}, f32[8,2,256]{2,1,0:T(2,128)}, u32[]{:S(2)}) copy-start(f32[8,2,256]{2,1,0:T(2,128)} %constant.11.clone.phase) | copy-start | bytes 49156
  8.7 4.1 %collective-permute-start.1 = (bf16[4,16,128]{2,1,0:T(8,128)(2,1)S(1)}, bf16[4,16,128]{2,1,0:T(8,128)(2,1)S(1)}, u32[]{:S(2)}, u32[]{:S(2)}) collective-permute-start(bf16[4,16,128]{2,1,0:T(8,128)(2,1)S(1)} %get-tuple-element.35), channel_id=1, source_target_pairs={{0,4},{4,8},{8,12},{12,16},{16,20},{20,24},{24,28},{28,0},{1,5},{5... | collective-permute-start | bytes 49160 | tf_op jit(solution)/shard_map/ppermute | solution.py:503
  8.7 4.1 %collective-permute-start.2 = (bf16[4,16,128]{2,1,0:T(8,128)(2,1)S(1)}, bf16[4,16,128]{2,1,0:T(8,128)(2,1)S(1)}, u32[]{:S(2)}, u32[]{:S(2)}) collective-permute-start(bf16[4,16,128]{2,1,0:T(8,128)(2,1)S(1)} %get-tuple-element.36), channel_id=1, source_target_pairs={{4,0},{8,4},{12,8},{16,12},{20,16},{24,20},{28,24},{0,28},{5,1},{9... | collective-permute-start | bytes 49160 | tf_op jit(solution)/shard_map/ppermute | solution.py:504
  12.8 11.8 %collective-permute-start.3 = (bf16[3,32,128]{2,1,0:T(8,128)(2,1)S(1)}, bf16[3,32,128]{2,1,0:T(8,128)(2,1)S(1)}, u32[]{:S(2)}, u32[]{:S(2)}) collective-permute-start(bf16[3,32,128]{2,1,0:T(8,128)(2,1)S(1)} %get-tuple-element.37.below), channel_id=1, source_target_pairs={{1,0},{2,1},{3,2},{5,4},{6,5},{7,6},{9,8},{10,9},{11,10},{13,12},{... | collective-permute-start | bytes 73736 | tf_op jit(solution)/shard_map/ppermute | solution.py:451
  14.1 13.3 %collective-permute-start.5 = (bf16[3,32,128]{2,1,0:T(8,128)(2,1)S(1)}, bf16[3,32,128]{2,1,0:T(8,128)(2,1)S(1)}, u32[]{:S(2)}, u32[]{:S(2)}) collective-permute-start(bf16[3,32,128]{2,1,0:T(8,128)(2,1)S(1)} %shard_map.105.after), channel_id=1, source_target_pairs={{0,1},{1,2},{2,3},{4,5},{5,6},{6,7},{8,9},{9,10},{10,11},{12,13},{... | collective-permute-start | bytes 73736 | tf_op jit(solution)/shard_map/ppermute | solution.py:451
  24.6 2.8 %copy-start.2 = (bf16[2,512,1056]{2,1,0:T(8,128)(2,1)S(1)}, bf16[2,512,1056]{2,1,0:T(8,128)(2,1)}, u32[]{:S(2)}) copy-start(bf16[2,512,1056]{2,1,0:T(8,128)(2,1)} %constant.12.clone.forward) | copy-start | bytes 6488068
  24.6 2.9 %copy-start.7 = (f32[2,256,1]{2,1,0:T(8,128)S(1)}, f32[2,256,1]{2,1,0:T(8,128)}, u32[]{:S(2)}) copy-start(f32[2,256,1]{2,1,0:T(8,128)} %constant.13.clone.leak) | copy-start | bytes 6148
  27.5 20.5 %copy-start.3 = (bf16[2,16,128,128]{3,2,1,0:T(8,128)(2,1)S(1)}, bf16[2,16,128,128]{3,2,1,0:T(8,128)(2,1)}, u32[]{:S(2)}) copy-start(bf16[2,16,128,128]{3,2,1,0:T(8,128)(2,1)} %real.3) | copy-start | bytes 3145732
  27.5 20.5 %copy-start.4 = (bf16[2,16,128,128]{3,2,1,0:T(8,128)(2,1)S(1)}, bf16[2,16,128,128]{3,2,1,0:T(8,128)(2,1)}, u32[]{:S(2)}) copy-start(bf16[2,16,128,128]{3,2,1,0:T(8,128)(2,1)} %imag.3) | copy-start | bytes 3145732
  27.5 20.5 %copy-start.8 = (bf16[8,64,128]{2,1,0:T(8,128)(2,1)S(1)}, bf16[8,64,128]{2,1,0:T(8,128)(2,1)}, u32[]{:S(2)}) copy-start(bf16[8,64,128]{2,1,0:T(8,128)(2,1)} %constant.14.clone.turn) | copy-start | bytes 393220
  33.3 32.5 %collective-permute-start.6 = (bf16[3,528,256]{2,1,0:T(8,128)(2,1)S(1)}, bf16[3,528,256]{2,1,0:T(8,128)(2,1)S(1)}, u32[]{:S(2)}, u32[]{:S(2)}) collective-permute-start(bf16[3,528,256]{2,1,0:T(8,128)(2,1)S(1)} %get-tuple-element.44), channel_id=1, source_target_pairs={{1,0},{2,1},{3,2},{5,4},{6,5},{7,6},{9,8},{10,9},{11,10},{13,12},{... | collective-permute-start | bytes 2433032 | tf_op jit(solution)/shard_map/ppermute | solution.py:451
  34.6 34.1 %collective-permute-start.13 = (bf16[3,528,256]{2,1,0:T(8,128)(2,1)S(1)}, bf16[3,528,256]{2,1,0:T(8,128)(2,1)S(1)}, u32[]{:S(2)}, u32[]{:S(2)}) collective-permute-start(bf16[3,528,256]{2,1,0:T(8,128)(2,1)S(1)} %get-tuple-element.55), channel_id=1, source_target_pairs={{0,1},{1,2},{2,3},{4,5},{5,6},{6,7},{8,9},{9,10},{10,11},{12,13},{... | collective-permute-start | bytes 2433032 | tf_op jit(solution)/shard_map/ppermute | solution.py:451
  39.2 1.6 %collective-permute-start.7 = (f32[128,512]{1,0:T(8,128)S(1)}, f32[128,512]{1,0:T(8,128)S(1)}, u32[]{:S(2)}, u32[]{:S(2)}) collective-permute-start(f32[128,512]{1,0:T(8,128)S(1)} %get-tuple-element.46), channel_id=1, source_target_pairs={{0,4},{4,0},{8,12},{12,8},{16,20},{20,16},{24,28},{28,24},{1,5},{5... | collective-permute-start | bytes 786440 | tf_op jit(solution)/shard_map/ppermute | solution.py:558
  40.9 4.9 %collective-permute-start.10 = (bf16[32,512]{1,0:T(8,128)(2,1)S(1)}, bf16[32,512]{1,0:T(8,128)(2,1)S(1)}, u32[]{:S(2)}, u32[]{:S(2)}) collective-permute-start(bf16[32,512]{1,0:T(8,128)(2,1)S(1)} %get-tuple-element.50), channel_id=1, source_target_pairs={{0,24},{4,28},{8,16},{12,20},{16,8},{20,12},{24,0},{28,4},{1,25},{... | collective-permute-start | bytes 98312 | tf_op jit(solution)/shard_map/ppermute | solution.py:558
  43.6 3.9 %collective-permute-start.8 = (bf16[32,512]{1,0:T(8,128)(2,1)S(1)}, bf16[32,512]{1,0:T(8,128)(2,1)S(1)}, u32[]{:S(2)}, u32[]{:S(2)}) collective-permute-start(bf16[32,512]{1,0:T(8,128)(2,1)S(1)} %get-tuple-element.48), channel_id=1, source_target_pairs={{0,8},{4,12},{8,0},{12,4},{16,24},{20,28},{24,16},{28,20},{1,9},{5... | collective-permute-start | bytes 98312 | tf_op jit(solution)/shard_map/ppermute | solution.py:558
  44.1 3.9 %collective-permute-start.9 = (bf16[32,512]{1,0:T(8,128)(2,1)S(1)}, bf16[32,512]{1,0:T(8,128)(2,1)S(1)}, u32[]{:S(2)}, u32[]{:S(2)}) collective-permute-start(bf16[32,512]{1,0:T(8,128)(2,1)S(1)} %get-tuple-element.49), channel_id=1, source_target_pairs={{0,16},{4,20},{8,24},{12,28},{16,0},{20,4},{24,8},{28,12},{1,17},{... | collective-permute-start | bytes 98312 | tf_op jit(solution)/shard_map/ppermute | solution.py:558
  57.8 6.6 %collective-permute-start.11 = (bf16[256,384]{1,0:T(8,128)(2,1)S(1)}, bf16[256,384]{1,0:T(8,128)(2,1)S(1)}, u32[]{:S(2)}, u32[]{:S(2)}) collective-permute-start(bf16[256,384]{1,0:T(8,128)(2,1)S(1)} %shard_map.111), channel_id=1, source_target_pairs={{0,1},{1,2},{2,3},{5,4},{6,5},{7,6},{8,9},{9,10},{10,11},{13,12},{... | collective-permute-start | bytes 589832 | tf_op jit(solution)/shard_map/ppermute | solution.py:584
  64.4 1.4 %collective-permute-start.12 = (bf16[256,384]{1,0:T(8,128)(2,1)S(1)}, bf16[256,384]{1,0:T(8,128)(2,1)S(1)}, u32[]{:S(2)}, u32[]{:S(2)}) collective-permute-start(bf16[256,384]{1,0:T(8,128)(2,1)S(1)} %collective-permute-done.11.mine), channel_id=1, source_target_pairs={{0,4},{4,0},{8,12},{12,8},{16,20},{20,16},{24,28},{28,24},{1,5},{5... | collective-permute-start | bytes 589832 | tf_op jit(solution)/shard_map/ppermute | solution.py:558
  74.8 1.6 %collective-permute-start.14 = (f32[128,512]{1,0:T(8,128)S(1)}, f32[128,512]{1,0:T(8,128)S(1)}, u32[]{:S(2)}, u32[]{:S(2)}) collective-permute-start(f32[128,512]{1,0:T(8,128)S(1)} %get-tuple-element.60), channel_id=1, source_target_pairs={{0,4},{4,0},{8,12},{12,8},{16,20},{20,16},{24,28},{28,24},{1,5},{5... | collective-permute-start | bytes 786440 | tf_op jit(solution)/shard_map/ppermute | solution.py:558
  76.4 4.0 %collective-permute-start.15 = (bf16[32,512]{1,0:T(8,128)(2,1)S(1)}, bf16[32,512]{1,0:T(8,128)(2,1)S(1)}, u32[]{:S(2)}, u32[]{:S(2)}) collective-permute-start(bf16[32,512]{1,0:T(8,128)(2,1)S(1)} %get-tuple-element.62), channel_id=1, source_target_pairs={{0,8},{4,12},{8,0},{12,4},{16,24},{20,28},{24,16},{28,20},{1,9},{5... | collective-permute-start | bytes 98312 | tf_op jit(solution)/shard_map/ppermute | solution.py:558
  77.0 3.9 %collective-permute-start.16 = (bf16[32,512]{1,0:T(8,128)(2,1)S(1)}, bf16[32,512]{1,0:T(8,128)(2,1)S(1)}, u32[]{:S(2)}, u32[]{:S(2)}) collective-permute-start(bf16[32,512]{1,0:T(8,128)(2,1)S(1)} %get-tuple-element.63), channel_id=1, source_target_pairs={{0,16},{4,20},{8,24},{12,28},{16,0},{20,4},{24,8},{28,12},{1,17},{... | collective-permute-start | bytes 98312 | tf_op jit(solution)/shard_map/ppermute | solution.py:558
  78.5 4.8 %collective-permute-start.17 = (bf16[32,512]{1,0:T(8,128)(2,1)S(1)}, bf16[32,512]{1,0:T(8,128)(2,1)S(1)}, u32[]{:S(2)}, u32[]{:S(2)}) collective-permute-start(bf16[32,512]{1,0:T(8,128)(2,1)S(1)} %get-tuple-element.64), channel_id=1, source_target_pairs={{0,24},{4,28},{8,16},{12,20},{16,8},{20,12},{24,0},{28,4},{1,25},{... | collective-permute-start | bytes 98312 | tf_op jit(solution)/shard_map/ppermute | solution.py:558

commit v4 on v3

--- a/solution.py
+++ b/solution.py
@@ -24,6 +24,14 @@
 PARAMS = pltpu.CompilerParams(vmem_limit_bytes=28 << 20)
 
 
+def odd_lat():
+    return lax.rem(lax.axis_index("lat"), 2)
+
+
+def flip(row, rows):
+    return row + odd_lat() * (rows - 1 - 2 * row)
+
+
 def tile_of(tiles):
     return max(n for n in range(1, 12) if tiles % n == 0) * RUNS
 
@@ -50,7 +58,7 @@
     c = kernels.shape[-1]
     zero = jnp.zeros((c, c), BF)
     for tap in range(3):
-        g0, g1, g2 = (kernels[block, layer, a, tap].astype(F32) for a in range(3))
+        g0, g1, g2 = (kernels[block, layer, flip(a, 3), tap].astype(F32) for a in range(3))
         if WINOGRAD:
             outer = g0 + g2
             parts = (0.5 * g0, 0.25 * (outer + g1), 0.25 * (outer - g1), 0.5 * g2)
@@ -174,38 +182,39 @@
 
 
 def prepare_kernel(own, own_edge, kernels, field, packed, later, line):
+    rows = own.shape[0]
     for layer in range(CONVS):
         build_weights(kernels, 0, packed, layer)
         build_weights(kernels, 1, later, layer)
-    for row in range(own.shape[0]):
-        pack_cells(own, own_edge, row, line.at[row % 2], field, row)
+    for row in range(rows):
+        pack_cells(own, own_edge, flip(row, rows), line.at[row % 2], field, row)
 
 
 def first_lower_kernel(down, down_edge, own, packed, bias, after, field, first, second, line):
     rows = own.shape[0]
     field[:rows] = own[...]
     for row in range(HALO):
-        pack_cells(down, down_edge, row, line.at[row % 2], field, rows + row)
+        pack_cells(down, down_edge, flip(row, HALO), line.at[row % 2], field, rows + row)
     lower_part(field, first, second, packed, bias, lat_edges(), rows)
 
 
 def first_upper_kernel(
     up, up_edge, field, first, second, packed, bias, forward, leak,
-    kept, sent, hidden, to_up, to_down, before,
+    kept, sent, hidden, to_partner, to_other, before,
     line, more, most, held,
 ):
     rows = field.shape[0] - HALO
     for row in range(HALO):
-        pack_cells(up, up_edge, row, line.at[row % 2], before, row)
+        pack_cells(up, up_edge, flip(row, HALO), line.at[row % 2], before, row)
 
     def emit(row, start, y):
         span = slice(start, start + y.shape[0])
         held[row, span] = y
         hidden[row, span] = y
         if row < HALO:
-            to_down[row, span] = y
+            to_other[HALO - 1 - row, span] = y
         if row >= rows - HALO:
-            to_up[row - (rows - HALO), span] = y
+            to_partner[rows - 1 - row, span] = y
 
     upper_part(before, field, first, second, (more, most), packed, bias, lat_edges(), emit)
     transform(forward, leak, bias, held, kept, sent)
@@ -252,16 +261,13 @@
 
 
 def halo_kernel(mixed, out):
-    lanes = out.shape[1]
+    c = out.shape[1] // HALO
+    rows = mixed.shape[1] // c
     even = lax.rem(lax.axis_index("lon"), 2) == 0
-
-    @pl.when(even)
-    def _():
-        out[...] = mixed[:, mixed.shape[1] - lanes :]
-
-    @pl.when(jnp.logical_not(even))
-    def _():
-        out[...] = mixed[:, :lanes]
+    for at in range(HALO):
+        last = mixed[:, (rows - 1 - at) * c : (rows - at) * c]
+        leading = mixed[:, (HALO - 1 - at) * c : (HALO - at) * c]
+        out[:, at * c : (at + 1) * c] = jnp.where(even, last, leading)
 
 
 def pick(mine, other, first):
@@ -301,7 +307,7 @@
     rows = own.shape[0]
     edge = lat_edges()
     state[:rows] = own[...]
-    mixed_down[...] = pick(mine, other, False)
+    mixed_down[...] = pick(mine, other, True)
     next_state((field, rows), (from_down,), mixed_down, inverse, state, rows, HALO, edge[1])
     lower_part(state, first, second, packed, bias, edge, rows)
 
@@ -311,7 +317,7 @@
     kept, sent, hidden, above, mixed_up, more, most, held,
 ):
     edge = lat_edges()
-    mixed_up[...] = pick(mine, other, True)
+    mixed_up[...] = pick(mine, other, False)
     next_state((before, 0), (from_up,), mixed_up, inverse, above, 0, HALO, edge[0])
 
     def emit(row, start, y):
@@ -338,7 +344,7 @@
                 for u in range(width // RUNS):
                     value = total[u * RUNS : (u + 1) * RUNS]
                     line[i, pl.ds(2 * u + e, RUNS, stride=run), :] = value
-            result[row] = line[i, PAD : PAD + cells].astype(BF)
+            result[flip(row, rows)] = line[i, PAD : PAD + cells].astype(BF)
 
 
 def cell_order(width):
@@ -403,10 +409,15 @@
     return np.stack([np.cos(phase), np.sin(phase)], 1).astype(np.float32)
 
 
+def facing(rows, partner):
+    odd = odd_lat()
+    return (rows - HALO) * ((1 - odd) if partner else odd)
+
+
 def slice_kernel(field, *rest):
     out, sem = rest[-2:]
-    at = 0 if len(rest) == 2 else field.shape[0] - HALO
-    copy = pltpu.make_async_copy(field.at[at : at + HALO], out, sem)
+    at = facing(field.shape[0], len(rest) == 2)
+    copy = pltpu.make_async_copy(field.at[pl.ds(at, HALO)], out, sem)
     copy.start()
     copy.wait()
 
@@ -421,17 +432,19 @@
     second.wait()
 
 
-def edge_kernel(from_left, from_right, edges, below):
-    for row in range(from_left.shape[0]):
-        both = jnp.concatenate([from_left[row], from_right[row]], axis=0)
-        edges[row] = both
-        if row < HALO:
-            below[row] = both
-
-
-def copy_kernel(edges, below, above):
-    rows = edges.shape[0]
-    above[...] = edges[rows - HALO :]
+def edge_kernel(from_left, from_right, edges, near):
+    rows = from_left.shape[0]
+    for row in range(rows):
+        edges[row] = jnp.concatenate([from_left[row], from_right[row]], axis=0)
+    at = facing(rows, True)
+    for row in range(HALO):
+        near[row] = jnp.concatenate([from_left[at + row], from_right[at + row]], axis=0)
+
+
+def copy_kernel(edges, near, other):
+    at = facing(edges.shape[0], False)
+    for row in range(HALO):
+        other[row] = edges[at + row]
 
 
 def inverse_kernel(parts, phase, after, inverse):
@@ -441,14 +454,19 @@
 
 
 def lat_edges():
-    me, size = lax.axis_index("lat"), lax.axis_size("lat")
-    return [(me > 0).astype(F32), (me < size - 1).astype(F32)]
-
-
-def move(array, up):
-    size = lax.axis_size("lat")
-    pairs = [(i, i + 1) if up else (i + 1, i) for i in range(size - 1)]
-    return lax.ppermute(array, "lat", pairs)
+    me, size, odd = lax.axis_index("lat"), lax.axis_size("lat"), odd_lat()
+    after, before = (me < size - 1).astype(F32), (me > 0).astype(F32)
+    even = (1 - odd).astype(F32)
+    return [even * before + (1.0 - even) * after, even * after + (1.0 - even) * before]
+
+
+def lat_pairs(partner):
+    pairs = [(i, i + 1) for i in range(0 if partner else 1, lax.axis_size("lat") - 1, 2)]
+    return pairs + [(j, i) for i, j in pairs]
+
+
+def move(array, partner):
+    return lax.ppermute(array, "lat", lat_pairs(partner))
 
 
 def shape(*dims):
@@ -480,7 +498,7 @@
     below = call(
         slice_kernel, (field,), [shape(HALO, cells, c)], [DMA], in_specs=[HBM], out_specs=[ANY]
     )[0]
-    down = move(below, False)
+    down = move(below, True)
     above = call(
         slice_kernel,
         (field, below),
@@ -489,7 +507,7 @@
         in_specs=[HBM, ANY],
         out_specs=[ANY],
     )[0]
-    up = move(above, True)
+    up = move(above, False)
     last, leading = call(
         side_kernel,
         (field, above),
@@ -508,11 +526,11 @@
         [shape(rows, 2 * PAD, c), shape(HALO, 2 * PAD, c)],
         [],
     )
-    down_edge = move(below, False)
+    down_edge = move(below, True)
     above = call(
         copy_kernel, (own_edge, below), [shape(HALO, 2 * PAD, c)], [], in_specs=[VMEM, ANY]
     )[0]
-    up_edge = move(above, True)
+    up_edge = move(above, False)
     tables = (cells, lon_total, modes, lon_size)
     inverse = call(
         inverse_kernel,
@@ -543,7 +561,7 @@
         [line],
         in_specs=[VMEM] * 5 + [ANY],
     )
-    kept, sent, hidden, to_up, to_down, before = call(
+    kept, sent, hidden, to_partner, to_other, before = call(
         first_upper_kernel,
         (up, up_edge, *low, packed, conv_bias[0], forward, leak),
         part_shape
@@ -552,7 +570,7 @@
         + [shape(HALO, wide, 2 * c)],
         [line] + upper,
     )
-    from_down, from_up = move(to_down, False), move(to_up, True)
+    from_down, from_up = move(to_partner, True), move(to_other, False)
 
     def swap(array, step):
         return lax.ppermute(array, "lon", [(i, i ^ step) for i in range(lon_size)])
@@ -578,9 +596,7 @@
     lat_size = lax.axis_size("lat")
     ways = []
     for i in range(lon_size):
-        for j in range(lat_size - 1):
-            here, there = i * lat_size + j, i * lat_size + j + 1
-            ways.append((here, there) if i % 2 == 0 else (there, here))
+        ways += [(i * lat_size + j, i * lat_size + k) for j, k in lat_pairs(i % 2 == 0)]
     mine = lax.ppermute(halo, ("lon", "lat"), ways)
     other = swap(mine, 1)
     own = call(middle_own_kernel, (low[0], hidden, mixed, inverse), [own_rows], [])[0]

time: 94.1 us -> 91.7 us (0.974)
  starting transfers between devices: 32.7 us -> 27.9 us
  waiting for transfers between devices: 19.2 us -> 21.7 us
    ppermute x6, starting transfers between devices: 18.9 us -> 11.6 us  [move(): return lax.ppermute(array, 'lat', lat_pairs(partner))]
    ppermute x1, starting transfers between devices: 3.64 us -> 6.18 us  [per_device(): mine = lax.ppermute(halo, ('lon', 'lat'), ways)]
    ppermute x6, waiting for transfers between devices: 4.26 us -> 6.31 us  [move(): return lax.ppermute(array, 'lat', lat_pairs(partner))]
where the time goes in v4:
time: 91.7 us; the launch traced here: 91.4 us
  starting transfers between devices  27.9 us (30%)
  Pallas kernels  22.6 us (25%)
  waiting for transfers between devices  21.7 us (24%)
  blocking collectives  17.7 us (19%)
  local copies, waits for them, and re-layouts  1.29 us (1%)
    pallas_call x18, Pallas kernels, call(): pl.pallas_call(kernel, grid=grid, out_shape=outs, in_specs=in_specs or [V...  22.6 us
    all_gather x2, blocking collectives, mix(): return lax.all_gather(mixed, 'lon', axis=0, tiled=True)  17.7 us
    ppermute x6, starting transfers between devices, move(): return lax.ppermute(array, 'lat', lat_pairs(partner))  11.6 us
    ppermute x9, waiting for transfers between devices, swap(): return lax.ppermute(array, 'lon', [(i, i ^ step) for i in range(lon_size)])  10.5 us
    ppermute x9, starting transfers between devices, swap(): return lax.ppermute(array, 'lon', [(i, i ^ step) for i in range(lon_size)])  7.39 us
    ppermute x6, waiting for transfers between devices, move(): return lax.ppermute(array, 'lat', lat_pairs(partner))  6.31 us
    ppermute x1, starting transfers between devices, per_device(): mine = lax.ppermute(halo, ('lon', 'lat'), ways)  6.18 us
    ppermute x1, waiting for transfers between devices, per_device(): mine = lax.ppermute(halo, ('lon', 'lat'), ways)  3.45 us
  transfers between devices with their start and end apart: 18, of which 12 were waited for; matrix products, arithmetic and copies ran while one was open for 0% of the time, Pallas kernels for 9%

profile of v4, /device:TPU:0, one launch (start us, length us, event | category | flops | bytes accessed | tf_op | source)
XLA Modules:
  0.0 91.4 jit_solution(3151679352059491319)
XLA Ops:
  0.0 1.2 %copy-done = bf16[4,1024,128]{2,1,0:T(8,128)(2,1)S(1)} copy-done((bf16[4,1024,128]{2,1,0:T(8,128)(2,1)S(1)}, bf16[4,1024,128]{2,1,0:T(8,128)(2,1)}, u32[]{:S(2)}) %copy-start) | copy-done | bytes 1048600
  1.2 0.1 shard_map.100.rest_0_
  1.3 3.1 %collective-permute-start = (bf16[3,1024,128]{2,1,0:T(8,128)(2,1)S(1)}, bf16[3,1024,128]{2,1,0:T(8,128)(2,1)S(1)}, u32[]{:S(2)}, u32[]{:S(2)}) collective-permute-start(bf16[3,1024,128]{2,1,0:T(8,128)(2,1)S(1)} %shard_map.100.rest_0_), channel_id=1, source_target_pairs={{0,1},{2,3},{1,0},{3,2},{4,5},{6,7},{5,4},{7,6},{8,9},{10,11},{9,8... | collective-permute-start | bytes 2359304 | tf_op jit(solution)/shard_map/ppermute | solution.py:469
  4.4 0.1 shard_map.101.after
  4.5 0.7 collective-permute-start.4
  5.3 0.0 copy-start.5
  5.3 0.0 copy-start.9
  5.3 0.1 collective-permute-start.1
  5.3 2.6 %collective-permute-start.2 = (bf16[4,16,128]{2,1,0:T(8,128)(2,1)S(1)}, bf16[4,16,128]{2,1,0:T(8,128)(2,1)S(1)}, u32[]{:S(2)}, u32[]{:S(2)}) collective-permute-start(bf16[4,16,128]{2,1,0:T(8,128)(2,1)S(1)} %get-tuple-element.36), channel_id=1, source_target_pairs={{4,0},{8,4},{12,8},{16,12},{20,16},{24,20},{28,24},{0,28},{5,1},{9... | collective-permute-start | bytes 49160 | tf_op jit(solution)/shard_map/ppermute | solution.py:522
  8.0 1.4 %collective-permute-done.1.from_left = bf16[4,16,128]{2,1,0:T(8,128)(2,1)S(1)} collective-permute-done((bf16[4,16,128]{2,1,0:T(8,128)(2,1)S(1)}, bf16[4,16,128]{2,1,0:T(8,128)(2,1)S(1)}, u32[]{:S(2)}, u32[]{:S(2)}) %collective-permute-start.1) | collective-permute-done | bytes 16416 | tf_op jit(solution)/shard_map/ppermute | solution.py:521
  9.4 0.0 collective-permute-done.2.from_right
  9.4 4.4 %collective-permute-start.3 = (bf16[3,32,128]{2,1,0:T(8,128)(2,1)S(1)}, bf16[3,32,128]{2,1,0:T(8,128)(2,1)S(1)}, u32[]{:S(2)}, u32[]{:S(2)}) collective-permute-start(bf16[3,32,128]{2,1,0:T(8,128)(2,1)S(1)} %get-tuple-element.37.near), channel_id=1, source_target_pairs={{0,1},{2,3},{1,0},{3,2},{4,5},{6,7},{5,4},{7,6},{8,9},{10,11},{9,8... | collective-permute-start | bytes 73736 | tf_op jit(solution)/shard_map/ppermute | solution.py:469
  13.9 0.7 collective-permute-start.5
  14.6 1.5 %shard_map.104 = (bf16[4,560,256]{2,1,0:T(8,128)(2,1)S(1)}, bf16[3,4,512,256]{3,2,1,0:T(8,128)(2,1)S(1)}, bf16[3,4,512,256]{3,2,1,0:T(8,128)(2,1)S(1)}) custom-call(bf16[4,1024,128]{2,1,0:T(8,128)(2,1)S(1)} %copy-done.1, bf16[4,32,128]{2,1,0:T(8,128)(2,1)S(1)} %get-tuple-element.38.own_edge.edges, bf16[2,3,3,3,128,128]{5,4,3,2,1,0:T(8,128)(2,1)S(1)} %copy-done.6), custom_call_target="tpu_custom_call" | custom-call | tf_op jit(solution)/shard_map/pallas_call | solution.py:477
  16.0 0.1 shard_map.106.after.inverse
  16.2 6.3 %collective-permute-done.3.down_edge = bf16[3,32,128]{2,1,0:T(8,128)(2,1)S(1)} collective-permute-done((bf16[3,32,128]{2,1,0:T(8,128)(2,1)S(1)}, bf16[3,32,128]{2,1,0:T(8,128)(2,1)S(1)}, u32[]{:S(2)}, u32[]{:S(2)}) %collective-permute-start.3) | collective-permute-done | bytes 24608 | tf_op jit(solution)/shard_map/ppermute | solution.py:469
  22.5 2.8 %shard_map.107 = (bf16[7,560,256]{2,1,0:T(8,128)(2,1)S(1)}, bf16[4,560,256]{2,1,0:T(8,128)(2,1)S(1)}, bf16[2,560,256]{2,1,0:T(8,128)(2,1)S(1)}) custom-call(bf16[3,1024,128]{2,1,0:T(8,128)(2,1)S(1)} %collective-permute-done.down, bf16[3,32,128]{2,1,0:T(8,128)(2,1)S(1)} %collective-permute-done.3.down_edge, bf16[4,560,256]{2,1,0:T(8,128)(2,1)S(1)} %get-tuple-element.39.own, ...), custom_call_target="tpu_custom_call" | custom-call | tf_op jit(solution)/shard_map/pallas_call | solution.py:477
  25.4 0.0 copy-start.8
  25.4 5.8 %shard_map.108 = (f32[128,512]{1,0:T(8,128)S(1)}, f32[128,512]{1,0:T(8,128)S(1)}, bf16[4,528,256]{2,1,0:T(8,128)(2,1)S(1)}, bf16[3,528,256]{2,1,0:T(8,128)(2,1)S...) custom-call(bf16[3,1024,128]{2,1,0:T(8,128)(2,1)S(1)} %collective-permute-done.4.up, ...), custom_call_target="tpu_custom_call" | custom-call | tf_op jit(solution)/shard_map/pallas_call | solution.py:477
  31.2 2.1 %collective-permute-start.6 = (bf16[3,528,256]{2,1,0:T(8,128)(2,1)S(1)}, bf16[3,528,256]{2,1,0:T(8,128)(2,1)S(1)}, u32[]{:S(2)}, u32[]{:S(2)}) collective-permute-start(bf16[3,528,256]{2,1,0:T(8,128)(2,1)S(1)} %get-tuple-element.44), channel_id=1, source_target_pairs={{0,1},{2,3},{1,0},{3,2},{4,5},{6,7},{5,4},{7,6},{8,9},{10,11},{9,8... | collective-permute-start | bytes 2433032 | tf_op jit(solution)/shard_map/ppermute | solution.py:469
  33.3 0.7 collective-permute-start.13
  34.0 0.1 collective-permute-start.7
  34.1 1.5 %collective-permute-done.7.got = f32[128,512]{1,0:T(8,128)S(1)} collective-permute-done((f32[128,512]{1,0:T(8,128)S(1)}, f32[128,512]{1,0:T(8,128)S(1)}, u32[]{:S(2)}, u32[]{:S(2)}) %collective-permute-start.7) | collective-permute-done | bytes 262176 | tf_op jit(solution)/shard_map/ppermute | solution.py:576
  35.6 2.5 %collective-permute-start.10 = (bf16[32,512]{1,0:T(8,128)(2,1)S(1)}, bf16[32,512]{1,0:T(8,128)(2,1)S(1)}, u32[]{:S(2)}, u32[]{:S(2)}) collective-permute-start(bf16[32,512]{1,0:T(8,128)(2,1)S(1)} %get-tuple-element.50), channel_id=1, source_target_pairs={{0,24},{4,28},{8,16},{12,20},{16,8},{20,12},{24,0},{28,4},{1,25},{... | collective-permute-start | bytes 98312 | tf_op jit(solution)/shard_map/ppermute | solution.py:576
  38.1 0.5 collective-permute-start.8
  38.7 0.5 collective-permute-start.9
  39.2 1.3 %collective-permute-done.10.rest_3_ = bf16[32,512]{1,0:T(8,128)(2,1)S(1)} collective-permute-done((bf16[32,512]{1,0:T(8,128)(2,1)S(1)}, bf16[32,512]{1,0:T(8,128)(2,1)S(1)}, u32[]{:S(2)}, u32[]{:S(2)}) %collective-permute-start.10) | collective-permute-done | bytes 32800 | tf_op jit(solution)/shard_map/ppermute | solution.py:576
  40.5 1.5 %collective-permute-done.8.rest_1_ = bf16[32,512]{1,0:T(8,128)(2,1)S(1)} collective-permute-done((bf16[32,512]{1,0:T(8,128)(2,1)S(1)}, bf16[32,512]{1,0:T(8,128)(2,1)S(1)}, u32[]{:S(2)}, u32[]{:S(2)}) %collective-permute-start.8) | collective-permute-done | bytes 32800 | tf_op jit(solution)/shard_map/ppermute | solution.py:576
  42.1 0.5 collective-permute-done.9.rest_2_
  42.6 0.4 shard_map.110
  43.0 9.3 %all_gather.6.mixed = bf16[256,512]{1,0:T(8,128)(2,1)S(1)} all-gather(bf16[32,512]{1,0:T(8,128)(2,1)S(1)} %shard_map.110), channel_id=1, replica_groups=mesh['lon'=8,'lat'=4] {'lon'}, dimensions={0}, use_global_device_ids=true | all-gather | bytes 294912 | tf_op jit(solution)/shard_map/all_gather | solution.py:592
  52.4 6.2 %collective-permute-start.11 = (bf16[256,384]{1,0:T(8,128)(2,1)S(1)}, bf16[256,384]{1,0:T(8,128)(2,1)S(1)}, u32[]{:S(2)}, u32[]{:S(2)}) collective-permute-start(bf16[256,384]{1,0:T(8,128)(2,1)S(1)} %shard_map.111), channel_id=1, source_target_pairs={{0,1},{2,3},{1,0},{3,2},{5,6},{6,5},{8,9},{10,11},{9,8},{11,10},{1... | collective-permute-start | bytes 589832 | tf_op jit(solution)/shard_map/ppermute | solution.py:600
  58.6 3.5 %collective-permute-done.11.mine = bf16[256,384]{1,0:T(8,128)(2,1)S(1)} collective-permute-done((bf16[256,384]{1,0:T(8,128)(2,1)S(1)}, bf16[256,384]{1,0:T(8,128)(2,1)S(1)}, u32[]{:S(2)}, u32[]{:S(2)}) %collective-permute-start.11) | collective-permute-done | bytes 196640 | tf_op jit(solution)/shard_map/ppermute | solution.py:600
  62.0 0.6 shard_map.112.own
  62.6 0.8 collective-permute-done.12.other
  63.5 3.0 %shard_map.113 = (bf16[7,560,256]{2,1,0:T(8,128)(2,1)S(1)}, bf16[4,560,256]{2,1,0:T(8,128)(2,1)S(1)}, bf16[2,560,256]{2,1,0:T(8,128)(2,1)S(1)}) custom-call(bf16[7,560,256]{2,1,0:T(8,128)(2,1)S(1)} %get-tuple-element.41.field, bf16[3,528,256]{2,1,0:T(8,128)(2,1)S(1)} %collective-permute-done.6.from_down, bf16[256,384]{1,0:T(8,128)(2,1)S(1)} %collective-permute-done.11.mine, ...), custom_call_target="tpu_custom_call" | custom-call | tf_op jit(solution)/shard_map/pallas_call | solution.py:477
  66.4 6.0 %shard_map.114 = (f32[128,512]{1,0:T(8,128)S(1)}, f32[128,512]{1,0:T(8,128)S(1)}, bf16[4,528,256]{2,1,0:T(8,128)(2,1)S(1)}) custom-call(bf16[3,560,256]{2,1,0:T(8,128)(2,1)S(1)} %get-tuple-element.54.before, bf16[3,528,256]{2,1,0:T(8,128)(2,1)S(1)} %collective-permute-done.13.from_up, bf16[256,384]{1,0:T(8,128)(2,1)S(1)} %collective-permute-done.11.mine, ...), custom_call_target="tpu_custom_call" | custom-call | tf_op jit(solution)/shard_map/pallas_call | solution.py:477
  72.5 0.2 collective-permute-start.14
  72.7 1.4 %collective-permute-done.14.got = f32[128,512]{1,0:T(8,128)S(1)} collective-permute-done((f32[128,512]{1,0:T(8,128)S(1)}, f32[128,512]{1,0:T(8,128)S(1)}, u32[]{:S(2)}, u32[]{:S(2)}) %collective-permute-start.14) | collective-permute-done | bytes 262176 | tf_op jit(solution)/shard_map/ppermute | solution.py:576
  74.1 0.6 collective-permute-start.15
  74.7 1.5 %collective-permute-start.16 = (bf16[32,512]{1,0:T(8,128)(2,1)S(1)}, bf16[32,512]{1,0:T(8,128)(2,1)S(1)}, u32[]{:S(2)}, u32[]{:S(2)}) collective-permute-start(bf16[32,512]{1,0:T(8,128)(2,1)S(1)} %get-tuple-element.63), channel_id=1, source_target_pairs={{0,16},{4,20},{8,24},{12,28},{16,0},{20,4},{24,8},{28,12},{1,17},{... | collective-permute-start | bytes 98312 | tf_op jit(solution)/shard_map/ppermute | solution.py:576
  76.2 1.5 %collective-permute-start.17 = (bf16[32,512]{1,0:T(8,128)(2,1)S(1)}, bf16[32,512]{1,0:T(8,128)(2,1)S(1)}, u32[]{:S(2)}, u32[]{:S(2)}) collective-permute-start(bf16[32,512]{1,0:T(8,128)(2,1)S(1)} %get-tuple-element.64), channel_id=1, source_target_pairs={{0,24},{4,28},{8,16},{12,20},{16,8},{20,12},{24,0},{28,4},{1,25},{... | collective-permute-start | bytes 98312 | tf_op jit(solution)/shard_map/ppermute | solution.py:576
  77.6 0.4 collective-permute-done.15.rest_1_
  78.1 0.6 collective-permute-done.16.rest_2_
  78.6 2.4 %collective-permute-done.17.rest_3_ = bf16[32,512]{1,0:T(8,128)(2,1)S(1)} collective-permute-done((bf16[32,512]{1,0:T(8,128)(2,1)S(1)}, bf16[32,512]{1,0:T(8,128)(2,1)S(1)}, u32[]{:S(2)}, u32[]{:S(2)}) %collective-permute-start.17) | collective-permute-done | bytes 32800 | tf_op jit(solution)/shard_map/ppermute | solution.py:576
  81.0 0.4 shard_map.116
  81.4 8.4 %all_gather.7.mixed = bf16[256,512]{1,0:T(8,128)(2,1)S(1)} all-gather(bf16[32,512]{1,0:T(8,128)(2,1)S(1)} %shard_map.116), channel_id=1, replica_groups=mesh['lon'=8,'lat'=4] {'lon'}, dimensions={0}, use_global_device_ids=true | all-gather | bytes 294912 | tf_op jit(solution)/shard_map/all_gather | solution.py:592
  89.8 1.7 %shard_map.117 = bf16[4,1024,128]{2,1,0:T(8,128)(2,1)} custom-call(bf16[7,560,256]{2,1,0:T(8,128)(2,1)S(1)} %get-tuple-element.53.state, bf16[4,528,256]{2,1,0:T(8,128)(2,1)S(1)} %get-tuple-element.58.hidden, bf16[256,512]{1,0:T(8,128)(2,1)S(1)} %all_gather.7.mixed, bf16[2,528,256]{2,1,0:T(8,128)(2,1)S(1)} %shard_map.106.after.inverse), custom_call_target="tpu_custom_call" | custom-call | tf_op jit(solution)/shard_map/pallas_call | solution.py:477
  (33 shorter events, 0.2 us)
Async XLA Ops:
  0.0 1.2 %copy-start = (bf16[4,1024,128]{2,1,0:T(8,128)(2,1)S(1)}, bf16[4,1024,128]{2,1,0:T(8,128)(2,1)}, u32[]{:S(2)}) copy-start(bf16[4,1024,128]{2,1,0:T(8,128)(2,1)} %own.1) | copy-start | bytes 3145732
  1.3 13.2 %copy-start.10 = (f32[2,3,128]{2,0,1:T(2,128)S(1)}, f32[2,3,128]{2,0,1:T(2,128)}, u32[]{:S(2)}) copy-start(f32[2,3,128]{2,0,1:T(2,128)} %param.12) | copy-start | bytes 9220
  1.3 13.2 %copy-start.1 = (bf16[4,1024,128]{2,1,0:T(8,128)(2,1)S(1)}, bf16[4,1024,128]{2,1,0:T(8,128)(2,1)}, u32[]{:S(2)}) copy-start(bf16[4,1024,128]{2,1,0:T(8,128)(2,1)} %own.1) | copy-start | bytes 3145732
  1.3 13.2 %copy-start.6 = (bf16[2,3,3,3,128,128]{5,4,3,2,1,0:T(8,128)(2,1)S(1)}, bf16[2,3,3,3,128,128]{5,4,3,2,1,0:T(8,128)(2,1)}, u32[]{:S(2)}) copy-start(bf16[2,3,3,3,128,128]{5,4,3,2,1,0:T(8,128)(2,1)} %kernels.1) | copy-start | bytes 5308420
  1.3 21.2 %collective-permute-start = (bf16[3,1024,128]{2,1,0:T(8,128)(2,1)S(1)}, bf16[3,1024,128]{2,1,0:T(8,128)(2,1)S(1)}, u32[]{:S(2)}, u32[]{:S(2)}) collective-permute-start(bf16[3,1024,128]{2,1,0:T(8,128)(2,1)S(1)} %shard_map.100.rest_0_), channel_id=1, source_target_pairs={{0,1},{2,3},{1,0},{3,2},{4,5},{6,7},{5,4},{7,6},{8,9},{10,11},{9,8... | collective-permute-start | bytes 2359304 | tf_op jit(solution)/shard_map/ppermute | solution.py:469
  4.5 20.8 %collective-permute-start.4 = (bf16[3,1024,128]{2,1,0:T(8,128)(2,1)S(1)}, bf16[3,1024,128]{2,1,0:T(8,128)(2,1)S(1)}, u32[]{:S(2)}, u32[]{:S(2)}) collective-permute-start(bf16[3,1024,128]{2,1,0:T(8,128)(2,1)S(1)} %shard_map.101.after), channel_id=1, source_target_pairs={{1,2},{2,1},{5,6},{6,5},{9,10},{10,9},{13,14},{14,13},{17,18},{18,... | collective-permute-start | bytes 2359304 | tf_op jit(solution)/shard_map/ppermute | solution.py:469
  5.3 10.8 %copy-start.5 = (f32[2,2,528,256]{3,2,1,0:T(8,128)S(1)}, f32[2,2,528,256]{3,2,1,0:T(8,128)}, u32[]{:S(2)}) copy-start(f32[2,2,528,256]{3,2,1,0:T(8,128)} %constant.10.clone.parts) | copy-start | bytes 6488068
  5.3 10.8 %copy-start.9 = (f32[8,2,256]{2,1,0:T(2,128)S(1)}, f32[8,2,256]{2,1,0:T(2,128)}, u32[]{:S(2)}) copy-start(f32[8,2,256]{2,1,0:T(2,128)} %constant.11.clone.phase) | copy-start | bytes 49156
  5.3 4.1 %collective-permute-start.1 = (bf16[4,16,128]{2,1,0:T(8,128)(2,1)S(1)}, bf16[4,16,128]{2,1,0:T(8,128)(2,1)S(1)}, u32[]{:S(2)}, u32[]{:S(2)}) collective-permute-start(bf16[4,16,128]{2,1,0:T(8,128)(2,1)S(1)} %get-tuple-element.35), channel_id=1, source_target_pairs={{0,4},{4,8},{8,12},{12,16},{16,20},{20,24},{24,28},{28,0},{1,5},{5... | collective-permute-start | bytes 49160 | tf_op jit(solution)/shard_map/ppermute | solution.py:521
  5.3 4.1 %collective-permute-start.2 = (bf16[4,16,128]{2,1,0:T(8,128)(2,1)S(1)}, bf16[4,16,128]{2,1,0:T(8,128)(2,1)S(1)}, u32[]{:S(2)}, u32[]{:S(2)}) collective-permute-start(bf16[4,16,128]{2,1,0:T(8,128)(2,1)S(1)} %get-tuple-element.36), channel_id=1, source_target_pairs={{4,0},{8,4},{12,8},{16,12},{20,16},{24,20},{28,24},{0,28},{5,1},{9... | collective-permute-start | bytes 49160 | tf_op jit(solution)/shard_map/ppermute | solution.py:522
  9.4 13.1 %collective-permute-start.3 = (bf16[3,32,128]{2,1,0:T(8,128)(2,1)S(1)}, bf16[3,32,128]{2,1,0:T(8,128)(2,1)S(1)}, u32[]{:S(2)}, u32[]{:S(2)}) collective-permute-start(bf16[3,32,128]{2,1,0:T(8,128)(2,1)S(1)} %get-tuple-element.37.near), channel_id=1, source_target_pairs={{0,1},{2,3},{1,0},{3,2},{4,5},{6,7},{5,4},{7,6},{8,9},{10,11},{9,8... | collective-permute-start | bytes 73736 | tf_op jit(solution)/shard_map/ppermute | solution.py:469
  13.9 11.5 %collective-permute-start.5 = (bf16[3,32,128]{2,1,0:T(8,128)(2,1)S(1)}, bf16[3,32,128]{2,1,0:T(8,128)(2,1)S(1)}, u32[]{:S(2)}, u32[]{:S(2)}) collective-permute-start(bf16[3,32,128]{2,1,0:T(8,128)(2,1)S(1)} %shard_map.105.after), channel_id=1, source_target_pairs={{1,2},{2,1},{5,6},{6,5},{9,10},{10,9},{13,14},{14,13},{17,18},{18,... | collective-permute-start | bytes 73736 | tf_op jit(solution)/shard_map/ppermute | solution.py:469
  22.5 2.8 %copy-start.2 = (bf16[2,512,1056]{2,1,0:T(8,128)(2,1)S(1)}, bf16[2,512,1056]{2,1,0:T(8,128)(2,1)}, u32[]{:S(2)}) copy-start(bf16[2,512,1056]{2,1,0:T(8,128)(2,1)} %constant.12.clone.forward) | copy-start | bytes 6488068
  22.5 2.9 %copy-start.7 = (f32[2,256,1]{2,1,0:T(8,128)S(1)}, f32[2,256,1]{2,1,0:T(8,128)}, u32[]{:S(2)}) copy-start(f32[2,256,1]{2,1,0:T(8,128)} %constant.13.clone.leak) | copy-start | bytes 6148
  25.4 17.2 %copy-start.3 = (bf16[2,16,128,128]{3,2,1,0:T(8,128)(2,1)S(1)}, bf16[2,16,128,128]{3,2,1,0:T(8,128)(2,1)}, u32[]{:S(2)}) copy-start(bf16[2,16,128,128]{3,2,1,0:T(8,128)(2,1)} %real.3) | copy-start | bytes 3145732
  25.4 17.2 %copy-start.4 = (bf16[2,16,128,128]{3,2,1,0:T(8,128)(2,1)S(1)}, bf16[2,16,128,128]{3,2,1,0:T(8,128)(2,1)}, u32[]{:S(2)}) copy-start(bf16[2,16,128,128]{3,2,1,0:T(8,128)(2,1)} %imag.3) | copy-start | bytes 3145732
  25.4 17.2 %copy-start.8 = (bf16[8,64,128]{2,1,0:T(8,128)(2,1)S(1)}, bf16[8,64,128]{2,1,0:T(8,128)(2,1)}, u32[]{:S(2)}) copy-start(bf16[8,64,128]{2,1,0:T(8,128)(2,1)} %constant.14.clone.turn) | copy-start | bytes 393220
  31.2 32.2 %collective-permute-start.6 = (bf16[3,528,256]{2,1,0:T(8,128)(2,1)S(1)}, bf16[3,528,256]{2,1,0:T(8,128)(2,1)S(1)}, u32[]{:S(2)}, u32[]{:S(2)}) collective-permute-start(bf16[3,528,256]{2,1,0:T(8,128)(2,1)S(1)} %get-tuple-element.44), channel_id=1, source_target_pairs={{0,1},{2,3},{1,0},{3,2},{4,5},{6,7},{5,4},{7,6},{8,9},{10,11},{9,8... | collective-permute-start | bytes 2433032 | tf_op jit(solution)/shard_map/ppermute | solution.py:469
  33.3 33.2 %collective-permute-start.13 = (bf16[3,528,256]{2,1,0:T(8,128)(2,1)S(1)}, bf16[3,528,256]{2,1,0:T(8,128)(2,1)S(1)}, u32[]{:S(2)}, u32[]{:S(2)}) collective-permute-start(bf16[3,528,256]{2,1,0:T(8,128)(2,1)S(1)} %get-tuple-element.55), channel_id=1, source_target_pairs={{1,2},{2,1},{5,6},{6,5},{9,10},{10,9},{13,14},{14,13},{17,18},{18,... | collective-permute-start | bytes 2433032 | tf_op jit(solution)/shard_map/ppermute | solution.py:469
  34.0 1.6 %collective-permute-start.7 = (f32[128,512]{1,0:T(8,128)S(1)}, f32[128,512]{1,0:T(8,128)S(1)}, u32[]{:S(2)}, u32[]{:S(2)}) collective-permute-start(f32[128,512]{1,0:T(8,128)S(1)} %get-tuple-element.46), channel_id=1, source_target_pairs={{0,4},{4,0},{8,12},{12,8},{16,20},{20,16},{24,28},{28,24},{1,5},{5... | collective-permute-start | bytes 786440 | tf_op jit(solution)/shard_map/ppermute | solution.py:576
  35.6 4.9 %collective-permute-start.10 = (bf16[32,512]{1,0:T(8,128)(2,1)S(1)}, bf16[32,512]{1,0:T(8,128)(2,1)S(1)}, u32[]{:S(2)}, u32[]{:S(2)}) collective-permute-start(bf16[32,512]{1,0:T(8,128)(2,1)S(1)} %get-tuple-element.50), channel_id=1, source_target_pairs={{0,24},{4,28},{8,16},{12,20},{16,8},{20,12},{24,0},{28,4},{1,25},{... | collective-permute-start | bytes 98312 | tf_op jit(solution)/shard_map/ppermute | solution.py:576
  38.1 3.9 %collective-permute-start.8 = (bf16[32,512]{1,0:T(8,128)(2,1)S(1)}, bf16[32,512]{1,0:T(8,128)(2,1)S(1)}, u32[]{:S(2)}, u32[]{:S(2)}) collective-permute-start(bf16[32,512]{1,0:T(8,128)(2,1)S(1)} %get-tuple-element.48), channel_id=1, source_target_pairs={{0,8},{4,12},{8,0},{12,4},{16,24},{20,28},{24,16},{28,20},{1,9},{5... | collective-permute-start | bytes 98312 | tf_op jit(solution)/shard_map/ppermute | solution.py:576
  38.7 3.9 %collective-permute-start.9 = (bf16[32,512]{1,0:T(8,128)(2,1)S(1)}, bf16[32,512]{1,0:T(8,128)(2,1)S(1)}, u32[]{:S(2)}, u32[]{:S(2)}) collective-permute-start(bf16[32,512]{1,0:T(8,128)(2,1)S(1)} %get-tuple-element.49), channel_id=1, source_target_pairs={{0,16},{4,20},{8,24},{12,28},{16,0},{20,4},{24,8},{28,12},{1,17},{... | collective-permute-start | bytes 98312 | tf_op jit(solution)/shard_map/ppermute | solution.py:576
  52.4 9.6 %collective-permute-start.11 = (bf16[256,384]{1,0:T(8,128)(2,1)S(1)}, bf16[256,384]{1,0:T(8,128)(2,1)S(1)}, u32[]{:S(2)}, u32[]{:S(2)}) collective-permute-start(bf16[256,384]{1,0:T(8,128)(2,1)S(1)} %shard_map.111), channel_id=1, source_target_pairs={{0,1},{2,3},{1,0},{3,2},{5,6},{6,5},{8,9},{10,11},{9,8},{11,10},{1... | collective-permute-start | bytes 589832 | tf_op jit(solution)/shard_map/ppermute | solution.py:600
  62.0 1.4 %collective-permute-start.12 = (bf16[256,384]{1,0:T(8,128)(2,1)S(1)}, bf16[256,384]{1,0:T(8,128)(2,1)S(1)}, u32[]{:S(2)}, u32[]{:S(2)}) collective-permute-start(bf16[256,384]{1,0:T(8,128)(2,1)S(1)} %collective-permute-done.11.mine), channel_id=1, source_target_pairs={{0,4},{4,0},{8,12},{12,8},{16,20},{20,16},{24,28},{28,24},{1,5},{5... | collective-permute-start | bytes 589832 | tf_op jit(solution)/shard_map/ppermute | solution.py:576
  72.5 1.6 %collective-permute-start.14 = (f32[128,512]{1,0:T(8,128)S(1)}, f32[128,512]{1,0:T(8,128)S(1)}, u32[]{:S(2)}, u32[]{:S(2)}) collective-permute-start(f32[128,512]{1,0:T(8,128)S(1)} %get-tuple-element.60), channel_id=1, source_target_pairs={{0,4},{4,0},{8,12},{12,8},{16,20},{20,16},{24,28},{28,24},{1,5},{5... | collective-permute-start | bytes 786440 | tf_op jit(solution)/shard_map/ppermute | solution.py:576
  74.1 4.0 %collective-permute-start.15 = (bf16[32,512]{1,0:T(8,128)(2,1)S(1)}, bf16[32,512]{1,0:T(8,128)(2,1)S(1)}, u32[]{:S(2)}, u32[]{:S(2)}) collective-permute-start(bf16[32,512]{1,0:T(8,128)(2,1)S(1)} %get-tuple-element.62), channel_id=1, source_target_pairs={{0,8},{4,12},{8,0},{12,4},{16,24},{20,28},{24,16},{28,20},{1,9},{5... | collective-permute-start | bytes 98312 | tf_op jit(solution)/shard_map/ppermute | solution.py:576
  74.7 3.9 %collective-permute-start.16 = (bf16[32,512]{1,0:T(8,128)(2,1)S(1)}, bf16[32,512]{1,0:T(8,128)(2,1)S(1)}, u32[]{:S(2)}, u32[]{:S(2)}) collective-permute-start(bf16[32,512]{1,0:T(8,128)(2,1)S(1)} %get-tuple-element.63), channel_id=1, source_target_pairs={{0,16},{4,20},{8,24},{12,28},{16,0},{20,4},{24,8},{28,12},{1,17},{... | collective-permute-start | bytes 98312 | tf_op jit(solution)/shard_map/ppermute | solution.py:576
  76.2 4.8 %collective-permute-start.17 = (bf16[32,512]{1,0:T(8,128)(2,1)S(1)}, bf16[32,512]{1,0:T(8,128)(2,1)S(1)}, u32[]{:S(2)}, u32[]{:S(2)}) collective-permute-start(bf16[32,512]{1,0:T(8,128)(2,1)S(1)} %get-tuple-element.64), channel_id=1, source_target_pairs={{0,24},{4,28},{8,16},{12,20},{16,8},{20,12},{24,0},{28,4},{1,25},{... | collective-permute-start | bytes 98312 | tf_op jit(solution)/shard_map/ppermute | solution.py:576

commit v5 on v4

--- a/solution.py
+++ b/solution.py
@@ -33,7 +33,7 @@
 
 
 def tile_of(tiles):
-    return max(n for n in range(1, 12) if tiles % n == 0) * RUNS
+    return max(n for n in range(1, 34) if tiles % n == 0) * RUNS
 
 
 def pack_row(line, wide, row):
@@ -147,9 +147,8 @@
             jnp.concatenate([held[row + i, :, e * c : (e + 1) * c] for i in range(2)], axis=1)
             for e in range(2)
         ]
-        both = dot(forward[core], jnp.concatenate(cells, axis=0))
-        modes2 = both.shape[0] // 2
-        total = both[:modes2] + both[modes2:]
+        total = dot(forward[core], jnp.concatenate(cells, axis=0))
+        modes2 = total.shape[0]
         total = total - leak[core] * jnp.concatenate([level, level], axis=1)
         lanes = slice(row * c, (row + 2) * c)
         kept[:, lanes] = total[: modes2 // 2]
@@ -165,41 +164,104 @@
     close_row(wide, at)
 
 
-def lower_part(field, first, second, packed, bias, edge, rows):
-    x, y, z = Rows((field, 0)), Rows((first, 2)), Rows((second, 3))
-    conv_rows(x, y, (2, rows + 2), 0, packed, bias, edge, rows)
-    conv_rows(y, z, (3, rows + 1), 1, packed, bias, edge, rows)
-
-
-def upper_part(before, field, first, second, more, packed, bias, edge, emit):
+def product(a, b, sign, start, tile, packed, layer, index):
+    left, right = window(*a, start, tile), window(*b, start, tile)
+    return dot(left + right if sign > 0 else left - right, packed[layer, index])
+
+
+def put(dst, start, half, bias, layer):
+    ref, at = dst
+    both = 0.5 * jnp.concatenate([bias[layer : layer + 1]] * 2, axis=1)
+    y = silu_of_half(half + both).astype(BF)
+    ref[at, start + RUNS : start + RUNS + y.shape[0]] = y
+
+
+def spans(ref):
+    width = ref.shape[1] - 2 * RUNS
+    tile = tile_of(width // RUNS)
+    return [(start, tile) for start in range(0, width, tile)]
+
+
+def early_part(field, inner, sums, packed, bias):
+    x, y = Rows((field, 0)), Rows((inner, 1))
+    for start, tile in spans(field):
+        span = slice(start, start + tile)
+        args = (start, tile, packed, 0)
+        m1 = product(x[0], x[1], 1, *args, 1)
+        m2 = product(x[1], x[0], -1, *args, 2)
+        m3 = product(x[0], x[2], -1, *args, 3)
+        sums[0, span] = m1 + m2
+        put(y[1], start, m1 - m2 - m3, bias, 0)
+        m0 = product(x[1], x[3], -1, *args, 0)
+        m1 = product(x[2], x[3], 1, *args, 1)
+        m2 = product(x[3], x[2], -1, *args, 2)
+        sums[1, span] = m1 - m2
+        put(y[2], start, (m1 + m2) + m0, bias, 0)
+    close_row(*y[1])
+    close_row(*y[2])
+    for start, tile in spans(field):
+        span = slice(start, start + tile)
+        args = (start, tile, packed, 1)
+        m1 = product(y[1], y[2], 1, *args, 1)
+        m2 = product(y[2], y[1], -1, *args, 2)
+        sums[2, span] = m1 + m2
+        sums[3, span] = m1 - m2
+
+
+def lower_part(field, inner, sums, first, second, packed, bias, edge, rows):
+    x, y, z = Rows((field, 0)), Rows((inner, 1), (first, 3)), Rows((second, 3))
+    for start, tile in spans(field):
+        m3 = product(x[2], x[4], -1, start, tile, packed, 0, 3)
+        put(y[3], start, sums[1, start : start + tile] - m3, bias, 0)
+    close_row(*y[3])
+    conv_rows(x, y, (4, 6), 0, packed, bias, edge, rows)
+    conv_rows(y, z, (3, 5), 1, packed, bias, edge, rows)
+
+
+def upper_part(before, field, inner, sums, first, second, more, packed, bias, edge, emit):
     rows = field.shape[0] - HALO
     x = Rows((before, -HALO), (field, 0))
-    y = Rows((more[0], -2), (first, 2))
+    y = Rows((more[0], -2), (inner, 1), (first, 3))
     z = Rows((more[1], -1), (second, 3))
-    conv_rows(x, y, (-2, 2), 0, packed, bias, edge, rows)
-    conv_rows(y, z, (-1, 3), 1, packed, bias, edge, rows)
+    conv_rows(x, y, (-2, 0), 0, packed, bias, edge, rows)
+    for start, tile in spans(field):
+        m0 = product(x[-1], x[1], -1, start, tile, packed, 0, 0)
+        put(y[0], start, sums[0, start : start + tile] + m0, bias, 0)
+    close_row(*y[0])
+    conv_rows(y, z, (-1, 1), 1, packed, bias, edge, rows)
+    for start, tile in spans(field):
+        span = slice(start, start + tile)
+        m0 = product(y[0], y[2], -1, start, tile, packed, 1, 0)
+        m3 = product(y[1], y[3], -1, start, tile, packed, 1, 3)
+        put(z[1], start, sums[2, span] + m0, bias, 1)
+        put(z[2], start, sums[3, span] - m3, bias, 1)
+    close_row(*z[1])
+    close_row(*z[2])
     conv_rows(z, emit, (0, rows), 2, packed, bias, edge, rows)
 
 
-def prepare_kernel(own, own_edge, kernels, field, packed, later, line):
+def prepare_kernel(own, own_edge, kernels, bias, after, field, packed, later, inner, sums, line):
     rows = own.shape[0]
     for layer in range(CONVS):
         build_weights(kernels, 0, packed, layer)
         build_weights(kernels, 1, later, layer)
     for row in range(rows):
         pack_cells(own, own_edge, flip(row, rows), line.at[row % 2], field, row)
-
-
-def first_lower_kernel(down, down_edge, own, packed, bias, after, field, first, second, line):
+    early_part(field, inner, sums, packed, bias)
+
+
+def first_lower_kernel(
+    down, down_edge, own, packed, inner, sums, bias, field, first, second, line
+):
     rows = own.shape[0]
     field[:rows] = own[...]
     for row in range(HALO):
         pack_cells(down, down_edge, flip(row, HALO), line.at[row % 2], field, rows + row)
-    lower_part(field, first, second, packed, bias, lat_edges(), rows)
+    lower_part(field, inner, sums, first, second, packed, bias, lat_edges(), rows)
 
 
 def first_upper_kernel(
-    up, up_edge, field, first, second, packed, bias, forward, leak,
+    up, up_edge, field, first, second, inner, sums, packed, bias, forward, leak,
     kept, sent, hidden, to_partner, to_other, before,
     line, more, most, held,
 ):
@@ -216,7 +278,8 @@
         if row >= rows - HALO:
             to_partner[rows - 1 - row, span] = y
 
-    upper_part(before, field, first, second, (more, most), packed, bias, lat_edges(), emit)
+    args = (before, field, inner, sums, first, second, (more, most), packed, bias)
+    upper_part(*args, lat_edges(), emit)
     transform(forward, leak, bias, held, kept, sent)
 
 
@@ -297,23 +360,26 @@
             close_row(new, at + pair + i)
 
 
-def middle_own_kernel(field, hidden, mixed, inverse, state):
+def middle_own_kernel(field, hidden, mixed, inverse, packed, bias, state, inner, sums):
     next_state((field, 0), (hidden,), mixed, inverse, state, 0, hidden.shape[0], None)
+    early_part(state, inner, sums, packed, bias)
 
 
 def middle_lower_kernel(
-    field, from_down, mine, other, own, inverse, packed, bias, state, first, second, mixed_down
+    field, from_down, mine, other, own, inner, sums, inverse, packed, bias,
+    state, first, second, mixed_down,
 ):
     rows = own.shape[0]
     edge = lat_edges()
     state[:rows] = own[...]
     mixed_down[...] = pick(mine, other, True)
     next_state((field, rows), (from_down,), mixed_down, inverse, state, rows, HALO, edge[1])
-    lower_part(state, first, second, packed, bias, edge, rows)
+    lower_part(state, inner, sums, first, second, packed, bias, edge, rows)
 
 
 def middle_upper_kernel(
-    before, from_up, mine, other, inverse, state, first, second, packed, bias, forward, leak,
+    before, from_up, mine, other, inverse, state, first, second, inner, sums,
+    packed, bias, forward, leak,
     kept, sent, hidden, above, mixed_up, more, most, held,
 ):
     edge = lat_edges()
@@ -325,14 +391,16 @@
         held[row, span] = y
         hidden[row, span] = y
 
-    upper_part(above, state, first, second, (more, most), packed, bias, edge, emit)
+    args = (above, state, inner, sums, first, second, (more, most), packed, bias)
+    upper_part(*args, edge, emit)
     transform(forward, leak, bias, held, kept, sent)
 
 
-def last_kernel(state, hidden, mixed, inverse, result, line):
+def last_kernel(state, hidden, mixed, inverse, result, line, done, sems):
     rows, width, c = hidden.shape[0], hidden.shape[1], hidden.shape[2] // 2
     cells = result.shape[1]
     run = 2 * width // RUNS
+    copies = []
     for pair in range(0, rows, 2):
         waves = [dot(inverse[e], mixed[:, pair * c : (pair + 2) * c]) for e in range(2)]
         for i in range(2):
@@ -344,7 +412,12 @@
                 for u in range(width // RUNS):
                     value = total[u * RUNS : (u + 1) * RUNS]
                     line[i, pl.ds(2 * u + e, RUNS, stride=run), :] = value
-            result[flip(row, rows)] = line[i, PAD : PAD + cells].astype(BF)
+            done[row] = line[i, PAD : PAD + cells].astype(BF)
+            copy = pltpu.make_async_copy(done.at[row], result.at[flip(row, rows)], sems.at[row])
+            copy.start()
+            copies.append(copy)
+    for copy in copies:
+        copy.wait()
 
 
 def cell_order(width):
@@ -363,11 +436,8 @@
         full = np.stack([np.cos(theta), -np.sin(theta)], 0) * inside
         full = full.reshape(2, lon_size // 2, 2, modes // lon_size, -1)
         full = full.transpose(2, 1, 0, 3, 4)[[core, 1 - core]]
-        full = full.reshape(2 * modes, -1).astype(np.float32)
-        leaks.append(full.astype(np.float64).sum(1, keepdims=True).astype(np.float32))
-        high = full.astype(ml_dtypes.bfloat16)
-        low = (full - high.astype(np.float32)).astype(ml_dtypes.bfloat16)
-        tables.append(np.concatenate([high, low], 0))
+        tables.append(full.reshape(2 * modes, -1).astype(ml_dtypes.bfloat16))
+        leaks.append(tables[-1].astype(np.float64).sum(1, keepdims=True).astype(np.float32))
     return np.stack(tables), np.stack(leaks)
 
 
@@ -473,7 +543,8 @@
     return jax.ShapeDtypeStruct(dims, BF)
 
 
-def call(kernel, args, outs, scratch, in_specs=None, out_specs=None, grid=()):
+def call(kernel, args, outs, scratch, in_specs=None, out_specs=None, grid=(), cost=0):
+    estimate = pl.CostEstimate(flops=int(cost * 8e8), bytes_accessed=0, transcendentals=0)
     return pl.pallas_call(
         kernel,
         grid=grid,
@@ -482,6 +553,7 @@
         out_specs=out_specs or [VMEM] * len(outs),
         scratch_shapes=scratch,
         compiler_params=PARAMS,
+        cost_estimate=estimate if cost else None,
     )(*(jnp.asarray(arg) for arg in args))
 
 
@@ -544,40 +616,46 @@
 
     line = pltpu.VMEM((2, width, c), F32)
     weights = shape(CONVS, 4 if WINOGRAD else 3, 4 * c, 2 * c)
-    lower = [shape(n, wide, 2 * c) for n in (rows + HALO, rows, rows - 2)]
+    lower = [shape(n, wide, 2 * c) for n in (rows + HALO, 3, 2)]
+    early = [shape(2, wide, 2 * c), jax.ShapeDtypeStruct((4, half, 2 * c), F32)]
     gathered = pltpu.VMEM((2 * modes, HALO * c), BF)
     upper = [pltpu.VMEM((4, wide, 2 * c), BF)] * 2 + [pltpu.VMEM((rows, half, 2 * c), BF)]
     hidden_shape = shape(rows, half, 2 * c)
     part_shape = [jax.ShapeDtypeStruct((modes, rows * c), F32)] * 2
 
     own_rows = shape(rows, wide, 2 * c)
-    own, packed, later = call(
-        prepare_kernel, (field, own_edge, conv_weight), [own_rows, weights, weights], [line]
+    own, packed, later, *inner = call(
+        prepare_kernel,
+        (field, own_edge, conv_weight, conv_bias[0], inverse),
+        [own_rows, weights, weights] + early,
+        [line],
+        in_specs=[VMEM] * 4 + [ANY],
+        cost=4,
     )
     low = call(
         first_lower_kernel,
-        (down, down_edge, own, packed, conv_bias[0], inverse),
+        (down, down_edge, own, packed, *inner, conv_bias[0]),
         lower,
         [line],
-        in_specs=[VMEM] * 5 + [ANY],
     )
     kept, sent, hidden, to_partner, to_other, before = call(
         first_upper_kernel,
-        (up, up_edge, *low, packed, conv_bias[0], forward, leak),
+        (up, up_edge, *low, *inner, packed, conv_bias[0], forward, leak),
         part_shape
         + [hidden_shape]
         + [shape(HALO, half, 2 * c)] * 2
         + [shape(HALO, wide, 2 * c)],
         [line] + upper,
     )
-    from_down, from_up = move(to_partner, True), move(to_other, False)
-
     def swap(array, step):
         return lax.ppermute(array, "lon", [(i, i ^ step) for i in range(lon_size)])
 
-    def mix(kept, sent, block):
-        chunk = shape(2 * local, rows * c)
-        own, *others = call(pair_kernel, (kept, swap(sent, 1)), [chunk] * (lon_size // 2), [])
+    chunk = shape(2 * local, rows * c)
+
+    def pair(kept, sent):
+        return call(pair_kernel, (kept, swap(sent, 1)), [chunk] * (lon_size // 2), [])
+
+    def mix(own, others, block):
         sums = [own] + [swap(other, 2 * i + 2) for i, other in enumerate(others)]
         turned = pltpu.VMEM((2 * rows * local, c), F32)
         weights = pl.BlockSpec((1, local, c, c), lambda i: (block, 0, 0, 0))
@@ -591,31 +669,45 @@
         )
         return lax.all_gather(mixed, "lon", axis=0, tiled=True)
 
-    mixed = mix(kept, sent, 0)
+    own, *others = pair(kept, sent)
+    to_partner, to_other, _ = lax.optimization_barrier((to_partner, to_other, own))
+    from_down, from_up = move(to_partner, True), move(to_other, False)
+    mixed = mix(own, others, 0)
     halo = call(halo_kernel, (mixed,), [shape(2 * modes, HALO * c)], [])[0]
     lat_size = lax.axis_size("lat")
     ways = []
     for i in range(lon_size):
         ways += [(i * lat_size + j, i * lat_size + k) for j, k in lat_pairs(i % 2 == 0)]
     mine = lax.ppermute(halo, ("lon", "lat"), ways)
-    other = swap(mine, 1)
-    own = call(middle_own_kernel, (low[0], hidden, mixed, inverse), [own_rows], [])[0]
+    own, *inner = call(
+        middle_own_kernel,
+        (low[0], hidden, mixed, inverse, later, conv_bias[1]),
+        [own_rows] + early,
+        [],
+        cost=3,
+    )
+    other = swap(lax.optimization_barrier((mine, own))[0], 1)
     state, *low = call(
         middle_lower_kernel,
-        (low[0], from_down, mine, other, own, inverse, later, conv_bias[1]),
+        (low[0], from_down, mine, other, own, *inner, inverse, later, conv_bias[1]),
         lower,
         [gathered],
     )
     kept, sent, hidden = call(
         middle_upper_kernel,
-        (before, from_up, mine, other, inverse, state, *low)
+        (before, from_up, mine, other, inverse, state, *low, *inner)
         + (later, conv_bias[1], forward, leak),
         part_shape + [hidden_shape],
         [pltpu.VMEM((HALO, wide, 2 * c), BF), gathered] + upper,
     )
-    mixed = mix(kept, sent, 1)
+    own, *others = pair(kept, sent)
+    mixed = mix(own, others, 1)
     (result,) = call(
-        last_kernel, (state, hidden, mixed, inverse), [shape(rows, cells, c)], [line]
+        last_kernel,
+        (state, hidden, mixed, inverse),
+        [shape(rows, cells, c)],
+        [line, pltpu.VMEM((rows, cells, c), BF), pltpu.SemaphoreType.DMA((rows,))],
+        out_specs=[ANY],
     )
     return result
 

time: 91.7 us -> 87.3 us (0.952)
  waiting for transfers between devices: 21.7 us -> 19.2 us
  Pallas kernels: 22.6 us -> 20.2 us
    pallas_call x18, Pallas kernels: 22.6 us -> 20.2 us  [call(): pl.pallas_call(kernel, grid=grid, out_shape=outs, in_specs=in_specs or [V...]
    ppermute x1, waiting for transfers between devices: 3.45 us -> 1.69 us  [per_device(): mine = lax.ppermute(halo, ('lon', 'lat'), ways)]
    ppermute x6, starting transfers between devices: 11.6 us -> 13 us  [move(): return lax.ppermute(array, 'lat', lat_pairs(partner))]
    ppermute x6, waiting for transfers between devices: 6.31 us -> 5 us  [move(): return lax.ppermute(array, 'lat', lat_pairs(partner))]
    ppermute x1, starting transfers between devices: 6.18 us -> 5.09 us  [per_device(): mine = lax.ppermute(halo, ('lon', 'lat'), ways)]
  transfers between devices with their start and end apart: 18 -> 18, of which waited for: 12 -> 12; matrix products, arithmetic and copies ran while one was open for 0% -> 0% of each run, Pallas kernels for 9% -> 11%
where the time goes in v5:
time: 87.3 us; the launch traced here: 87 us
  starting transfers between devices  28.1 us (32%)
  Pallas kernels  20.2 us (23%)
  waiting for transfers between devices  19.2 us (22%)
  blocking collectives  17.6 us (20%)
  local copies, waits for them, and re-layouts  1.29 us (1%)
    pallas_call x18, Pallas kernels, call(): pl.pallas_call(kernel, grid=grid, out_shape=outs, in_specs=in_specs or [V...  20.2 us
    all_gather x2, blocking collectives, mix(): return lax.all_gather(mixed, 'lon', axis=0, tiled=True)  17.6 us
    ppermute x6, starting transfers between devices, move(): return lax.ppermute(array, 'lat', lat_pairs(partner))  13 us
    ppermute x9, waiting for transfers between devices, swap(): return lax.ppermute(array, 'lon', [(i, i ^ step) for i in range(lon_size)])  11.1 us
    ppermute x9, starting transfers between devices, swap(): return lax.ppermute(array, 'lon', [(i, i ^ step) for i in range(lon_size)])  7.39 us
    ppermute x1, starting transfers between devices, per_device(): mine = lax.ppermute(halo, ('lon', 'lat'), ways)  5.09 us
    ppermute x6, waiting for transfers between devices, move(): return lax.ppermute(array, 'lat', lat_pairs(partner))  5 us
    ppermute x1, starting transfers between devices, per_device(): from_right = lax.ppermute(leading, 'lon', left)  2.63 us
  transfers between devices with their start and end apart: 18, of which 12 were waited for; matrix products, arithmetic and copies ran while one was open for 0% of the time, Pallas kernels for 11%

profile of v5, /device:TPU:0, one launch (start us, length us, event | category | flops | bytes accessed | tf_op | source)
XLA Modules:
  0.0 87.0 jit_solution(9944597654594970502)
XLA Ops:
  0.0 1.2 %copy-done = bf16[4,1024,128]{2,1,0:T(8,128)(2,1)S(1)} copy-done((bf16[4,1024,128]{2,1,0:T(8,128)(2,1)S(1)}, bf16[4,1024,128]{2,1,0:T(8,128)(2,1)}, u32[]{:S(2)}) %copy-start) | copy-done | bytes 1048600
  1.2 0.1 shard_map.100.rest_0_
  1.3 0.0 copy-start.5
  1.3 0.0 copy-start.8
  1.3 3.1 %collective-permute-start = (bf16[3,1024,128]{2,1,0:T(8,128)(2,1)S(1)}, bf16[3,1024,128]{2,1,0:T(8,128)(2,1)S(1)}, u32[]{:S(2)}, u32[]{:S(2)}) collective-permute-start(bf16[3,1024,128]{2,1,0:T(8,128)(2,1)S(1)} %shard_map.100.rest_0_), channel_id=1, source_target_pairs={{0,1},{2,3},{1,0},{3,2},{4,5},{6,7},{5,4},{7,6},{8,9},{10,11},{9,8... | collective-permute-start | bytes 2359304 | tf_op jit(solution)/shard_map/ppermute | solution.py:539
  4.4 0.1 shard_map.101.after
  4.5 0.8 collective-permute-start.4
  5.4 0.1 collective-permute-start.1
  5.5 2.6 %collective-permute-start.2 = (bf16[4,16,128]{2,1,0:T(8,128)(2,1)S(1)}, bf16[4,16,128]{2,1,0:T(8,128)(2,1)S(1)}, u32[]{:S(2)}, u32[]{:S(2)}) collective-permute-start(bf16[4,16,128]{2,1,0:T(8,128)(2,1)S(1)} %get-tuple-element.44), channel_id=1, source_target_pairs={{4,0},{8,4},{12,8},{16,12},{20,16},{24,20},{28,24},{0,28},{5,1},{9... | collective-permute-start | bytes 49160 | tf_op jit(solution)/shard_map/ppermute | solution.py:594
  8.1 1.4 %collective-permute-done.1.from_left = bf16[4,16,128]{2,1,0:T(8,128)(2,1)S(1)} collective-permute-done((bf16[4,16,128]{2,1,0:T(8,128)(2,1)S(1)}, bf16[4,16,128]{2,1,0:T(8,128)(2,1)S(1)}, u32[]{:S(2)}, u32[]{:S(2)}) %collective-permute-start.1) | collective-permute-done | bytes 16416 | tf_op jit(solution)/shard_map/ppermute | solution.py:593
  9.5 0.0 collective-permute-done.2.from_right
  9.6 4.5 %collective-permute-start.3 = (bf16[3,32,128]{2,1,0:T(8,128)(2,1)S(1)}, bf16[3,32,128]{2,1,0:T(8,128)(2,1)S(1)}, u32[]{:S(2)}, u32[]{:S(2)}) collective-permute-start(bf16[3,32,128]{2,1,0:T(8,128)(2,1)S(1)} %get-tuple-element.45.near), channel_id=1, source_target_pairs={{0,1},{2,3},{1,0},{3,2},{4,5},{6,7},{5,4},{7,6},{8,9},{10,11},{9,8... | collective-permute-start | bytes 73736 | tf_op jit(solution)/shard_map/ppermute | solution.py:539
  14.1 0.7 collective-permute-start.5
  14.8 0.1 shard_map.105.after.inverse
  15.0 2.5 %shard_map.106 = (bf16[4,560,256]{2,1,0:T(8,128)(2,1)S(1)}, bf16[3,4,512,256]{3,2,1,0:T(8,128)(2,1)S(1)}, bf16[3,4,512,256]{3,2,1,0:T(8,128)(2,1)S(1)}, bf16[2,5...) custom-call(bf16[4,1024,128]{2,1,0:T(8,128)(2,1)S(1)} %copy-done.1, bf16[4,32,128]{2,1,0:T(8,128)(2,1)S(1)} %get-tuple-element.46.edges.own_edge, ...), custom_call_target="tpu_custom_call" | custom-call | flops 3200000000 | tf_op jit(solution)/shard_map/pallas_call | solution.py:548
  17.5 5.0 %collective-permute-done.3.down_edge = bf16[3,32,128]{2,1,0:T(8,128)(2,1)S(1)} collective-permute-done((bf16[3,32,128]{2,1,0:T(8,128)(2,1)S(1)}, bf16[3,32,128]{2,1,0:T(8,128)(2,1)S(1)}, u32[]{:S(2)}, u32[]{:S(2)}) %collective-permute-start.3) | collective-permute-done | bytes 24608 | tf_op jit(solution)/shard_map/ppermute | solution.py:539
  22.5 2.0 %shard_map.107 = (bf16[7,560,256]{2,1,0:T(8,128)(2,1)S(1)}, bf16[3,560,256]{2,1,0:T(8,128)(2,1)S(1)}, bf16[2,560,256]{2,1,0:T(8,128)(2,1)S(1)}) custom-call(bf16[3,1024,128]{2,1,0:T(8,128)(2,1)S(1)} %collective-permute-done.down, bf16[3,32,128]{2,1,0:T(8,128)(2,1)S(1)} %collective-permute-done.3.down_edge, bf16[4,560,256]{2,1,0:T(8,128)(2,1)S(1)} %get-tuple-element.47.own, ...), custom_call_target="tpu_custom_call" | custom-call | tf_op jit(solution)/shard_map/pallas_call | solution.py:548
  24.6 0.0 copy-start.7
  24.6 4.2 %shard_map.108 = (f32[128,512]{1,0:T(8,128)S(1)}, f32[128,512]{1,0:T(8,128)S(1)}, bf16[4,528,256]{2,1,0:T(8,128)(2,1)S(1)}, bf16[3,528,256]{2,1,0:T(8,128)(2,1)S...) custom-call(bf16[3,1024,128]{2,1,0:T(8,128)(2,1)S(1)} %collective-permute-done.4.up, ...), custom_call_target="tpu_custom_call" | custom-call | tf_op jit(solution)/shard_map/pallas_call | solution.py:548
  28.8 0.1 collective-permute-start.6
  28.9 1.5 %collective-permute-done.6.got = f32[128,512]{1,0:T(8,128)S(1)} collective-permute-done((f32[128,512]{1,0:T(8,128)S(1)}, f32[128,512]{1,0:T(8,128)S(1)}, u32[]{:S(2)}, u32[]{:S(2)}) %collective-permute-start.6) | collective-permute-done | bytes 262176 | tf_op jit(solution)/shard_map/ppermute | solution.py:651
  30.5 3.1 %collective-permute-start.7 = (bf16[3,528,256]{2,1,0:T(8,128)(2,1)S(1)}, bf16[3,528,256]{2,1,0:T(8,128)(2,1)S(1)}, u32[]{:S(2)}, u32[]{:S(2)}) collective-permute-start(bf16[3,528,256]{2,1,0:T(8,128)(2,1)S(1)} %get-tuple-element.59), channel_id=1, source_target_pairs={{0,1},{2,3},{1,0},{3,2},{4,5},{6,7},{5,4},{7,6},{8,9},{10,11},{9,8... | collective-permute-start | bytes 2433032 | tf_op jit(solution)/shard_map/ppermute | solution.py:539
  33.6 0.7 collective-permute-start.13
  34.3 2.5 %collective-permute-start.10 = (bf16[32,512]{1,0:T(8,128)(2,1)S(1)}, bf16[32,512]{1,0:T(8,128)(2,1)S(1)}, u32[]{:S(2)}, u32[]{:S(2)}) collective-permute-start(bf16[32,512]{1,0:T(8,128)(2,1)S(1)} %get-tuple-element.62), channel_id=1, source_target_pairs={{0,24},{4,28},{8,16},{12,20},{16,8},{20,12},{24,0},{28,4},{1,25},{... | collective-permute-start | bytes 98312 | tf_op jit(solution)/shard_map/ppermute | solution.py:651
  36.8 0.5 collective-permute-start.8
  37.4 0.5 collective-permute-start.9
  37.9 1.6 %collective-permute-done.10.rest_3_ = bf16[32,512]{1,0:T(8,128)(2,1)S(1)} collective-permute-done((bf16[32,512]{1,0:T(8,128)(2,1)S(1)}, bf16[32,512]{1,0:T(8,128)(2,1)S(1)}, u32[]{:S(2)}, u32[]{:S(2)}) %collective-permute-start.10) | collective-permute-done | bytes 32800 | tf_op jit(solution)/shard_map/ppermute | solution.py:651
  39.5 1.3 %collective-permute-done.8.rest_1_ = bf16[32,512]{1,0:T(8,128)(2,1)S(1)} collective-permute-done((bf16[32,512]{1,0:T(8,128)(2,1)S(1)}, bf16[32,512]{1,0:T(8,128)(2,1)S(1)}, u32[]{:S(2)}, u32[]{:S(2)}) %collective-permute-start.8) | collective-permute-done | bytes 32800 | tf_op jit(solution)/shard_map/ppermute | solution.py:651
  40.8 0.5 collective-permute-done.9.rest_2_
  41.3 0.4 shard_map.110
  41.7 9.3 %all_gather.6.mixed = bf16[256,512]{1,0:T(8,128)(2,1)S(1)} all-gather(bf16[32,512]{1,0:T(8,128)(2,1)S(1)} %shard_map.110), channel_id=1, replica_groups=mesh['lon'=8,'lat'=4] {'lon'}, dimensions={0}, use_global_device_ids=true | all-gather | bytes 294912 | tf_op jit(solution)/shard_map/all_gather | solution.py:670
  51.1 5.1 %collective-permute-start.11 = (bf16[256,384]{1,0:T(8,128)(2,1)S(1)}, bf16[256,384]{1,0:T(8,128)(2,1)S(1)}, u32[]{:S(2)}, u32[]{:S(2)}) collective-permute-start(bf16[256,384]{1,0:T(8,128)(2,1)S(1)} %shard_map.111), channel_id=1, source_target_pairs={{0,1},{2,3},{1,0},{3,2},{5,6},{6,5},{8,9},{10,11},{9,8},{11,10},{1... | collective-permute-start | bytes 589832 | tf_op jit(solution)/shard_map/ppermute | solution.py:681
  56.2 1.8 %shard_map.112 = (bf16[4,560,256]{2,1,0:T(8,128)(2,1)S(1)}, bf16[2,560,256]{2,1,0:T(8,128)(2,1)S(1)}, f32[4,528,256]{2,1,0:T(8,128)S(1)}) custom-call(bf16[7,560,256]{2,1,0:T(8,128)(2,1)S(1)} %get-tuple-element.51.field, bf16[4,528,256]{2,1,0:T(8,128)(2,1)S(1)} %get-tuple-element.63.hidden, bf16[256,512]{1,0:T(8,128)(2,1)S(1)} %all_gather.6.mixed, ...), custom_call_target="tpu_custom_call" | custom-call | flops 2400000000 | tf_op jit(solution)/shard_map/pallas_call | solution.py:548
  57.9 1.7 %collective-permute-done.11.mine = bf16[256,384]{1,0:T(8,128)(2,1)S(1)} collective-permute-done((bf16[256,384]{1,0:T(8,128)(2,1)S(1)}, bf16[256,384]{1,0:T(8,128)(2,1)S(1)}, u32[]{:S(2)}, u32[]{:S(2)}) %collective-permute-start.11) | collective-permute-done | bytes 196640 | tf_op jit(solution)/shard_map/ppermute | solution.py:681
  59.6 1.4 %collective-permute-done.12.other = bf16[256,384]{1,0:T(8,128)(2,1)S(1)} collective-permute-done((bf16[256,384]{1,0:T(8,128)(2,1)S(1)}, bf16[256,384]{1,0:T(8,128)(2,1)S(1)}, u32[]{:S(2)}, u32[]{:S(2)}) %collective-permute-start.12) | collective-permute-done | bytes 196640 | tf_op jit(solution)/shard_map/ppermute | solution.py:651
  61.1 2.2 %shard_map.113 = (bf16[7,560,256]{2,1,0:T(8,128)(2,1)S(1)}, bf16[3,560,256]{2,1,0:T(8,128)(2,1)S(1)}, bf16[2,560,256]{2,1,0:T(8,128)(2,1)S(1)}) custom-call(bf16[7,560,256]{2,1,0:T(8,128)(2,1)S(1)} %get-tuple-element.51.field, bf16[3,528,256]{2,1,0:T(8,128)(2,1)S(1)} %collective-permute-done.7.from_down, bf16[256,384]{1,0:T(8,128)(2,1)S(1)} %collective-permute-done.11.mine, ...), custom_call_target="tpu_custom_call" | custom-call | tf_op jit(solution)/shard_map/pallas_call | solution.py:548
  63.3 4.7 %shard_map.114 = (f32[128,512]{1,0:T(8,128)S(1)}, f32[128,512]{1,0:T(8,128)S(1)}, bf16[4,528,256]{2,1,0:T(8,128)(2,1)S(1)}) custom-call(bf16[3,560,256]{2,1,0:T(8,128)(2,1)S(1)} %get-tuple-element.70.before, bf16[3,528,256]{2,1,0:T(8,128)(2,1)S(1)} %collective-permute-done.13.from_up, bf16[256,384]{1,0:T(8,128)(2,1)S(1)} %collective-permute-done.11.mine, ...), custom_call_target="tpu_custom_call" | custom-call | tf_op jit(solution)/shard_map/pallas_call | solution.py:548
  68.0 0.2 collective-permute-start.14
  68.2 1.4 %collective-permute-done.14.got = f32[128,512]{1,0:T(8,128)S(1)} collective-permute-done((f32[128,512]{1,0:T(8,128)S(1)}, f32[128,512]{1,0:T(8,128)S(1)}, u32[]{:S(2)}, u32[]{:S(2)}) %collective-permute-start.14) | collective-permute-done | bytes 262176 | tf_op jit(solution)/shard_map/ppermute | solution.py:651
  69.6 0.6 collective-permute-start.15
  70.2 1.5 %collective-permute-start.16 = (bf16[32,512]{1,0:T(8,128)(2,1)S(1)}, bf16[32,512]{1,0:T(8,128)(2,1)S(1)}, u32[]{:S(2)}, u32[]{:S(2)}) collective-permute-start(bf16[32,512]{1,0:T(8,128)(2,1)S(1)} %get-tuple-element.79), channel_id=1, source_target_pairs={{0,16},{4,20},{8,24},{12,28},{16,0},{20,4},{24,8},{28,12},{1,17},{... | collective-permute-start | bytes 98312 | tf_op jit(solution)/shard_map/ppermute | solution.py:651
  71.7 1.5 %collective-permute-start.17 = (bf16[32,512]{1,0:T(8,128)(2,1)S(1)}, bf16[32,512]{1,0:T(8,128)(2,1)S(1)}, u32[]{:S(2)}, u32[]{:S(2)}) collective-permute-start(bf16[32,512]{1,0:T(8,128)(2,1)S(1)} %get-tuple-element.80), channel_id=1, source_target_pairs={{0,24},{4,28},{8,16},{12,20},{16,8},{20,12},{24,0},{28,4},{1,25},{... | collective-permute-start | bytes 98312 | tf_op jit(solution)/shard_map/ppermute | solution.py:651
  73.2 0.4 collective-permute-done.15.rest_1_
  73.6 0.5 collective-permute-done.16.rest_2_
  74.2 2.4 %collective-permute-done.17.rest_3_ = bf16[32,512]{1,0:T(8,128)(2,1)S(1)} collective-permute-done((bf16[32,512]{1,0:T(8,128)(2,1)S(1)}, bf16[32,512]{1,0:T(8,128)(2,1)S(1)}, u32[]{:S(2)}, u32[]{:S(2)}) %collective-permute-start.17) | collective-permute-done | bytes 32800 | tf_op jit(solution)/shard_map/ppermute | solution.py:651
  76.5 0.4 shard_map.116
  77.0 8.3 %all_gather.7.mixed = bf16[256,512]{1,0:T(8,128)(2,1)S(1)} all-gather(bf16[32,512]{1,0:T(8,128)(2,1)S(1)} %shard_map.116), channel_id=1, replica_groups=mesh['lon'=8,'lat'=4] {'lon'}, dimensions={0}, use_global_device_ids=true | all-gather | bytes 294912 | tf_op jit(solution)/shard_map/all_gather | solution.py:670
  85.3 1.5 %shard_map.117 = bf16[4,1024,128]{2,1,0:T(8,128)(2,1)} custom-call(bf16[7,560,256]{2,1,0:T(8,128)(2,1)S(1)} %get-tuple-element.69.state, bf16[4,528,256]{2,1,0:T(8,128)(2,1)S(1)} %get-tuple-element.74.hidden, bf16[256,512]{1,0:T(8,128)(2,1)S(1)} %all_gather.7.mixed, bf16[2,528,256]{2,1,0:T(8,128)(2,1)S(1)} %shard_map.105.after.inverse), custom_call_target="tpu_custom_call" | custom-call | tf_op jit(solution)/shard_map/pallas_call | solution.py:548
  (33 shorter events, 0.2 us)
Async XLA Ops:
  0.0 1.2 %copy-start = (bf16[4,1024,128]{2,1,0:T(8,128)(2,1)S(1)}, bf16[4,1024,128]{2,1,0:T(8,128)(2,1)}, u32[]{:S(2)}) copy-start(bf16[4,1024,128]{2,1,0:T(8,128)(2,1)} %own.1) | copy-start | bytes 3145732
  1.3 6.8 %copy-start.10 = (f32[2,3,128]{2,0,1:T(2,128)S(1)}, f32[2,3,128]{2,0,1:T(2,128)}, u32[]{:S(2)}) copy-start(f32[2,3,128]{2,0,1:T(2,128)} %param.12) | copy-start | bytes 9220
  1.3 13.5 %copy-start.5 = (f32[2,2,528,256]{3,2,1,0:T(8,128)S(1)}, f32[2,2,528,256]{3,2,1,0:T(8,128)}, u32[]{:S(2)}) copy-start(f32[2,2,528,256]{3,2,1,0:T(8,128)} %constant.10.clone.parts) | copy-start | bytes 6488068
  1.3 13.5 %copy-start.8 = (f32[8,2,256]{2,1,0:T(2,128)S(1)}, f32[8,2,256]{2,1,0:T(2,128)}, u32[]{:S(2)}) copy-start(f32[8,2,256]{2,1,0:T(2,128)} %constant.11.clone.phase) | copy-start | bytes 49156
  1.3 21.2 %collective-permute-start = (bf16[3,1024,128]{2,1,0:T(8,128)(2,1)S(1)}, bf16[3,1024,128]{2,1,0:T(8,128)(2,1)S(1)}, u32[]{:S(2)}, u32[]{:S(2)}) collective-permute-start(bf16[3,1024,128]{2,1,0:T(8,128)(2,1)S(1)} %shard_map.100.rest_0_), channel_id=1, source_target_pairs={{0,1},{2,3},{1,0},{3,2},{4,5},{6,7},{5,4},{7,6},{8,9},{10,11},{9,8... | collective-permute-start | bytes 2359304 | tf_op jit(solution)/shard_map/ppermute | solution.py:539
  4.5 10.4 %copy-start.1 = (bf16[4,1024,128]{2,1,0:T(8,128)(2,1)S(1)}, bf16[4,1024,128]{2,1,0:T(8,128)(2,1)}, u32[]{:S(2)}) copy-start(bf16[4,1024,128]{2,1,0:T(8,128)(2,1)} %own.1) | copy-start | bytes 3145732
  4.5 10.4 %copy-start.9 = (bf16[2,3,3,3,128,128]{5,4,3,2,1,0:T(8,128)(2,1)S(1)}, bf16[2,3,3,3,128,128]{5,4,3,2,1,0:T(8,128)(2,1)}, u32[]{:S(2)}) copy-start(bf16[2,3,3,3,128,128]{5,4,3,2,1,0:T(8,128)(2,1)} %kernels.1) | copy-start | bytes 5308420
  4.5 20.0 %collective-permute-start.4 = (bf16[3,1024,128]{2,1,0:T(8,128)(2,1)S(1)}, bf16[3,1024,128]{2,1,0:T(8,128)(2,1)S(1)}, u32[]{:S(2)}, u32[]{:S(2)}) collective-permute-start(bf16[3,1024,128]{2,1,0:T(8,128)(2,1)S(1)} %shard_map.101.after), channel_id=1, source_target_pairs={{1,2},{2,1},{5,6},{6,5},{9,10},{10,9},{13,14},{14,13},{17,18},{18,... | collective-permute-start | bytes 2359304 | tf_op jit(solution)/shard_map/ppermute | solution.py:539
  5.4 4.1 %collective-permute-start.1 = (bf16[4,16,128]{2,1,0:T(8,128)(2,1)S(1)}, bf16[4,16,128]{2,1,0:T(8,128)(2,1)S(1)}, u32[]{:S(2)}, u32[]{:S(2)}) collective-permute-start(bf16[4,16,128]{2,1,0:T(8,128)(2,1)S(1)} %get-tuple-element.43), channel_id=1, source_target_pairs={{0,4},{4,8},{8,12},{12,16},{16,20},{20,24},{24,28},{28,0},{1,5},{5... | collective-permute-start | bytes 49160 | tf_op jit(solution)/shard_map/ppermute | solution.py:593
  5.5 4.1 %collective-permute-start.2 = (bf16[4,16,128]{2,1,0:T(8,128)(2,1)S(1)}, bf16[4,16,128]{2,1,0:T(8,128)(2,1)S(1)}, u32[]{:S(2)}, u32[]{:S(2)}) collective-permute-start(bf16[4,16,128]{2,1,0:T(8,128)(2,1)S(1)} %get-tuple-element.44), channel_id=1, source_target_pairs={{4,0},{8,4},{12,8},{16,12},{20,16},{24,20},{28,24},{0,28},{5,1},{9... | collective-permute-start | bytes 49160 | tf_op jit(solution)/shard_map/ppermute | solution.py:594
  9.6 12.9 %collective-permute-start.3 = (bf16[3,32,128]{2,1,0:T(8,128)(2,1)S(1)}, bf16[3,32,128]{2,1,0:T(8,128)(2,1)S(1)}, u32[]{:S(2)}, u32[]{:S(2)}) collective-permute-start(bf16[3,32,128]{2,1,0:T(8,128)(2,1)S(1)} %get-tuple-element.45.near), channel_id=1, source_target_pairs={{0,1},{2,3},{1,0},{3,2},{4,5},{6,7},{5,4},{7,6},{8,9},{10,11},{9,8... | collective-permute-start | bytes 73736 | tf_op jit(solution)/shard_map/ppermute | solution.py:539
  14.1 10.4 %collective-permute-start.5 = (bf16[3,32,128]{2,1,0:T(8,128)(2,1)S(1)}, bf16[3,32,128]{2,1,0:T(8,128)(2,1)S(1)}, u32[]{:S(2)}, u32[]{:S(2)}) collective-permute-start(bf16[3,32,128]{2,1,0:T(8,128)(2,1)S(1)} %shard_map.104.after), channel_id=1, source_target_pairs={{1,2},{2,1},{5,6},{6,5},{9,10},{10,9},{13,14},{14,13},{17,18},{18,... | collective-permute-start | bytes 73736 | tf_op jit(solution)/shard_map/ppermute | solution.py:539
  22.5 2.0 %copy-start.2 = (bf16[2,256,1056]{2,1,0:T(8,128)(2,1)S(1)}, bf16[2,256,1056]{2,1,0:T(8,128)(2,1)}, u32[]{:S(2)}) copy-start(bf16[2,256,1056]{2,1,0:T(8,128)(2,1)} %constant.12.clone.forward) | copy-start | bytes 3244036
  22.5 2.1 %copy-start.6 = (f32[2,256,1]{2,1,0:T(8,128)S(1)}, f32[2,256,1]{2,1,0:T(8,128)}, u32[]{:S(2)}) copy-start(f32[2,256,1]{2,1,0:T(8,128)} %constant.13.clone.leak) | copy-start | bytes 6148
  24.6 16.7 %copy-start.3 = (bf16[2,16,128,128]{3,2,1,0:T(8,128)(2,1)S(1)}, bf16[2,16,128,128]{3,2,1,0:T(8,128)(2,1)}, u32[]{:S(2)}) copy-start(bf16[2,16,128,128]{3,2,1,0:T(8,128)(2,1)} %real.3) | copy-start | bytes 3145732
  24.6 16.7 %copy-start.4 = (bf16[2,16,128,128]{3,2,1,0:T(8,128)(2,1)S(1)}, bf16[2,16,128,128]{3,2,1,0:T(8,128)(2,1)}, u32[]{:S(2)}) copy-start(bf16[2,16,128,128]{3,2,1,0:T(8,128)(2,1)} %imag.3) | copy-start | bytes 3145732
  24.6 16.7 %copy-start.7 = (bf16[8,64,128]{2,1,0:T(8,128)(2,1)S(1)}, bf16[8,64,128]{2,1,0:T(8,128)(2,1)}, u32[]{:S(2)}) copy-start(bf16[8,64,128]{2,1,0:T(8,128)(2,1)} %constant.14.clone.turn) | copy-start | bytes 393220
  28.8 1.6 %collective-permute-start.6 = (f32[128,512]{1,0:T(8,128)S(1)}, f32[128,512]{1,0:T(8,128)S(1)}, u32[]{:S(2)}, u32[]{:S(2)}) collective-permute-start(f32[128,512]{1,0:T(8,128)S(1)} %get-tuple-element.57), channel_id=1, source_target_pairs={{0,4},{4,0},{8,12},{12,8},{16,20},{20,16},{24,28},{28,24},{1,5},{5... | collective-permute-start | bytes 786440 | tf_op jit(solution)/shard_map/ppermute | solution.py:651
  30.5 30.6 %collective-permute-start.7 = (bf16[3,528,256]{2,1,0:T(8,128)(2,1)S(1)}, bf16[3,528,256]{2,1,0:T(8,128)(2,1)S(1)}, u32[]{:S(2)}, u32[]{:S(2)}) collective-permute-start(bf16[3,528,256]{2,1,0:T(8,128)(2,1)S(1)} %get-tuple-element.59), channel_id=1, source_target_pairs={{0,1},{2,3},{1,0},{3,2},{4,5},{6,7},{5,4},{7,6},{8,9},{10,11},{9,8... | collective-permute-start | bytes 2433032 | tf_op jit(solution)/shard_map/ppermute | solution.py:539
  33.6 29.7 %collective-permute-start.13 = (bf16[3,528,256]{2,1,0:T(8,128)(2,1)S(1)}, bf16[3,528,256]{2,1,0:T(8,128)(2,1)S(1)}, u32[]{:S(2)}, u32[]{:S(2)}) collective-permute-start(bf16[3,528,256]{2,1,0:T(8,128)(2,1)S(1)} %get-tuple-element.71), channel_id=1, source_target_pairs={{1,2},{2,1},{5,6},{6,5},{9,10},{10,9},{13,14},{14,13},{17,18},{18,... | collective-permute-start | bytes 2433032 | tf_op jit(solution)/shard_map/ppermute | solution.py:539
  34.3 5.1 %collective-permute-start.10 = (bf16[32,512]{1,0:T(8,128)(2,1)S(1)}, bf16[32,512]{1,0:T(8,128)(2,1)S(1)}, u32[]{:S(2)}, u32[]{:S(2)}) collective-permute-start(bf16[32,512]{1,0:T(8,128)(2,1)S(1)} %get-tuple-element.62), channel_id=1, source_target_pairs={{0,24},{4,28},{8,16},{12,20},{16,8},{20,12},{24,0},{28,4},{1,25},{... | collective-permute-start | bytes 98312 | tf_op jit(solution)/shard_map/ppermute | solution.py:651
  36.8 3.9 %collective-permute-start.8 = (bf16[32,512]{1,0:T(8,128)(2,1)S(1)}, bf16[32,512]{1,0:T(8,128)(2,1)S(1)}, u32[]{:S(2)}, u32[]{:S(2)}) collective-permute-start(bf16[32,512]{1,0:T(8,128)(2,1)S(1)} %get-tuple-element.60), channel_id=1, source_target_pairs={{0,8},{4,12},{8,0},{12,4},{16,24},{20,28},{24,16},{28,20},{1,9},{5... | collective-permute-start | bytes 98312 | tf_op jit(solution)/shard_map/ppermute | solution.py:651
  37.4 3.9 %collective-permute-start.9 = (bf16[32,512]{1,0:T(8,128)(2,1)S(1)}, bf16[32,512]{1,0:T(8,128)(2,1)S(1)}, u32[]{:S(2)}, u32[]{:S(2)}) collective-permute-start(bf16[32,512]{1,0:T(8,128)(2,1)S(1)} %get-tuple-element.61), channel_id=1, source_target_pairs={{0,16},{4,20},{8,24},{12,28},{16,0},{20,4},{24,8},{28,12},{1,17},{... | collective-permute-start | bytes 98312 | tf_op jit(solution)/shard_map/ppermute | solution.py:651
  51.1 8.6 %collective-permute-start.11 = (bf16[256,384]{1,0:T(8,128)(2,1)S(1)}, bf16[256,384]{1,0:T(8,128)(2,1)S(1)}, u32[]{:S(2)}, u32[]{:S(2)}) collective-permute-start(bf16[256,384]{1,0:T(8,128)(2,1)S(1)} %shard_map.111), channel_id=1, source_target_pairs={{0,1},{2,3},{1,0},{3,2},{5,6},{6,5},{8,9},{10,11},{9,8},{11,10},{1... | collective-permute-start | bytes 589832 | tf_op jit(solution)/shard_map/ppermute | solution.py:681
  59.6 1.4 %collective-permute-start.12 = (bf16[256,384]{1,0:T(8,128)(2,1)S(1)}, bf16[256,384]{1,0:T(8,128)(2,1)S(1)}, u32[]{:S(2)}, u32[]{:S(2)}) collective-permute-start(bf16[256,384]{1,0:T(8,128)(2,1)S(1)} %collective-permute-done.11.mine), channel_id=1, source_target_pairs={{0,4},{4,0},{8,12},{12,8},{16,20},{20,16},{24,28},{28,24},{1,5},{5... | collective-permute-start | bytes 589832 | tf_op jit(solution)/shard_map/ppermute | solution.py:651
  68.0 1.6 %collective-permute-start.14 = (f32[128,512]{1,0:T(8,128)S(1)}, f32[128,512]{1,0:T(8,128)S(1)}, u32[]{:S(2)}, u32[]{:S(2)}) collective-permute-start(f32[128,512]{1,0:T(8,128)S(1)} %get-tuple-element.76), channel_id=1, source_target_pairs={{0,4},{4,0},{8,12},{12,8},{16,20},{20,16},{24,28},{28,24},{1,5},{5... | collective-permute-start | bytes 786440 | tf_op jit(solution)/shard_map/ppermute | solution.py:651
  69.6 4.0 %collective-permute-start.15 = (bf16[32,512]{1,0:T(8,128)(2,1)S(1)}, bf16[32,512]{1,0:T(8,128)(2,1)S(1)}, u32[]{:S(2)}, u32[]{:S(2)}) collective-permute-start(bf16[32,512]{1,0:T(8,128)(2,1)S(1)} %get-tuple-element.78), channel_id=1, source_target_pairs={{0,8},{4,12},{8,0},{12,4},{16,24},{20,28},{24,16},{28,20},{1,9},{5... | collective-permute-start | bytes 98312 | tf_op jit(solution)/shard_map/ppermute | solution.py:651
  70.2 3.9 %collective-permute-start.16 = (bf16[32,512]{1,0:T(8,128)(2,1)S(1)}, bf16[32,512]{1,0:T(8,128)(2,1)S(1)}, u32[]{:S(2)}, u32[]{:S(2)}) collective-permute-start(bf16[32,512]{1,0:T(8,128)(2,1)S(1)} %get-tuple-element.79), channel_id=1, source_target_pairs={{0,16},{4,20},{8,24},{12,28},{16,0},{20,4},{24,8},{28,12},{1,17},{... | collective-permute-start | bytes 98312 | tf_op jit(solution)/shard_map/ppermute | solution.py:651
  71.7 4.8 %collective-permute-start.17 = (bf16[32,512]{1,0:T(8,128)(2,1)S(1)}, bf16[32,512]{1,0:T(8,128)(2,1)S(1)}, u32[]{:S(2)}, u32[]{:S(2)}) collective-permute-start(bf16[32,512]{1,0:T(8,128)(2,1)S(1)} %get-tuple-element.80), channel_id=1, source_target_pairs={{0,24},{4,28},{8,16},{12,20},{16,8},{20,12},{24,0},{28,4},{1,25},{... | collective-permute-start | bytes 98312 | tf_op jit(solution)/shard_map/ppermute | solution.py:651

commit v6 on v5

--- a/solution.py
+++ b/solution.py
@@ -38,7 +38,7 @@
 
 def pack_row(line, wide, row):
     c = line.shape[1]
-    run = line.shape[0] // RUNS
+    run = 2 * (wide.shape[1] // RUNS - 2)
     for cell in range(run):
         lanes = slice(cell % 2 * c, (cell % 2 + 1) * c)
         at = RUNS * (cell // 2 + 1)
@@ -159,7 +159,7 @@
     cells = body.shape[1]
     line[0:PAD] = ends[source, :PAD].astype(F32)
     line[PAD : PAD + cells] = body[source].astype(F32)
-    line[PAD + cells :] = ends[source, PAD:].astype(F32)
+    line[PAD + cells : 2 * PAD + cells] = ends[source, PAD:].astype(F32)
     pack_row(line, wide, at)
     close_row(wide, at)
 
@@ -316,11 +316,9 @@
         out = out[: 2 * rows] + out[2 * rows :]
         turned = pltpu.roll(out[:, c:], rows, 0)
         spread_out[2 * rows * k : 2 * rows * (k + 1)] = out[:, :c] + sign * turned
-    for half in range(2):
-        for row in range(rows):
-            value = spread_out[pl.ds(half * rows + row, modes, stride=2 * rows), :].astype(BF)
-            span = slice(half * modes, (half + 1) * modes)
-            mixed[span, row * c : (row + 1) * c] = value
+    for row in range(rows):
+        parts = [spread_out[pl.ds(i * rows + row, modes, stride=2 * rows), :] for i in range(2)]
+        mixed[:, row * c : (row + 1) * c] = jnp.concatenate(parts, axis=0).astype(BF)
 
 
 def halo_kernel(mixed, out):
@@ -614,7 +612,7 @@
     forward, leak = forward_table(*tables)
     turn = turn_table(lon_size, local, 1.0 / lon_total)
 
-    line = pltpu.VMEM((2, width, c), F32)
+    line = pltpu.VMEM((2, width + 2 * half // RUNS + 8, c), F32)
     weights = shape(CONVS, 4 if WINOGRAD else 3, 4 * c, 2 * c)
     lower = [shape(n, wide, 2 * c) for n in (rows + HALO, 3, 2)]
     early = [shape(2, wide, 2 * c), jax.ShapeDtypeStruct((4, half, 2 * c), F32)]
@@ -657,7 +655,7 @@
 
     def mix(own, others, block):
         sums = [own] + [swap(other, 2 * i + 2) for i, other in enumerate(others)]
-        turned = pltpu.VMEM((2 * rows * local, c), F32)
+        turned = pltpu.VMEM((2 * rows * (local + 1), c), F32)
         weights = pl.BlockSpec((1, local, c, c), lambda i: (block, 0, 0, 0))
         (mixed,) = call(
             mix_kernel,
@@ -669,9 +667,8 @@
         )
         return lax.all_gather(mixed, "lon", axis=0, tiled=True)
 
+    from_down, from_up = move(to_partner, True), move(to_other, False)
     own, *others = pair(kept, sent)
-    to_partner, to_other, _ = lax.optimization_barrier((to_partner, to_other, own))
-    from_down, from_up = move(to_partner, True), move(to_other, False)
     mixed = mix(own, others, 0)
     halo = call(halo_kernel, (mixed,), [shape(2 * modes, HALO * c)], [])[0]
     lat_size = lax.axis_size("lat")

time: 87.3 us -> 87.3 us (level)
  no operation moved by 1% of the time
where the time goes in v6:
time: 87.3 us; the launch traced here: 87 us
  starting transfers between devices  28.1 us (32%)
  Pallas kernels  20.2 us (23%)
  waiting for transfers between devices  19.2 us (22%)
  blocking collectives  17.6 us (20%)
  local copies, waits for them, and re-layouts  1.29 us (1%)
    pallas_call x18, Pallas kernels, call(): pl.pallas_call(kernel, grid=grid, out_shape=outs, in_specs=in_specs or [V...  20.2 us
    all_gather x2, blocking collectives, mix(): return lax.all_gather(mixed, 'lon', axis=0, tiled=True)  17.6 us
    ppermute x6, starting transfers between devices, move(): return lax.ppermute(array, 'lat', lat_pairs(partner))  13 us
    ppermute x9, waiting for transfers between devices, swap(): return lax.ppermute(array, 'lon', [(i, i ^ step) for i in range(lon_size)])  11.1 us
    ppermute x9, starting transfers between devices, swap(): return lax.ppermute(array, 'lon', [(i, i ^ step) for i in range(lon_size)])  7.38 us
    ppermute x1, starting transfers between devices, per_device(): mine = lax.ppermute(halo, ('lon', 'lat'), ways)  5.09 us
    ppermute x6, waiting for transfers between devices, move(): return lax.ppermute(array, 'lat', lat_pairs(partner))  5 us
    ppermute x1, starting transfers between devices, per_device(): from_right = lax.ppermute(leading, 'lon', left)  2.63 us
  transfers between devices with their start and end apart: 18, of which 12 were waited for; matrix products, arithmetic and copies ran while one was open for 0% of the time, Pallas kernels for 11%

profile of v6, /device:TPU:0, one launch (start us, length us, event | category | flops | bytes accessed | tf_op | source)
XLA Modules:
  0.0 87.0 jit_solution(10418824039640055601)
XLA Ops:
  0.0 1.2 %copy-done = bf16[4,1024,128]{2,1,0:T(8,128)(2,1)S(1)} copy-done((bf16[4,1024,128]{2,1,0:T(8,128)(2,1)S(1)}, bf16[4,1024,128]{2,1,0:T(8,128)(2,1)}, u32[]{:S(2)}) %copy-start) | copy-done | bytes 1048600
  1.2 0.1 shard_map.100.rest_0_
  1.3 0.0 copy-start.5
  1.3 0.0 copy-start.8
  1.3 3.1 %collective-permute-start = (bf16[3,1024,128]{2,1,0:T(8,128)(2,1)S(1)}, bf16[3,1024,128]{2,1,0:T(8,128)(2,1)S(1)}, u32[]{:S(2)}, u32[]{:S(2)}) collective-permute-start(bf16[3,1024,128]{2,1,0:T(8,128)(2,1)S(1)} %shard_map.100.rest_0_), channel_id=1, source_target_pairs={{0,1},{2,3},{1,0},{3,2},{4,5},{6,7},{5,4},{7,6},{8,9},{10,11},{9,8... | collective-permute-start | bytes 2359304 | tf_op jit(solution)/shard_map/ppermute | solution.py:537
  4.4 0.1 shard_map.101.after
  4.5 0.8 collective-permute-start.4
  5.4 0.1 collective-permute-start.1
  5.5 2.6 %collective-permute-start.2 = (bf16[4,16,128]{2,1,0:T(8,128)(2,1)S(1)}, bf16[4,16,128]{2,1,0:T(8,128)(2,1)S(1)}, u32[]{:S(2)}, u32[]{:S(2)}) collective-permute-start(bf16[4,16,128]{2,1,0:T(8,128)(2,1)S(1)} %get-tuple-element.42), channel_id=1, source_target_pairs={{4,0},{8,4},{12,8},{16,12},{20,16},{24,20},{28,24},{0,28},{5,1},{9... | collective-permute-start | bytes 49160 | tf_op jit(solution)/shard_map/ppermute | solution.py:592
  8.1 1.4 %collective-permute-done.1.from_left = bf16[4,16,128]{2,1,0:T(8,128)(2,1)S(1)} collective-permute-done((bf16[4,16,128]{2,1,0:T(8,128)(2,1)S(1)}, bf16[4,16,128]{2,1,0:T(8,128)(2,1)S(1)}, u32[]{:S(2)}, u32[]{:S(2)}) %collective-permute-start.1) | collective-permute-done | bytes 16416 | tf_op jit(solution)/shard_map/ppermute | solution.py:591
  9.5 0.0 collective-permute-done.2.from_right
  9.6 4.5 %collective-permute-start.3 = (bf16[3,32,128]{2,1,0:T(8,128)(2,1)S(1)}, bf16[3,32,128]{2,1,0:T(8,128)(2,1)S(1)}, u32[]{:S(2)}, u32[]{:S(2)}) collective-permute-start(bf16[3,32,128]{2,1,0:T(8,128)(2,1)S(1)} %get-tuple-element.43.near), channel_id=1, source_target_pairs={{0,1},{2,3},{1,0},{3,2},{4,5},{6,7},{5,4},{7,6},{8,9},{10,11},{9,8... | collective-permute-start | bytes 73736 | tf_op jit(solution)/shard_map/ppermute | solution.py:537
  14.1 0.7 collective-permute-start.5
  14.8 0.1 shard_map.105.after.inverse
  15.0 2.5 %shard_map.106 = (bf16[4,560,256]{2,1,0:T(8,128)(2,1)S(1)}, bf16[3,4,512,256]{3,2,1,0:T(8,128)(2,1)S(1)}, bf16[3,4,512,256]{3,2,1,0:T(8,128)(2,1)S(1)}, bf16[2,5...) custom-call(bf16[4,1024,128]{2,1,0:T(8,128)(2,1)S(1)} %copy-done.1, bf16[4,32,128]{2,1,0:T(8,128)(2,1)S(1)} %get-tuple-element.44.edges.own_edge, ...), custom_call_target="tpu_custom_call" | custom-call | flops 3200000000 | tf_op jit(solution)/shard_map/pallas_call | solution.py:546
  17.5 5.0 %collective-permute-done.3.down_edge = bf16[3,32,128]{2,1,0:T(8,128)(2,1)S(1)} collective-permute-done((bf16[3,32,128]{2,1,0:T(8,128)(2,1)S(1)}, bf16[3,32,128]{2,1,0:T(8,128)(2,1)S(1)}, u32[]{:S(2)}, u32[]{:S(2)}) %collective-permute-start.3) | collective-permute-done | bytes 24608 | tf_op jit(solution)/shard_map/ppermute | solution.py:537
  22.5 2.0 %shard_map.107 = (bf16[7,560,256]{2,1,0:T(8,128)(2,1)S(1)}, bf16[3,560,256]{2,1,0:T(8,128)(2,1)S(1)}, bf16[2,560,256]{2,1,0:T(8,128)(2,1)S(1)}) custom-call(bf16[3,1024,128]{2,1,0:T(8,128)(2,1)S(1)} %collective-permute-done.down, bf16[3,32,128]{2,1,0:T(8,128)(2,1)S(1)} %collective-permute-done.3.down_edge, bf16[4,560,256]{2,1,0:T(8,128)(2,1)S(1)} %get-tuple-element.45.own, ...), custom_call_target="tpu_custom_call" | custom-call | tf_op jit(solution)/shard_map/pallas_call | solution.py:546
  24.6 0.0 copy-start.7
  24.6 4.2 %shard_map.108 = (f32[128,512]{1,0:T(8,128)S(1)}, f32[128,512]{1,0:T(8,128)S(1)}, bf16[4,528,256]{2,1,0:T(8,128)(2,1)S(1)}, bf16[3,528,256]{2,1,0:T(8,128)(2,1)S...) custom-call(bf16[3,1024,128]{2,1,0:T(8,128)(2,1)S(1)} %collective-permute-done.4.up, ...), custom_call_target="tpu_custom_call" | custom-call | tf_op jit(solution)/shard_map/pallas_call | solution.py:546
  28.8 3.1 %collective-permute-start.6 = (bf16[3,528,256]{2,1,0:T(8,128)(2,1)S(1)}, bf16[3,528,256]{2,1,0:T(8,128)(2,1)S(1)}, u32[]{:S(2)}, u32[]{:S(2)}) collective-permute-start(bf16[3,528,256]{2,1,0:T(8,128)(2,1)S(1)} %get-tuple-element.52), channel_id=1, source_target_pairs={{0,1},{2,3},{1,0},{3,2},{4,5},{6,7},{5,4},{7,6},{8,9},{10,11},{9,8... | collective-permute-start | bytes 2433032 | tf_op jit(solution)/shard_map/ppermute | solution.py:537
  32.0 0.7 collective-permute-start.13
  32.7 0.1 collective-permute-start.7
  32.8 1.5 %collective-permute-done.7.got = f32[128,512]{1,0:T(8,128)S(1)} collective-permute-done((f32[128,512]{1,0:T(8,128)S(1)}, f32[128,512]{1,0:T(8,128)S(1)}, u32[]{:S(2)}, u32[]{:S(2)}) %collective-permute-start.7) | collective-permute-done | bytes 262176 | tf_op jit(solution)/shard_map/ppermute | solution.py:649
  34.3 2.5 %collective-permute-start.10 = (bf16[32,512]{1,0:T(8,128)(2,1)S(1)}, bf16[32,512]{1,0:T(8,128)(2,1)S(1)}, u32[]{:S(2)}, u32[]{:S(2)}) collective-permute-start(bf16[32,512]{1,0:T(8,128)(2,1)S(1)} %get-tuple-element.58), channel_id=1, source_target_pairs={{0,24},{4,28},{8,16},{12,20},{16,8},{20,12},{24,0},{28,4},{1,25},{... | collective-permute-start | bytes 98312 | tf_op jit(solution)/shard_map/ppermute | solution.py:649
  36.8 0.5 collective-permute-start.8
  37.4 0.5 collective-permute-start.9
  37.9 1.3 %collective-permute-done.10.rest_3_ = bf16[32,512]{1,0:T(8,128)(2,1)S(1)} collective-permute-done((bf16[32,512]{1,0:T(8,128)(2,1)S(1)}, bf16[32,512]{1,0:T(8,128)(2,1)S(1)}, u32[]{:S(2)}, u32[]{:S(2)}) %collective-permute-start.10) | collective-permute-done | bytes 32800 | tf_op jit(solution)/shard_map/ppermute | solution.py:649
  39.2 1.6 %collective-permute-done.8.rest_1_ = bf16[32,512]{1,0:T(8,128)(2,1)S(1)} collective-permute-done((bf16[32,512]{1,0:T(8,128)(2,1)S(1)}, bf16[32,512]{1,0:T(8,128)(2,1)S(1)}, u32[]{:S(2)}, u32[]{:S(2)}) %collective-permute-start.8) | collective-permute-done | bytes 32800 | tf_op jit(solution)/shard_map/ppermute | solution.py:649
  40.8 0.5 collective-permute-done.9.rest_2_
  41.3 0.4 shard_map.110
  41.7 9.3 %all_gather.6.mixed = bf16[256,512]{1,0:T(8,128)(2,1)S(1)} all-gather(bf16[32,512]{1,0:T(8,128)(2,1)S(1)} %shard_map.110), channel_id=1, replica_groups=mesh['lon'=8,'lat'=4] {'lon'}, dimensions={0}, use_global_device_ids=true | all-gather | bytes 294912 | tf_op jit(solution)/shard_map/all_gather | solution.py:668
  51.1 5.1 %collective-permute-start.11 = (bf16[256,384]{1,0:T(8,128)(2,1)S(1)}, bf16[256,384]{1,0:T(8,128)(2,1)S(1)}, u32[]{:S(2)}, u32[]{:S(2)}) collective-permute-start(bf16[256,384]{1,0:T(8,128)(2,1)S(1)} %shard_map.111), channel_id=1, source_target_pairs={{0,1},{2,3},{1,0},{3,2},{5,6},{6,5},{8,9},{10,11},{9,8},{11,10},{1... | collective-permute-start | bytes 589832 | tf_op jit(solution)/shard_map/ppermute | solution.py:678
  56.2 1.8 %shard_map.112 = (bf16[4,560,256]{2,1,0:T(8,128)(2,1)S(1)}, bf16[2,560,256]{2,1,0:T(8,128)(2,1)S(1)}, f32[4,528,256]{2,1,0:T(8,128)S(1)}) custom-call(bf16[7,560,256]{2,1,0:T(8,128)(2,1)S(1)} %get-tuple-element.49.field, bf16[4,528,256]{2,1,0:T(8,128)(2,1)S(1)} %get-tuple-element.59.hidden, bf16[256,512]{1,0:T(8,128)(2,1)S(1)} %all_gather.6.mixed, ...), custom_call_target="tpu_custom_call" | custom-call | flops 2400000000 | tf_op jit(solution)/shard_map/pallas_call | solution.py:546
  57.9 1.7 %collective-permute-done.11.mine = bf16[256,384]{1,0:T(8,128)(2,1)S(1)} collective-permute-done((bf16[256,384]{1,0:T(8,128)(2,1)S(1)}, bf16[256,384]{1,0:T(8,128)(2,1)S(1)}, u32[]{:S(2)}, u32[]{:S(2)}) %collective-permute-start.11) | collective-permute-done | bytes 196640 | tf_op jit(solution)/shard_map/ppermute | solution.py:678
  59.6 1.4 %collective-permute-done.12.other = bf16[256,384]{1,0:T(8,128)(2,1)S(1)} collective-permute-done((bf16[256,384]{1,0:T(8,128)(2,1)S(1)}, bf16[256,384]{1,0:T(8,128)(2,1)S(1)}, u32[]{:S(2)}, u32[]{:S(2)}) %collective-permute-start.12) | collective-permute-done | bytes 196640 | tf_op jit(solution)/shard_map/ppermute | solution.py:649
  61.1 2.2 %shard_map.113 = (bf16[7,560,256]{2,1,0:T(8,128)(2,1)S(1)}, bf16[3,560,256]{2,1,0:T(8,128)(2,1)S(1)}, bf16[2,560,256]{2,1,0:T(8,128)(2,1)S(1)}) custom-call(bf16[7,560,256]{2,1,0:T(8,128)(2,1)S(1)} %get-tuple-element.49.field, bf16[3,528,256]{2,1,0:T(8,128)(2,1)S(1)} %collective-permute-done.6.from_down, bf16[256,384]{1,0:T(8,128)(2,1)S(1)} %collective-permute-done.11.mine, ...), custom_call_target="tpu_custom_call" | custom-call | tf_op jit(solution)/shard_map/pallas_call | solution.py:546
  63.3 4.7 %shard_map.114 = (f32[128,512]{1,0:T(8,128)S(1)}, f32[128,512]{1,0:T(8,128)S(1)}, bf16[4,528,256]{2,1,0:T(8,128)(2,1)S(1)}) custom-call(bf16[3,560,256]{2,1,0:T(8,128)(2,1)S(1)} %get-tuple-element.66.before, bf16[3,528,256]{2,1,0:T(8,128)(2,1)S(1)} %collective-permute-done.13.from_up, bf16[256,384]{1,0:T(8,128)(2,1)S(1)} %collective-permute-done.11.mine, ...), custom_call_target="tpu_custom_call" | custom-call | tf_op jit(solution)/shard_map/pallas_call | solution.py:546
  68.0 0.2 collective-permute-start.14
  68.2 1.4 %collective-permute-done.14.got = f32[128,512]{1,0:T(8,128)S(1)} collective-permute-done((f32[128,512]{1,0:T(8,128)S(1)}, f32[128,512]{1,0:T(8,128)S(1)}, u32[]{:S(2)}, u32[]{:S(2)}) %collective-permute-start.14) | collective-permute-done | bytes 262176 | tf_op jit(solution)/shard_map/ppermute | solution.py:649
  69.6 0.6 collective-permute-start.15
  70.2 1.5 %collective-permute-start.16 = (bf16[32,512]{1,0:T(8,128)(2,1)S(1)}, bf16[32,512]{1,0:T(8,128)(2,1)S(1)}, u32[]{:S(2)}, u32[]{:S(2)}) collective-permute-start(bf16[32,512]{1,0:T(8,128)(2,1)S(1)} %get-tuple-element.75), channel_id=1, source_target_pairs={{0,16},{4,20},{8,24},{12,28},{16,0},{20,4},{24,8},{28,12},{1,17},{... | collective-permute-start | bytes 98312 | tf_op jit(solution)/shard_map/ppermute | solution.py:649
  71.7 1.5 %collective-permute-start.17 = (bf16[32,512]{1,0:T(8,128)(2,1)S(1)}, bf16[32,512]{1,0:T(8,128)(2,1)S(1)}, u32[]{:S(2)}, u32[]{:S(2)}) collective-permute-start(bf16[32,512]{1,0:T(8,128)(2,1)S(1)} %get-tuple-element.76), channel_id=1, source_target_pairs={{0,24},{4,28},{8,16},{12,20},{16,8},{20,12},{24,0},{28,4},{1,25},{... | collective-permute-start | bytes 98312 | tf_op jit(solution)/shard_map/ppermute | solution.py:649
  73.2 0.4 collective-permute-done.15.rest_1_
  73.6 0.5 collective-permute-done.16.rest_2_
  74.2 2.4 %collective-permute-done.17.rest_3_ = bf16[32,512]{1,0:T(8,128)(2,1)S(1)} collective-permute-done((bf16[32,512]{1,0:T(8,128)(2,1)S(1)}, bf16[32,512]{1,0:T(8,128)(2,1)S(1)}, u32[]{:S(2)}, u32[]{:S(2)}) %collective-permute-start.17) | collective-permute-done | bytes 32800 | tf_op jit(solution)/shard_map/ppermute | solution.py:649
  76.5 0.4 shard_map.116
  77.0 8.3 %all_gather.7.mixed = bf16[256,512]{1,0:T(8,128)(2,1)S(1)} all-gather(bf16[32,512]{1,0:T(8,128)(2,1)S(1)} %shard_map.116), channel_id=1, replica_groups=mesh['lon'=8,'lat'=4] {'lon'}, dimensions={0}, use_global_device_ids=true | all-gather | bytes 294912 | tf_op jit(solution)/shard_map/all_gather | solution.py:668
  85.3 1.5 %shard_map.117 = bf16[4,1024,128]{2,1,0:T(8,128)(2,1)} custom-call(bf16[7,560,256]{2,1,0:T(8,128)(2,1)S(1)} %get-tuple-element.65.state, bf16[4,528,256]{2,1,0:T(8,128)(2,1)S(1)} %get-tuple-element.70.hidden, bf16[256,512]{1,0:T(8,128)(2,1)S(1)} %all_gather.7.mixed, bf16[2,528,256]{2,1,0:T(8,128)(2,1)S(1)} %shard_map.105.after.inverse), custom_call_target="tpu_custom_call" | custom-call | tf_op jit(solution)/shard_map/pallas_call | solution.py:546
  (33 shorter events, 0.2 us)
Async XLA Ops:
  0.0 1.2 %copy-start = (bf16[4,1024,128]{2,1,0:T(8,128)(2,1)S(1)}, bf16[4,1024,128]{2,1,0:T(8,128)(2,1)}, u32[]{:S(2)}) copy-start(bf16[4,1024,128]{2,1,0:T(8,128)(2,1)} %own.1) | copy-start | bytes 3145732
  1.3 6.8 %copy-start.10 = (f32[2,3,128]{2,0,1:T(2,128)S(1)}, f32[2,3,128]{2,0,1:T(2,128)}, u32[]{:S(2)}) copy-start(f32[2,3,128]{2,0,1:T(2,128)} %param.12) | copy-start | bytes 9220
  1.3 13.5 %copy-start.5 = (f32[2,2,528,256]{3,2,1,0:T(8,128)S(1)}, f32[2,2,528,256]{3,2,1,0:T(8,128)}, u32[]{:S(2)}) copy-start(f32[2,2,528,256]{3,2,1,0:T(8,128)} %constant.10.clone.parts) | copy-start | bytes 6488068
  1.3 13.5 %copy-start.8 = (f32[8,2,256]{2,1,0:T(2,128)S(1)}, f32[8,2,256]{2,1,0:T(2,128)}, u32[]{:S(2)}) copy-start(f32[8,2,256]{2,1,0:T(2,128)} %constant.11.clone.phase) | copy-start | bytes 49156
  1.3 21.2 %collective-permute-start = (bf16[3,1024,128]{2,1,0:T(8,128)(2,1)S(1)}, bf16[3,1024,128]{2,1,0:T(8,128)(2,1)S(1)}, u32[]{:S(2)}, u32[]{:S(2)}) collective-permute-start(bf16[3,1024,128]{2,1,0:T(8,128)(2,1)S(1)} %shard_map.100.rest_0_), channel_id=1, source_target_pairs={{0,1},{2,3},{1,0},{3,2},{4,5},{6,7},{5,4},{7,6},{8,9},{10,11},{9,8... | collective-permute-start | bytes 2359304 | tf_op jit(solution)/shard_map/ppermute | solution.py:537
  4.5 10.4 %copy-start.1 = (bf16[4,1024,128]{2,1,0:T(8,128)(2,1)S(1)}, bf16[4,1024,128]{2,1,0:T(8,128)(2,1)}, u32[]{:S(2)}) copy-start(bf16[4,1024,128]{2,1,0:T(8,128)(2,1)} %own.1) | copy-start | bytes 3145732
  4.5 10.4 %copy-start.9 = (bf16[2,3,3,3,128,128]{5,4,3,2,1,0:T(8,128)(2,1)S(1)}, bf16[2,3,3,3,128,128]{5,4,3,2,1,0:T(8,128)(2,1)}, u32[]{:S(2)}) copy-start(bf16[2,3,3,3,128,128]{5,4,3,2,1,0:T(8,128)(2,1)} %kernels.1) | copy-start | bytes 5308420
  4.5 20.0 %collective-permute-start.4 = (bf16[3,1024,128]{2,1,0:T(8,128)(2,1)S(1)}, bf16[3,1024,128]{2,1,0:T(8,128)(2,1)S(1)}, u32[]{:S(2)}, u32[]{:S(2)}) collective-permute-start(bf16[3,1024,128]{2,1,0:T(8,128)(2,1)S(1)} %shard_map.101.after), channel_id=1, source_target_pairs={{1,2},{2,1},{5,6},{6,5},{9,10},{10,9},{13,14},{14,13},{17,18},{18,... | collective-permute-start | bytes 2359304 | tf_op jit(solution)/shard_map/ppermute | solution.py:537
  5.4 4.1 %collective-permute-start.1 = (bf16[4,16,128]{2,1,0:T(8,128)(2,1)S(1)}, bf16[4,16,128]{2,1,0:T(8,128)(2,1)S(1)}, u32[]{:S(2)}, u32[]{:S(2)}) collective-permute-start(bf16[4,16,128]{2,1,0:T(8,128)(2,1)S(1)} %get-tuple-element.41), channel_id=1, source_target_pairs={{0,4},{4,8},{8,12},{12,16},{16,20},{20,24},{24,28},{28,0},{1,5},{5... | collective-permute-start | bytes 49160 | tf_op jit(solution)/shard_map/ppermute | solution.py:591
  5.5 4.1 %collective-permute-start.2 = (bf16[4,16,128]{2,1,0:T(8,128)(2,1)S(1)}, bf16[4,16,128]{2,1,0:T(8,128)(2,1)S(1)}, u32[]{:S(2)}, u32[]{:S(2)}) collective-permute-start(bf16[4,16,128]{2,1,0:T(8,128)(2,1)S(1)} %get-tuple-element.42), channel_id=1, source_target_pairs={{4,0},{8,4},{12,8},{16,12},{20,16},{24,20},{28,24},{0,28},{5,1},{9... | collective-permute-start | bytes 49160 | tf_op jit(solution)/shard_map/ppermute | solution.py:592
  9.6 12.9 %collective-permute-start.3 = (bf16[3,32,128]{2,1,0:T(8,128)(2,1)S(1)}, bf16[3,32,128]{2,1,0:T(8,128)(2,1)S(1)}, u32[]{:S(2)}, u32[]{:S(2)}) collective-permute-start(bf16[3,32,128]{2,1,0:T(8,128)(2,1)S(1)} %get-tuple-element.43.near), channel_id=1, source_target_pairs={{0,1},{2,3},{1,0},{3,2},{4,5},{6,7},{5,4},{7,6},{8,9},{10,11},{9,8... | collective-permute-start | bytes 73736 | tf_op jit(solution)/shard_map/ppermute | solution.py:537
  14.1 10.4 %collective-permute-start.5 = (bf16[3,32,128]{2,1,0:T(8,128)(2,1)S(1)}, bf16[3,32,128]{2,1,0:T(8,128)(2,1)S(1)}, u32[]{:S(2)}, u32[]{:S(2)}) collective-permute-start(bf16[3,32,128]{2,1,0:T(8,128)(2,1)S(1)} %shard_map.104.after), channel_id=1, source_target_pairs={{1,2},{2,1},{5,6},{6,5},{9,10},{10,9},{13,14},{14,13},{17,18},{18,... | collective-permute-start | bytes 73736 | tf_op jit(solution)/shard_map/ppermute | solution.py:537
  22.5 2.0 %copy-start.2 = (bf16[2,256,1056]{2,1,0:T(8,128)(2,1)S(1)}, bf16[2,256,1056]{2,1,0:T(8,128)(2,1)}, u32[]{:S(2)}) copy-start(bf16[2,256,1056]{2,1,0:T(8,128)(2,1)} %constant.12.clone.forward) | copy-start | bytes 3244036
  22.5 2.1 %copy-start.6 = (f32[2,256,1]{2,1,0:T(8,128)S(1)}, f32[2,256,1]{2,1,0:T(8,128)}, u32[]{:S(2)}) copy-start(f32[2,256,1]{2,1,0:T(8,128)} %constant.13.clone.leak) | copy-start | bytes 6148
  24.6 16.7 %copy-start.3 = (bf16[2,16,128,128]{3,2,1,0:T(8,128)(2,1)S(1)}, bf16[2,16,128,128]{3,2,1,0:T(8,128)(2,1)}, u32[]{:S(2)}) copy-start(bf16[2,16,128,128]{3,2,1,0:T(8,128)(2,1)} %real.3) | copy-start | bytes 3145732
  24.6 16.7 %copy-start.4 = (bf16[2,16,128,128]{3,2,1,0:T(8,128)(2,1)S(1)}, bf16[2,16,128,128]{3,2,1,0:T(8,128)(2,1)}, u32[]{:S(2)}) copy-start(bf16[2,16,128,128]{3,2,1,0:T(8,128)(2,1)} %imag.3) | copy-start | bytes 3145732
  24.6 16.7 %copy-start.7 = (bf16[8,64,128]{2,1,0:T(8,128)(2,1)S(1)}, bf16[8,64,128]{2,1,0:T(8,128)(2,1)}, u32[]{:S(2)}) copy-start(bf16[8,64,128]{2,1,0:T(8,128)(2,1)} %constant.14.clone.turn) | copy-start | bytes 393220
  28.8 32.2 %collective-permute-start.6 = (bf16[3,528,256]{2,1,0:T(8,128)(2,1)S(1)}, bf16[3,528,256]{2,1,0:T(8,128)(2,1)S(1)}, u32[]{:S(2)}, u32[]{:S(2)}) collective-permute-start(bf16[3,528,256]{2,1,0:T(8,128)(2,1)S(1)} %get-tuple-element.52), channel_id=1, source_target_pairs={{0,1},{2,3},{1,0},{3,2},{4,5},{6,7},{5,4},{7,6},{8,9},{10,11},{9,8... | collective-permute-start | bytes 2433032 | tf_op jit(solution)/shard_map/ppermute | solution.py:537
  32.0 31.3 %collective-permute-start.13 = (bf16[3,528,256]{2,1,0:T(8,128)(2,1)S(1)}, bf16[3,528,256]{2,1,0:T(8,128)(2,1)S(1)}, u32[]{:S(2)}, u32[]{:S(2)}) collective-permute-start(bf16[3,528,256]{2,1,0:T(8,128)(2,1)S(1)} %get-tuple-element.67), channel_id=1, source_target_pairs={{1,2},{2,1},{5,6},{6,5},{9,10},{10,9},{13,14},{14,13},{17,18},{18,... | collective-permute-start | bytes 2433032 | tf_op jit(solution)/shard_map/ppermute | solution.py:537
  32.7 1.6 %collective-permute-start.7 = (f32[128,512]{1,0:T(8,128)S(1)}, f32[128,512]{1,0:T(8,128)S(1)}, u32[]{:S(2)}, u32[]{:S(2)}) collective-permute-start(f32[128,512]{1,0:T(8,128)S(1)} %get-tuple-element.54), channel_id=1, source_target_pairs={{0,4},{4,0},{8,12},{12,8},{16,20},{20,16},{24,28},{28,24},{1,5},{5... | collective-permute-start | bytes 786440 | tf_op jit(solution)/shard_map/ppermute | solution.py:649
  34.3 4.9 %collective-permute-start.10 = (bf16[32,512]{1,0:T(8,128)(2,1)S(1)}, bf16[32,512]{1,0:T(8,128)(2,1)S(1)}, u32[]{:S(2)}, u32[]{:S(2)}) collective-permute-start(bf16[32,512]{1,0:T(8,128)(2,1)S(1)} %get-tuple-element.58), channel_id=1, source_target_pairs={{0,24},{4,28},{8,16},{12,20},{16,8},{20,12},{24,0},{28,4},{1,25},{... | collective-permute-start | bytes 98312 | tf_op jit(solution)/shard_map/ppermute | solution.py:649
  36.8 3.9 %collective-permute-start.8 = (bf16[32,512]{1,0:T(8,128)(2,1)S(1)}, bf16[32,512]{1,0:T(8,128)(2,1)S(1)}, u32[]{:S(2)}, u32[]{:S(2)}) collective-permute-start(bf16[32,512]{1,0:T(8,128)(2,1)S(1)} %get-tuple-element.56), channel_id=1, source_target_pairs={{0,8},{4,12},{8,0},{12,4},{16,24},{20,28},{24,16},{28,20},{1,9},{5... | collective-permute-start | bytes 98312 | tf_op jit(solution)/shard_map/ppermute | solution.py:649
  37.4 3.9 %collective-permute-start.9 = (bf16[32,512]{1,0:T(8,128)(2,1)S(1)}, bf16[32,512]{1,0:T(8,128)(2,1)S(1)}, u32[]{:S(2)}, u32[]{:S(2)}) collective-permute-start(bf16[32,512]{1,0:T(8,128)(2,1)S(1)} %get-tuple-element.57), channel_id=1, source_target_pairs={{0,16},{4,20},{8,24},{12,28},{16,0},{20,4},{24,8},{28,12},{1,17},{... | collective-permute-start | bytes 98312 | tf_op jit(solution)/shard_map/ppermute | solution.py:649
  51.1 8.6 %collective-permute-start.11 = (bf16[256,384]{1,0:T(8,128)(2,1)S(1)}, bf16[256,384]{1,0:T(8,128)(2,1)S(1)}, u32[]{:S(2)}, u32[]{:S(2)}) collective-permute-start(bf16[256,384]{1,0:T(8,128)(2,1)S(1)} %shard_map.111), channel_id=1, source_target_pairs={{0,1},{2,3},{1,0},{3,2},{5,6},{6,5},{8,9},{10,11},{9,8},{11,10},{1... | collective-permute-start | bytes 589832 | tf_op jit(solution)/shard_map/ppermute | solution.py:678
  59.6 1.4 %collective-permute-start.12 = (bf16[256,384]{1,0:T(8,128)(2,1)S(1)}, bf16[256,384]{1,0:T(8,128)(2,1)S(1)}, u32[]{:S(2)}, u32[]{:S(2)}) collective-permute-start(bf16[256,384]{1,0:T(8,128)(2,1)S(1)} %collective-permute-done.11.mine), channel_id=1, source_target_pairs={{0,4},{4,0},{8,12},{12,8},{16,20},{20,16},{24,28},{28,24},{1,5},{5... | collective-permute-start | bytes 589832 | tf_op jit(solution)/shard_map/ppermute | solution.py:649
  68.0 1.6 %collective-permute-start.14 = (f32[128,512]{1,0:T(8,128)S(1)}, f32[128,512]{1,0:T(8,128)S(1)}, u32[]{:S(2)}, u32[]{:S(2)}) collective-permute-start(f32[128,512]{1,0:T(8,128)S(1)} %get-tuple-element.72), channel_id=1, source_target_pairs={{0,4},{4,0},{8,12},{12,8},{16,20},{20,16},{24,28},{28,24},{1,5},{5... | collective-permute-start | bytes 786440 | tf_op jit(solution)/shard_map/ppermute | solution.py:649
  69.6 4.0 %collective-permute-start.15 = (bf16[32,512]{1,0:T(8,128)(2,1)S(1)}, bf16[32,512]{1,0:T(8,128)(2,1)S(1)}, u32[]{:S(2)}, u32[]{:S(2)}) collective-permute-start(bf16[32,512]{1,0:T(8,128)(2,1)S(1)} %get-tuple-element.74), channel_id=1, source_target_pairs={{0,8},{4,12},{8,0},{12,4},{16,24},{20,28},{24,16},{28,20},{1,9},{5... | collective-permute-start | bytes 98312 | tf_op jit(solution)/shard_map/ppermute | solution.py:649
  70.2 3.9 %collective-permute-start.16 = (bf16[32,512]{1,0:T(8,128)(2,1)S(1)}, bf16[32,512]{1,0:T(8,128)(2,1)S(1)}, u32[]{:S(2)}, u32[]{:S(2)}) collective-permute-start(bf16[32,512]{1,0:T(8,128)(2,1)S(1)} %get-tuple-element.75), channel_id=1, source_target_pairs={{0,16},{4,20},{8,24},{12,28},{16,0},{20,4},{24,8},{28,12},{1,17},{... | collective-permute-start | bytes 98312 | tf_op jit(solution)/shard_map/ppermute | solution.py:649
  71.7 4.8 %collective-permute-start.17 = (bf16[32,512]{1,0:T(8,128)(2,1)S(1)}, bf16[32,512]{1,0:T(8,128)(2,1)S(1)}, u32[]{:S(2)}, u32[]{:S(2)}) collective-permute-start(bf16[32,512]{1,0:T(8,128)(2,1)S(1)} %get-tuple-element.76), channel_id=1, source_target_pairs={{0,24},{4,28},{8,16},{12,20},{16,8},{20,12},{24,0},{28,4},{1,25},{... | collective-permute-start | bytes 98312 | tf_op jit(solution)/shard_map/ppermute | solution.py:649

commit v7 on v6

--- a/solution.py
+++ b/solution.py
@@ -85,6 +85,11 @@
 
 def dot(a, b):
     return jnp.dot(a, b, preferred_element_type=F32)
+
+
+def halves(x):
+    high = x.astype(BF)
+    return high, (x - high.astype(F32)).astype(BF)
 
 
 def silu_of_half(half):
@@ -137,22 +142,19 @@
                 close_row(*dst[pair + i])
 
 
-def transform(forward, leak, bias, held, kept, sent):
+def transform(forward, held, kept, sent):
     core = lax.rem(lax.axis_index("lon"), 2)
     rows, c = held.shape[0], held.shape[2] // 2
-    half = 0.5 * bias[CONVS - 1 : CONVS]
-    level = silu_of_half(half)
     for row in range(0, rows, 2):
         cells = [
             jnp.concatenate([held[row + i, :, e * c : (e + 1) * c] for i in range(2)], axis=1)
             for e in range(2)
         ]
         total = dot(forward[core], jnp.concatenate(cells, axis=0))
-        modes2 = total.shape[0]
-        total = total - leak[core] * jnp.concatenate([level, level], axis=1)
+        half = total.shape[0] // 2
         lanes = slice(row * c, (row + 2) * c)
-        kept[:, lanes] = total[: modes2 // 2]
-        sent[:, lanes] = total[modes2 // 2 :]
+        kept[:, lanes] = total[:half]
+        sent[:, lanes] = total[half:]
 
 
 def pack_cells(body, ends, source, line, wide, at):
@@ -261,7 +263,7 @@
 
 
 def first_upper_kernel(
-    up, up_edge, field, first, second, inner, sums, packed, bias, forward, leak,
+    up, up_edge, field, first, second, inner, sums, packed, bias, forward,
     kept, sent, hidden, to_partner, to_other, before,
     line, more, most, held,
 ):
@@ -280,7 +282,7 @@
 
     args = (before, field, inner, sums, first, second, (more, most), packed, bias)
     upper_part(*args, lat_edges(), emit)
-    transform(forward, leak, bias, held, kept, sent)
+    transform(forward, held, kept, sent)
 
 
 def pair_kernel(kept, got, *outs):
@@ -288,29 +290,27 @@
     rows = outs[0].shape[0]
     for step, out in enumerate(outs):
         span = pl.ds(pl.multiple_of((chip ^ step) * rows, rows), rows)
-        out[...] = (kept[span, :] + got[span, :]).astype(BF)
-
-
-def mix_kernel(turn, real, imag, bias, *rest):
+        out[...] = kept[span, :] + got[span, :]
+
+
+def mix_kernel(turn, real, imag, *rest):
     *sums, mixed, spread_in, spread_out = rest
     me = lax.axis_index("lon")
     modes, c = real.shape[1], real.shape[2]
-    summed = dot(turn[me], jnp.concatenate([x[...] for x in sums], axis=0))
+    high, low = halves(jnp.concatenate([x[...] for x in sums], axis=0))
+    summed = dot(turn[me], high)
     summed = summed[: 2 * modes] + summed[2 * modes :]
+    summed = summed + dot(turn[me, : 2 * modes], low)
     rows = summed.shape[1] // c
-    level = (me == 0).astype(F32) * silu_of_half(0.5 * bias[CONVS - 1 : CONVS])
     for half in range(2):
         for row in range(rows):
             spread_in[pl.ds(half * rows + row, modes, stride=2 * rows), :] = summed[
                 half * modes : (half + 1) * modes, row * c : (row + 1) * c
             ]
-    spread_in[0:rows] = spread_in[0:rows] + level
     sign = jnp.where(lax.broadcasted_iota(jnp.int32, (2 * rows, c), 0) < rows, -1.0, 1.0)
     for k in range(modes):
         wide = spread_in[2 * rows * k : 2 * rows * (k + 1)]
-        high = wide.astype(BF)
-        low = (wide - high.astype(F32)).astype(BF)
-        both = jnp.concatenate([high, low], axis=0)
+        both = jnp.concatenate(halves(wide), axis=0)
         weight = jnp.concatenate([real[0, k], imag[0, k]], axis=1)
         out = jnp.dot(both, weight, preferred_element_type=F32)
         out = out[: 2 * rows] + out[2 * rows :]
@@ -318,7 +318,7 @@
         spread_out[2 * rows * k : 2 * rows * (k + 1)] = out[:, :c] + sign * turned
     for row in range(rows):
         parts = [spread_out[pl.ds(i * rows + row, modes, stride=2 * rows), :] for i in range(2)]
-        mixed[:, row * c : (row + 1) * c] = jnp.concatenate(parts, axis=0).astype(BF)
+        mixed[:, row * c : (row + 1) * c] = jnp.concatenate(parts, axis=0)
 
 
 def halo_kernel(mixed, out):
@@ -328,12 +328,19 @@
     for at in range(HALO):
         last = mixed[:, (rows - 1 - at) * c : (rows - at) * c]
         leading = mixed[:, (HALO - 1 - at) * c : (HALO - at) * c]
-        out[:, at * c : (at + 1) * c] = jnp.where(even, last, leading)
+        out[:, at * c : (at + 1) * c] = jnp.where(even, last, leading).astype(BF)
 
 
 def pick(mine, other, first):
     even = lax.rem(lax.axis_index("lon"), 2) == 0
     return jnp.where(even == first, mine[...], other[...])
+
+
+def wave_of(inverse, mixed):
+    if mixed.dtype == BF:
+        return dot(inverse, mixed)
+    high, low = halves(mixed)
+    return dot(inverse, high) + dot(inverse, low)
 
 
 def next_state(old, conv, mixed, inverse, new, at, count, mask):
@@ -345,7 +352,7 @@
         for start in range(0, width, tile):
             span = slice(start, start + tile)
             wide = slice(start + RUNS, start + RUNS + tile)
-            waves = [dot(inverse[e, span], mixed[:, lanes]) for e in range(2)]
+            waves = [wave_of(inverse[e, span], mixed[:, lanes]) for e in range(2)]
             for i in range(min(2, count - pair)):
                 wave = jnp.concatenate([w[:, i * c : (i + 1) * c] for w in waves], axis=1)
                 total = old[0][old[1] + pair + i, wide].astype(F32)
@@ -377,7 +384,7 @@
 
 def middle_upper_kernel(
     before, from_up, mine, other, inverse, state, first, second, inner, sums,
-    packed, bias, forward, leak,
+    packed, bias, forward,
     kept, sent, hidden, above, mixed_up, more, most, held,
 ):
     edge = lat_edges()
@@ -391,7 +398,7 @@
 
     args = (above, state, inner, sums, first, second, (more, most), packed, bias)
     upper_part(*args, edge, emit)
-    transform(forward, leak, bias, held, kept, sent)
+    transform(forward, held, kept, sent)
 
 
 def last_kernel(state, hidden, mixed, inverse, result, line, done, sems):
@@ -400,7 +407,8 @@
     run = 2 * width // RUNS
     copies = []
     for pair in range(0, rows, 2):
-        waves = [dot(inverse[e], mixed[:, pair * c : (pair + 2) * c]) for e in range(2)]
+        lanes = slice(pair * c, (pair + 2) * c)
+        waves = [wave_of(inverse[e], mixed[:, lanes]) for e in range(2)]
         for i in range(2):
             row = pair + i
             for e in range(2):
@@ -428,15 +436,14 @@
     order = cell_order(cells + 2 * PAD).reshape(-1) - PAD
     inside = (order >= 0) & (order < cells)
     waves = np.arange(modes)
-    tables, leaks = [], []
+    tables = []
     for core in range(2):
         theta = (2 * np.pi / lon_total) * (np.outer(waves, order + core * cells) % lon_total)
         full = np.stack([np.cos(theta), -np.sin(theta)], 0) * inside
         full = full.reshape(2, lon_size // 2, 2, modes // lon_size, -1)
         full = full.transpose(2, 1, 0, 3, 4)[[core, 1 - core]]
         tables.append(full.reshape(2 * modes, -1).astype(ml_dtypes.bfloat16))
-        leaks.append(tables[-1].astype(np.float64).sum(1, keepdims=True).astype(np.float32))
-    return np.stack(tables), np.stack(leaks)
+    return np.stack(tables)
 
 
 def turn_table(lon_size, local, scale):
@@ -609,7 +616,7 @@
         [],
         in_specs=[VMEM, VMEM, ANY],
     )[0]
-    forward, leak = forward_table(*tables)
+    forward = forward_table(*tables)
     turn = turn_table(lon_size, local, 1.0 / lon_total)
 
     line = pltpu.VMEM((2, width + 2 * half // RUNS + 8, c), F32)
@@ -638,7 +645,7 @@
     )
     kept, sent, hidden, to_partner, to_other, before = call(
         first_upper_kernel,
-        (up, up_edge, *low, *inner, packed, conv_bias[0], forward, leak),
+        (up, up_edge, *low, *inner, packed, conv_bias[0], forward),
         part_shape
         + [hidden_shape]
         + [shape(HALO, half, 2 * c)] * 2
@@ -648,7 +655,7 @@
     def swap(array, step):
         return lax.ppermute(array, "lon", [(i, i ^ step) for i in range(lon_size)])
 
-    chunk = shape(2 * local, rows * c)
+    chunk = jax.ShapeDtypeStruct((2 * local, rows * c), F32)
 
     def pair(kept, sent):
         return call(pair_kernel, (kept, swap(sent, 1)), [chunk] * (lon_size // 2), [])
@@ -659,10 +666,10 @@
         weights = pl.BlockSpec((1, local, c, c), lambda i: (block, 0, 0, 0))
         (mixed,) = call(
             mix_kernel,
-            (turn, spec_real, spec_imag, conv_bias[block], *sums),
+            (turn, spec_real, spec_imag, *sums),
             [chunk],
             [turned, turned],
-            in_specs=[VMEM, weights, weights] + [VMEM] * (1 + len(sums)),
+            in_specs=[VMEM, weights, weights] + [VMEM] * len(sums),
             grid=(1,),
         )
         return lax.all_gather(mixed, "lon", axis=0, tiled=True)
@@ -693,7 +700,7 @@
     kept, sent, hidden = call(
         middle_upper_kernel,
         (before, from_up, mine, other, inverse, state, *low, *inner)
-        + (later, conv_bias[1], forward, leak),
+        + (later, conv_bias[1], forward),
         part_shape + [hidden_shape],
         [pltpu.VMEM((HALO, wide, 2 * c), BF), gathered] + upper,
     )

time: 87.3 us -> 87.9 us (level)
  blocking collectives: 17.6 us -> 18.8 us
  waiting for transfers between devices: 19.2 us -> 18.1 us
    all_gather x2, blocking collectives: 17.6 us -> 18.8 us  [mix(): return lax.all_gather(mixed, 'lon', axis=0, tiled=True)]
  transfers between devices with their start and end apart: 18 -> 18, of which waited for: 12 -> 11; matrix products, arithmetic and copies ran while one was open for 0% -> 0% of each run, Pallas kernels for 11% -> 11%
where the time goes in v7:
time: 87.9 us; the launch traced here: 87.7 us
  starting transfers between devices  28.1 us (32%)
  Pallas kernels  20.8 us (24%)
  blocking collectives  18.8 us (21%)
  waiting for transfers between devices  18.1 us (21%)
  local copies, waits for them, and re-layouts  1.29 us (1%)
    pallas_call x18, Pallas kernels, call(): pl.pallas_call(kernel, grid=grid, out_shape=outs, in_specs=in_specs or [V...  20.8 us
    all_gather x2, blocking collectives, mix(): return lax.all_gather(mixed, 'lon', axis=0, tiled=True)  18.8 us
    ppermute x6, starting transfers between devices, move(): return lax.ppermute(array, 'lat', lat_pairs(partner))  13 us
    ppermute x9, waiting for transfers between devices, swap(): return lax.ppermute(array, 'lon', [(i, i ^ step) for i in range(lon_size)])  10.3 us
    ppermute x9, starting transfers between devices, swap(): return lax.ppermute(array, 'lon', [(i, i ^ step) for i in range(lon_size)])  7.38 us
    ppermute x1, starting transfers between devices, per_device(): mine = lax.ppermute(halo, ('lon', 'lat'), ways)  5.1 us
    ppermute x6, waiting for transfers between devices, move(): return lax.ppermute(array, 'lat', lat_pairs(partner))  5 us
    ppermute x1, starting transfers between devices, per_device(): from_right = lax.ppermute(leading, 'lon', left)  2.63 us
  transfers between devices with their start and end apart: 18, of which 11 were waited for; matrix products, arithmetic and copies ran while one was open for 0% of the time, Pallas kernels for 11%

profile of v7, /device:TPU:0, one launch (start us, length us, event | category | flops | bytes accessed | tf_op | source)
XLA Modules:
  0.0 87.7 jit_solution(11039092988336532206)
XLA Ops:
  0.0 1.2 %copy-done = bf16[4,1024,128]{2,1,0:T(8,128)(2,1)S(1)} copy-done((bf16[4,1024,128]{2,1,0:T(8,128)(2,1)S(1)}, bf16[4,1024,128]{2,1,0:T(8,128)(2,1)}, u32[]{:S(2)}) %copy-start) | copy-done | bytes 1048600
  1.2 0.1 shard_map.91.rest_0_
  1.3 0.0 copy-start.5
  1.3 0.0 copy-start.7
  1.3 3.1 %collective-permute-start = (bf16[3,1024,128]{2,1,0:T(8,128)(2,1)S(1)}, bf16[3,1024,128]{2,1,0:T(8,128)(2,1)S(1)}, u32[]{:S(2)}, u32[]{:S(2)}) collective-permute-start(bf16[3,1024,128]{2,1,0:T(8,128)(2,1)S(1)} %shard_map.91.rest_0_), channel_id=1, source_target_pairs={{0,1},{2,3},{1,0},{3,2},{4,5},{6,7},{5,4},{7,6},{8,9},{10,11},{9,8... | collective-permute-start | bytes 2359304 | tf_op jit(solution)/shard_map/ppermute | solution.py:544
  4.4 0.1 shard_map.92.after
  4.5 0.8 collective-permute-start.4
  5.4 0.1 collective-permute-start.1
  5.5 2.6 %collective-permute-start.2 = (bf16[4,16,128]{2,1,0:T(8,128)(2,1)S(1)}, bf16[4,16,128]{2,1,0:T(8,128)(2,1)S(1)}, u32[]{:S(2)}, u32[]{:S(2)}) collective-permute-start(bf16[4,16,128]{2,1,0:T(8,128)(2,1)S(1)} %get-tuple-element.42), channel_id=1, source_target_pairs={{4,0},{8,4},{12,8},{16,12},{20,16},{24,20},{28,24},{0,28},{5,1},{9... | collective-permute-start | bytes 49160 | tf_op jit(solution)/shard_map/ppermute | solution.py:599
  8.1 1.4 %collective-permute-done.1.from_left = bf16[4,16,128]{2,1,0:T(8,128)(2,1)S(1)} collective-permute-done((bf16[4,16,128]{2,1,0:T(8,128)(2,1)S(1)}, bf16[4,16,128]{2,1,0:T(8,128)(2,1)S(1)}, u32[]{:S(2)}, u32[]{:S(2)}) %collective-permute-start.1) | collective-permute-done | bytes 16416 | tf_op jit(solution)/shard_map/ppermute | solution.py:598
  9.5 0.0 collective-permute-done.2.from_right
  9.6 4.5 %collective-permute-start.3 = (bf16[3,32,128]{2,1,0:T(8,128)(2,1)S(1)}, bf16[3,32,128]{2,1,0:T(8,128)(2,1)S(1)}, u32[]{:S(2)}, u32[]{:S(2)}) collective-permute-start(bf16[3,32,128]{2,1,0:T(8,128)(2,1)S(1)} %get-tuple-element.43.near), channel_id=1, source_target_pairs={{0,1},{2,3},{1,0},{3,2},{4,5},{6,7},{5,4},{7,6},{8,9},{10,11},{9,8... | collective-permute-start | bytes 73736 | tf_op jit(solution)/shard_map/ppermute | solution.py:544
  14.1 0.7 collective-permute-start.5
  14.8 0.1 shard_map.96.after.inverse
  15.0 2.5 %shard_map.97 = (bf16[4,560,256]{2,1,0:T(8,128)(2,1)S(1)}, bf16[3,4,512,256]{3,2,1,0:T(8,128)(2,1)S(1)}, bf16[3,4,512,256]{3,2,1,0:T(8,128)(2,1)S(1)}, bf16[2,56...) custom-call(bf16[4,1024,128]{2,1,0:T(8,128)(2,1)S(1)} %copy-done.1, bf16[4,32,128]{2,1,0:T(8,128)(2,1)S(1)} %get-tuple-element.44.edges.own_edge, ...), custom_call_target="tpu_custom_call" | custom-call | flops 3200000000 | tf_op jit(solution)/shard_map/pallas_call | solution.py:553
  17.5 5.0 %collective-permute-done.3.down_edge = bf16[3,32,128]{2,1,0:T(8,128)(2,1)S(1)} collective-permute-done((bf16[3,32,128]{2,1,0:T(8,128)(2,1)S(1)}, bf16[3,32,128]{2,1,0:T(8,128)(2,1)S(1)}, u32[]{:S(2)}, u32[]{:S(2)}) %collective-permute-start.3) | collective-permute-done | bytes 24608 | tf_op jit(solution)/shard_map/ppermute | solution.py:544
  22.5 2.0 %shard_map.98 = (bf16[7,560,256]{2,1,0:T(8,128)(2,1)S(1)}, bf16[3,560,256]{2,1,0:T(8,128)(2,1)S(1)}, bf16[2,560,256]{2,1,0:T(8,128)(2,1)S(1)}) custom-call(bf16[3,1024,128]{2,1,0:T(8,128)(2,1)S(1)} %collective-permute-done.down, bf16[3,32,128]{2,1,0:T(8,128)(2,1)S(1)} %collective-permute-done.3.down_edge, bf16[4,560,256]{2,1,0:T(8,128)(2,1)S(1)} %get-tuple-element.45.own, ...), custom_call_target="tpu_custom_call" | custom-call | tf_op jit(solution)/shard_map/pallas_call | solution.py:553
  24.6 0.0 copy-start.6
  24.6 4.2 %shard_map.99 = (f32[128,512]{1,0:T(8,128)S(1)}, f32[128,512]{1,0:T(8,128)S(1)}, bf16[4,528,256]{2,1,0:T(8,128)(2,1)S(1)}, bf16[3,528,256]{2,1,0:T(8,128)(2,1)S(...) custom-call(bf16[3,1024,128]{2,1,0:T(8,128)(2,1)S(1)} %collective-permute-done.4.up, ...), custom_call_target="tpu_custom_call" | custom-call | tf_op jit(solution)/shard_map/pallas_call | solution.py:553
  28.8 0.1 collective-permute-start.7
  28.9 3.1 %collective-permute-start.6 = (bf16[3,528,256]{2,1,0:T(8,128)(2,1)S(1)}, bf16[3,528,256]{2,1,0:T(8,128)(2,1)S(1)}, u32[]{:S(2)}, u32[]{:S(2)}) collective-permute-start(bf16[3,528,256]{2,1,0:T(8,128)(2,1)S(1)} %get-tuple-element.52), channel_id=1, source_target_pairs={{0,1},{2,3},{1,0},{3,2},{4,5},{6,7},{5,4},{7,6},{8,9},{10,11},{9,8... | collective-permute-start | bytes 2433032 | tf_op jit(solution)/shard_map/ppermute | solution.py:544
  32.0 0.7 collective-permute-start.13
  32.7 0.1 shard_map.100
  32.8 2.5 %collective-permute-start.10 = (f32[32,512]{1,0:T(8,128)S(1)}, f32[32,512]{1,0:T(8,128)S(1)}, u32[]{:S(2)}, u32[]{:S(2)}) collective-permute-start(f32[32,512]{1,0:T(8,128)S(1)} %get-tuple-element.58), channel_id=1, source_target_pairs={{0,24},{4,28},{8,16},{12,20},{16,8},{20,12},{24,0},{28,4},{1,25},{... | collective-permute-start | bytes 196616 | tf_op jit(solution)/shard_map/ppermute | solution.py:656
  35.3 0.5 collective-permute-start.8
  35.8 0.5 collective-permute-start.9
  36.4 2.1 %collective-permute-done.10.rest_3_ = f32[32,512]{1,0:T(8,128)S(1)} collective-permute-done((f32[32,512]{1,0:T(8,128)S(1)}, f32[32,512]{1,0:T(8,128)S(1)}, u32[]{:S(2)}, u32[]{:S(2)}) %collective-permute-start.10) | collective-permute-done | bytes 65568 | tf_op jit(solution)/shard_map/ppermute | solution.py:656
  38.4 1.2 %collective-permute-done.8.rest_1_ = f32[32,512]{1,0:T(8,128)S(1)} collective-permute-done((f32[32,512]{1,0:T(8,128)S(1)}, f32[32,512]{1,0:T(8,128)S(1)}, u32[]{:S(2)}, u32[]{:S(2)}) %collective-permute-start.8) | collective-permute-done | bytes 65568 | tf_op jit(solution)/shard_map/ppermute | solution.py:656
  39.6 0.5 collective-permute-done.9.rest_2_
  40.1 0.4 shard_map.101
  40.5 9.8 %all_gather.6.mixed = f32[256,512]{1,0:T(8,128)S(1)} all-gather(f32[32,512]{1,0:T(8,128)S(1)} %shard_map.101), channel_id=1, replica_groups=mesh['lon'=8,'lat'=4] {'lon'}, dimensions={0}, use_global_device_ids=true | all-gather | bytes 589824 | tf_op jit(solution)/shard_map/all_gather | solution.py:675
  50.4 5.1 %collective-permute-start.11 = (bf16[256,384]{1,0:T(8,128)(2,1)S(1)}, bf16[256,384]{1,0:T(8,128)(2,1)S(1)}, u32[]{:S(2)}, u32[]{:S(2)}) collective-permute-start(bf16[256,384]{1,0:T(8,128)(2,1)S(1)} %shard_map.102), channel_id=1, source_target_pairs={{0,1},{2,3},{1,0},{3,2},{5,6},{6,5},{8,9},{10,11},{9,8},{11,10},{1... | collective-permute-start | bytes 589832 | tf_op jit(solution)/shard_map/ppermute | solution.py:685
  55.5 2.1 %shard_map.103 = (bf16[4,560,256]{2,1,0:T(8,128)(2,1)S(1)}, bf16[2,560,256]{2,1,0:T(8,128)(2,1)S(1)}, f32[4,528,256]{2,1,0:T(8,128)S(1)}) custom-call(bf16[7,560,256]{2,1,0:T(8,128)(2,1)S(1)} %get-tuple-element.49.field, bf16[4,528,256]{2,1,0:T(8,128)(2,1)S(1)} %get-tuple-element.59.hidden, f32[256,512]{1,0:T(8,128)S(1)} %all_gather.6.mixed, ...), custom_call_target="tpu_custom_call" | custom-call | flops 2400000000 | tf_op jit(solution)/shard_map/pallas_call | solution.py:553
  57.6 1.4 %collective-permute-done.11.mine = bf16[256,384]{1,0:T(8,128)(2,1)S(1)} collective-permute-done((bf16[256,384]{1,0:T(8,128)(2,1)S(1)}, bf16[256,384]{1,0:T(8,128)(2,1)S(1)}, u32[]{:S(2)}, u32[]{:S(2)}) %collective-permute-start.11) | collective-permute-done | bytes 196640 | tf_op jit(solution)/shard_map/ppermute | solution.py:685
  59.0 1.4 %collective-permute-done.12.other = bf16[256,384]{1,0:T(8,128)(2,1)S(1)} collective-permute-done((bf16[256,384]{1,0:T(8,128)(2,1)S(1)}, bf16[256,384]{1,0:T(8,128)(2,1)S(1)}, u32[]{:S(2)}, u32[]{:S(2)}) %collective-permute-start.12) | collective-permute-done | bytes 196640 | tf_op jit(solution)/shard_map/ppermute | solution.py:656
  60.4 2.3 %shard_map.104 = (bf16[7,560,256]{2,1,0:T(8,128)(2,1)S(1)}, bf16[3,560,256]{2,1,0:T(8,128)(2,1)S(1)}, bf16[2,560,256]{2,1,0:T(8,128)(2,1)S(1)}) custom-call(bf16[7,560,256]{2,1,0:T(8,128)(2,1)S(1)} %get-tuple-element.49.field, bf16[3,528,256]{2,1,0:T(8,128)(2,1)S(1)} %collective-permute-done.6.from_down, bf16[256,384]{1,0:T(8,128)(2,1)S(1)} %collective-permute-done.11.mine, ...), custom_call_target="tpu_custom_call" | custom-call | tf_op jit(solution)/shard_map/pallas_call | solution.py:553
  62.8 4.7 %shard_map.105 = (f32[128,512]{1,0:T(8,128)S(1)}, f32[128,512]{1,0:T(8,128)S(1)}, bf16[4,528,256]{2,1,0:T(8,128)(2,1)S(1)}) custom-call(bf16[3,560,256]{2,1,0:T(8,128)(2,1)S(1)} %get-tuple-element.66.before, bf16[3,528,256]{2,1,0:T(8,128)(2,1)S(1)} %collective-permute-done.13.from_up, bf16[256,384]{1,0:T(8,128)(2,1)S(1)} %collective-permute-done.11.mine, ...), custom_call_target="tpu_custom_call" | custom-call | tf_op jit(solution)/shard_map/pallas_call | solution.py:553
  67.4 0.2 collective-permute-start.14
  67.6 1.4 %collective-permute-done.14.got = f32[128,512]{1,0:T(8,128)S(1)} collective-permute-done((f32[128,512]{1,0:T(8,128)S(1)}, f32[128,512]{1,0:T(8,128)S(1)}, u32[]{:S(2)}, u32[]{:S(2)}) %collective-permute-start.14) | collective-permute-done | bytes 262176 | tf_op jit(solution)/shard_map/ppermute | solution.py:656
  69.1 0.7 collective-permute-start.15
  69.8 1.4 %collective-permute-start.16 = (f32[32,512]{1,0:T(8,128)S(1)}, f32[32,512]{1,0:T(8,128)S(1)}, u32[]{:S(2)}, u32[]{:S(2)}) collective-permute-start(f32[32,512]{1,0:T(8,128)S(1)} %get-tuple-element.75), channel_id=1, source_target_pairs={{0,16},{4,20},{8,24},{12,28},{16,0},{20,4},{24,8},{28,12},{1,17},{... | collective-permute-start | bytes 196616 | tf_op jit(solution)/shard_map/ppermute | solution.py:656
  71.2 1.5 %collective-permute-start.17 = (f32[32,512]{1,0:T(8,128)S(1)}, f32[32,512]{1,0:T(8,128)S(1)}, u32[]{:S(2)}, u32[]{:S(2)}) collective-permute-start(f32[32,512]{1,0:T(8,128)S(1)} %get-tuple-element.76), channel_id=1, source_target_pairs={{0,24},{4,28},{8,16},{12,20},{16,8},{20,12},{24,0},{28,4},{1,25},{... | collective-permute-start | bytes 196616 | tf_op jit(solution)/shard_map/ppermute | solution.py:656
  72.6 0.8 collective-permute-done.15.rest_1_
  73.4 0.6 collective-permute-done.16.rest_2_
  74.1 2.3 %collective-permute-done.17.rest_3_ = f32[32,512]{1,0:T(8,128)S(1)} collective-permute-done((f32[32,512]{1,0:T(8,128)S(1)}, f32[32,512]{1,0:T(8,128)S(1)}, u32[]{:S(2)}, u32[]{:S(2)}) %collective-permute-start.17) | collective-permute-done | bytes 65568 | tf_op jit(solution)/shard_map/ppermute | solution.py:656
  76.3 0.4 shard_map.107
  76.8 9.0 %all_gather.7.mixed = f32[256,512]{1,0:T(8,128)S(1)} all-gather(f32[32,512]{1,0:T(8,128)S(1)} %shard_map.107), channel_id=1, replica_groups=mesh['lon'=8,'lat'=4] {'lon'}, dimensions={0}, use_global_device_ids=true | all-gather | bytes 589824 | tf_op jit(solution)/shard_map/all_gather | solution.py:675
  85.8 1.8 %shard_map.108 = bf16[4,1024,128]{2,1,0:T(8,128)(2,1)} custom-call(bf16[7,560,256]{2,1,0:T(8,128)(2,1)S(1)} %get-tuple-element.65.state, bf16[4,528,256]{2,1,0:T(8,128)(2,1)S(1)} %get-tuple-element.70.hidden, f32[256,512]{1,0:T(8,128)S(1)} %all_gather.7.mixed, bf16[2,528,256]{2,1,0:T(8,128)(2,1)S(1)} %shard_map.96.after.inverse), custom_call_target="tpu_custom_call" | custom-call | tf_op jit(solution)/shard_map/pallas_call | solution.py:553
  (31 shorter events, 0.2 us)
Async XLA Ops:
  0.0 1.2 %copy-start = (bf16[4,1024,128]{2,1,0:T(8,128)(2,1)S(1)}, bf16[4,1024,128]{2,1,0:T(8,128)(2,1)}, u32[]{:S(2)}) copy-start(bf16[4,1024,128]{2,1,0:T(8,128)(2,1)} %own.1) | copy-start | bytes 3145732
  1.3 6.8 %copy-start.9 = (f32[2,3,128]{2,0,1:T(2,128)S(1)}, f32[2,3,128]{2,0,1:T(2,128)}, u32[]{:S(2)}) copy-start(f32[2,3,128]{2,0,1:T(2,128)} %param.11) | copy-start | bytes 9220
  1.3 13.5 %copy-start.5 = (f32[2,2,528,256]{3,2,1,0:T(8,128)S(1)}, f32[2,2,528,256]{3,2,1,0:T(8,128)}, u32[]{:S(2)}) copy-start(f32[2,2,528,256]{3,2,1,0:T(8,128)} %constant.8.clone.parts) | copy-start | bytes 6488068
  1.3 13.5 %copy-start.7 = (f32[8,2,256]{2,1,0:T(2,128)S(1)}, f32[8,2,256]{2,1,0:T(2,128)}, u32[]{:S(2)}) copy-start(f32[8,2,256]{2,1,0:T(2,128)} %constant.9.clone.phase) | copy-start | bytes 49156
  1.3 21.2 %collective-permute-start = (bf16[3,1024,128]{2,1,0:T(8,128)(2,1)S(1)}, bf16[3,1024,128]{2,1,0:T(8,128)(2,1)S(1)}, u32[]{:S(2)}, u32[]{:S(2)}) collective-permute-start(bf16[3,1024,128]{2,1,0:T(8,128)(2,1)S(1)} %shard_map.91.rest_0_), channel_id=1, source_target_pairs={{0,1},{2,3},{1,0},{3,2},{4,5},{6,7},{5,4},{7,6},{8,9},{10,11},{9,8... | collective-permute-start | bytes 2359304 | tf_op jit(solution)/shard_map/ppermute | solution.py:544
  4.5 10.4 %copy-start.1 = (bf16[4,1024,128]{2,1,0:T(8,128)(2,1)S(1)}, bf16[4,1024,128]{2,1,0:T(8,128)(2,1)}, u32[]{:S(2)}) copy-start(bf16[4,1024,128]{2,1,0:T(8,128)(2,1)} %own.1) | copy-start | bytes 3145732
  4.5 10.4 %copy-start.8 = (bf16[2,3,3,3,128,128]{5,4,3,2,1,0:T(8,128)(2,1)S(1)}, bf16[2,3,3,3,128,128]{5,4,3,2,1,0:T(8,128)(2,1)}, u32[]{:S(2)}) copy-start(bf16[2,3,3,3,128,128]{5,4,3,2,1,0:T(8,128)(2,1)} %kernels.1) | copy-start | bytes 5308420
  4.5 20.0 %collective-permute-start.4 = (bf16[3,1024,128]{2,1,0:T(8,128)(2,1)S(1)}, bf16[3,1024,128]{2,1,0:T(8,128)(2,1)S(1)}, u32[]{:S(2)}, u32[]{:S(2)}) collective-permute-start(bf16[3,1024,128]{2,1,0:T(8,128)(2,1)S(1)} %shard_map.92.after), channel_id=1, source_target_pairs={{1,2},{2,1},{5,6},{6,5},{9,10},{10,9},{13,14},{14,13},{17,18},{18,... | collective-permute-start | bytes 2359304 | tf_op jit(solution)/shard_map/ppermute | solution.py:544
  5.4 4.1 %collective-permute-start.1 = (bf16[4,16,128]{2,1,0:T(8,128)(2,1)S(1)}, bf16[4,16,128]{2,1,0:T(8,128)(2,1)S(1)}, u32[]{:S(2)}, u32[]{:S(2)}) collective-permute-start(bf16[4,16,128]{2,1,0:T(8,128)(2,1)S(1)} %get-tuple-element.41), channel_id=1, source_target_pairs={{0,4},{4,8},{8,12},{12,16},{16,20},{20,24},{24,28},{28,0},{1,5},{5... | collective-permute-start | bytes 49160 | tf_op jit(solution)/shard_map/ppermute | solution.py:598
  5.5 4.1 %collective-permute-start.2 = (bf16[4,16,128]{2,1,0:T(8,128)(2,1)S(1)}, bf16[4,16,128]{2,1,0:T(8,128)(2,1)S(1)}, u32[]{:S(2)}, u32[]{:S(2)}) collective-permute-start(bf16[4,16,128]{2,1,0:T(8,128)(2,1)S(1)} %get-tuple-element.42), channel_id=1, source_target_pairs={{4,0},{8,4},{12,8},{16,12},{20,16},{24,20},{28,24},{0,28},{5,1},{9... | collective-permute-start | bytes 49160 | tf_op jit(solution)/shard_map/ppermute | solution.py:599
  9.6 12.9 %collective-permute-start.3 = (bf16[3,32,128]{2,1,0:T(8,128)(2,1)S(1)}, bf16[3,32,128]{2,1,0:T(8,128)(2,1)S(1)}, u32[]{:S(2)}, u32[]{:S(2)}) collective-permute-start(bf16[3,32,128]{2,1,0:T(8,128)(2,1)S(1)} %get-tuple-element.43.near), channel_id=1, source_target_pairs={{0,1},{2,3},{1,0},{3,2},{4,5},{6,7},{5,4},{7,6},{8,9},{10,11},{9,8... | collective-permute-start | bytes 73736 | tf_op jit(solution)/shard_map/ppermute | solution.py:544
  14.1 10.4 %collective-permute-start.5 = (bf16[3,32,128]{2,1,0:T(8,128)(2,1)S(1)}, bf16[3,32,128]{2,1,0:T(8,128)(2,1)S(1)}, u32[]{:S(2)}, u32[]{:S(2)}) collective-permute-start(bf16[3,32,128]{2,1,0:T(8,128)(2,1)S(1)} %shard_map.95.after), channel_id=1, source_target_pairs={{1,2},{2,1},{5,6},{6,5},{9,10},{10,9},{13,14},{14,13},{17,18},{18,... | collective-permute-start | bytes 73736 | tf_op jit(solution)/shard_map/ppermute | solution.py:544
  22.5 2.0 %copy-start.2 = (bf16[2,256,1056]{2,1,0:T(8,128)(2,1)S(1)}, bf16[2,256,1056]{2,1,0:T(8,128)(2,1)}, u32[]{:S(2)}) copy-start(bf16[2,256,1056]{2,1,0:T(8,128)(2,1)} %constant.10.clone.forward) | copy-start | bytes 3244036
  24.5 15.6 %copy-start.3 = (bf16[2,16,128,128]{3,2,1,0:T(8,128)(2,1)S(1)}, bf16[2,16,128,128]{3,2,1,0:T(8,128)(2,1)}, u32[]{:S(2)}) copy-start(bf16[2,16,128,128]{3,2,1,0:T(8,128)(2,1)} %real.3) | copy-start | bytes 3145732
  24.6 15.6 %copy-start.4 = (bf16[2,16,128,128]{3,2,1,0:T(8,128)(2,1)S(1)}, bf16[2,16,128,128]{3,2,1,0:T(8,128)(2,1)}, u32[]{:S(2)}) copy-start(bf16[2,16,128,128]{3,2,1,0:T(8,128)(2,1)} %imag.3) | copy-start | bytes 3145732
  24.6 15.6 %copy-start.6 = (bf16[8,64,128]{2,1,0:T(8,128)(2,1)S(1)}, bf16[8,64,128]{2,1,0:T(8,128)(2,1)}, u32[]{:S(2)}) copy-start(bf16[8,64,128]{2,1,0:T(8,128)(2,1)} %constant.11.clone.turn) | copy-start | bytes 393220
  28.8 3.9 %collective-permute-start.7 = (f32[128,512]{1,0:T(8,128)S(1)}, f32[128,512]{1,0:T(8,128)S(1)}, u32[]{:S(2)}, u32[]{:S(2)}) collective-permute-start(f32[128,512]{1,0:T(8,128)S(1)} %get-tuple-element.54), channel_id=1, source_target_pairs={{0,4},{4,0},{8,12},{12,8},{16,20},{20,16},{24,28},{28,24},{1,5},{5... | collective-permute-start | bytes 786440 | tf_op jit(solution)/shard_map/ppermute | solution.py:656
  28.9 31.6 %collective-permute-start.6 = (bf16[3,528,256]{2,1,0:T(8,128)(2,1)S(1)}, bf16[3,528,256]{2,1,0:T(8,128)(2,1)S(1)}, u32[]{:S(2)}, u32[]{:S(2)}) collective-permute-start(bf16[3,528,256]{2,1,0:T(8,128)(2,1)S(1)} %get-tuple-element.52), channel_id=1, source_target_pairs={{0,1},{2,3},{1,0},{3,2},{4,5},{6,7},{5,4},{7,6},{8,9},{10,11},{9,8... | collective-permute-start | bytes 2433032 | tf_op jit(solution)/shard_map/ppermute | solution.py:544
  32.0 30.7 %collective-permute-start.13 = (bf16[3,528,256]{2,1,0:T(8,128)(2,1)S(1)}, bf16[3,528,256]{2,1,0:T(8,128)(2,1)S(1)}, u32[]{:S(2)}, u32[]{:S(2)}) collective-permute-start(bf16[3,528,256]{2,1,0:T(8,128)(2,1)S(1)} %get-tuple-element.67), channel_id=1, source_target_pairs={{1,2},{2,1},{5,6},{6,5},{9,10},{10,9},{13,14},{14,13},{17,18},{18,... | collective-permute-start | bytes 2433032 | tf_op jit(solution)/shard_map/ppermute | solution.py:544
  32.8 5.6 %collective-permute-start.10 = (f32[32,512]{1,0:T(8,128)S(1)}, f32[32,512]{1,0:T(8,128)S(1)}, u32[]{:S(2)}, u32[]{:S(2)}) collective-permute-start(f32[32,512]{1,0:T(8,128)S(1)} %get-tuple-element.58), channel_id=1, source_target_pairs={{0,24},{4,28},{8,16},{12,20},{16,8},{20,12},{24,0},{28,4},{1,25},{... | collective-permute-start | bytes 196616 | tf_op jit(solution)/shard_map/ppermute | solution.py:656
  35.3 4.3 %collective-permute-start.8 = (f32[32,512]{1,0:T(8,128)S(1)}, f32[32,512]{1,0:T(8,128)S(1)}, u32[]{:S(2)}, u32[]{:S(2)}) collective-permute-start(f32[32,512]{1,0:T(8,128)S(1)} %get-tuple-element.56), channel_id=1, source_target_pairs={{0,8},{4,12},{8,0},{12,4},{16,24},{20,28},{24,16},{28,20},{1,9},{5... | collective-permute-start | bytes 196616 | tf_op jit(solution)/shard_map/ppermute | solution.py:656
  35.8 4.3 %collective-permute-start.9 = (f32[32,512]{1,0:T(8,128)S(1)}, f32[32,512]{1,0:T(8,128)S(1)}, u32[]{:S(2)}, u32[]{:S(2)}) collective-permute-start(f32[32,512]{1,0:T(8,128)S(1)} %get-tuple-element.57), channel_id=1, source_target_pairs={{0,16},{4,20},{8,24},{12,28},{16,0},{20,4},{24,8},{28,12},{1,17},{... | collective-permute-start | bytes 196616 | tf_op jit(solution)/shard_map/ppermute | solution.py:656
  50.4 8.6 %collective-permute-start.11 = (bf16[256,384]{1,0:T(8,128)(2,1)S(1)}, bf16[256,384]{1,0:T(8,128)(2,1)S(1)}, u32[]{:S(2)}, u32[]{:S(2)}) collective-permute-start(bf16[256,384]{1,0:T(8,128)(2,1)S(1)} %shard_map.102), channel_id=1, source_target_pairs={{0,1},{2,3},{1,0},{3,2},{5,6},{6,5},{8,9},{10,11},{9,8},{11,10},{1... | collective-permute-start | bytes 589832 | tf_op jit(solution)/shard_map/ppermute | solution.py:685
  59.0 1.4 %collective-permute-start.12 = (bf16[256,384]{1,0:T(8,128)(2,1)S(1)}, bf16[256,384]{1,0:T(8,128)(2,1)S(1)}, u32[]{:S(2)}, u32[]{:S(2)}) collective-permute-start(bf16[256,384]{1,0:T(8,128)(2,1)S(1)} %collective-permute-done.11.mine), channel_id=1, source_target_pairs={{0,4},{4,0},{8,12},{12,8},{16,20},{20,16},{24,28},{28,24},{1,5},{5... | collective-permute-start | bytes 589832 | tf_op jit(solution)/shard_map/ppermute | solution.py:656
  67.4 1.6 %collective-permute-start.14 = (f32[128,512]{1,0:T(8,128)S(1)}, f32[128,512]{1,0:T(8,128)S(1)}, u32[]{:S(2)}, u32[]{:S(2)}) collective-permute-start(f32[128,512]{1,0:T(8,128)S(1)} %get-tuple-element.72), channel_id=1, source_target_pairs={{0,4},{4,0},{8,12},{12,8},{16,20},{20,16},{24,28},{28,24},{1,5},{5... | collective-permute-start | bytes 786440 | tf_op jit(solution)/shard_map/ppermute | solution.py:656
  69.1 4.3 %collective-permute-start.15 = (f32[32,512]{1,0:T(8,128)S(1)}, f32[32,512]{1,0:T(8,128)S(1)}, u32[]{:S(2)}, u32[]{:S(2)}) collective-permute-start(f32[32,512]{1,0:T(8,128)S(1)} %get-tuple-element.74), channel_id=1, source_target_pairs={{0,8},{4,12},{8,0},{12,4},{16,24},{20,28},{24,16},{28,20},{1,9},{5... | collective-permute-start | bytes 196616 | tf_op jit(solution)/shard_map/ppermute | solution.py:656
  69.8 4.3 %collective-permute-start.16 = (f32[32,512]{1,0:T(8,128)S(1)}, f32[32,512]{1,0:T(8,128)S(1)}, u32[]{:S(2)}, u32[]{:S(2)}) collective-permute-start(f32[32,512]{1,0:T(8,128)S(1)} %get-tuple-element.75), channel_id=1, source_target_pairs={{0,16},{4,20},{8,24},{12,28},{16,0},{20,4},{24,8},{28,12},{1,17},{... | collective-permute-start | bytes 196616 | tf_op jit(solution)/shard_map/ppermute | solution.py:656
  71.2 5.2 %collective-permute-start.17 = (f32[32,512]{1,0:T(8,128)S(1)}, f32[32,512]{1,0:T(8,128)S(1)}, u32[]{:S(2)}, u32[]{:S(2)}) collective-permute-start(f32[32,512]{1,0:T(8,128)S(1)} %get-tuple-element.76), channel_id=1, source_target_pairs={{0,24},{4,28},{8,16},{12,20},{16,8},{20,12},{24,0},{28,4},{1,25},{... | collective-permute-start | bytes 196616 | tf_op jit(solution)/shard_map/ppermute | solution.py:656

commit v8 on v6

--- a/solution.py
+++ b/solution.py
@@ -681,7 +681,7 @@
         (low[0], hidden, mixed, inverse, later, conv_bias[1]),
         [own_rows] + early,
         [],
-        cost=3,
+        cost=12,
     )
     other = swap(lax.optimization_barrier((mine, own))[0], 1)
     state, *low = call(

time: 87.3 us -> 86.1 us (0.986)
  waiting for transfers between devices: 19.2 us -> 17.3 us
    ppermute x9, waiting for transfers between devices: 11.1 us -> 8.7 us  [swap(): return lax.ppermute(array, 'lon', [(i, i ^ step) for i in range(lon_size)])]
  transfers between devices with their start and end apart: 18 -> 18, of which waited for: 12 -> 9; matrix products, arithmetic and copies ran while one was open for 0% -> 0% of each run, Pallas kernels for 11% -> 11%
where the time goes in v8:
time: 86.1 us; the launch traced here: 85.1 us
  starting transfers between devices  28.1 us (33%)
  Pallas kernels  20.2 us (23%)
  blocking collectives  17.7 us (21%)
  waiting for transfers between devices  17.3 us (20%)
  local copies, waits for them, and re-layouts  1.29 us (1%)
    pallas_call x18, Pallas kernels, call(): pl.pallas_call(kernel, grid=grid, out_shape=outs, in_specs=in_specs or [V...  20.2 us
    all_gather x2, blocking collectives, mix(): return lax.all_gather(mixed, 'lon', axis=0, tiled=True)  17.7 us
    ppermute x6, starting transfers between devices, move(): return lax.ppermute(array, 'lat', lat_pairs(partner))  12.9 us
    ppermute x9, waiting for transfers between devices, swap(): return lax.ppermute(array, 'lon', [(i, i ^ step) for i in range(lon_size)])  8.7 us
    ppermute x9, starting transfers between devices, swap(): return lax.ppermute(array, 'lon', [(i, i ^ step) for i in range(lon_size)])  7.39 us
    ppermute x1, starting transfers between devices, per_device(): mine = lax.ppermute(halo, ('lon', 'lat'), ways)  5.1 us
    ppermute x6, waiting for transfers between devices, move(): return lax.ppermute(array, 'lat', lat_pairs(partner))  5 us
    ppermute x1, starting transfers between devices, per_device(): from_right = lax.ppermute(leading, 'lon', left)  2.63 us
  transfers between devices with their start and end apart: 18, of which 9 were waited for; matrix products, arithmetic and copies ran while one was open for 0% of the time, Pallas kernels for 11%

profile of v8, /device:TPU:0, one launch (start us, length us, event | category | flops | bytes accessed | tf_op | source)
XLA Modules:
  0.0 85.1 jit_solution(13908186190984389883)
XLA Ops:
  0.0 1.2 %copy-done = bf16[4,1024,128]{2,1,0:T(8,128)(2,1)S(1)} copy-done((bf16[4,1024,128]{2,1,0:T(8,128)(2,1)S(1)}, bf16[4,1024,128]{2,1,0:T(8,128)(2,1)}, u32[]{:S(2)}) %copy-start) | copy-done | bytes 1048600
  1.2 0.1 shard_map.100.rest_0_
  1.3 0.0 copy-start.5
  1.3 0.0 copy-start.8
  1.3 3.1 %collective-permute-start = (bf16[3,1024,128]{2,1,0:T(8,128)(2,1)S(1)}, bf16[3,1024,128]{2,1,0:T(8,128)(2,1)S(1)}, u32[]{:S(2)}, u32[]{:S(2)}) collective-permute-start(bf16[3,1024,128]{2,1,0:T(8,128)(2,1)S(1)} %shard_map.100.rest_0_), channel_id=1, source_target_pairs={{0,1},{2,3},{1,0},{3,2},{4,5},{6,7},{5,4},{7,6},{8,9},{10,11},{9,8... | collective-permute-start | bytes 2359304 | tf_op jit(solution)/shard_map/ppermute | solution.py:537
  4.4 0.1 shard_map.101.after
  4.5 0.0 copy-start.1
  4.5 0.8 collective-permute-start.4
  5.4 0.1 collective-permute-start.1
  5.5 2.6 %collective-permute-start.2 = (bf16[4,16,128]{2,1,0:T(8,128)(2,1)S(1)}, bf16[4,16,128]{2,1,0:T(8,128)(2,1)S(1)}, u32[]{:S(2)}, u32[]{:S(2)}) collective-permute-start(bf16[4,16,128]{2,1,0:T(8,128)(2,1)S(1)} %get-tuple-element.42), channel_id=1, source_target_pairs={{4,0},{8,4},{12,8},{16,12},{20,16},{24,20},{28,24},{0,28},{5,1},{9... | collective-permute-start | bytes 49160 | tf_op jit(solution)/shard_map/ppermute | solution.py:592
  8.1 1.4 %collective-permute-done.1.from_left = bf16[4,16,128]{2,1,0:T(8,128)(2,1)S(1)} collective-permute-done((bf16[4,16,128]{2,1,0:T(8,128)(2,1)S(1)}, bf16[4,16,128]{2,1,0:T(8,128)(2,1)S(1)}, u32[]{:S(2)}, u32[]{:S(2)}) %collective-permute-start.1) | collective-permute-done | bytes 16416 | tf_op jit(solution)/shard_map/ppermute | solution.py:591
  9.5 0.0 collective-permute-done.2.from_right
  9.6 4.5 %collective-permute-start.3 = (bf16[3,32,128]{2,1,0:T(8,128)(2,1)S(1)}, bf16[3,32,128]{2,1,0:T(8,128)(2,1)S(1)}, u32[]{:S(2)}, u32[]{:S(2)}) collective-permute-start(bf16[3,32,128]{2,1,0:T(8,128)(2,1)S(1)} %get-tuple-element.43.near), channel_id=1, source_target_pairs={{0,1},{2,3},{1,0},{3,2},{4,5},{6,7},{5,4},{7,6},{8,9},{10,11},{9,8... | collective-permute-start | bytes 73736 | tf_op jit(solution)/shard_map/ppermute | solution.py:537
  14.1 0.7 collective-permute-start.5
  14.8 0.1 shard_map.105.after.inverse
  15.0 2.5 %shard_map.106 = (bf16[4,560,256]{2,1,0:T(8,128)(2,1)S(1)}, bf16[3,4,512,256]{3,2,1,0:T(8,128)(2,1)S(1)}, bf16[3,4,512,256]{3,2,1,0:T(8,128)(2,1)S(1)}, bf16[2,5...) custom-call(bf16[4,1024,128]{2,1,0:T(8,128)(2,1)S(1)} %copy-done.1, bf16[4,32,128]{2,1,0:T(8,128)(2,1)S(1)} %get-tuple-element.44.edges.own_edge, ...), custom_call_target="tpu_custom_call" | custom-call | flops 3200000000 | tf_op jit(solution)/shard_map/pallas_call | solution.py:546
  17.5 5.0 %collective-permute-done.3.down_edge = bf16[3,32,128]{2,1,0:T(8,128)(2,1)S(1)} collective-permute-done((bf16[3,32,128]{2,1,0:T(8,128)(2,1)S(1)}, bf16[3,32,128]{2,1,0:T(8,128)(2,1)S(1)}, u32[]{:S(2)}, u32[]{:S(2)}) %collective-permute-start.3) | collective-permute-done | bytes 24608 | tf_op jit(solution)/shard_map/ppermute | solution.py:537
  22.5 2.0 %shard_map.107 = (bf16[7,560,256]{2,1,0:T(8,128)(2,1)S(1)}, bf16[3,560,256]{2,1,0:T(8,128)(2,1)S(1)}, bf16[2,560,256]{2,1,0:T(8,128)(2,1)S(1)}) custom-call(bf16[3,1024,128]{2,1,0:T(8,128)(2,1)S(1)} %collective-permute-done.down, bf16[3,32,128]{2,1,0:T(8,128)(2,1)S(1)} %collective-permute-done.3.down_edge, bf16[4,560,256]{2,1,0:T(8,128)(2,1)S(1)} %get-tuple-element.45.own, ...), custom_call_target="tpu_custom_call" | custom-call | tf_op jit(solution)/shard_map/pallas_call | solution.py:546
  24.6 0.0 copy-start.3
  24.6 0.0 copy-start.4
  24.6 0.0 copy-start.7
  24.6 4.2 %shard_map.108 = (f32[128,512]{1,0:T(8,128)S(1)}, f32[128,512]{1,0:T(8,128)S(1)}, bf16[4,528,256]{2,1,0:T(8,128)(2,1)S(1)}, bf16[3,528,256]{2,1,0:T(8,128)(2,1)S...) custom-call(bf16[3,1024,128]{2,1,0:T(8,128)(2,1)S(1)} %collective-permute-done.4.up, ...), custom_call_target="tpu_custom_call" | custom-call | tf_op jit(solution)/shard_map/pallas_call | solution.py:546
  28.8 0.1 collective-permute-start.7
  28.9 1.5 %collective-permute-done.7.got = f32[128,512]{1,0:T(8,128)S(1)} collective-permute-done((f32[128,512]{1,0:T(8,128)S(1)}, f32[128,512]{1,0:T(8,128)S(1)}, u32[]{:S(2)}, u32[]{:S(2)}) %collective-permute-start.7) | collective-permute-done | bytes 262176 | tf_op jit(solution)/shard_map/ppermute | solution.py:649
  30.5 2.7 %collective-permute-start.10 = (bf16[32,512]{1,0:T(8,128)(2,1)S(1)}, bf16[32,512]{1,0:T(8,128)(2,1)S(1)}, u32[]{:S(2)}, u32[]{:S(2)}) collective-permute-start(bf16[32,512]{1,0:T(8,128)(2,1)S(1)} %get-tuple-element.58), channel_id=1, source_target_pairs={{0,24},{4,28},{8,16},{12,20},{16,8},{20,12},{24,0},{28,4},{1,25},{... | collective-permute-start | bytes 98312 | tf_op jit(solution)/shard_map/ppermute | solution.py:649
  33.2 0.5 collective-permute-start.8
  33.7 0.3 collective-permute-start.9
  34.0 3.1 %collective-permute-start.6 = (bf16[3,528,256]{2,1,0:T(8,128)(2,1)S(1)}, bf16[3,528,256]{2,1,0:T(8,128)(2,1)S(1)}, u32[]{:S(2)}, u32[]{:S(2)}) collective-permute-start(bf16[3,528,256]{2,1,0:T(8,128)(2,1)S(1)} %get-tuple-element.52), channel_id=1, source_target_pairs={{0,1},{2,3},{1,0},{3,2},{4,5},{6,7},{5,4},{7,6},{8,9},{10,11},{9,8... | collective-permute-start | bytes 2433032 | tf_op jit(solution)/shard_map/ppermute | solution.py:537
  37.1 0.7 collective-permute-start.13
  37.9 0.4 shard_map.110
  38.3 9.3 %all_gather.6.mixed = bf16[256,512]{1,0:T(8,128)(2,1)S(1)} all-gather(bf16[32,512]{1,0:T(8,128)(2,1)S(1)} %shard_map.110), channel_id=1, replica_groups=mesh['lon'=8,'lat'=4] {'lon'}, dimensions={0}, use_global_device_ids=true | all-gather | bytes 294912 | tf_op jit(solution)/shard_map/all_gather | solution.py:668
  47.7 5.1 %collective-permute-start.11 = (bf16[256,384]{1,0:T(8,128)(2,1)S(1)}, bf16[256,384]{1,0:T(8,128)(2,1)S(1)}, u32[]{:S(2)}, u32[]{:S(2)}) collective-permute-start(bf16[256,384]{1,0:T(8,128)(2,1)S(1)} %shard_map.111), channel_id=1, source_target_pairs={{0,1},{2,3},{1,0},{3,2},{5,6},{6,5},{8,9},{10,11},{9,8},{11,10},{1... | collective-permute-start | bytes 589832 | tf_op jit(solution)/shard_map/ppermute | solution.py:678
  52.8 1.8 %shard_map.112 = (bf16[4,560,256]{2,1,0:T(8,128)(2,1)S(1)}, bf16[2,560,256]{2,1,0:T(8,128)(2,1)S(1)}, f32[4,528,256]{2,1,0:T(8,128)S(1)}) custom-call(bf16[7,560,256]{2,1,0:T(8,128)(2,1)S(1)} %get-tuple-element.49.field, bf16[4,528,256]{2,1,0:T(8,128)(2,1)S(1)} %get-tuple-element.59.hidden, bf16[256,512]{1,0:T(8,128)(2,1)S(1)} %all_gather.6.mixed, ...), custom_call_target="tpu_custom_call" | custom-call | flops 9600000000 | tf_op jit(solution)/shard_map/pallas_call | solution.py:546
  54.5 2.2 %collective-permute-done.11.mine = bf16[256,384]{1,0:T(8,128)(2,1)S(1)} collective-permute-done((bf16[256,384]{1,0:T(8,128)(2,1)S(1)}, bf16[256,384]{1,0:T(8,128)(2,1)S(1)}, u32[]{:S(2)}, u32[]{:S(2)}) %collective-permute-start.11) | collective-permute-done | bytes 196640 | tf_op jit(solution)/shard_map/ppermute | solution.py:678
  56.7 1.4 %collective-permute-done.12.other = bf16[256,384]{1,0:T(8,128)(2,1)S(1)} collective-permute-done((bf16[256,384]{1,0:T(8,128)(2,1)S(1)}, bf16[256,384]{1,0:T(8,128)(2,1)S(1)}, u32[]{:S(2)}, u32[]{:S(2)}) %collective-permute-start.12) | collective-permute-done | bytes 196640 | tf_op jit(solution)/shard_map/ppermute | solution.py:649
  58.2 2.2 %shard_map.113 = (bf16[7,560,256]{2,1,0:T(8,128)(2,1)S(1)}, bf16[3,560,256]{2,1,0:T(8,128)(2,1)S(1)}, bf16[2,560,256]{2,1,0:T(8,128)(2,1)S(1)}) custom-call(bf16[7,560,256]{2,1,0:T(8,128)(2,1)S(1)} %get-tuple-element.49.field, bf16[3,528,256]{2,1,0:T(8,128)(2,1)S(1)} %collective-permute-done.6.from_down, bf16[256,384]{1,0:T(8,128)(2,1)S(1)} %collective-permute-done.11.mine, ...), custom_call_target="tpu_custom_call" | custom-call | tf_op jit(solution)/shard_map/pallas_call | solution.py:546
  60.4 4.7 %shard_map.114 = (f32[128,512]{1,0:T(8,128)S(1)}, f32[128,512]{1,0:T(8,128)S(1)}, bf16[4,528,256]{2,1,0:T(8,128)(2,1)S(1)}) custom-call(bf16[3,560,256]{2,1,0:T(8,128)(2,1)S(1)} %get-tuple-element.66.before, bf16[3,528,256]{2,1,0:T(8,128)(2,1)S(1)} %collective-permute-done.13.from_up, bf16[256,384]{1,0:T(8,128)(2,1)S(1)} %collective-permute-done.11.mine, ...), custom_call_target="tpu_custom_call" | custom-call | tf_op jit(solution)/shard_map/pallas_call | solution.py:546
  65.1 0.2 collective-permute-start.14
  65.3 1.4 %collective-permute-done.14.got = f32[128,512]{1,0:T(8,128)S(1)} collective-permute-done((f32[128,512]{1,0:T(8,128)S(1)}, f32[128,512]{1,0:T(8,128)S(1)}, u32[]{:S(2)}, u32[]{:S(2)}) %collective-permute-start.14) | collective-permute-done | bytes 262176 | tf_op jit(solution)/shard_map/ppermute | solution.py:649
  66.8 1.6 %collective-permute-start.15 = (bf16[32,512]{1,0:T(8,128)(2,1)S(1)}, bf16[32,512]{1,0:T(8,128)(2,1)S(1)}, u32[]{:S(2)}, u32[]{:S(2)}) collective-permute-start(bf16[32,512]{1,0:T(8,128)(2,1)S(1)} %get-tuple-element.74), channel_id=1, source_target_pairs={{0,8},{4,12},{8,0},{12,4},{16,24},{20,28},{24,16},{28,20},{1,9},{5... | collective-permute-start | bytes 98312 | tf_op jit(solution)/shard_map/ppermute | solution.py:649
  68.3 1.5 %collective-permute-start.16 = (bf16[32,512]{1,0:T(8,128)(2,1)S(1)}, bf16[32,512]{1,0:T(8,128)(2,1)S(1)}, u32[]{:S(2)}, u32[]{:S(2)}) collective-permute-start(bf16[32,512]{1,0:T(8,128)(2,1)S(1)} %get-tuple-element.75), channel_id=1, source_target_pairs={{0,16},{4,20},{8,24},{12,28},{16,0},{20,4},{24,8},{28,12},{1,17},{... | collective-permute-start | bytes 98312 | tf_op jit(solution)/shard_map/ppermute | solution.py:649
  69.8 0.5 collective-permute-start.17
  70.3 0.4 collective-permute-done.15.rest_1_
  70.7 1.5 %collective-permute-done.16.rest_2_ = bf16[32,512]{1,0:T(8,128)(2,1)S(1)} collective-permute-done((bf16[32,512]{1,0:T(8,128)(2,1)S(1)}, bf16[32,512]{1,0:T(8,128)(2,1)S(1)}, u32[]{:S(2)}, u32[]{:S(2)}) %collective-permute-start.16) | collective-permute-done | bytes 32800 | tf_op jit(solution)/shard_map/ppermute | solution.py:649
  72.2 2.4 %collective-permute-done.17.rest_3_ = bf16[32,512]{1,0:T(8,128)(2,1)S(1)} collective-permute-done((bf16[32,512]{1,0:T(8,128)(2,1)S(1)}, bf16[32,512]{1,0:T(8,128)(2,1)S(1)}, u32[]{:S(2)}, u32[]{:S(2)}) %collective-permute-start.17) | collective-permute-done | bytes 32800 | tf_op jit(solution)/shard_map/ppermute | solution.py:649
  74.6 0.4 shard_map.116
  75.1 8.3 %all_gather.7.mixed = bf16[256,512]{1,0:T(8,128)(2,1)S(1)} all-gather(bf16[32,512]{1,0:T(8,128)(2,1)S(1)} %shard_map.116), channel_id=1, replica_groups=mesh['lon'=8,'lat'=4] {'lon'}, dimensions={0}, use_global_device_ids=true | all-gather | bytes 294912 | tf_op jit(solution)/shard_map/all_gather | solution.py:668
  83.4 1.5 %shard_map.117 = bf16[4,1024,128]{2,1,0:T(8,128)(2,1)} custom-call(bf16[7,560,256]{2,1,0:T(8,128)(2,1)S(1)} %get-tuple-element.65.state, bf16[4,528,256]{2,1,0:T(8,128)(2,1)S(1)} %get-tuple-element.70.hidden, bf16[256,512]{1,0:T(8,128)(2,1)S(1)} %all_gather.7.mixed, bf16[2,528,256]{2,1,0:T(8,128)(2,1)S(1)} %shard_map.105.after.inverse), custom_call_target="tpu_custom_call" | custom-call | tf_op jit(solution)/shard_map/pallas_call | solution.py:546
  (33 shorter events, 0.2 us)
Async XLA Ops:
  0.0 1.2 %copy-start = (bf16[4,1024,128]{2,1,0:T(8,128)(2,1)S(1)}, bf16[4,1024,128]{2,1,0:T(8,128)(2,1)}, u32[]{:S(2)}) copy-start(bf16[4,1024,128]{2,1,0:T(8,128)(2,1)} %own.1) | copy-start | bytes 3145732
  1.3 6.8 %copy-start.10 = (f32[2,3,128]{2,0,1:T(2,128)S(1)}, f32[2,3,128]{2,0,1:T(2,128)}, u32[]{:S(2)}) copy-start(f32[2,3,128]{2,0,1:T(2,128)} %param.12) | copy-start | bytes 9220
  1.3 13.5 %copy-start.5 = (f32[2,2,528,256]{3,2,1,0:T(8,128)S(1)}, f32[2,2,528,256]{3,2,1,0:T(8,128)}, u32[]{:S(2)}) copy-start(f32[2,2,528,256]{3,2,1,0:T(8,128)} %constant.10.clone.parts) | copy-start | bytes 6488068
  1.3 13.5 %copy-start.8 = (f32[8,2,256]{2,1,0:T(2,128)S(1)}, f32[8,2,256]{2,1,0:T(2,128)}, u32[]{:S(2)}) copy-start(f32[8,2,256]{2,1,0:T(2,128)} %constant.11.clone.phase) | copy-start | bytes 49156
  1.3 21.2 %collective-permute-start = (bf16[3,1024,128]{2,1,0:T(8,128)(2,1)S(1)}, bf16[3,1024,128]{2,1,0:T(8,128)(2,1)S(1)}, u32[]{:S(2)}, u32[]{:S(2)}) collective-permute-start(bf16[3,1024,128]{2,1,0:T(8,128)(2,1)S(1)} %shard_map.100.rest_0_), channel_id=1, source_target_pairs={{0,1},{2,3},{1,0},{3,2},{4,5},{6,7},{5,4},{7,6},{8,9},{10,11},{9,8... | collective-permute-start | bytes 2359304 | tf_op jit(solution)/shard_map/ppermute | solution.py:537
  4.5 10.4 %copy-start.1 = (bf16[4,1024,128]{2,1,0:T(8,128)(2,1)S(1)}, bf16[4,1024,128]{2,1,0:T(8,128)(2,1)}, u32[]{:S(2)}) copy-start(bf16[4,1024,128]{2,1,0:T(8,128)(2,1)} %own.1) | copy-start | bytes 3145732
  4.5 10.4 %copy-start.9 = (bf16[2,3,3,3,128,128]{5,4,3,2,1,0:T(8,128)(2,1)S(1)}, bf16[2,3,3,3,128,128]{5,4,3,2,1,0:T(8,128)(2,1)}, u32[]{:S(2)}) copy-start(bf16[2,3,3,3,128,128]{5,4,3,2,1,0:T(8,128)(2,1)} %kernels.1) | copy-start | bytes 5308420
  4.5 20.0 %collective-permute-start.4 = (bf16[3,1024,128]{2,1,0:T(8,128)(2,1)S(1)}, bf16[3,1024,128]{2,1,0:T(8,128)(2,1)S(1)}, u32[]{:S(2)}, u32[]{:S(2)}) collective-permute-start(bf16[3,1024,128]{2,1,0:T(8,128)(2,1)S(1)} %shard_map.101.after), channel_id=1, source_target_pairs={{1,2},{2,1},{5,6},{6,5},{9,10},{10,9},{13,14},{14,13},{17,18},{18,... | collective-permute-start | bytes 2359304 | tf_op jit(solution)/shard_map/ppermute | solution.py:537
  5.4 4.1 %collective-permute-start.1 = (bf16[4,16,128]{2,1,0:T(8,128)(2,1)S(1)}, bf16[4,16,128]{2,1,0:T(8,128)(2,1)S(1)}, u32[]{:S(2)}, u32[]{:S(2)}) collective-permute-start(bf16[4,16,128]{2,1,0:T(8,128)(2,1)S(1)} %get-tuple-element.41), channel_id=1, source_target_pairs={{0,4},{4,8},{8,12},{12,16},{16,20},{20,24},{24,28},{28,0},{1,5},{5... | collective-permute-start | bytes 49160 | tf_op jit(solution)/shard_map/ppermute | solution.py:591
  5.5 4.1 %collective-permute-start.2 = (bf16[4,16,128]{2,1,0:T(8,128)(2,1)S(1)}, bf16[4,16,128]{2,1,0:T(8,128)(2,1)S(1)}, u32[]{:S(2)}, u32[]{:S(2)}) collective-permute-start(bf16[4,16,128]{2,1,0:T(8,128)(2,1)S(1)} %get-tuple-element.42), channel_id=1, source_target_pairs={{4,0},{8,4},{12,8},{16,12},{20,16},{24,20},{28,24},{0,28},{5,1},{9... | collective-permute-start | bytes 49160 | tf_op jit(solution)/shard_map/ppermute | solution.py:592
  9.6 12.9 %collective-permute-start.3 = (bf16[3,32,128]{2,1,0:T(8,128)(2,1)S(1)}, bf16[3,32,128]{2,1,0:T(8,128)(2,1)S(1)}, u32[]{:S(2)}, u32[]{:S(2)}) collective-permute-start(bf16[3,32,128]{2,1,0:T(8,128)(2,1)S(1)} %get-tuple-element.43.near), channel_id=1, source_target_pairs={{0,1},{2,3},{1,0},{3,2},{4,5},{6,7},{5,4},{7,6},{8,9},{10,11},{9,8... | collective-permute-start | bytes 73736 | tf_op jit(solution)/shard_map/ppermute | solution.py:537
  14.1 10.4 %collective-permute-start.5 = (bf16[3,32,128]{2,1,0:T(8,128)(2,1)S(1)}, bf16[3,32,128]{2,1,0:T(8,128)(2,1)S(1)}, u32[]{:S(2)}, u32[]{:S(2)}) collective-permute-start(bf16[3,32,128]{2,1,0:T(8,128)(2,1)S(1)} %shard_map.104.after), channel_id=1, source_target_pairs={{1,2},{2,1},{5,6},{6,5},{9,10},{10,9},{13,14},{14,13},{17,18},{18,... | collective-permute-start | bytes 73736 | tf_op jit(solution)/shard_map/ppermute | solution.py:537
  22.5 2.0 %copy-start.2 = (bf16[2,256,1056]{2,1,0:T(8,128)(2,1)S(1)}, bf16[2,256,1056]{2,1,0:T(8,128)(2,1)}, u32[]{:S(2)}) copy-start(bf16[2,256,1056]{2,1,0:T(8,128)(2,1)} %constant.12.clone.forward) | copy-start | bytes 3244036
  22.5 2.1 %copy-start.6 = (f32[2,256,1]{2,1,0:T(8,128)S(1)}, f32[2,256,1]{2,1,0:T(8,128)}, u32[]{:S(2)}) copy-start(f32[2,256,1]{2,1,0:T(8,128)} %constant.13.clone.leak) | copy-start | bytes 6148
  24.6 13.3 %copy-start.3 = (bf16[2,16,128,128]{3,2,1,0:T(8,128)(2,1)S(1)}, bf16[2,16,128,128]{3,2,1,0:T(8,128)(2,1)}, u32[]{:S(2)}) copy-start(bf16[2,16,128,128]{3,2,1,0:T(8,128)(2,1)} %real.3) | copy-start | bytes 3145732
  24.6 13.3 %copy-start.4 = (bf16[2,16,128,128]{3,2,1,0:T(8,128)(2,1)S(1)}, bf16[2,16,128,128]{3,2,1,0:T(8,128)(2,1)}, u32[]{:S(2)}) copy-start(bf16[2,16,128,128]{3,2,1,0:T(8,128)(2,1)} %imag.3) | copy-start | bytes 3145732
  24.6 13.3 %copy-start.7 = (bf16[8,64,128]{2,1,0:T(8,128)(2,1)S(1)}, bf16[8,64,128]{2,1,0:T(8,128)(2,1)}, u32[]{:S(2)}) copy-start(bf16[8,64,128]{2,1,0:T(8,128)(2,1)} %constant.14.clone.turn) | copy-start | bytes 393220
  28.8 1.6 %collective-permute-start.7 = (f32[128,512]{1,0:T(8,128)S(1)}, f32[128,512]{1,0:T(8,128)S(1)}, u32[]{:S(2)}, u32[]{:S(2)}) collective-permute-start(f32[128,512]{1,0:T(8,128)S(1)} %get-tuple-element.54), channel_id=1, source_target_pairs={{0,4},{4,0},{8,12},{12,8},{16,20},{20,16},{24,28},{28,24},{1,5},{5... | collective-permute-start | bytes 786440 | tf_op jit(solution)/shard_map/ppermute | solution.py:649
  30.5 7.3 %collective-permute-start.10 = (bf16[32,512]{1,0:T(8,128)(2,1)S(1)}, bf16[32,512]{1,0:T(8,128)(2,1)S(1)}, u32[]{:S(2)}, u32[]{:S(2)}) collective-permute-start(bf16[32,512]{1,0:T(8,128)(2,1)S(1)} %get-tuple-element.58), channel_id=1, source_target_pairs={{0,24},{4,28},{8,16},{12,20},{16,8},{20,12},{24,0},{28,4},{1,25},{... | collective-permute-start | bytes 98312 | tf_op jit(solution)/shard_map/ppermute | solution.py:649
  33.2 4.7 %collective-permute-start.8 = (bf16[32,512]{1,0:T(8,128)(2,1)S(1)}, bf16[32,512]{1,0:T(8,128)(2,1)S(1)}, u32[]{:S(2)}, u32[]{:S(2)}) collective-permute-start(bf16[32,512]{1,0:T(8,128)(2,1)S(1)} %get-tuple-element.56), channel_id=1, source_target_pairs={{0,8},{4,12},{8,0},{12,4},{16,24},{20,28},{24,16},{28,20},{1,9},{5... | collective-permute-start | bytes 98312 | tf_op jit(solution)/shard_map/ppermute | solution.py:649
  33.7 4.2 %collective-permute-start.9 = (bf16[32,512]{1,0:T(8,128)(2,1)S(1)}, bf16[32,512]{1,0:T(8,128)(2,1)S(1)}, u32[]{:S(2)}, u32[]{:S(2)}) collective-permute-start(bf16[32,512]{1,0:T(8,128)(2,1)S(1)} %get-tuple-element.57), channel_id=1, source_target_pairs={{0,16},{4,20},{8,24},{12,28},{16,0},{20,4},{24,8},{28,12},{1,17},{... | collective-permute-start | bytes 98312 | tf_op jit(solution)/shard_map/ppermute | solution.py:649
  34.0 24.2 %collective-permute-start.6 = (bf16[3,528,256]{2,1,0:T(8,128)(2,1)S(1)}, bf16[3,528,256]{2,1,0:T(8,128)(2,1)S(1)}, u32[]{:S(2)}, u32[]{:S(2)}) collective-permute-start(bf16[3,528,256]{2,1,0:T(8,128)(2,1)S(1)} %get-tuple-element.52), channel_id=1, source_target_pairs={{0,1},{2,3},{1,0},{3,2},{4,5},{6,7},{5,4},{7,6},{8,9},{10,11},{9,8... | collective-permute-start | bytes 2433032 | tf_op jit(solution)/shard_map/ppermute | solution.py:537
  37.1 23.3 %collective-permute-start.13 = (bf16[3,528,256]{2,1,0:T(8,128)(2,1)S(1)}, bf16[3,528,256]{2,1,0:T(8,128)(2,1)S(1)}, u32[]{:S(2)}, u32[]{:S(2)}) collective-permute-start(bf16[3,528,256]{2,1,0:T(8,128)(2,1)S(1)} %get-tuple-element.67), channel_id=1, source_target_pairs={{1,2},{2,1},{5,6},{6,5},{9,10},{10,9},{13,14},{14,13},{17,18},{18,... | collective-permute-start | bytes 2433032 | tf_op jit(solution)/shard_map/ppermute | solution.py:537
  47.7 9.1 %collective-permute-start.11 = (bf16[256,384]{1,0:T(8,128)(2,1)S(1)}, bf16[256,384]{1,0:T(8,128)(2,1)S(1)}, u32[]{:S(2)}, u32[]{:S(2)}) collective-permute-start(bf16[256,384]{1,0:T(8,128)(2,1)S(1)} %shard_map.111), channel_id=1, source_target_pairs={{0,1},{2,3},{1,0},{3,2},{5,6},{6,5},{8,9},{10,11},{9,8},{11,10},{1... | collective-permute-start | bytes 589832 | tf_op jit(solution)/shard_map/ppermute | solution.py:678
  56.7 1.4 %collective-permute-start.12 = (bf16[256,384]{1,0:T(8,128)(2,1)S(1)}, bf16[256,384]{1,0:T(8,128)(2,1)S(1)}, u32[]{:S(2)}, u32[]{:S(2)}) collective-permute-start(bf16[256,384]{1,0:T(8,128)(2,1)S(1)} %collective-permute-done.11.mine), channel_id=1, source_target_pairs={{0,4},{4,0},{8,12},{12,8},{16,20},{20,16},{24,28},{28,24},{1,5},{5... | collective-permute-start | bytes 589832 | tf_op jit(solution)/shard_map/ppermute | solution.py:649
  65.1 1.6 %collective-permute-start.14 = (f32[128,512]{1,0:T(8,128)S(1)}, f32[128,512]{1,0:T(8,128)S(1)}, u32[]{:S(2)}, u32[]{:S(2)}) collective-permute-start(f32[128,512]{1,0:T(8,128)S(1)} %get-tuple-element.72), channel_id=1, source_target_pairs={{0,4},{4,0},{8,12},{12,8},{16,20},{20,16},{24,28},{28,24},{1,5},{5... | collective-permute-start | bytes 786440 | tf_op jit(solution)/shard_map/ppermute | solution.py:649
  66.8 4.0 %collective-permute-start.15 = (bf16[32,512]{1,0:T(8,128)(2,1)S(1)}, bf16[32,512]{1,0:T(8,128)(2,1)S(1)}, u32[]{:S(2)}, u32[]{:S(2)}) collective-permute-start(bf16[32,512]{1,0:T(8,128)(2,1)S(1)} %get-tuple-element.74), channel_id=1, source_target_pairs={{0,8},{4,12},{8,0},{12,4},{16,24},{20,28},{24,16},{28,20},{1,9},{5... | collective-permute-start | bytes 98312 | tf_op jit(solution)/shard_map/ppermute | solution.py:649
  68.3 3.9 %collective-permute-start.16 = (bf16[32,512]{1,0:T(8,128)(2,1)S(1)}, bf16[32,512]{1,0:T(8,128)(2,1)S(1)}, u32[]{:S(2)}, u32[]{:S(2)}) collective-permute-start(bf16[32,512]{1,0:T(8,128)(2,1)S(1)} %get-tuple-element.75), channel_id=1, source_target_pairs={{0,16},{4,20},{8,24},{12,28},{16,0},{20,4},{24,8},{28,12},{1,17},{... | collective-permute-start | bytes 98312 | tf_op jit(solution)/shard_map/ppermute | solution.py:649
  69.8 4.8 %collective-permute-start.17 = (bf16[32,512]{1,0:T(8,128)(2,1)S(1)}, bf16[32,512]{1,0:T(8,128)(2,1)S(1)}, u32[]{:S(2)}, u32[]{:S(2)}) collective-permute-start(bf16[32,512]{1,0:T(8,128)(2,1)S(1)} %get-tuple-element.76), channel_id=1, source_target_pairs={{0,24},{4,28},{8,16},{12,20},{16,8},{20,12},{24,0},{28,4},{1,25},{... | collective-permute-start | bytes 98312 | tf_op jit(solution)/shard_map/ppermute | solution.py:649

commit v9 on v7

--- a/solution.py
+++ b/solution.py
@@ -318,7 +318,7 @@
         spread_out[2 * rows * k : 2 * rows * (k + 1)] = out[:, :c] + sign * turned
     for row in range(rows):
         parts = [spread_out[pl.ds(i * rows + row, modes, stride=2 * rows), :] for i in range(2)]
-        mixed[:, row * c : (row + 1) * c] = jnp.concatenate(parts, axis=0)
+        mixed[:, row * c : (row + 1) * c] = jnp.concatenate(parts, axis=0).astype(mixed.dtype)
 
 
 def halo_kernel(mixed, out):
@@ -667,7 +667,7 @@
         (mixed,) = call(
             mix_kernel,
             (turn, spec_real, spec_imag, *sums),
-            [chunk],
+            [shape(2 * local, rows * c) if block == 0 else chunk],
             [turned, turned],
             in_specs=[VMEM, weights, weights] + [VMEM] * len(sums),
             grid=(1,),
@@ -688,7 +688,7 @@
         (low[0], hidden, mixed, inverse, later, conv_bias[1]),
         [own_rows] + early,
         [],
-        cost=3,
+        cost=12,
     )
     other = swap(lax.optimization_barrier((mine, own))[0], 1)
     state, *low = call(

time: 87.9 us -> 87.3 us (level)
    ppermute x9, waiting for transfers between devices: 10.3 us -> 9.15 us  [swap(): return lax.ppermute(array, 'lon', [(i, i ^ step) for i in range(lon_size)])]
  transfers between devices with their start and end apart: 18 -> 18, of which waited for: 11 -> 10; matrix products, arithmetic and copies ran while one was open for 0% -> 0% of each run, Pallas kernels for 11% -> 11%
where the time goes in v9:
time: 87.3 us; the launch traced here: 86.3 us
  starting transfers between devices  28 us (32%)
  Pallas kernels  20.6 us (24%)
  blocking collectives  18.2 us (21%)
  waiting for transfers between devices  17.7 us (20%)
  local copies, waits for them, and re-layouts  1.29 us (1%)
    pallas_call x18, Pallas kernels, call(): pl.pallas_call(kernel, grid=grid, out_shape=outs, in_specs=in_specs or [V...  20.6 us
    all_gather x2, blocking collectives, mix(): return lax.all_gather(mixed, 'lon', axis=0, tiled=True)  18.2 us
    ppermute x6, starting transfers between devices, move(): return lax.ppermute(array, 'lat', lat_pairs(partner))  12.9 us
    ppermute x9, waiting for transfers between devices, swap(): return lax.ppermute(array, 'lon', [(i, i ^ step) for i in range(lon_size)])  9.15 us
    ppermute x9, starting transfers between devices, swap(): return lax.ppermute(array, 'lon', [(i, i ^ step) for i in range(lon_size)])  7.39 us
    ppermute x1, starting transfers between devices, per_device(): mine = lax.ppermute(halo, ('lon', 'lat'), ways)  5.05 us
    ppermute x6, waiting for transfers between devices, move(): return lax.ppermute(array, 'lat', lat_pairs(partner))  5 us
    ppermute x1, starting transfers between devices, per_device(): from_right = lax.ppermute(leading, 'lon', left)  2.63 us
  transfers between devices with their start and end apart: 18, of which 10 were waited for; matrix products, arithmetic and copies ran while one was open for 0% of the time, Pallas kernels for 11%

profile of v9, /device:TPU:0, one launch (start us, length us, event | category | flops | bytes accessed | tf_op | source)
XLA Modules:
  0.0 86.3 jit_solution(11079675376497334083)
XLA Ops:
  0.0 1.2 %copy-done = bf16[4,1024,128]{2,1,0:T(8,128)(2,1)S(1)} copy-done((bf16[4,1024,128]{2,1,0:T(8,128)(2,1)S(1)}, bf16[4,1024,128]{2,1,0:T(8,128)(2,1)}, u32[]{:S(2)}) %copy-start) | copy-done | bytes 1048600
  1.2 0.1 shard_map.91.rest_0_
  1.3 0.0 copy-start.9
  1.3 0.0 copy-start.5
  1.3 0.0 copy-start.7
  1.3 3.1 %collective-permute-start = (bf16[3,1024,128]{2,1,0:T(8,128)(2,1)S(1)}, bf16[3,1024,128]{2,1,0:T(8,128)(2,1)S(1)}, u32[]{:S(2)}, u32[]{:S(2)}) collective-permute-start(bf16[3,1024,128]{2,1,0:T(8,128)(2,1)S(1)} %shard_map.91.rest_0_), channel_id=1, source_target_pairs={{0,1},{2,3},{1,0},{3,2},{4,5},{6,7},{5,4},{7,6},{8,9},{10,11},{9,8... | collective-permute-start | bytes 2359304 | tf_op jit(solution)/shard_map/ppermute | solution.py:544
  4.4 0.1 shard_map.92.after
  4.5 0.0 copy-start.8
  4.5 0.8 collective-permute-start.4
  5.4 0.1 collective-permute-start.1
  5.5 2.6 %collective-permute-start.2 = (bf16[4,16,128]{2,1,0:T(8,128)(2,1)S(1)}, bf16[4,16,128]{2,1,0:T(8,128)(2,1)S(1)}, u32[]{:S(2)}, u32[]{:S(2)}) collective-permute-start(bf16[4,16,128]{2,1,0:T(8,128)(2,1)S(1)} %get-tuple-element.42), channel_id=1, source_target_pairs={{4,0},{8,4},{12,8},{16,12},{20,16},{24,20},{28,24},{0,28},{5,1},{9... | collective-permute-start | bytes 49160 | tf_op jit(solution)/shard_map/ppermute | solution.py:599
  8.1 1.4 %collective-permute-done.1.from_left = bf16[4,16,128]{2,1,0:T(8,128)(2,1)S(1)} collective-permute-done((bf16[4,16,128]{2,1,0:T(8,128)(2,1)S(1)}, bf16[4,16,128]{2,1,0:T(8,128)(2,1)S(1)}, u32[]{:S(2)}, u32[]{:S(2)}) %collective-permute-start.1) | collective-permute-done | bytes 16416 | tf_op jit(solution)/shard_map/ppermute | solution.py:598
  9.5 0.0 collective-permute-done.2.from_right
  9.6 4.5 %collective-permute-start.3 = (bf16[3,32,128]{2,1,0:T(8,128)(2,1)S(1)}, bf16[3,32,128]{2,1,0:T(8,128)(2,1)S(1)}, u32[]{:S(2)}, u32[]{:S(2)}) collective-permute-start(bf16[3,32,128]{2,1,0:T(8,128)(2,1)S(1)} %get-tuple-element.43.near), channel_id=1, source_target_pairs={{0,1},{2,3},{1,0},{3,2},{4,5},{6,7},{5,4},{7,6},{8,9},{10,11},{9,8... | collective-permute-start | bytes 73736 | tf_op jit(solution)/shard_map/ppermute | solution.py:544
  14.1 0.7 collective-permute-start.5
  14.8 0.1 shard_map.96.after.inverse
  15.0 2.5 %shard_map.97 = (bf16[4,560,256]{2,1,0:T(8,128)(2,1)S(1)}, bf16[3,4,512,256]{3,2,1,0:T(8,128)(2,1)S(1)}, bf16[3,4,512,256]{3,2,1,0:T(8,128)(2,1)S(1)}, bf16[2,56...) custom-call(bf16[4,1024,128]{2,1,0:T(8,128)(2,1)S(1)} %copy-done.1, bf16[4,32,128]{2,1,0:T(8,128)(2,1)S(1)} %get-tuple-element.44.edges.own_edge, ...), custom_call_target="tpu_custom_call" | custom-call | flops 3200000000 | tf_op jit(solution)/shard_map/pallas_call | solution.py:553
  17.5 5.0 %collective-permute-done.3.down_edge = bf16[3,32,128]{2,1,0:T(8,128)(2,1)S(1)} collective-permute-done((bf16[3,32,128]{2,1,0:T(8,128)(2,1)S(1)}, bf16[3,32,128]{2,1,0:T(8,128)(2,1)S(1)}, u32[]{:S(2)}, u32[]{:S(2)}) %collective-permute-start.3) | collective-permute-done | bytes 24608 | tf_op jit(solution)/shard_map/ppermute | solution.py:544
  22.5 2.0 %shard_map.98 = (bf16[7,560,256]{2,1,0:T(8,128)(2,1)S(1)}, bf16[3,560,256]{2,1,0:T(8,128)(2,1)S(1)}, bf16[2,560,256]{2,1,0:T(8,128)(2,1)S(1)}) custom-call(bf16[3,1024,128]{2,1,0:T(8,128)(2,1)S(1)} %collective-permute-done.down, bf16[3,32,128]{2,1,0:T(8,128)(2,1)S(1)} %collective-permute-done.3.down_edge, bf16[4,560,256]{2,1,0:T(8,128)(2,1)S(1)} %get-tuple-element.45.own, ...), custom_call_target="tpu_custom_call" | custom-call | tf_op jit(solution)/shard_map/pallas_call | solution.py:553
  24.6 0.0 copy-start.6
  24.6 4.2 %shard_map.99 = (f32[128,512]{1,0:T(8,128)S(1)}, f32[128,512]{1,0:T(8,128)S(1)}, bf16[4,528,256]{2,1,0:T(8,128)(2,1)S(1)}, bf16[3,528,256]{2,1,0:T(8,128)(2,1)S(...) custom-call(bf16[3,1024,128]{2,1,0:T(8,128)(2,1)S(1)} %collective-permute-done.4.up, ...), custom_call_target="tpu_custom_call" | custom-call | tf_op jit(solution)/shard_map/pallas_call | solution.py:553
  28.8 0.1 collective-permute-start.7
  28.9 1.5 %collective-permute-done.7.got = f32[128,512]{1,0:T(8,128)S(1)} collective-permute-done((f32[128,512]{1,0:T(8,128)S(1)}, f32[128,512]{1,0:T(8,128)S(1)}, u32[]{:S(2)}, u32[]{:S(2)}) %collective-permute-start.7) | collective-permute-done | bytes 262176 | tf_op jit(solution)/shard_map/ppermute | solution.py:656
  30.5 2.7 %collective-permute-start.10 = (f32[32,512]{1,0:T(8,128)S(1)}, f32[32,512]{1,0:T(8,128)S(1)}, u32[]{:S(2)}, u32[]{:S(2)}) collective-permute-start(f32[32,512]{1,0:T(8,128)S(1)} %get-tuple-element.58), channel_id=1, source_target_pairs={{0,24},{4,28},{8,16},{12,20},{16,8},{20,12},{24,0},{28,4},{1,25},{... | collective-permute-start | bytes 196616 | tf_op jit(solution)/shard_map/ppermute | solution.py:656
  33.1 0.5 collective-permute-start.8
  33.7 0.3 collective-permute-start.9
  34.0 3.1 %collective-permute-start.6 = (bf16[3,528,256]{2,1,0:T(8,128)(2,1)S(1)}, bf16[3,528,256]{2,1,0:T(8,128)(2,1)S(1)}, u32[]{:S(2)}, u32[]{:S(2)}) collective-permute-start(bf16[3,528,256]{2,1,0:T(8,128)(2,1)S(1)} %get-tuple-element.52), channel_id=1, source_target_pairs={{0,1},{2,3},{1,0},{3,2},{4,5},{6,7},{5,4},{7,6},{8,9},{10,11},{9,8... | collective-permute-start | bytes 2433032 | tf_op jit(solution)/shard_map/ppermute | solution.py:544
  37.1 0.7 collective-permute-start.13
  37.8 0.1 collective-permute-done.9.rest_2_
  37.9 0.4 shard_map.101
  38.4 9.3 %all_gather.6.mixed = bf16[256,512]{1,0:T(8,128)(2,1)S(1)} all-gather(bf16[32,512]{1,0:T(8,128)(2,1)S(1)} %shard_map.101), channel_id=1, replica_groups=mesh['lon'=8,'lat'=4] {'lon'}, dimensions={0}, use_global_device_ids=true | all-gather | bytes 294912 | tf_op jit(solution)/shard_map/all_gather | solution.py:675
  47.7 5.0 %collective-permute-start.11 = (bf16[256,384]{1,0:T(8,128)(2,1)S(1)}, bf16[256,384]{1,0:T(8,128)(2,1)S(1)}, u32[]{:S(2)}, u32[]{:S(2)}) collective-permute-start(bf16[256,384]{1,0:T(8,128)(2,1)S(1)} %shard_map.102), channel_id=1, source_target_pairs={{0,1},{2,3},{1,0},{3,2},{5,6},{6,5},{8,9},{10,11},{9,8},{11,10},{1... | collective-permute-start | bytes 589832 | tf_op jit(solution)/shard_map/ppermute | solution.py:685
  52.8 1.8 %shard_map.103 = (bf16[4,560,256]{2,1,0:T(8,128)(2,1)S(1)}, bf16[2,560,256]{2,1,0:T(8,128)(2,1)S(1)}, f32[4,528,256]{2,1,0:T(8,128)S(1)}) custom-call(bf16[7,560,256]{2,1,0:T(8,128)(2,1)S(1)} %get-tuple-element.49.field, bf16[4,528,256]{2,1,0:T(8,128)(2,1)S(1)} %get-tuple-element.59.hidden, bf16[256,512]{1,0:T(8,128)(2,1)S(1)} %all_gather.6.mixed, ...), custom_call_target="tpu_custom_call" | custom-call | flops 9600000000 | tf_op jit(solution)/shard_map/pallas_call | solution.py:553
  54.6 2.1 %collective-permute-done.11.mine = bf16[256,384]{1,0:T(8,128)(2,1)S(1)} collective-permute-done((bf16[256,384]{1,0:T(8,128)(2,1)S(1)}, bf16[256,384]{1,0:T(8,128)(2,1)S(1)}, u32[]{:S(2)}, u32[]{:S(2)}) %collective-permute-start.11) | collective-permute-done | bytes 196640 | tf_op jit(solution)/shard_map/ppermute | solution.py:685
  56.7 1.4 %collective-permute-done.12.other = bf16[256,384]{1,0:T(8,128)(2,1)S(1)} collective-permute-done((bf16[256,384]{1,0:T(8,128)(2,1)S(1)}, bf16[256,384]{1,0:T(8,128)(2,1)S(1)}, u32[]{:S(2)}, u32[]{:S(2)}) %collective-permute-start.12) | collective-permute-done | bytes 196640 | tf_op jit(solution)/shard_map/ppermute | solution.py:656
  58.2 2.3 %shard_map.104 = (bf16[7,560,256]{2,1,0:T(8,128)(2,1)S(1)}, bf16[3,560,256]{2,1,0:T(8,128)(2,1)S(1)}, bf16[2,560,256]{2,1,0:T(8,128)(2,1)S(1)}) custom-call(bf16[7,560,256]{2,1,0:T(8,128)(2,1)S(1)} %get-tuple-element.49.field, bf16[3,528,256]{2,1,0:T(8,128)(2,1)S(1)} %collective-permute-done.6.from_down, bf16[256,384]{1,0:T(8,128)(2,1)S(1)} %collective-permute-done.11.mine, ...), custom_call_target="tpu_custom_call" | custom-call | tf_op jit(solution)/shard_map/pallas_call | solution.py:553
  60.5 4.7 %shard_map.105 = (f32[128,512]{1,0:T(8,128)S(1)}, f32[128,512]{1,0:T(8,128)S(1)}, bf16[4,528,256]{2,1,0:T(8,128)(2,1)S(1)}) custom-call(bf16[3,560,256]{2,1,0:T(8,128)(2,1)S(1)} %get-tuple-element.66.before, bf16[3,528,256]{2,1,0:T(8,128)(2,1)S(1)} %collective-permute-done.13.from_up, bf16[256,384]{1,0:T(8,128)(2,1)S(1)} %collective-permute-done.11.mine, ...), custom_call_target="tpu_custom_call" | custom-call | tf_op jit(solution)/shard_map/pallas_call | solution.py:553
  65.2 0.2 collective-permute-start.14
  65.4 1.4 %collective-permute-done.14.got = f32[128,512]{1,0:T(8,128)S(1)} collective-permute-done((f32[128,512]{1,0:T(8,128)S(1)}, f32[128,512]{1,0:T(8,128)S(1)}, u32[]{:S(2)}, u32[]{:S(2)}) %collective-permute-start.14) | collective-permute-done | bytes 262176 | tf_op jit(solution)/shard_map/ppermute | solution.py:656
  66.8 1.5 %collective-permute-start.15 = (f32[32,512]{1,0:T(8,128)S(1)}, f32[32,512]{1,0:T(8,128)S(1)}, u32[]{:S(2)}, u32[]{:S(2)}) collective-permute-start(f32[32,512]{1,0:T(8,128)S(1)} %get-tuple-element.74), channel_id=1, source_target_pairs={{0,8},{4,12},{8,0},{12,4},{16,24},{20,28},{24,16},{28,20},{1,9},{5... | collective-permute-start | bytes 196616 | tf_op jit(solution)/shard_map/ppermute | solution.py:656
  68.4 1.5 %collective-permute-start.16 = (f32[32,512]{1,0:T(8,128)S(1)}, f32[32,512]{1,0:T(8,128)S(1)}, u32[]{:S(2)}, u32[]{:S(2)}) collective-permute-start(f32[32,512]{1,0:T(8,128)S(1)} %get-tuple-element.75), channel_id=1, source_target_pairs={{0,16},{4,20},{8,24},{12,28},{16,0},{20,4},{24,8},{28,12},{1,17},{... | collective-permute-start | bytes 196616 | tf_op jit(solution)/shard_map/ppermute | solution.py:656
  69.9 0.5 collective-permute-start.17
  70.4 0.8 collective-permute-done.15.rest_1_
  71.2 1.5 %collective-permute-done.16.rest_2_ = f32[32,512]{1,0:T(8,128)S(1)} collective-permute-done((f32[32,512]{1,0:T(8,128)S(1)}, f32[32,512]{1,0:T(8,128)S(1)}, u32[]{:S(2)}, u32[]{:S(2)}) %collective-permute-start.16) | collective-permute-done | bytes 65568 | tf_op jit(solution)/shard_map/ppermute | solution.py:656
  72.6 2.4 %collective-permute-done.17.rest_3_ = f32[32,512]{1,0:T(8,128)S(1)} collective-permute-done((f32[32,512]{1,0:T(8,128)S(1)}, f32[32,512]{1,0:T(8,128)S(1)}, u32[]{:S(2)}, u32[]{:S(2)}) %collective-permute-start.17) | collective-permute-done | bytes 65568 | tf_op jit(solution)/shard_map/ppermute | solution.py:656
  75.1 0.4 shard_map.107
  75.5 8.9 %all_gather.7.mixed = f32[256,512]{1,0:T(8,128)S(1)} all-gather(f32[32,512]{1,0:T(8,128)S(1)} %shard_map.107), channel_id=1, replica_groups=mesh['lon'=8,'lat'=4] {'lon'}, dimensions={0}, use_global_device_ids=true | all-gather | bytes 589824 | tf_op jit(solution)/shard_map/all_gather | solution.py:675
  84.4 1.8 %shard_map.108 = bf16[4,1024,128]{2,1,0:T(8,128)(2,1)} custom-call(bf16[7,560,256]{2,1,0:T(8,128)(2,1)S(1)} %get-tuple-element.65.state, bf16[4,528,256]{2,1,0:T(8,128)(2,1)S(1)} %get-tuple-element.70.hidden, f32[256,512]{1,0:T(8,128)S(1)} %all_gather.7.mixed, bf16[2,528,256]{2,1,0:T(8,128)(2,1)S(1)} %shard_map.96.after.inverse), custom_call_target="tpu_custom_call" | custom-call | tf_op jit(solution)/shard_map/pallas_call | solution.py:553
  (31 shorter events, 0.2 us)
Async XLA Ops:
  0.0 1.2 %copy-start = (bf16[4,1024,128]{2,1,0:T(8,128)(2,1)S(1)}, bf16[4,1024,128]{2,1,0:T(8,128)(2,1)}, u32[]{:S(2)}) copy-start(bf16[4,1024,128]{2,1,0:T(8,128)(2,1)} %own.1) | copy-start | bytes 3145732
  1.3 6.8 %copy-start.9 = (f32[2,3,128]{2,0,1:T(2,128)S(1)}, f32[2,3,128]{2,0,1:T(2,128)}, u32[]{:S(2)}) copy-start(f32[2,3,128]{2,0,1:T(2,128)} %param.11) | copy-start | bytes 9220
  1.3 13.5 %copy-start.5 = (f32[2,2,528,256]{3,2,1,0:T(8,128)S(1)}, f32[2,2,528,256]{3,2,1,0:T(8,128)}, u32[]{:S(2)}) copy-start(f32[2,2,528,256]{3,2,1,0:T(8,128)} %constant.8.clone.parts) | copy-start | bytes 6488068
  1.3 13.5 %copy-start.7 = (f32[8,2,256]{2,1,0:T(2,128)S(1)}, f32[8,2,256]{2,1,0:T(2,128)}, u32[]{:S(2)}) copy-start(f32[8,2,256]{2,1,0:T(2,128)} %constant.9.clone.phase) | copy-start | bytes 49156
  1.3 21.2 %collective-permute-start = (bf16[3,1024,128]{2,1,0:T(8,128)(2,1)S(1)}, bf16[3,1024,128]{2,1,0:T(8,128)(2,1)S(1)}, u32[]{:S(2)}, u32[]{:S(2)}) collective-permute-start(bf16[3,1024,128]{2,1,0:T(8,128)(2,1)S(1)} %shard_map.91.rest_0_), channel_id=1, source_target_pairs={{0,1},{2,3},{1,0},{3,2},{4,5},{6,7},{5,4},{7,6},{8,9},{10,11},{9,8... | collective-permute-start | bytes 2359304 | tf_op jit(solution)/shard_map/ppermute | solution.py:544
  4.5 10.4 %copy-start.1 = (bf16[4,1024,128]{2,1,0:T(8,128)(2,1)S(1)}, bf16[4,1024,128]{2,1,0:T(8,128)(2,1)}, u32[]{:S(2)}) copy-start(bf16[4,1024,128]{2,1,0:T(8,128)(2,1)} %own.1) | copy-start | bytes 3145732
  4.5 10.4 %copy-start.8 = (bf16[2,3,3,3,128,128]{5,4,3,2,1,0:T(8,128)(2,1)S(1)}, bf16[2,3,3,3,128,128]{5,4,3,2,1,0:T(8,128)(2,1)}, u32[]{:S(2)}) copy-start(bf16[2,3,3,3,128,128]{5,4,3,2,1,0:T(8,128)(2,1)} %kernels.1) | copy-start | bytes 5308420
  4.5 20.0 %collective-permute-start.4 = (bf16[3,1024,128]{2,1,0:T(8,128)(2,1)S(1)}, bf16[3,1024,128]{2,1,0:T(8,128)(2,1)S(1)}, u32[]{:S(2)}, u32[]{:S(2)}) collective-permute-start(bf16[3,1024,128]{2,1,0:T(8,128)(2,1)S(1)} %shard_map.92.after), channel_id=1, source_target_pairs={{1,2},{2,1},{5,6},{6,5},{9,10},{10,9},{13,14},{14,13},{17,18},{18,... | collective-permute-start | bytes 2359304 | tf_op jit(solution)/shard_map/ppermute | solution.py:544
  5.4 4.1 %collective-permute-start.1 = (bf16[4,16,128]{2,1,0:T(8,128)(2,1)S(1)}, bf16[4,16,128]{2,1,0:T(8,128)(2,1)S(1)}, u32[]{:S(2)}, u32[]{:S(2)}) collective-permute-start(bf16[4,16,128]{2,1,0:T(8,128)(2,1)S(1)} %get-tuple-element.41), channel_id=1, source_target_pairs={{0,4},{4,8},{8,12},{12,16},{16,20},{20,24},{24,28},{28,0},{1,5},{5... | collective-permute-start | bytes 49160 | tf_op jit(solution)/shard_map/ppermute | solution.py:598
  5.5 4.1 %collective-permute-start.2 = (bf16[4,16,128]{2,1,0:T(8,128)(2,1)S(1)}, bf16[4,16,128]{2,1,0:T(8,128)(2,1)S(1)}, u32[]{:S(2)}, u32[]{:S(2)}) collective-permute-start(bf16[4,16,128]{2,1,0:T(8,128)(2,1)S(1)} %get-tuple-element.42), channel_id=1, source_target_pairs={{4,0},{8,4},{12,8},{16,12},{20,16},{24,20},{28,24},{0,28},{5,1},{9... | collective-permute-start | bytes 49160 | tf_op jit(solution)/shard_map/ppermute | solution.py:599
  9.6 12.9 %collective-permute-start.3 = (bf16[3,32,128]{2,1,0:T(8,128)(2,1)S(1)}, bf16[3,32,128]{2,1,0:T(8,128)(2,1)S(1)}, u32[]{:S(2)}, u32[]{:S(2)}) collective-permute-start(bf16[3,32,128]{2,1,0:T(8,128)(2,1)S(1)} %get-tuple-element.43.near), channel_id=1, source_target_pairs={{0,1},{2,3},{1,0},{3,2},{4,5},{6,7},{5,4},{7,6},{8,9},{10,11},{9,8... | collective-permute-start | bytes 73736 | tf_op jit(solution)/shard_map/ppermute | solution.py:544
  14.1 10.4 %collective-permute-start.5 = (bf16[3,32,128]{2,1,0:T(8,128)(2,1)S(1)}, bf16[3,32,128]{2,1,0:T(8,128)(2,1)S(1)}, u32[]{:S(2)}, u32[]{:S(2)}) collective-permute-start(bf16[3,32,128]{2,1,0:T(8,128)(2,1)S(1)} %shard_map.95.after), channel_id=1, source_target_pairs={{1,2},{2,1},{5,6},{6,5},{9,10},{10,9},{13,14},{14,13},{17,18},{18,... | collective-permute-start | bytes 73736 | tf_op jit(solution)/shard_map/ppermute | solution.py:544
  22.5 2.0 %copy-start.2 = (bf16[2,256,1056]{2,1,0:T(8,128)(2,1)S(1)}, bf16[2,256,1056]{2,1,0:T(8,128)(2,1)}, u32[]{:S(2)}) copy-start(bf16[2,256,1056]{2,1,0:T(8,128)(2,1)} %constant.10.clone.forward) | copy-start | bytes 3244036
  24.5 13.4 %copy-start.3 = (bf16[2,16,128,128]{3,2,1,0:T(8,128)(2,1)S(1)}, bf16[2,16,128,128]{3,2,1,0:T(8,128)(2,1)}, u32[]{:S(2)}) copy-start(bf16[2,16,128,128]{3,2,1,0:T(8,128)(2,1)} %real.3) | copy-start | bytes 3145732
  24.6 13.4 %copy-start.4 = (bf16[2,16,128,128]{3,2,1,0:T(8,128)(2,1)S(1)}, bf16[2,16,128,128]{3,2,1,0:T(8,128)(2,1)}, u32[]{:S(2)}) copy-start(bf16[2,16,128,128]{3,2,1,0:T(8,128)(2,1)} %imag.3) | copy-start | bytes 3145732
  24.6 13.4 %copy-start.6 = (bf16[8,64,128]{2,1,0:T(8,128)(2,1)S(1)}, bf16[8,64,128]{2,1,0:T(8,128)(2,1)}, u32[]{:S(2)}) copy-start(bf16[8,64,128]{2,1,0:T(8,128)(2,1)} %constant.11.clone.turn) | copy-start | bytes 393220
  28.8 1.6 %collective-permute-start.7 = (f32[128,512]{1,0:T(8,128)S(1)}, f32[128,512]{1,0:T(8,128)S(1)}, u32[]{:S(2)}, u32[]{:S(2)}) collective-permute-start(f32[128,512]{1,0:T(8,128)S(1)} %get-tuple-element.54), channel_id=1, source_target_pairs={{0,4},{4,0},{8,12},{12,8},{16,20},{20,16},{24,28},{28,24},{1,5},{5... | collective-permute-start | bytes 786440 | tf_op jit(solution)/shard_map/ppermute | solution.py:656
  30.5 7.4 %collective-permute-start.10 = (f32[32,512]{1,0:T(8,128)S(1)}, f32[32,512]{1,0:T(8,128)S(1)}, u32[]{:S(2)}, u32[]{:S(2)}) collective-permute-start(f32[32,512]{1,0:T(8,128)S(1)} %get-tuple-element.58), channel_id=1, source_target_pairs={{0,24},{4,28},{8,16},{12,20},{16,8},{20,12},{24,0},{28,4},{1,25},{... | collective-permute-start | bytes 196616 | tf_op jit(solution)/shard_map/ppermute | solution.py:656
  33.1 4.7 %collective-permute-start.8 = (f32[32,512]{1,0:T(8,128)S(1)}, f32[32,512]{1,0:T(8,128)S(1)}, u32[]{:S(2)}, u32[]{:S(2)}) collective-permute-start(f32[32,512]{1,0:T(8,128)S(1)} %get-tuple-element.56), channel_id=1, source_target_pairs={{0,8},{4,12},{8,0},{12,4},{16,24},{20,28},{24,16},{28,20},{1,9},{5... | collective-permute-start | bytes 196616 | tf_op jit(solution)/shard_map/ppermute | solution.py:656
  33.7 4.3 %collective-permute-start.9 = (f32[32,512]{1,0:T(8,128)S(1)}, f32[32,512]{1,0:T(8,128)S(1)}, u32[]{:S(2)}, u32[]{:S(2)}) collective-permute-start(f32[32,512]{1,0:T(8,128)S(1)} %get-tuple-element.57), channel_id=1, source_target_pairs={{0,16},{4,20},{8,24},{12,28},{16,0},{20,4},{24,8},{28,12},{1,17},{... | collective-permute-start | bytes 196616 | tf_op jit(solution)/shard_map/ppermute | solution.py:656
  34.0 24.2 %collective-permute-start.6 = (bf16[3,528,256]{2,1,0:T(8,128)(2,1)S(1)}, bf16[3,528,256]{2,1,0:T(8,128)(2,1)S(1)}, u32[]{:S(2)}, u32[]{:S(2)}) collective-permute-start(bf16[3,528,256]{2,1,0:T(8,128)(2,1)S(1)} %get-tuple-element.52), channel_id=1, source_target_pairs={{0,1},{2,3},{1,0},{3,2},{4,5},{6,7},{5,4},{7,6},{8,9},{10,11},{9,8... | collective-permute-start | bytes 2433032 | tf_op jit(solution)/shard_map/ppermute | solution.py:544
  37.1 23.4 %collective-permute-start.13 = (bf16[3,528,256]{2,1,0:T(8,128)(2,1)S(1)}, bf16[3,528,256]{2,1,0:T(8,128)(2,1)S(1)}, u32[]{:S(2)}, u32[]{:S(2)}) collective-permute-start(bf16[3,528,256]{2,1,0:T(8,128)(2,1)S(1)} %get-tuple-element.67), channel_id=1, source_target_pairs={{1,2},{2,1},{5,6},{6,5},{9,10},{10,9},{13,14},{14,13},{17,18},{18,... | collective-permute-start | bytes 2433032 | tf_op jit(solution)/shard_map/ppermute | solution.py:544
  47.7 9.0 %collective-permute-start.11 = (bf16[256,384]{1,0:T(8,128)(2,1)S(1)}, bf16[256,384]{1,0:T(8,128)(2,1)S(1)}, u32[]{:S(2)}, u32[]{:S(2)}) collective-permute-start(bf16[256,384]{1,0:T(8,128)(2,1)S(1)} %shard_map.102), channel_id=1, source_target_pairs={{0,1},{2,3},{1,0},{3,2},{5,6},{6,5},{8,9},{10,11},{9,8},{11,10},{1... | collective-permute-start | bytes 589832 | tf_op jit(solution)/shard_map/ppermute | solution.py:685
  56.7 1.4 %collective-permute-start.12 = (bf16[256,384]{1,0:T(8,128)(2,1)S(1)}, bf16[256,384]{1,0:T(8,128)(2,1)S(1)}, u32[]{:S(2)}, u32[]{:S(2)}) collective-permute-start(bf16[256,384]{1,0:T(8,128)(2,1)S(1)} %collective-permute-done.11.mine), channel_id=1, source_target_pairs={{0,4},{4,0},{8,12},{12,8},{16,20},{20,16},{24,28},{28,24},{1,5},{5... | collective-permute-start | bytes 589832 | tf_op jit(solution)/shard_map/ppermute | solution.py:656
  65.2 1.6 %collective-permute-start.14 = (f32[128,512]{1,0:T(8,128)S(1)}, f32[128,512]{1,0:T(8,128)S(1)}, u32[]{:S(2)}, u32[]{:S(2)}) collective-permute-start(f32[128,512]{1,0:T(8,128)S(1)} %get-tuple-element.72), channel_id=1, source_target_pairs={{0,4},{4,0},{8,12},{12,8},{16,20},{20,16},{24,28},{28,24},{1,5},{5... | collective-permute-start | bytes 786440 | tf_op jit(solution)/shard_map/ppermute | solution.py:656
  66.8 4.3 %collective-permute-start.15 = (f32[32,512]{1,0:T(8,128)S(1)}, f32[32,512]{1,0:T(8,128)S(1)}, u32[]{:S(2)}, u32[]{:S(2)}) collective-permute-start(f32[32,512]{1,0:T(8,128)S(1)} %get-tuple-element.74), channel_id=1, source_target_pairs={{0,8},{4,12},{8,0},{12,4},{16,24},{20,28},{24,16},{28,20},{1,9},{5... | collective-permute-start | bytes 196616 | tf_op jit(solution)/shard_map/ppermute | solution.py:656
  68.4 4.3 %collective-permute-start.16 = (f32[32,512]{1,0:T(8,128)S(1)}, f32[32,512]{1,0:T(8,128)S(1)}, u32[]{:S(2)}, u32[]{:S(2)}) collective-permute-start(f32[32,512]{1,0:T(8,128)S(1)} %get-tuple-element.75), channel_id=1, source_target_pairs={{0,16},{4,20},{8,24},{12,28},{16,0},{20,4},{24,8},{28,12},{1,17},{... | collective-permute-start | bytes 196616 | tf_op jit(solution)/shard_map/ppermute | solution.py:656
  69.9 5.2 %collective-permute-start.17 = (f32[32,512]{1,0:T(8,128)S(1)}, f32[32,512]{1,0:T(8,128)S(1)}, u32[]{:S(2)}, u32[]{:S(2)}) collective-permute-start(f32[32,512]{1,0:T(8,128)S(1)} %get-tuple-element.76), channel_id=1, source_target_pairs={{0,24},{4,28},{8,16},{12,20},{16,8},{20,12},{24,0},{28,4},{1,25},{... | collective-permute-start | bytes 196616 | tf_op jit(solution)/shard_map/ppermute | solution.py:656
